TPU v7x, 32 devices: a whole 2x2x4 slice. The times are simulated.
32 devices in a mesh: leaf: 4 (over x, core), turn: 8 (over z, y).
Axes of the slice: x: 2, y: 2, z: 4, core: 2. Of those that a mesh axis runs over, the one named last changes fastest.
Arguments:
- echoes: bfloat16 [2048, 64, 256], P(('leaf', 'turn')), may hold values from -6 to 6
- chirp: bfloat16 [2, 128], replicated, may hold values from -0.375 to 0.375
- taps: int32 [2, 2, 128, 8], replicated, may hold values from 0 to 127, as said below
- slots: int32 [4, 8], P('leaf'), may hold values from 0 to 7, each once within a row
Outputs:
- image: bfloat16 [128, 64, 256], P('leaf', 'turn')
Inputs may be any that keep to these rules, and one draw needn't show every extreme that they name: Each row of taps is 8 consecutive beam indices starting at a - 4 + s with s from -3 to 3, clipped to the beams. Each row of slots is a permutation.
All inputs are finite; a program needn't handle non-finite values.
Results may differ from a plain program's by a relative error of at most 0.008.
Values may be sent and summed in bfloat16 or wider, within the bound.
No kernel may reach another device: no remote copies, remote signals or barrier semaphores. Data moves between devices by JAX's collectives and lax.ppermute only.
A program may use at most 128 MiB of HBM per device.

v0:
```python
import math

import jax
import jax.numpy as jnp
from jax import lax
from jax.sharding import PartitionSpec as P

SUBP = 64


WEIGHTS = (-1.0 / 32, 3.0 / 32, -7.0 / 32, 21.0 / 32, 21.0 / 32, -7.0 / 32, 3.0 / 32, -1.0 / 32)


def swapped(array, axis, stride):
    return lax.ppermute(array, axis, [(i, i ^ 1 << stride) for i in range(lax.axis_size(axis))])


def chirp_matrices(chirp):
    width = chirp.shape[1]
    rows = jnp.arange(width, dtype=jnp.int32)[:, None]
    cols = jnp.arange(width, dtype=jnp.int32)[None, :]
    offset = jnp.remainder(rows - cols, width)
    picks = (offset[:, :, None] == jnp.arange(width, dtype=jnp.int32)[None, None, :]).astype(
        jnp.float32
    )
    table = jnp.einsum(
        "jik,ck->cji", picks, chirp.astype(jnp.float32), precision=lax.Precision.HIGHEST
    )
    lower = rows >= cols

    def complex_block(mask):
        real_part = jnp.where(mask, table[0], 0.0)
        imag_part = jnp.where(mask, table[1], 0.0)
        upper_half = jnp.concatenate([real_part, imag_part], axis=1)
        lower_half = jnp.concatenate([-imag_part, real_part], axis=1)
        return jnp.concatenate([upper_half, lower_half], axis=0).astype(jnp.bfloat16)

    return (complex_block(lower), complex_block(jnp.logical_not(lower)))


def compress(blocks, following, first_matrix, second_matrix):
    width = blocks.shape[-1]
    total = jnp.dot(blocks.reshape(-1, width), first_matrix, preferred_element_type=jnp.float32)
    total = total + jnp.dot(
        following.reshape(-1, width), second_matrix, preferred_element_type=jnp.float32
    )
    return total.astype(jnp.bfloat16).reshape(blocks.shape)


def steering(slot_row, beams, sub_len):
    count = slot_row.shape[0]
    beam = jnp.arange(beams, dtype=jnp.int32)[:, None, None]
    place = jnp.arange(sub_len, dtype=jnp.int32)[None, None, :]
    slot = slot_row[None, :, None]
    period = 8 * sub_len
    phase_int = jnp.remainder(
        (2 * beam + 1 - beams) * (2 * place + 1 - sub_len)
        + 3 * (beam + 1) * (2 * slot + 1) * (2 * place + 1),
        period,
    )
    angle = phase_int.astype(jnp.float32) * (2.0 * math.pi / period)
    scale = 1.0 / math.sqrt(2.0 * count * sub_len)
    cos_part = (jnp.cos(angle) * scale).reshape(beams, count * sub_len)
    sin_part = (jnp.sin(angle) * scale).reshape(beams, count * sub_len)
    first = jnp.stack([cos_part, -sin_part], axis=1)
    second = jnp.stack([sin_part, cos_part], axis=1)
    return jnp.stack([first, second], axis=1).astype(jnp.bfloat16)


def backproject(data, steer):
    pulses, blocks, width = data.shape
    split = data.reshape(pulses, blocks, 2, width // 2)
    out = jnp.einsum("aecp,pbcj->abej", steer, split, preferred_element_type=jnp.float32)
    return out.astype(jnp.bfloat16).reshape(steer.shape[0], blocks, width)


def merge_step(level_taps, level, side, first_block, child):
    beams, blocks, width = child.shape
    half = width // 2
    weights = jnp.array(WEIGHTS, jnp.float32)
    cells = jnp.arange(beams, dtype=jnp.int32)
    beam = cells[:, None, None]
    bins = (first_block * half + jnp.arange(blocks * half, dtype=jnp.int32)).reshape(
        1, blocks, half
    )
    picks = (level_taps[side][:, :, None] == cells[None, None, :]).astype(jnp.float32)
    matrix = jnp.einsum("atk,t->ak", picks, weights, precision=lax.Precision.HIGHEST)
    moved = jnp.dot(matrix, child.reshape(beams, -1), precision=lax.Precision.HIGHEST).reshape(
        beams, blocks, 2, half
    )
    sign = 2 * side - 1
    phase_int = jnp.remainder(
        (2 * beam + 1 - beams) * (bins + 1) * (sign * (level + 2)) + beam * beam * (side + 1), 4096
    )
    angle = phase_int.astype(jnp.float32) * (2.0 * math.pi / 4096)
    cos_part = jnp.cos(angle)
    sin_part = jnp.sin(angle)
    real_part = cos_part * moved[:, :, 0] - sin_part * moved[:, :, 1]
    imag_part = cos_part * moved[:, :, 1] + sin_part * moved[:, :, 0]
    return jnp.stack([real_part, imag_part], axis=2).reshape(beams, blocks, width)


def merge_pair(level_taps, level, first_block, left, right):
    return merge_step(level_taps, level, 0, first_block, left) + merge_step(
        level_taps, level, 1, first_block, right
    )


def per_device(echoes, chirp, taps, slots):
    first_matrix, second_matrix = chirp_matrices(chirp)
    width = echoes.shape[2]
    following = jnp.concatenate(
        [echoes[:, 1:], jnp.zeros((echoes.shape[0], 1, width), jnp.bfloat16)], axis=1
    )
    compressed = compress(echoes, following, first_matrix, second_matrix)
    tile_data = lax.all_to_all(compressed, "turn", split_axis=1, concat_axis=0, tiled=True)
    beams = taps.shape[2]
    image = backproject(tile_data, steering(slots[0], beams, SUBP))
    first_block = lax.axis_index("turn") * tile_data.shape[1]
    levels = lax.axis_size("leaf").bit_length() - 1
    position = lax.axis_index("leaf")
    own_rows = beams // lax.axis_size("leaf")
    current = image.astype(jnp.float32)
    for level in range(levels):
        sibling = swapped(current, "leaf", level)
        upper = position >> level & 1 == 1
        left = jnp.where(upper, sibling, current)
        right = jnp.where(upper, current, sibling)
        current = merge_pair(taps[level], level, first_block, left, right)
    result = lax.dynamic_slice_in_dim(current, position * own_rows, own_rows, 0)
    return result.astype(jnp.bfloat16)


def solution(mesh):
    placed = (P(("leaf", "turn"), None, None), P(), P(), P("leaf", None))
    return jax.shard_map(
        per_device, mesh=mesh, in_specs=placed, out_specs=P("leaf", "turn", None), check_vma=False
    )
```

profile of v0, /device:TPU:0, one launch (start us, length us, event | category | flops | bytes accessed | tf_op | source)
XLA Modules:
  0.0 116.0 jit_solution(12833916832826076247)
XLA Ops:
  0.0 0.6 copy-done
  0.7 3.7 %fusion.14 = f32[2,128,128]{2,0,1:T(2,128)S(1)} fusion(s32[128,128]{1,0:T(8,128)S(1)} %add_select_fusion.5, bf16[2,128]{1,0:T(2,128)(2,1)S(1)} %copy-done), kind=kOutput, calls=%fused_computation.15 | convolution fusion | flops 10485760 | bytes 197120 | tf_op jit(solution)/shard_map/jik,ck->cji/dot_general | solution.py:26
  4.5 1.3 %slice.69 = bf16[64,63,256]{2,1,0:T(8,128)(2,1)S(1)} slice(bf16[64,64,256]{2,1,0:T(8,128)(2,1)S(1)} %copy-done.1), slice={[0:64], [1:64], [0:256]} | slice | bytes 4128768 | tf_op jit(solution)/shard_map/slice | solution.py:113
  5.8 0.3 concatenate.30
  6.1 0.8 convolution_bitcast_fusion
  6.9 2.1 %fusion.1 = bf16[4096,256]{0,1:T(8,128)(2,1)} fusion(f32[4096,256]{0,1:T(8,128)S(1)} %convolution_bitcast_fusion, bf16[4096,256]{1,0:T(8,128)(2,1)S(1)} %bitcast.120, bf16[128,128]{1,0:T(8,128)(2,1)S(1)} %get-tuple-element.29, bf16[128,128]{1,0:T(8,128)(2,1)S(1)} %get-tuple-element.27, bf16[128,128]{1,0:T(8,128)(2,1)S(1)} %get-tuple-element.40), kind=kOutput, calls=%fused_computation.4 | convolution fusion | flops 539492352 | bytes 8486912 | tf_op jit(solution)/shard_map/dot_general | solution.py:44
  9.0 3.3 %copy.33 = bf16[4096,256]{1,0:T(8,128)(2,1)S(1)} copy(bf16[4096,256]{0,1:T(8,128)(2,1)} %fusion.1) | data formatting | bytes 4194304 | tf_op jit(solution)/shard_map/convert_element_type | solution.py:47
  12.3 2.5 %copy.34 = bf16[64,64,256]{2,0,1:T(8,128)(2,1)} copy(bf16[64,64,256]{2,1,0:T(8,128)(2,1)S(1)} %bitcast.119) | data formatting | bytes 4194304 | tf_op jit(solution)/shard_map/reshape | solution.py:47
  14.8 7.4 %all-to-all-start = ((bf16[64,64,256]{2,0,1:T(8,128)(2,1)}), bf16[64,64,256]{2,0,1:T(8,128)(2,1)S(1)}, u32[]{:S(2)}, u32[]{:S(2)}) async-start(bf16[64,64,256]{2,0,1:T(8,128)(2,1)} %copy.34), calls=%async_computation | async-start | bytes 4194304 | tf_op jit(solution)/shard_map/all_to_all | solution.py:116
  22.3 0.1 copy.38
  22.8 1.0 negate_convert_fusion
  23.8 1.0 fusion.52
  24.9 45.6 %all-to-all-done = bf16[64,64,256]{2,0,1:T(8,128)(2,1)S(1)} async-done(((bf16[64,64,256]{2,0,1:T(8,128)(2,1)}), bf16[64,64,256]{2,0,1:T(8,128)(2,1)S(1)}, u32[]{:S(2)}, u32[]{:S(2)}) %all-to-all-start) | async-done | bytes 2097184 | tf_op jit(solution)/shard_map/all_to_all | solution.py:116
  70.5 1.3 %copy.36 = bf16[8,64,8,256]{3,2,1,0:T(8,128)(2,1)S(1)} copy(bf16[8,64,8,256]{3,1,2,0:T(8,128)(2,1)S(1)} %bitcast.118) | data formatting | bytes 4194304 | tf_op jit(solution)/shard_map/all_to_all | solution.py:116
  71.8 0.9 fusion.11
  73.0 0.5 fusion.34
  73.5 0.5 fusion.35
  74.0 1.4 %collective-permute-done = f32[128,8,256]{0,2,1:T(8,128)S(1)} collective-permute-done((f32[128,8,256]{0,2,1:T(8,128)S(1)}, f32[128,8,256]{0,2,1:T(8,128)S(1)}, u32[]{:S(2)}, u32[]{:S(2)}) %collective-permute-start) | collective-permute-done | bytes 1048608 | tf_op jit(solution)/shard_map/ppermute | solution.py:15
  75.4 0.2 broadcast_select_fusion
  75.6 1.0 fusion.83
  76.7 1.0 fusion.84
  77.7 4.7 %multiply_subtract_fusion.2 = (f32[128,8,1,128]{0,3,2,1:T(8,128)S(1)}, f32[128,8,1,128]{0,3,2,1:T(8,128)S(1)}, f32[128,8,1,128]{0,3,2,1:T(8,128)S(1)}, f32[128,8,1,128]{0,3,2,1:T(8,128)S(1)}) fusion(f32[128,8,2,128]{0,3,2,1:T(8,128)S(1)} %fusion.84, s32[128]{0:T(128)S(1)} %broadcast_multiply_fusion.2, s32[8,128]{1,0:T(8,128)S(1)} %add_add_fusion, ...), kind=kLoop, calls=%fused_computation.55 | loop fusion | flops 5636096 | bytes 4199936 | tf_op jit(solution)/shard_map/sub | solution.py:98
  82.5 1.6 %collective-permute-start.1 = (f32[128,8,256]{0,2,1:T(8,128)S(1)}, f32[128,8,256]{0,2,1:T(8,128)S(1)}, u32[]{:S(2)}, u32[]{:S(2)}) collective-permute-start(f32[128,8,256]{0,2,1:T(8,128)S(1)} %bitcast.121), channel_id=1, source_target_pairs={{0,16},{8,24},{16,0},{24,8},{1,17},{9,25},{17,1},{25,9},{2,18},{10... | collective-permute-start | bytes 3145736 | tf_op jit(solution)/shard_map/ppermute | solution.py:15
  84.3 0.5 fusion.33
  84.7 0.5 fusion.36
  85.2 22.6 %collective-permute-done.1 = f32[128,8,256]{0,2,1:T(8,128)S(1)} collective-permute-done((f32[128,8,256]{0,2,1:T(8,128)S(1)}, f32[128,8,256]{0,2,1:T(8,128)S(1)}, u32[]{:S(2)}, u32[]{:S(2)}) %collective-permute-start.1) | collective-permute-done | bytes 1048608 | tf_op jit(solution)/shard_map/ppermute | solution.py:15
  107.8 0.2 broadcast_select_fusion.2
  108.0 1.0 fusion.85
  109.0 1.0 fusion.86
  110.0 4.7 %multiply_subtract_fusion = (f32[128,8,1,128]{0,3,2,1:T(8,128)S(1)}, f32[128,8,1,128]{0,3,2,1:T(8,128)S(1)}, f32[128,8,1,128]{0,3,2,1:T(8,128)S(1)}, f32[128,8,1,128]{0,3,2,1:T(8,128)S(1)}) fusion(f32[128,8,2,128]{0,3,2,1:T(8,128)S(1)} %fusion.86, s32[128]{0:T(128)S(1)} %broadcast_multiply_fusion.2, s32[8,128]{1,0:T(8,128)S(1)} %add_add_fusion, ...), kind=kLoop, calls=%fused_computation.50 | loop fusion | flops 5636096 | bytes 4199936 | tf_op jit(solution)/shard_map/sub | solution.py:98
  114.9 0.2 constant_dynamic-slice_fusion
  115.1 0.9 copy.58
  (36 shorter events, 1.4 us)
Async XLA Ops:
  0.0 0.7 copy-start
  0.0 4.5 %copy-start.1 = (bf16[64,64,256]{2,1,0:T(8,128)(2,1)S(1)}, bf16[64,64,256]{2,1,0:T(8,128)(2,1)}, u32[]{:S(2)}) copy-start(bf16[64,64,256]{2,1,0:T(8,128)(2,1)} %param.8) | copy-start | bytes 6291460
  14.8 7.7 %copy-start.3 = (s32[1,8]{1,0:T(1,128)S(1)}, s32[1,8]{1,0:T(1,128)}, u32[]{:S(2)}) copy-start(s32[1,8]{1,0:T(1,128)} %param.11) | copy-start | bytes 100
  14.8 55.6 %all-to-all-start = ((bf16[64,64,256]{2,0,1:T(8,128)(2,1)}), bf16[64,64,256]{2,0,1:T(8,128)(2,1)S(1)}, u32[]{:S(2)}, u32[]{:S(2)}) async-start(bf16[64,64,256]{2,0,1:T(8,128)(2,1)} %copy.34), calls=%async_computation | async-start | bytes 4194304 | tf_op jit(solution)/shard_map/all_to_all | solution.py:116
  71.7 1.0 copy-start.2
  71.8 1.3 %copy-start.4 = (f32[8,1,1]{0,1,2:T(1,128)S(1)}, f32[8,1,1]{0,1,2:T(1,128)}, u32[]{:S(2)}) copy-start(f32[8,1,1]{0,1,2:T(1,128)} %constant.115) | copy-start | bytes 100
  72.7 2.7 %collective-permute-start = (f32[128,8,256]{0,2,1:T(8,128)S(1)}, f32[128,8,256]{0,2,1:T(8,128)S(1)}, u32[]{:S(2)}, u32[]{:S(2)}) collective-permute-start(f32[128,8,256]{0,2,1:T(8,128)S(1)} %bitcast.128), channel_id=1, source_target_pairs={{0,8},{8,0},{16,24},{24,16},{1,9},{9,1},{17,25},{25,17},{2,10},{10... | collective-permute-start | bytes 3145736 | tf_op jit(solution)/shard_map/ppermute | solution.py:15
  82.5 25.3 %collective-permute-start.1 = (f32[128,8,256]{0,2,1:T(8,128)S(1)}, f32[128,8,256]{0,2,1:T(8,128)S(1)}, u32[]{:S(2)}, u32[]{:S(2)}) collective-permute-start(f32[128,8,256]{0,2,1:T(8,128)S(1)} %bitcast.121), channel_id=1, source_target_pairs={{0,16},{8,24},{16,0},{24,8},{1,17},{9,25},{17,1},{25,9},{2,18},{10... | collective-permute-start | bytes 3145736 | tf_op jit(solution)/shard_map/ppermute | solution.py:15
where the time goes:
time: 116 us
  waiting for transfers between devices  69.6 us (60%)
  matrix products  13.3 us (11%)
  other arithmetic  12.4 us (11%)
  local copies, waits for them, and re-layouts  11.3 us (10%)
  starting transfers between devices  9.05 us (8%)
    all_to_all x1, waiting for transfers between devices, per_device(): lax.all_to_all(compressed, 'turn', split_axis=1, concat_axis=0, tiled=True)  45.6 us
    ppermute x2, waiting for transfers between devices, swapped(): lax.ppermute(array, axis, [(i, i ^ 1 << stride) for i in range(lax.axis_s...  24 us
    sub x2, other arithmetic, merge_step(): real_part = cos_part * moved[:, :, 0] - sin_part * moved[:, :, 1]  9.44 us
    all_to_all x1, starting transfers between devices, per_device(): lax.all_to_all(compressed, 'turn', split_axis=1, concat_axis=0, tiled=True)  7.42 us
    dot_general x4, matrix products, merge_step(): jnp.dot(matrix, child.reshape(beams, -1), precision=lax.Precision.HIGHEST)  4.01 us
    dot_general x1, matrix products, chirp_matrices(): jnp.einsum('jik,ck->cji', picks, chirp.astype(jnp.float32), precision=lax...  3.66 us
    convert_element_type x1, local copies, waits for them, and re-layouts, compress(): return total.astype(jnp.bfloat16).reshape(blocks.shape)  3.27 us
    reshape x1, local copies, waits for them, and re-layouts, compress(): return total.astype(jnp.bfloat16).reshape(blocks.shape)  2.53 us
  transfers between devices with their start and end apart: 3, of which 3 were waited for; matrix products, arithmetic and copies ran while one was open for 4% of the time, Pallas kernels for 0%

commit v1 on v0

v1 whole, which is shorter than its diff:
```python
import functools
import math

import jax
import jax.numpy as jnp
from jax import lax
from jax.experimental import pallas as pl
from jax.experimental.pallas import tpu as pltpu
from jax.sharding import Mesh, PartitionSpec as P

WEIGHTS = (-1.0 / 32, 3.0 / 32, -7.0 / 32, 21.0 / 32, 21.0 / 32, -7.0 / 32, 3.0 / 32, -1.0 / 32)
PERIOD = 4096


def unit(phase_int, period):
    angle = jnp.remainder(phase_int, period).astype(jnp.float32) * (2.0 * math.pi / period)
    return jnp.cos(angle), jnp.sin(angle)


def compress_kernel(dims, chirp_ref, echo_ref, out_ref, weights, sums, carry):
    leaf, ty, inner, pulses, half = dims
    blocks = leaf * ty * inner

    @pl.when(pl.program_id(0) == 0)
    def _():
        rows = lax.broadcasted_iota(jnp.int32, (half, half), 0)
        cols = lax.broadcasted_iota(jnp.int32, (half, half), 1)
        taps = chirp_ref[...].astype(jnp.float32)
        tables = []
        for c in range(2):
            wide = jnp.broadcast_to(taps[c : c + 1], (half, half))
            tables.append(pltpu.roll(wide, 0, 1, stride=1, stride_axis=0).T)
        for m, mask in enumerate((rows >= cols, rows < cols)):
            re, im = (jnp.where(mask, t, 0.0) for t in tables)
            top = jnp.concatenate([re, im], axis=1)
            low = jnp.concatenate([-im, re], axis=1)
            full = jnp.concatenate([top, low], axis=0)
            weights[:, m * 2 * half : (m + 1) * 2 * half] = full.astype(jnp.bfloat16)
        carry[...] = jnp.zeros_like(carry)

    data = echo_ref[...].reshape(pulses * blocks, 2 * half)
    for n in range(4):
        sums[n] = jnp.dot(
            data, weights[:, n * half : (n + 1) * half], preferred_element_type=jnp.float32
        )
    for y in range(ty):
        for l in range(leaf):
            for i in range(inner):
                b = (y * leaf + l) * inner + i
                for c in range(2):
                    total = sums[c, pl.ds(b, pulses, stride=blocks), :]
                    if b + 1 < blocks:
                        total += sums[2 + c, pl.ds(b + 1, pulses, stride=blocks), :]
                    else:
                        total += carry[c]
                    out_ref[l, y, 0, i, :, c * half : (c + 1) * half] = total.astype(jnp.bfloat16)
    for c in range(2):
        carry[c] = sums[2 + c, pl.ds(0, pulses, stride=blocks), :]


def compress(echoes, chirp, leaf, tz, ty):
    pulses, blocks, width = echoes.shape
    half = width // 2
    inner = blocks // (leaf * tz * ty)
    per = leaf * ty * inner
    return pl.pallas_call(
        functools.partial(compress_kernel, (leaf, ty, inner, pulses, half)),
        grid=(tz,),
        in_specs=[
            pl.BlockSpec((2, half), lambda z: (0, 0)),
            pl.BlockSpec((pulses, per, width), lambda z: (0, tz - 1 - z, 0)),
        ],
        out_specs=pl.BlockSpec(
            (leaf, ty, 1, inner, pulses, width), lambda z: (0, 0, tz - 1 - z, 0, 0, 0)
        ),
        out_shape=jax.ShapeDtypeStruct((leaf, ty, tz, inner, pulses, width), jnp.bfloat16),
        scratch_shapes=[
            pltpu.VMEM((width, 2 * width), jnp.bfloat16),
            pltpu.VMEM((4, pulses * per, half), jnp.float32),
            pltpu.VMEM((2, pulses, half), jnp.float32),
        ],
        compiler_params=pltpu.CompilerParams(vmem_limit_bytes=48 * 2**20),
        cost_estimate=pl.CostEstimate(
            flops=4 * pulses * blocks * width * width,
            bytes_accessed=4 * pulses * blocks * width,
            transcendentals=0,
        ),
        name="compress",
    )(chirp, echoes)


def image_kernel(dims, data_ref, steer_ref, interp_ref, phase_ref, out_ref):
    leaf, ty, inner, pulses, half, beams, levels = dims
    wide = inner * half

    def turned(phase, re, im):
        c, s = phase
        return c * re - s * im, c * im + s * re

    def total(left, right):
        return left[0] + right[0], left[1] + right[1]

    current = []
    cos, sin = phase_ref[0, 0], phase_ref[0, 1]
    for l in range(leaf):
        parts = []
        for y in range(ty):
            for c in range(2):
                cols = slice(c * half, (c + 1) * half)
                parts.append(
                    jnp.concatenate([data_ref[l, y, 0, i, :, cols] for i in range(inner)], axis=1)
                )
        raw = jnp.dot(
            steer_ref[l], jnp.concatenate(parts, axis=0), preferred_element_type=jnp.float32
        )
        side = turned((cos, sin if l & 1 else -sin), raw[:beams], raw[beams:])
        if l & 1:
            current[-1] = total(current[-1], side)
        else:
            current.append(side)
    for level in range(1, levels):
        merged = []
        for n, (re, im) in enumerate(current):
            side = n & 1
            both = jnp.concatenate([re, im], axis=1)
            high = both.astype(jnp.bfloat16)
            low = (both - high.astype(jnp.float32)).astype(jnp.bfloat16)
            moved = jnp.dot(
                interp_ref[level - 1, side],
                jnp.concatenate([high, low], axis=0),
                preferred_element_type=jnp.float32,
            )
            at = 2 + 4 * (level - 1) + 2 * side
            phase = (phase_ref[0, at], phase_ref[0, at + 1])
            moved = turned(phase, moved[:, :wide], moved[:, wide:])
            if side:
                merged[-1] = total(merged[-1], moved)
            else:
                merged.append(moved)
        current = merged
    rows = beams // leaf
    for c in range(2):
        image = current[0][c].astype(jnp.bfloat16)
        for l in range(leaf):
            for i in range(inner):
                out_ref[l, 0, i, :, c * half : (c + 1) * half] = image[
                    l * rows : (l + 1) * rows, i * half : (i + 1) * half
                ]


def backproject(data, steer, interp, phases):
    leaf, ty, tz, inner, pulses, width = data.shape
    half = width // 2
    beams = steer.shape[1] // 2
    levels = leaf.bit_length() - 1
    rows = beams // leaf
    tables = phases.shape[1]
    flops = 4 * beams * leaf * ty * pulses * tz * inner * width
    return pl.pallas_call(
        functools.partial(image_kernel, (leaf, ty, inner, pulses, half, beams, levels)),
        grid=(tz,),
        in_specs=[
            pl.BlockSpec((leaf, ty, 1, inner, pulses, width), lambda z: (0, 0, z, 0, 0, 0)),
            pl.BlockSpec(steer.shape, lambda z: (0, 0, 0)),
            pl.BlockSpec(interp.shape, lambda z: (0, 0, 0, 0)),
            pl.BlockSpec((1, tables, beams, inner * half), lambda z: (z, 0, 0, 0)),
        ],
        out_specs=pl.BlockSpec((leaf, 1, inner, rows, width), lambda z: (0, z, 0, 0, 0)),
        out_shape=jax.ShapeDtypeStruct((leaf, tz, inner, rows, width), jnp.bfloat16),
        compiler_params=pltpu.CompilerParams(vmem_limit_bytes=48 * 2**20),
        cost_estimate=pl.CostEstimate(
            flops=flops, bytes_accessed=2 * data.size + 4 * phases.size, transcendentals=0
        ),
        name="image",
    )(data, steer, interp, phases)


def sum_kernel(dims, parts_ref, out_ref, rows_ref):
    leaf, tz, inner, rows, width = dims
    blocks = leaf * inner
    for l in range(leaf):
        for i in range(inner):
            acc = parts_ref[l, 0, i].astype(jnp.float32)
            for z in range(1, tz):
                acc += parts_ref[l, z, i].astype(jnp.float32)
            for c in range(2):
                cols = slice(c * width // 2, (c + 1) * width // 2)
                rows_ref[c, pl.ds(l * inner + i, rows, stride=blocks), :] = acc[:, cols]
    both = jnp.concatenate([rows_ref[0], rows_ref[1]], axis=1)
    out_ref[...] = both.reshape(rows, blocks, width).astype(jnp.bfloat16)


def reduce_parts(parts):
    leaf, tz, inner, rows, width = parts.shape
    blocks = leaf * inner
    return pl.pallas_call(
        functools.partial(sum_kernel, parts.shape),
        out_shape=jax.ShapeDtypeStruct((rows, blocks, width), jnp.bfloat16),
        scratch_shapes=[pltpu.VMEM((2, rows * blocks, width // 2), jnp.float32)],
        name="sum_parts",
    )(parts)


def interpolation(taps, beams):
    cells = jnp.arange(beams, dtype=jnp.int32)
    weights = jnp.array(WEIGHTS, jnp.float32)
    picks = taps[..., None] == cells
    return jnp.where(picks, weights[:, None], 0.0).sum(axis=-2)


def steering(slots, matrices, beams, pulses, scale):
    leaf, ty = slots.shape
    beam = jnp.arange(beams, dtype=jnp.int32)[None, :, None, None]
    place = jnp.arange(pulses, dtype=jnp.int32)
    slot = slots[:, None, :, None]
    cos, sin = unit(
        (2 * beam + 1 - beams) * (2 * place + 1 - pulses)
        + 3 * (beam + 1) * (2 * slot + 1) * (2 * place + 1),
        8 * pulses,
    )
    pair = jnp.stack([cos * scale, sin * scale], axis=3).astype(jnp.bfloat16)
    pair = pair.reshape(leaf // 2, 2, beams, ty * 2 * pulses)
    moved = jnp.einsum(
        "cab,kcbn->kcan",
        matrices.astype(jnp.bfloat16),
        pair,
        preferred_element_type=jnp.float32,
    ).reshape(leaf, beams, ty, 2, pulses)
    re, im = moved[:, :, :, 0], moved[:, :, :, 1]
    row = jnp.arange(beams, dtype=jnp.int32)
    side = (jnp.arange(leaf, dtype=jnp.int32) & 1)[:, None]
    c, s = (t[:, :, None, None] for t in unit(row * row * (side + 1), PERIOD))
    re, im = c * re - s * im, c * im + s * re
    top = jnp.stack([re, -im], axis=3)
    low = jnp.stack([im, re], axis=3)
    full = jnp.concatenate([top, low], axis=1)
    return full.reshape(leaf, 2 * beams, ty * 2 * pulses).astype(jnp.bfloat16)


def phase_tables(first, steps, tz, inner, half, beams, levels):
    row = jnp.arange(beams, dtype=jnp.int32)[None, :, None]
    place = jnp.arange(inner * half, dtype=jnp.int32)[None, None, :]
    z = jnp.arange(tz, dtype=jnp.int32)[:, None, None]
    bins = first + z * steps + place + 1
    lean = (2 * row + 1 - beams) * bins
    tables = list(unit(2 * lean, PERIOD))
    for level in range(1, levels):
        for side in range(2):
            tables += unit((2 * side - 1) * (level + 2) * lean + row * row * (side + 1), PERIOD)
    return jnp.stack(tables, axis=1)


def per_device(leaf, tz, ty, echoes, chirp, taps, slots):
    pulses, blocks, width = echoes.shape
    half = width // 2
    beams = taps.shape[2]
    levels = leaf.bit_length() - 1
    inner = blocks // (leaf * tz * ty)
    sent = compress(echoes, chirp, leaf, tz, ty)
    data = lax.all_to_all(
        sent.reshape((leaf * ty,) + sent.shape[2:]), ("leaf", "ty"), 0, 0, tiled=True
    ).reshape(sent.shape)

    own_leaf, own_z, own_y = (lax.axis_index(name) for name in ("leaf", "tz", "ty"))
    all_slots = lax.all_gather(slots, "leaf", axis=0, tiled=True)
    own_slots = lax.dynamic_slice_in_dim(all_slots, own_z * ty, ty, 1)
    matrices = interpolation(taps, beams)
    scale = 1.0 / math.sqrt(2.0 * all_slots.shape[1] * pulses)
    steer = steering(own_slots, matrices[0], beams, pulses, scale)
    interp = jnp.concatenate([matrices[1:]] * 2, axis=-1).astype(jnp.bfloat16)
    first = (own_y * leaf + own_leaf) * inner * half
    phases = phase_tables(first, ty * leaf * inner * half, tz, inner, half, beams, levels)

    parts = backproject(data, steer, interp, phases)
    parts = lax.all_to_all(
        parts.reshape((leaf * tz,) + parts.shape[2:]), ("leaf", "tz"), 0, 0, tiled=True
    ).reshape(parts.shape)
    return reduce_parts(parts)


def solution(mesh):
    leaf, turn = mesh.shape["leaf"], mesh.shape["turn"]
    ty = 1 << (turn.bit_length() - 1) // 2
    tz = turn // ty
    fine = Mesh(mesh.devices.reshape(leaf, tz, ty), ("leaf", "tz", "ty"))
    placed = (P(("leaf", "tz", "ty"), None, None), P(), P(), P("leaf", None))
    return jax.shard_map(
        functools.partial(per_device, leaf, tz, ty),
        mesh=fine,
        in_specs=placed,
        out_specs=P("leaf", ("tz", "ty"), None),
        check_vma=False,
    )
```

time: 116 us -> 90.7 us (0.78)
  waiting for transfers between devices: 69.6 us -> 0.01 us
  blocking collectives: 0 us -> 47.2 us
  matrix products: 13.3 us -> 0.23 us
  Pallas kernels: 0 us -> 11.8 us
  other arithmetic: 12.4 us -> 21.3 us
  local copies, waits for them, and re-layouts: 11.3 us -> 4.22 us
  starting transfers between devices: 9.05 us -> 5.31 us
    all_to_all x1, waiting for transfers between devices: 45.6 us -> 0.01 us  [per_device(): lax.all_to_all(sent.reshape((leaf * ty,) + sent.shape[2:]), ('leaf', 'ty'...]
    all_gather x0 -> x1, blocking collectives: none -> 26.6 us  [per_device(): all_slots = lax.all_gather(slots, 'leaf', axis=0, tiled=True)]
    ppermute x2 -> x0, waiting for transfers between devices: 24 us -> none  [swapped(): lax.ppermute(array, axis, [(i, i ^ 1 << stride) for i in range(lax.axis_s...]
    all_to_all x0 -> x1, blocking collectives: none -> 20.6 us  [per_device(): lax.all_to_all(parts.reshape((leaf * tz,) + parts.shape[2:]), ('leaf', 't...]
    unnamed x0 -> x5, other arithmetic: none -> 14.1 us
    dot_general x12 -> x1, matrix products: 13.3 us -> 0.23 us  [steering(): jnp.einsum('cab,kcbn->kcan', matrices.astype(jnp.bfloat16), pair, preferr...]
    pallas_call x0 -> x3, Pallas kernels: none -> 11.8 us  [the longest x1 5.75 us: compress(): pl.pallas_call(functools.partial(compress_kernel, (leaf, ty, inner, pulse...]
    sub x3 -> x2, other arithmetic: 9.45 us -> 0.01 us  [the longest x1 0.01 us: steering(): 2 * place + 1 - pulses]
  transfers between devices with their start and end apart: 3 -> 1, of which waited for: 3 -> 0; matrix products, arithmetic and copies ran while one was open for 4% -> 25% of each run, Pallas kernels for 0% -> 0%
where the time goes in v1:
time: 90.7 us; the launch traced here: 90.3 us
  blocking collectives  47.2 us (52%)
  other arithmetic  21.3 us (23%)
  Pallas kernels  11.8 us (13%)
  starting transfers between devices  5.31 us (6%)
  local copies, waits for them, and re-layouts  4.22 us (5%)
    all_gather x1, blocking collectives, per_device(): all_slots = lax.all_gather(slots, 'leaf', axis=0, tiled=True)  26.6 us
    all_to_all x1, blocking collectives, per_device(): lax.all_to_all(parts.reshape((leaf * tz,) + parts.shape[2:]), ('leaf', 't...  20.6 us
    unnamed x5, other arithmetic  14.1 us
    pallas_call x1, Pallas kernels, compress(): pl.pallas_call(functools.partial(compress_kernel, (leaf, ty, inner, pulse...  5.75 us
    all_to_all x1, starting transfers between devices, per_device(): lax.all_to_all(sent.reshape((leaf * ty,) + sent.shape[2:]), ('leaf', 'ty'...  5.31 us
    pallas_call x1, Pallas kernels, backproject(): pl.pallas_call(functools.partial(image_kernel, (leaf, ty, inner, pulses,...  4.28 us
    unnamed x14, local copies, waits for them, and re-layouts  3.81 us
    another operation x1, other arithmetic, phase_tables(): return jnp.stack(tables, axis=1)  2.85 us
  transfers between devices with their start and end apart: 1, of which 0 were waited for; matrix products, arithmetic and copies ran while one was open for 25% of the time, Pallas kernels for 0%

profile of v1, /device:TPU:0, one launch (start us, length us, event | category | flops | bytes accessed | tf_op | source)
XLA Modules:
  0.0 90.3 jit_solution(6520656653292318191)
XLA Ops:
  0.0 1.6 %copy-done.1 = bf16[64,64,256]{2,1,0:T(8,128)(2,1)S(1)} copy-done((bf16[64,64,256]{2,1,0:T(8,128)(2,1)S(1)}, bf16[64,64,256]{2,1,0:T(8,128)(2,1)}, u32[]{:S(2)}) %copy-start.1) | copy-done | bytes 2097176
  1.6 0.7 copy-done.2
  2.2 5.8 %compress.1 = bf16[4,2,4,2,64,256]{5,4,3,2,1,0:T(8,128)(2,1)S(1)} custom-call(bf16[2,128]{1,0:T(2,128)(2,1)S(1)} %copy-done.2, bf16[64,64,256]{2,1,0:T(8,128)(2,1)S(1)} %copy-done.1), custom_call_target="tpu_custom_call" | custom-call | flops 1073741824 | bytes 4194304 | tf_op jit(solution)/shard_map/compress/pallas_call | solution.py:66
  8.0 0.0 copy-start
  8.0 1.3 %copy-done = bf16[4,2,4,2,64,256]{5,4,3,2,1,0:T(8,128)(2,1)} copy-done((bf16[4,2,4,2,64,256]{5,4,3,2,1,0:T(8,128)(2,1)}, bf16[4,2,4,2,64,256]{5,4,3,2,1,0:T(8,128)(2,1)S(1)}, u32[]{:S(2)}) %copy-start) | copy-done | bytes 2097176
  9.4 5.3 %all-to-all-start = ((bf16[8,4,2,64,256]{4,3,2,1,0:T(8,128)(2,1)}), bf16[8,4,2,64,256]{4,3,2,1,0:T(8,128)(2,1)S(1)}, u32[]{:S(2)}, u32[]{:S(2)}) async-start(bf16[8,4,2,64,256]{4,3,2,1,0:T(8,128)(2,1)} %bitcast.19), calls=%async_computation | async-start | bytes 4194304 | tf_op jit(solution)/shard_map/all_to_all | solution.py:260
  14.7 0.0 copy-done.5
  14.7 26.6 %all-gather = s32[4,1,8]{2,1,0:T(1,128)S(1)} all-gather(s32[1,1,8]{2,1,0:T(1,128)S(1)} %bitcast.25), channel_id=1, replica_groups=mesh['leaf'=4,'tz'=4,'ty'=2] {'leaf'}, dimensions={0}, use_global_device_ids=true | all-gather | bytes 160 | tf_op jit(solution)/shard_map/all_gather | solution.py:265
  41.3 0.1 constant_dynamic-slice_fusion
  41.4 0.1 copy.34
  41.5 0.1 copy.28
  41.6 0.1 copy.29
  41.8 2.6 %select_reduce_fusion = bf16[2,2,128,128]{3,2,1,0:T(8,128)(2,1)S(1)} fusion(f32[8]{0:T(128)S(1)} %copy-done.4, s32[2,2,128,8]{3,2,1,0:T(8,128)S(1)} %copy.29), kind=kLoop, calls=%fused_computation | loop fusion | flops 1507328 | bytes 147488 | tf_op jit(solution)/shard_map/reduce_sum | solution.py:208
  44.4 0.1 broadcast_multiply_fusion.1
  44.4 0.1 broadcast_multiply_fusion
  44.5 1.3 %multiply_convert_fusion.1 = (bf16[4,128,2,1,64]{1,4,3,2,0:T(8,128)(2,1)S(1)}, bf16[4,128,2,1,64]{1,4,3,2,0:T(8,128)(2,1)S(1)}) fusion(s32[64]{0:T(128)S(1)} %fusion.26, s32[4,128,2]{1,2,0:T(2,128)S(1)} %broadcast_multiply_fusion.1, s32[128,64]{0,1:T(8,128)S(1)} %broadcast_multiply_fusion), kind=kLoop, calls=%fused_computation.47 | loop fusion | flops 1245184 | bytes 299264 | tf_op jit(solution)/shard_map/convert.9
  45.8 0.2 convolution_bitcast_fusion
  46.1 0.1 fusion.25
  46.2 0.1 negate_convert_fusion
  46.3 0.1 maximum_maximum_fusion
  46.4 0.2 copy.32.steer_ref
  46.6 0.1 add_add_fusion
  46.7 2.8 %cosine_dynamic-update-slice_fusion.2 = f32[4,6,128,256]{3,2,1,0:T(8,128)} fusion(s32[4,256]{1,0:T(4,128)S(1)} %add_add_fusion, s32[128]{0:T(128)S(1)} %get-tuple-element.12), kind=kLoop, calls=%fused_computation.34 | loop fusion | flops 1966079 | bytes 528896
  49.5 2.8 %sine_dynamic-update-slice_fusion.2 = f32[4,6,128,256]{3,2,1,0:T(8,128)} fusion(f32[4,6,128,256]{3,2,1,0:T(8,128)} %cosine_dynamic-update-slice_fusion.2, s32[4,256]{1,0:T(4,128)S(1)} %add_add_fusion, s32[128]{0:T(128)S(1)} %get-tuple-element.12), kind=kLoop, calls=%fused_computation.33 | loop fusion | flops 1966080 | bytes 528896
  52.3 2.8 %cosine_dynamic-update-slice_fusion.1 = f32[4,6,128,256]{3,2,1,0:T(8,128)} fusion(f32[4,6,128,256]{3,2,1,0:T(8,128)} %sine_dynamic-update-slice_fusion.2, s32[128]{0:T(128)S(1)} %iota_multiply_fusion.1, s32[4,256]{1,0:T(4,128)S(1)} %add_add_fusion, s32[128]{0:T(128)S(1)} %get-tuple-element.12), kind=kLoop, calls=%fused_computation.32 | loop fusion | flops 2097152 | bytes 529408
  55.1 2.8 %sine_dynamic-update-slice_fusion.1 = f32[4,6,128,256]{3,2,1,0:T(8,128)} fusion(f32[4,6,128,256]{3,2,1,0:T(8,128)} %cosine_dynamic-update-slice_fusion.1, s32[128]{0:T(128)S(1)} %iota_multiply_fusion.1, s32[4,256]{1,0:T(4,128)S(1)} %add_add_fusion, s32[128]{0:T(128)S(1)} %get-tuple-element.12), kind=kLoop, calls=%fused_computation.31 | loop fusion | flops 2097152 | bytes 529408
  57.9 2.8 %cosine_dynamic-update-slice_fusion = f32[4,6,128,256]{3,2,1,0:T(8,128)} fusion(f32[4,6,128,256]{3,2,1,0:T(8,128)} %sine_dynamic-update-slice_fusion.1, s32[128]{0:T(128)S(1)} %get-tuple-element.13, s32[4,256]{1,0:T(4,128)S(1)} %add_add_fusion, s32[128]{0:T(128)S(1)} %get-tuple-element.12), kind=kLoop, calls=%fused_computation.30 | loop fusion | flops 2097152 | bytes 529408
  60.8 2.8 %sine_dynamic-update-slice_fusion.phase_ref = f32[4,6,128,256]{3,2,1,0:T(8,128)} fusion(f32[4,6,128,256]{3,2,1,0:T(8,128)} %cosine_dynamic-update-slice_fusion, s32[128]{0:T(128)S(1)} %get-tuple-element.13, s32[4,256]{1,0:T(4,128)S(1)} %add_add_fusion, s32[128]{0:T(128)S(1)} %get-tuple-element.12), kind=kLoop, calls=%fused_computation.29 | loop fusion | flops 2097152 | bytes 529408 | tf_op jit(solution)/shard_map/stack | solution.py:250
  63.6 0.0 all-to-all-done
  63.6 4.3 %image.1 = bf16[4,4,2,32,256]{4,3,2,1,0:T(8,128)(2,1)S(1)} custom-call(bf16[4,2,4,2,64,256]{5,4,3,2,1,0:T(8,128)(2,1)S(1)} %bitcast.18, bf16[4,256,256]{2,1,0:T(8,128)(2,1)S(1)} %copy.32.steer_ref, bf16[1,2,128,256]{3,2,1,0:T(8,128)(2,1)S(1)} %pad_maximum_fusion.1.interp_ref, f32[4,6,128,256]{3,2,1,0:T(8,128)} %sine_dynamic-update-slice_fusion.phase_ref), custom_call_target="tpu_custom_call" | custom-call | flops 536870912 | bytes 5242880 | tf_op jit(solution)/shard_map/image/pallas_call | solution.py:159
  67.9 20.6 %all_to_all.10 = bf16[16,2,32,256]{3,2,1,0:T(8,128)(2,1)} all-to-all(bf16[16,2,32,256]{3,2,1,0:T(8,128)(2,1)S(1)} %bitcast.20), channel_id=1, replica_groups=mesh['leaf'=4,'tz'=4,'ty'=2] {'leaf','tz'}, dimensions={0} | all-to-all | bytes 1048576 | tf_op jit(solution)/shard_map/all_to_all | solution.py:275
  88.5 1.8 %sum_parts.1 = bf16[32,8,256]{2,1,0:T(8,128)(2,1)} custom-call(bf16[4,4,2,32,256]{4,3,2,1,0:T(8,128)(2,1)} %bitcast.23), custom_call_target="tpu_custom_call" | custom-call | tf_op jit(solution)/shard_map/sum_parts/pallas_call | solution.py:196
  (19 shorter events, 0.1 us)
Async XLA Ops:
  0.0 1.6 %copy-start.1 = (bf16[64,64,256]{2,1,0:T(8,128)(2,1)S(1)}, bf16[64,64,256]{2,1,0:T(8,128)(2,1)}, u32[]{:S(2)}) copy-start(bf16[64,64,256]{2,1,0:T(8,128)(2,1)} %echo_ref.1) | copy-start | bytes 6291460
  1.6 0.7 copy-start.2
  8.0 1.3 %copy-start = (bf16[4,2,4,2,64,256]{5,4,3,2,1,0:T(8,128)(2,1)}, bf16[4,2,4,2,64,256]{5,4,3,2,1,0:T(8,128)(2,1)S(1)}, u32[]{:S(2)}) copy-start(bf16[4,2,4,2,64,256]{5,4,3,2,1,0:T(8,128)(2,1)S(1)} %compress.1) | copy-start | bytes 6291460
  9.4 5.4 %copy-start.5 = (s32[1,8]{1,0:T(1,128)S(1)}, s32[1,8]{1,0:T(1,128)}, u32[]{:S(2)}) copy-start(s32[1,8]{1,0:T(1,128)} %param.8) | copy-start | bytes 100
  9.4 32.3 %copy-start.3 = (s32[2,2,128,8]{2,3,1,0:T(8,128)S(1)}, s32[2,2,128,8]{2,3,1,0:T(8,128)}, u32[]{:S(2)}) copy-start(s32[2,2,128,8]{2,3,1,0:T(8,128)} %param.7) | copy-start | bytes 49156
  9.4 32.4 %copy-start.4 = (f32[8]{0:T(128)S(1)}, f32[8]{0:T(128)}, u32[]{:S(2)}) copy-start(f32[8]{0:T(128)} %constant.110.clone) | copy-start | bytes 100
  9.4 54.3 %all-to-all-start = ((bf16[8,4,2,64,256]{4,3,2,1,0:T(8,128)(2,1)}), bf16[8,4,2,64,256]{4,3,2,1,0:T(8,128)(2,1)S(1)}, u32[]{:S(2)}, u32[]{:S(2)}) async-start(bf16[8,4,2,64,256]{4,3,2,1,0:T(8,128)(2,1)} %bitcast.19), calls=%async_computation | async-start | bytes 4194304 | tf_op jit(solution)/shard_map/all_to_all | solution.py:260

commit v2 on v1

--- a/solution.py
+++ b/solution.py
@@ -21,7 +21,7 @@
     leaf, ty, inner, pulses, half = dims
     blocks = leaf * ty * inner
 
-    @pl.when(pl.program_id(0) == 0)
+    @pl.when((pl.program_id(0) == 0) & (pl.program_id(1) == 0))
     def _():
         rows = lax.broadcasted_iota(jnp.int32, (half, half), 0)
         cols = lax.broadcasted_iota(jnp.int32, (half, half), 1)
@@ -62,16 +62,21 @@
     pulses, blocks, width = echoes.shape
     half = width // 2
     inner = blocks // (leaf * tz * ty)
-    per = leaf * ty * inner
+    each = min(2, ty)
+    cuts = ty // each
+    per = leaf * each * inner
     return pl.pallas_call(
-        functools.partial(compress_kernel, (leaf, ty, inner, pulses, half)),
-        grid=(tz,),
+        functools.partial(compress_kernel, (leaf, each, inner, pulses, half)),
+        grid=(tz, cuts),
         in_specs=[
-            pl.BlockSpec((2, half), lambda z: (0, 0)),
-            pl.BlockSpec((pulses, per, width), lambda z: (0, tz - 1 - z, 0)),
+            pl.BlockSpec((2, half), lambda z, y: (0, 0)),
+            pl.BlockSpec(
+                (pulses, per, width), lambda z, y: (0, (tz - 1 - z) * cuts + cuts - 1 - y, 0)
+            ),
         ],
         out_specs=pl.BlockSpec(
-            (leaf, ty, 1, inner, pulses, width), lambda z: (0, 0, tz - 1 - z, 0, 0, 0)
+            (leaf, each, 1, inner, pulses, width),
+            lambda z, y: (0, cuts - 1 - y, tz - 1 - z, 0, 0, 0),
         ),
         out_shape=jax.ShapeDtypeStruct((leaf, ty, tz, inner, pulses, width), jnp.bfloat16),
         scratch_shapes=[
@@ -79,7 +84,7 @@
             pltpu.VMEM((4, pulses * per, half), jnp.float32),
             pltpu.VMEM((2, pulses, half), jnp.float32),
         ],
-        compiler_params=pltpu.CompilerParams(vmem_limit_bytes=48 * 2**20),
+        compiler_params=pltpu.CompilerParams(vmem_limit_bytes=60 * 2**20),
         cost_estimate=pl.CostEstimate(
             flops=4 * pulses * blocks * width * width,
             bytes_accessed=4 * pulses * blocks * width,
@@ -89,7 +94,7 @@
     )(chirp, echoes)
 
 
-def image_kernel(dims, data_ref, steer_ref, interp_ref, phase_ref, out_ref):
+def image_kernel(dims, data_ref, steer_ref, interp_ref, base_ref, step_ref, out_ref):
     leaf, ty, inner, pulses, half, beams, levels = dims
     wide = inner * half
 
@@ -100,8 +105,12 @@
     def total(left, right):
         return left[0] + right[0], left[1] + right[1]
 
+    def phase(level, at, sign):
+        base = [jnp.concatenate([base_ref[0, at + n]] * inner, axis=1) for n in range(2)]
+        return turned(base, step_ref[level, 0], sign * step_ref[level, 1])
+
     current = []
-    cos, sin = phase_ref[0, 0], phase_ref[0, 1]
+    cos, sin = phase(0, 0, 1.0)
     for l in range(leaf):
         parts = []
         for y in range(ty):
@@ -131,8 +140,9 @@
                 preferred_element_type=jnp.float32,
             )
             at = 2 + 4 * (level - 1) + 2 * side
-            phase = (phase_ref[0, at], phase_ref[0, at + 1])
-            moved = turned(phase, moved[:, :wide], moved[:, wide:])
+            moved = turned(
+                phase(level, at, 2.0 * side - 1.0), moved[:, :wide], moved[:, wide:]
+            )
             if side:
                 merged[-1] = total(merged[-1], moved)
             else:
@@ -148,13 +158,12 @@
                 ]
 
 
-def backproject(data, steer, interp, phases):
+def backproject(data, steer, interp, base, step):
     leaf, ty, tz, inner, pulses, width = data.shape
     half = width // 2
     beams = steer.shape[1] // 2
     levels = leaf.bit_length() - 1
     rows = beams // leaf
-    tables = phases.shape[1]
     flops = 4 * beams * leaf * ty * pulses * tz * inner * width
     return pl.pallas_call(
         functools.partial(image_kernel, (leaf, ty, inner, pulses, half, beams, levels)),
@@ -163,16 +172,17 @@
             pl.BlockSpec((leaf, ty, 1, inner, pulses, width), lambda z: (0, 0, z, 0, 0, 0)),
             pl.BlockSpec(steer.shape, lambda z: (0, 0, 0)),
             pl.BlockSpec(interp.shape, lambda z: (0, 0, 0, 0)),
-            pl.BlockSpec((1, tables, beams, inner * half), lambda z: (z, 0, 0, 0)),
+            pl.BlockSpec((1,) + base.shape[1:], lambda z: (z, 0, 0, 0)),
+            pl.BlockSpec(step.shape, lambda z: (0, 0, 0, 0)),
         ],
         out_specs=pl.BlockSpec((leaf, 1, inner, rows, width), lambda z: (0, z, 0, 0, 0)),
         out_shape=jax.ShapeDtypeStruct((leaf, tz, inner, rows, width), jnp.bfloat16),
-        compiler_params=pltpu.CompilerParams(vmem_limit_bytes=48 * 2**20),
+        compiler_params=pltpu.CompilerParams(vmem_limit_bytes=60 * 2**20),
         cost_estimate=pl.CostEstimate(
-            flops=flops, bytes_accessed=2 * data.size + 4 * phases.size, transcendentals=0
+            flops=flops, bytes_accessed=2 * data.size + 4 * base.size, transcendentals=0
         ),
         name="image",
-    )(data, steer, interp, phases)
+    )(data, steer, interp, base, step)
 
 
 def sum_kernel(dims, parts_ref, out_ref, rows_ref):
@@ -238,16 +248,20 @@
 
 
 def phase_tables(first, steps, tz, inner, half, beams, levels):
-    row = jnp.arange(beams, dtype=jnp.int32)[None, :, None]
-    place = jnp.arange(inner * half, dtype=jnp.int32)[None, None, :]
-    z = jnp.arange(tz, dtype=jnp.int32)[:, None, None]
-    bins = first + z * steps + place + 1
-    lean = (2 * row + 1 - beams) * bins
-    tables = list(unit(2 * lean, PERIOD))
+    row = jnp.arange(beams, dtype=jnp.int32)
+    lean = 2 * row + 1 - beams
+    start = first + jnp.arange(tz, dtype=jnp.int32)[:, None] * steps
+    base = list(unit(2 * lean * start, PERIOD))
     for level in range(1, levels):
         for side in range(2):
-            tables += unit((2 * side - 1) * (level + 2) * lean + row * row * (side + 1), PERIOD)
-    return jnp.stack(tables, axis=1)
+            base += unit(
+                (2 * side - 1) * (level + 2) * lean * start + row * row * (side + 1), PERIOD
+            )
+    base = jnp.stack(base, axis=1)[..., None]
+    place = jnp.arange(inner * half, dtype=jnp.int32) + 1
+    level = jnp.arange(levels, dtype=jnp.int32)[:, None, None]
+    step = jnp.stack(unit((level + 2) * lean[:, None] * place, PERIOD), axis=1)
+    return jnp.broadcast_to(base, base.shape[:-1] + (half,)), step
 
 
 def per_device(leaf, tz, ty, echoes, chirp, taps, slots):
@@ -256,22 +270,26 @@
     beams = taps.shape[2]
     levels = leaf.bit_length() - 1
     inner = blocks // (leaf * tz * ty)
+    own_leaf, own_z, own_y = (lax.axis_index(name) for name in ("leaf", "tz", "ty"))
+    own_slot = lax.dynamic_slice_in_dim(slots, own_z * ty + own_y, 1, 1)
+    own_slots = lax.all_to_all(
+        jnp.broadcast_to(own_slot[:, :, None], (leaf * ty, 1, 128)), ("leaf", "ty"), 0, 0, tiled=True
+    )
     sent = compress(echoes, chirp, leaf, tz, ty)
+    sent, own_slots = lax.optimization_barrier((sent, own_slots))
+    own_slots = own_slots[:, 0, 0].reshape(leaf, ty)
     data = lax.all_to_all(
         sent.reshape((leaf * ty,) + sent.shape[2:]), ("leaf", "ty"), 0, 0, tiled=True
     ).reshape(sent.shape)
 
-    own_leaf, own_z, own_y = (lax.axis_index(name) for name in ("leaf", "tz", "ty"))
-    all_slots = lax.all_gather(slots, "leaf", axis=0, tiled=True)
-    own_slots = lax.dynamic_slice_in_dim(all_slots, own_z * ty, ty, 1)
     matrices = interpolation(taps, beams)
-    scale = 1.0 / math.sqrt(2.0 * all_slots.shape[1] * pulses)
+    scale = 1.0 / math.sqrt(2.0 * slots.shape[1] * pulses)
     steer = steering(own_slots, matrices[0], beams, pulses, scale)
     interp = jnp.concatenate([matrices[1:]] * 2, axis=-1).astype(jnp.bfloat16)
     first = (own_y * leaf + own_leaf) * inner * half
-    phases = phase_tables(first, ty * leaf * inner * half, tz, inner, half, beams, levels)
-
-    parts = backproject(data, steer, interp, phases)
+    base, step = phase_tables(first, ty * leaf * inner * half, tz, inner, half, beams, levels)
+
+    parts = backproject(data, steer, interp, base, step)
     parts = lax.all_to_all(
         parts.reshape((leaf * tz,) + parts.shape[2:]), ("leaf", "tz"), 0, 0, tiled=True
     ).reshape(parts.shape)
@@ -280,7 +298,7 @@
 
 def solution(mesh):
     leaf, turn = mesh.shape["leaf"], mesh.shape["turn"]
-    ty = 1 << (turn.bit_length() - 1) // 2
+    ty = 1 << turn.bit_length() // 2
     tz = turn // ty
     fine = Mesh(mesh.devices.reshape(leaf, tz, ty), ("leaf", "tz", "ty"))
     placed = (P(("leaf", "tz", "ty"), None, None), P(), P(), P("leaf", None))

time: 90.7 us -> 77.3 us (0.85)
  blocking collectives: 47.2 us -> 16.2 us
  waiting for transfers between devices: 0.01 us -> 19.4 us
  other arithmetic: 21.3 us -> 9.62 us
  starting transfers between devices: 5.31 us -> 11.5 us
  local copies, waits for them, and re-layouts: 4.22 us -> 6.5 us
  Pallas kernels: 11.8 us -> 13 us
    all_gather x1 -> x0, blocking collectives: 26.6 us -> none  [per_device(): all_slots = lax.all_gather(slots, 'leaf', axis=0, tiled=True)]
    all_to_all x1, waiting for transfers between devices: 0.01 us -> 19.4 us  [per_device(): lax.all_to_all(sent.reshape((leaf * ty,) + sent.shape[2:]), ('leaf', 'ty'...]
    unnamed x5 -> x0, other arithmetic: 14.1 us -> none
    all_to_all x0 -> x1, starting transfers between devices: none -> 6.29 us  [per_device(): lax.all_to_all(jnp.broadcast_to(own_slot[:, :, None], (leaf * ty, 1, 128)...]
    all_to_all x1, blocking collectives: 20.6 us -> 16.2 us  [per_device(): lax.all_to_all(parts.reshape((leaf * tz,) + parts.shape[2:]), ('leaf', 't...]
    broadcast_in_dim x0 -> x2, local copies, waits for them, and re-layouts: none -> 2.61 us  [the longest x1 1.37 us: phase_tables(): return (jnp.broadcast_to(base, base.shape[:-1] + (half,)), step)]
    unnamed x14 -> x9, local copies, waits for them, and re-layouts: 3.81 us -> 1.69 us
    pallas_call x1, Pallas kernels: 5.75 us -> 7.41 us  [compress(): pl.pallas_call(functools.partial(compress_kernel, (leaf, each, inner, pul...]
  transfers between devices with their start and end apart: 1 -> 2, of which waited for: 0 -> 1; matrix products, arithmetic and copies ran while one was open for 25% -> 16% of each run, Pallas kernels for 0% -> 10%
where the time goes in v2:
time: 77.3 us; the launch traced here: 76.8 us
  waiting for transfers between devices  19.4 us (25%)
  blocking collectives  16.2 us (21%)
  Pallas kernels  13 us (17%)
  starting transfers between devices  11.5 us (15%)
  other arithmetic  9.62 us (12%)
  local copies, waits for them, and re-layouts  6.5 us (8%)
    all_to_all x1, waiting for transfers between devices, per_device(): lax.all_to_all(sent.reshape((leaf * ty,) + sent.shape[2:]), ('leaf', 'ty'...  19.4 us
    all_to_all x1, blocking collectives, per_device(): lax.all_to_all(parts.reshape((leaf * tz,) + parts.shape[2:]), ('leaf', 't...  16.2 us
    pallas_call x1, Pallas kernels, compress(): pl.pallas_call(functools.partial(compress_kernel, (leaf, each, inner, pul...  7.41 us
    all_to_all x1, starting transfers between devices, per_device(): lax.all_to_all(jnp.broadcast_to(own_slot[:, :, None], (leaf * ty, 1, 128)...  6.29 us
    all_to_all x1, starting transfers between devices, per_device(): lax.all_to_all(sent.reshape((leaf * ty,) + sent.shape[2:]), ('leaf', 'ty'...  5.25 us
    pallas_call x1, Pallas kernels, backproject(): pl.pallas_call(functools.partial(image_kernel, (leaf, ty, inner, pulses,...  3.87 us
    reduce_sum x1, other arithmetic, interpolation(): return jnp.where(picks, weights[:, None], 0.0).sum(axis=-2)  3.17 us
    another operation x2, other arithmetic  2.74 us
  transfers between devices with their start and end apart: 2, of which 1 were waited for; matrix products, arithmetic and copies ran while one was open for 16% of the time, Pallas kernels for 10%

profile of v2, /device:TPU:0, one launch (start us, length us, event | category | flops | bytes accessed | tf_op | source)
XLA Modules:
  0.0 76.8 jit_solution(17449355557069850456)
XLA Ops:
  0.0 0.7 copy-done
  0.7 0.6 constant_dynamic-slice_fusion
  1.2 1.2 %broadcast_in_dim.19 = s32[16,1,128]{2,1,0:T(1,128)} broadcast(s32[]{:T(128)} %bitcast), dimensions={} | broadcast | bytes 8196 | tf_op jit(solution)/shard_map/broadcast_in_dim | solution.py:276
  2.5 6.3 %all-to-all-start = ((s32[16,1,128]{2,1,0:T(1,128)}), s32[16,1,128]{2,1,0:T(1,128)S(1)}, u32[]{:S(2)}, u32[]{:S(2)}) async-start(s32[16,1,128]{2,1,0:T(1,128)} %broadcast_in_dim.19), calls=%async_computation | async-start | bytes 16384 | tf_op jit(solution)/shard_map/all_to_all | solution.py:275
  8.8 0.8 %copy.19 = s32[2,2,128,8]{3,2,1,0:T(8,128)S(1)} copy(s32[2,2,128,8]{2,3,1,0:T(8,128)} %param.7) | data formatting | bytes 32768 | tf_op args[2]
  9.6 3.2 %select_reduce_fusion = bf16[2,2,128,128]{3,2,1,0:T(8,128)(2,1)S(1)} fusion(f32[8]{0:T(128)} %constant.120.clone, s32[2,2,128,8]{3,2,1,0:T(8,128)S(1)} %copy.19), kind=kLoop, calls=%fused_computation | loop fusion | flops 1507328 | bytes 147488 | tf_op jit(solution)/shard_map/reduce_sum | solution.py:218
  12.8 0.0 copy-start.2
  12.8 7.4 %compress.1 = bf16[4,4,2,2,64,256]{5,4,3,2,1,0:T(8,128)(2,1)} custom-call(bf16[2,128]{1,0:T(2,128)(2,1)} %chirp_ref.1, bf16[64,64,256]{2,1,0:T(8,128)(2,1)} %echo_ref.1), custom_call_target="tpu_custom_call" | custom-call | flops 1073741824 | bytes 4194304 | tf_op jit(solution)/shard_map/compress/pallas_call | solution.py:68
  20.2 5.3 %all-to-all-start.1 = ((bf16[16,2,2,64,256]{4,3,2,1,0:T(8,128)(2,1)}), bf16[16,2,2,64,256]{4,3,2,1,0:T(8,128)(2,1)S(1)}, u32[]{:S(2)}, u32[]{:S(2)}) async-start(bf16[16,2,2,64,256]{4,3,2,1,0:T(8,128)(2,1)} %bitcast.17), calls=%async_computation.1 | async-start | bytes 4194304 | tf_op jit(solution)/shard_map/all_to_all | solution.py:281
  25.6 0.2 fusion.30
  26.0 0.7 pad_maximum_fusion.2.interp_ref
  26.6 0.1 broadcast_multiply_fusion.2
  26.7 1.1 %fusion.8 = (f32[2,1,128,256]{3,2,1,0:T(8,128)S(1)}, f32[2,1,128,256]{3,2,1,0:T(8,128)S(1)}) fusion(s32[256]{0:T(256)S(1)} %iota_add_fusion, s32[2,128]{1,0:T(2,128)S(1)} %broadcast_multiply_fusion.2), kind=kLoop, calls=%fused_computation.30 | loop fusion | flops 917504 | bytes 526336 | tf_op jit(solution)/shard_map/cos | solution.py:17
  27.8 0.8 %pad_maximum_fusion.1.step_ref = f32[2,2,128,256]{3,2,1,0:T(8,128)} fusion(f32[2,1,128,256]{3,2,1,0:T(8,128)S(1)} %get-tuple-element.19, f32[2,1,128,256]{3,2,1,0:T(8,128)S(1)} %get-tuple-element.18), kind=kLoop, calls=%fused_computation.11 | loop fusion | flops 131072 | bytes 1048576 | tf_op jit(solution)/shard_map/stack | solution.py:263
  28.6 0.1 fusion.25
  28.7 0.1 broadcast_multiply_fusion
  28.8 0.4 add_reduce_fusion
  29.2 0.1 add.298
  29.3 0.1 broadcast_multiply_fusion.1
  29.4 2.5 %multiply_convert_fusion.1 = (bf16[4,128,4,1,64]{1,4,3,2,0:T(8,128)(2,1)S(1)}, bf16[4,128,4,1,64]{1,4,3,2,0:T(8,128)(2,1)S(1)}) fusion(s32[64]{0:T(128)S(1)} %fusion.26, s32[4,128,4]{1,2,0:T(4,128)S(1)} %broadcast_multiply_fusion.1, s32[128,64]{0,1:T(8,128)S(1)} %broadcast_multiply_fusion), kind=kLoop, calls=%fused_computation.17 | loop fusion | flops 2490368 | bytes 565504 | tf_op jit(solution)/shard_map/convert.9
  31.9 0.1 pad_maximum_fusion
  31.9 0.3 convolution_bitcast_fusion
  32.2 0.1 copy.21
  32.3 0.2 negate_convert_fusion
  32.6 0.1 maximum_maximum_fusion
  32.7 1.3 %copy.22.steer_ref = bf16[4,256,512]{2,1,0:T(8,128)(2,1)} copy(bf16[4,256,512]{1,2,0:T(8,128)(2,1)S(1)} %bitcast.19) | data formatting | bytes 2097152 | tf_op jit(solution)/shard_map/convert_element_type | solution.py:247
  34.0 19.4 %all-to-all-done.1 = bf16[16,2,2,64,256]{4,3,2,1,0:T(8,128)(2,1)S(1)} async-done(((bf16[16,2,2,64,256]{4,3,2,1,0:T(8,128)(2,1)}), bf16[16,2,2,64,256]{4,3,2,1,0:T(8,128)(2,1)S(1)}, u32[]{:S(2)}, u32[]{:S(2)}) %all-to-all-start.1) | async-done | bytes 2097184 | tf_op jit(solution)/shard_map/all_to_all | solution.py:281
  53.5 1.4 %broadcast_in_dim.22.base_ref = f32[2,6,128,128]{3,2,1,0:T(8,128)} broadcast(f32[2,6,128]{2,1,0:T(8,128)S(1)} %stack.16), dimensions={0,1,2} | broadcast | bytes 792576 | tf_op jit(solution)/shard_map/broadcast_in_dim | solution.py:264
  54.8 0.2 copy-done.1
  55.0 3.9 %image.1 = bf16[4,2,2,32,256]{4,3,2,1,0:T(8,128)(2,1)} custom-call(bf16[4,4,2,2,64,256]{5,4,3,2,1,0:T(8,128)(2,1)} %bitcast.16, bf16[4,256,512]{2,1,0:T(8,128)(2,1)} %copy.22.steer_ref, bf16[1,2,128,256]{3,2,1,0:T(8,128)(2,1)} %pad_maximum_fusion.2.interp_ref, f32[2,6,128,128]{3,2,1,0:T(8,128)} %broadcast_in_dim.22.base_ref, ...), custom_call_target="tpu_custom_call" | custom-call | flops 536870912 | bytes 2883584 | tf_op jit(solution)/shard_map/image/pallas_call | solution.py:168
  58.9 16.2 %all_to_all.15 = bf16[8,2,32,256]{3,2,1,0:T(8,128)(2,1)} all-to-all(bf16[8,2,32,256]{3,2,1,0:T(8,128)(2,1)} %bitcast.21), channel_id=1, replica_groups=mesh['leaf'=4,'tz'=2,'ty'=4] {'leaf','tz'}, dimensions={0} | all-to-all | bytes 524288 | tf_op jit(solution)/shard_map/all_to_all | solution.py:293
  75.1 1.7 %sum_parts.1 = bf16[32,8,256]{2,1,0:T(8,128)(2,1)} custom-call(bf16[4,2,2,32,256]{4,3,2,1,0:T(8,128)(2,1)} %bitcast.22), custom_call_target="tpu_custom_call" | custom-call | tf_op jit(solution)/shard_map/sum_parts/pallas_call | solution.py:206
  (22 shorter events, 0.2 us)
Async XLA Ops:
  0.0 0.7 copy-start
  2.5 17.8 %all-to-all-start = ((s32[16,1,128]{2,1,0:T(1,128)}), s32[16,1,128]{2,1,0:T(1,128)S(1)}, u32[]{:S(2)}, u32[]{:S(2)}) async-start(s32[16,1,128]{2,1,0:T(1,128)} %broadcast_in_dim.19), calls=%async_computation | async-start | bytes 16384 | tf_op jit(solution)/shard_map/all_to_all | solution.py:275
  12.8 7.4 %copy-start.2 = (bf16[2,2,128,128]{3,2,1,0:T(8,128)(2,1)}, bf16[2,2,128,128]{3,2,1,0:T(8,128)(2,1)S(1)}, u32[]{:S(2)}) copy-start(bf16[2,2,128,128]{3,2,1,0:T(8,128)(2,1)S(1)} %select_reduce_fusion) | copy-start | bytes 393220
  20.2 5.7 %slice-start = ((bf16[2,2,128,128]{3,2,1,0:T(8,128)(2,1)}), bf16[1,2,128,128]{3,2,1,0:T(8,128)(2,1)S(1)}, s32[]{:S(2)}) async-start(bf16[2,2,128,128]{3,2,1,0:T(8,128)(2,1)} %copy-done.2), calls=%async_computation.3 | async-start | bytes 131072 | tf_op jit(solution)/shard_map/slice | solution.py:288
  20.2 33.2 %all-to-all-start.1 = ((bf16[16,2,2,64,256]{4,3,2,1,0:T(8,128)(2,1)}), bf16[16,2,2,64,256]{4,3,2,1,0:T(8,128)(2,1)S(1)}, u32[]{:S(2)}, u32[]{:S(2)}) async-start(bf16[16,2,2,64,256]{4,3,2,1,0:T(8,128)(2,1)} %bitcast.17), calls=%async_computation.1 | async-start | bytes 4194304 | tf_op jit(solution)/shard_map/all_to_all | solution.py:281
  25.5 6.4 %copy-start.3 = (bf16[2,2,128,128]{3,2,1,0:T(8,128)(2,1)S(1)}, bf16[2,2,128,128]{3,2,1,0:T(8,128)(2,1)}, u32[]{:S(2)}) copy-start(bf16[2,2,128,128]{3,2,1,0:T(8,128)(2,1)} %copy-done.2) | copy-start | bytes 393220
  53.5 1.6 %copy-start.1 = (bf16[16,2,2,64,256]{4,3,2,1,0:T(8,128)(2,1)}, bf16[16,2,2,64,256]{4,3,2,1,0:T(8,128)(2,1)S(1)}, u32[]{:S(2)}) copy-start(bf16[16,2,2,64,256]{4,3,2,1,0:T(8,128)(2,1)S(1)} %all-to-all-done.1) | copy-start | bytes 6291460

commit v3 on v1

v3 whole, which is shorter than its diff:
```python
import functools
import math

import jax
import jax.numpy as jnp
from jax import lax
from jax.experimental import pallas as pl
from jax.experimental.pallas import tpu as pltpu
from jax.sharding import PartitionSpec as P

WEIGHTS = (-1.0 / 32, 3.0 / 32, -7.0 / 32, 21.0 / 32, 21.0 / 32, -7.0 / 32, 3.0 / 32, -1.0 / 32)
PERIOD = 4096
VMEM_BYTES = 56 * 2**20
SCALARS = pl.BlockSpec(memory_space=pltpu.SMEM)


def bits_of(count):
    return count.bit_length() - 1


def swapped(array, axis, bit):
    return lax.ppermute(array, axis, [(i, i ^ 1 << bit) for i in range(lax.axis_size(axis))])


def unit(phase_int, period):
    angle = jnp.remainder(phase_int, period).astype(jnp.float32) * (2.0 * math.pi / period)
    return jnp.cos(angle), jnp.sin(angle)


def compress_kernel(
    dims, own_ref, chirp_ref, echo_ref, keep_y, send_y, keep_z, send_z, weights, sums, carry
):
    each, pulses, half = dims
    tile = 2 * each
    blocks = 2 * tile
    mids = pl.num_programs(2)
    mid = mids - 1 - pl.program_id(2)
    near = 1 - pl.program_id(1)

    @pl.when((pl.program_id(0) == 0) & (pl.program_id(1) == 0) & (pl.program_id(2) == 0))
    def _():
        rows = lax.broadcasted_iota(jnp.int32, (half, half), 0)
        cols = lax.broadcasted_iota(jnp.int32, (half, half), 1)
        taps = chirp_ref[...].astype(jnp.float32)
        tables = []
        for c in range(2):
            wide = jnp.broadcast_to(taps[c : c + 1], (half, half))
            tables.append(pltpu.roll(wide, 0, 1, stride=1, stride_axis=0).T)
        for m, mask in enumerate((rows >= cols, rows < cols)):
            re, im = (jnp.where(mask, t, 0.0) for t in tables)
            top = jnp.concatenate([re, im], axis=1)
            low = jnp.concatenate([-im, re], axis=1)
            full = jnp.concatenate([top, low], axis=0)
            weights[:, m * 2 * half : (m + 1) * 2 * half] = full.astype(jnp.bfloat16)
        carry[...] = jnp.zeros_like(carry)

    data = echo_ref[...].reshape(pulses * blocks, 2 * half)
    for n in range(4):
        sums[n] = jnp.dot(
            data, weights[:, n * half : (n + 1) * half], preferred_element_type=jnp.float32
        )

    def filtered(b, last=False):
        parts = []
        for c in range(2):
            own = sums[c, pl.ds(b, pulses, stride=blocks), :]
            after = carry[c] if last else sums[2 + c, pl.ds(b + 1, pulses, stride=blocks), :]
            parts.append((own + after).astype(jnp.bfloat16))
        return jnp.concatenate(parts, axis=1)

    own_u = own_ref[0]
    for i in range(each):
        keep_y[0, 0, 0, i] = filtered(own_u * tile + i)
        send_y[0, 0, 0, i] = filtered((1 - own_u) * tile + i)

    def far_chain(out_ref):
        for u in range(2):
            for i in range(each):
                b = u * tile + each + i
                out_ref[0, mid, u, i] = filtered(b, b + 1 == blocks)

    @pl.when(near == own_ref[1])
    def _():
        far_chain(keep_z)

    @pl.when(near != own_ref[1])
    def _():
        far_chain(send_z)

    for c in range(2):
        carry[c] = sums[2 + c, pl.ds(0, pulses, stride=blocks), :]


def compress(own, chirp, echoes, high, mids):
    pulses, blocks, width = echoes.shape
    half = width // 2
    each = blocks // (8 * high * mids)
    shape_y = (high, 2, mids, each, pulses, width)
    shape_z = (high, mids, 2, each, pulses, width)
    spec_y = pl.BlockSpec(
        (1, 1, 1) + shape_y[3:], lambda h, v, m: (high - 1 - h, 1 - v, mids - 1 - m, 0, 0, 0)
    )
    spec_z = pl.BlockSpec((1,) + shape_z[1:], lambda h, v, m: (high - 1 - h, 0, 0, 0, 0, 0))
    return pl.pallas_call(
        functools.partial(compress_kernel, (each, pulses, half)),
        grid=(high, 2, mids),
        in_specs=[
            SCALARS,
            pl.BlockSpec((2, half), lambda h, v, m: (0, 0)),
            pl.BlockSpec(
                (pulses, 4 * each, width),
                lambda h, v, m: (0, ((high - 1 - h) * 2 + 1 - v) * mids + mids - 1 - m, 0),
            ),
        ],
        out_specs=[spec_y, spec_y, spec_z, spec_z],
        out_shape=[
            jax.ShapeDtypeStruct(s, jnp.bfloat16) for s in (shape_y, shape_y, shape_z, shape_z)
        ],
        scratch_shapes=[
            pltpu.VMEM((width, 2 * width), jnp.bfloat16),
            pltpu.VMEM((4, pulses * 4 * each, half), jnp.float32),
            pltpu.VMEM((2, pulses, half), jnp.float32),
        ],
        compiler_params=pltpu.CompilerParams(vmem_limit_bytes=VMEM_BYTES),
        cost_estimate=pl.CostEstimate(
            flops=4 * pulses * blocks * width * width,
            bytes_accessed=4 * pulses * blocks * width,
            transcendentals=0,
        ),
        name="compress",
    )(own, chirp, echoes)


def image_kernel(
    dims, own_ref, keep_ref, got_ref, steer_ref, interp_ref, base_ref, step_ref, out_keep, out_send
):
    leaf, each, half, beams, levels = dims
    rows = beams // leaf
    pair = 2
    own = own_ref[0]

    def turned(phase, re, im):
        c, s = phase
        return c * re - s * im, c * im + s * re

    bases = []
    for n in range(2 * levels):
        bases.append(jnp.broadcast_to(base_ref[0, n : n + 1, :], (half, beams)).T)
    for at in range(0, each, pair):
        parts = []
        for ref in (keep_ref, got_ref):
            for c in range(2):
                cols = slice(c * half, (c + 1) * half)
                parts.append(
                    jnp.concatenate([ref[0, at + i, :, cols] for i in range(pair)], axis=1)
                )
        raw = jnp.dot(
            steer_ref[...], jnp.concatenate(parts, axis=0), preferred_element_type=jnp.float32
        )
        re, im = raw[:beams], raw[beams:]
        for level in range(levels):
            if level:
                both = jnp.concatenate([re, im], axis=1)
                big = both.astype(jnp.bfloat16)
                low = (both - big.astype(jnp.float32)).astype(jnp.bfloat16)
                moved = jnp.dot(
                    interp_ref[level - 1],
                    jnp.concatenate([big, low], axis=0),
                    preferred_element_type=jnp.float32,
                )
                re, im = moved[:, : pair * half], moved[:, pair * half :]
            sides = []
            for i in range(pair):
                lanes = slice((at + i) * half, (at + i + 1) * half)
                phase = turned(
                    (bases[2 * level], bases[2 * level + 1]),
                    step_ref[level, 0, :, lanes],
                    step_ref[level, 1, :, lanes],
                )
                cut = slice(i * half, (i + 1) * half)
                sides.append(turned(phase, re[:, cut], im[:, cut]))
            re, im = (jnp.concatenate([s[c] for s in sides], axis=1) for c in range(2))
        for i in range(pair):
            cut = slice(i * half, (i + 1) * half)
            for g in range(leaf // 2):
                for side in range(2):
                    first = (2 * g + side) * rows
                    value = jnp.concatenate(
                        [t[first : first + rows, cut] for t in (re, im)], axis=1
                    )

                    @pl.when(own == side)
                    def _(value=value, g=g, i=i):
                        out_keep[g, 0, at + i] = value

                    @pl.when(own != side)
                    def _(value=value, g=g, i=i):
                        out_send[g, 0, at + i] = value.astype(jnp.bfloat16)


def backproject(own, keep, got, steer, interp, base, step, leaf):
    count, each, pulses, width = keep.shape
    half = width // 2
    beams = steer.shape[0] // 2
    levels = bits_of(leaf)
    rows = beams // leaf
    shape = (leaf // 2, count, each, rows, width)
    out_spec = pl.BlockSpec((leaf // 2, 1) + shape[2:], lambda n: (0, n, 0, 0, 0))
    in_spec = pl.BlockSpec((1, each, pulses, width), lambda n: (n, 0, 0, 0))
    return pl.pallas_call(
        functools.partial(image_kernel, (leaf, each, half, beams, levels)),
        grid=(count,),
        in_specs=[
            SCALARS,
            in_spec,
            in_spec,
            pl.BlockSpec(steer.shape, lambda n: (0, 0)),
            pl.BlockSpec(interp.shape, lambda n: (0, 0, 0)),
            pl.BlockSpec((1,) + base.shape[1:], lambda n: (n, 0, 0)),
            pl.BlockSpec(step.shape, lambda n: (0, 0, 0, 0)),
        ],
        out_specs=[out_spec, out_spec],
        out_shape=[
            jax.ShapeDtypeStruct(shape, jnp.float32),
            jax.ShapeDtypeStruct(shape, jnp.bfloat16),
        ],
        compiler_params=pltpu.CompilerParams(vmem_limit_bytes=VMEM_BYTES),
        cost_estimate=pl.CostEstimate(
            flops=12 * beams * pulses * keep.shape[0] * each * width,
            bytes_accessed=4 * keep.size + 6 * shape[0] * count * each * rows * width,
            transcendentals=0,
        ),
        name="image",
    )(own, keep, got, steer, interp, base, step)


def fold_kernel(own_ref, keep_ref, got_ref, out_keep, out_send):
    own = own_ref[0]
    for a in range(keep_ref.shape[0]):
        out_send[a] = (
            keep_ref[a, 1 - own] + got_ref[a, 1 - own].astype(jnp.float32)
        ).astype(jnp.bfloat16)
        out_keep[a] = keep_ref[a, own] + got_ref[a, own].astype(jnp.float32)


def fold(own, keep, got):
    shape = keep.shape[:1] + keep.shape[2:]
    return pl.pallas_call(
        fold_kernel,
        in_specs=[SCALARS] + [pl.BlockSpec(memory_space=pltpu.VMEM)] * 2,
        out_specs=[pl.BlockSpec(memory_space=pltpu.VMEM)] * 2,
        out_shape=[
            jax.ShapeDtypeStruct(shape, jnp.float32),
            jax.ShapeDtypeStruct(shape, jnp.bfloat16),
        ],
        compiler_params=pltpu.CompilerParams(vmem_limit_bytes=VMEM_BYTES),
        cost_estimate=pl.CostEstimate(
            flops=keep.size, bytes_accessed=9 * keep.size, transcendentals=0
        ),
        name="fold",
    )(own, keep, got)


def last_kernel(keep_y, got_y, keep_z, got_z, out_ref, rows_ref):
    each, rows, width = keep_y.shape
    blocks = 2 * each
    for n, (keep, got) in enumerate(((keep_y, got_y), (keep_z, got_z))):
        for i in range(each):
            value = keep[i] + got[i].astype(jnp.float32)
            for c in range(2):
                cols = slice(c * width // 2, (c + 1) * width // 2)
                rows_ref[c, pl.ds(n * each + i, rows, stride=blocks), :] = value[:, cols]
    both = jnp.concatenate([rows_ref[0], rows_ref[1]], axis=1)
    out_ref[...] = both.reshape(rows, blocks, width).astype(jnp.bfloat16)


def last_sum(keep_y, got_y, keep_z, got_z):
    each, rows, width = keep_y.shape
    return pl.pallas_call(
        last_kernel,
        out_shape=jax.ShapeDtypeStruct((rows, 2 * each, width), jnp.bfloat16),
        scratch_shapes=[pltpu.VMEM((2, rows * 2 * each, width // 2), jnp.float32)],
        name="last_sum",
    )(keep_y, got_y, keep_z, got_z)


def interpolation(taps, beams):
    cells = jnp.arange(beams, dtype=jnp.int32)
    weights = jnp.array(WEIGHTS, jnp.float32)
    picks = taps[..., None] == cells
    return jnp.where(picks, weights[:, None], 0.0).sum(axis=-2)


def steering(slots, matrix, side, beams, pulses, scale):
    count = slots.shape[0]
    beam = jnp.arange(beams, dtype=jnp.int32)[:, None, None]
    place = jnp.arange(pulses, dtype=jnp.int32)
    slot = slots[None, :, None]
    cos, sin = unit(
        (2 * beam + 1 - beams) * (2 * place + 1 - pulses)
        + 3 * (beam + 1) * (2 * slot + 1) * (2 * place + 1),
        8 * pulses,
    )
    pair = jnp.concatenate([cos * scale, sin * scale], axis=2).astype(jnp.bfloat16)
    moved = jnp.dot(
        matrix.astype(jnp.bfloat16),
        pair.reshape(beams, count * 2 * pulses),
        preferred_element_type=jnp.float32,
    ).reshape(beams, count, 2 * pulses)
    re, im = moved[:, :, :pulses], moved[:, :, pulses:]
    row = jnp.arange(beams, dtype=jnp.int32)
    c, s = (t[:, None, None] for t in unit(row * row * (side + 1), PERIOD))
    re, im = c * re - s * im, c * im + s * re
    top = jnp.concatenate([re, -im], axis=2)
    low = jnp.concatenate([im, re], axis=2)
    return jnp.concatenate([top, low], axis=0).astype(jnp.bfloat16)


def bit(value, at):
    return value >> at & 1


def per_device(echoes, chirp, taps, slots):
    leaf, turn = lax.axis_size("leaf"), lax.axis_size("turn")
    pulses, blocks, width = echoes.shape
    half = width // 2
    beams = taps.shape[2]
    levels = bits_of(leaf)
    far = (bits_of(turn) + 1) // 2 - 1 if turn > 4 else 1
    mids = 1 << far - 1
    high = turn >> far + 1
    each = blocks // (2 * turn)
    rows = beams // leaf
    own_leaf, own_turn = lax.axis_index("leaf"), lax.axis_index("turn")

    def scalar(value):
        return jnp.asarray(value, jnp.int32).reshape(1)

    own_bits = jnp.concatenate([scalar(bit(own_turn, 0)), scalar(bit(own_turn, far))])
    keep_y, send_y, keep_z, send_z = compress(own_bits, chirp, echoes, high, mids)
    got_y = swapped(send_y, "turn", 0)
    got_z = swapped(send_z, "turn", far)

    own_sides = [bit(own_leaf, level) for level in range(levels)]
    own_taps = jnp.stack(
        [lax.dynamic_index_in_dim(taps[n], own_sides[n], 0, False) for n in range(levels)]
    )
    matrices = interpolation(own_taps, beams)
    scale = 1.0 / math.sqrt(2.0 * slots.shape[1] * pulses)
    own_slots = jnp.concatenate(
        [
            lax.dynamic_index_in_dim(slots[0], own_turn ^ other, 0, True)
            for other in (0, 1, 1 << far)
        ]
    )
    steer = steering(own_slots, matrices[0], own_sides[0], beams, pulses, scale)
    steer_y = steer[:, :2].reshape(2 * beams, 4 * pulses)
    steer_z = jnp.concatenate([steer[:, :1], steer[:, 2:]], axis=1).reshape(2 * beams, 4 * pulses)
    interp = jnp.concatenate([matrices[1:]] * 2, axis=-1).astype(jnp.bfloat16)

    row = jnp.arange(beams, dtype=jnp.int32)
    lean = 2 * row + 1 - beams
    place = jnp.arange(each * half, dtype=jnp.int32) + 1
    slopes = jnp.stack([(2 * own_sides[n] - 1) * (n + 2) for n in range(levels)])
    step = jnp.stack(unit(slopes[:, None, None] * lean[:, None] * place, PERIOD), axis=1)
    squares = jnp.stack(
        [row * row * (own_sides[n] + 1) * (1 if n else 0) for n in range(levels)]
    )

    def bases(tiles, shift):
        start = ((tiles * 2 + shift) * each * half)[:, None, None]
        both = jnp.stack(unit(slopes[:, None] * lean * start + squares, PERIOD), axis=2)
        return both.reshape(tiles.shape[0], 2 * levels, beams)

    count = turn // 2
    index = jnp.arange(count, dtype=jnp.int32)
    tiles_y = 2 * index + bit(own_turn, 0)
    low_part = index & (1 << far) - 1
    tiles_z = ((index >> far) * 2 + bit(own_turn, far)) * (1 << far) + low_part

    own_core = scalar(bit(own_leaf, 0))
    final = []
    for name, keep, got, steer_own, tiles in (
        ("y", keep_y, got_y, steer_y, tiles_y),
        ("z", keep_z, got_z, steer_z, tiles_z),
    ):
        shape = (count, each, pulses, width)
        base = bases(tiles, 0 if name == "y" else 1)
        kept, sent = backproject(
            own_core, keep.reshape(shape), got.reshape(shape), steer_own, interp, base, step, leaf
        )
        gone = 0 if name == "y" else far
        leading = [("leaf", b) for b in range(levels - 1, 0, -1)]
        leading += [("turn", b) for b in range(bits_of(turn) - 1, -1, -1) if b != gone]
        order = [("leaf", b) for b in range(1, levels)]
        rest = [("turn", b) for b in range(bits_of(turn)) if b not in (0, far)]
        order = order + [("turn", far)] if name == "y" else [("turn", 0)] + order
        arrived = swapped(sent, "leaf", 0)
        for axis, b in order + rest:
            at = leading.index((axis, b))
            before, after = 1 << at, (1 << len(leading) - at - 1) * each
            leading.pop(at)
            split = (before, 2, after, rows, width)
            own = scalar(bit(own_leaf if axis == "leaf" else own_turn, b))
            kept, sent = fold(own, kept.reshape(split), arrived.reshape(split))
            arrived = swapped(sent, axis, b)
        final += [kept.reshape(each, rows, width), arrived.reshape(each, rows, width)]
    return last_sum(*final)


def solution(mesh):
    placed = (P(("leaf", "turn"), None, None), P(), P(), P("leaf", None))
    return jax.shard_map(
        per_device, mesh=mesh, in_specs=placed, out_specs=P("leaf", "turn", None), check_vma=False
    )
```

time: 90.7 us -> 74.4 us (0.82)
  blocking collectives: 47.2 us -> 0 us
  Pallas kernels: 11.8 us -> 33.9 us
  other arithmetic: 21.3 us -> 7.83 us
  starting transfers between devices: 5.31 us -> 14.5 us
  waiting for transfers between devices: 0.01 us -> 7.31 us
  local copies, waits for them, and re-layouts: 4.22 us -> 10.1 us
    all_gather x1 -> x0, blocking collectives: 26.6 us -> none  [per_device(): all_slots = lax.all_gather(slots, 'leaf', axis=0, tiled=True)]
    pallas_call x3 -> x10, Pallas kernels: 11.8 us -> 33.9 us  [the longest x2 12.7 us: backproject(): pl.pallas_call(functools.partial(image_kernel, (leaf, each, half, beams,...]
    all_to_all x1 -> x0, blocking collectives: 20.6 us -> none  [per_device(): lax.all_to_all(parts.reshape((leaf * tz,) + parts.shape[2:]), ('leaf', 't...]
    ppermute x0 -> x10, starting transfers between devices: none -> 14.5 us  [swapped(): lax.ppermute(array, axis, [(i, i ^ 1 << bit) for i in range(lax.axis_size...]
    unnamed x5 -> x0, other arithmetic: 14.1 us -> none
    ppermute x0 -> x10, waiting for transfers between devices: none -> 7.31 us  [swapped(): lax.ppermute(array, axis, [(i, i ^ 1 << bit) for i in range(lax.axis_size...]
    all_to_all x1 -> x0, starting transfers between devices: 5.31 us -> none  [per_device(): lax.all_to_all(sent.reshape((leaf * ty,) + sent.shape[2:]), ('leaf', 'ty'...]
    unnamed x14 -> x26, local copies, waits for them, and re-layouts: 3.81 us -> 6.57 us
  transfers between devices with their start and end apart: 1 -> 10, of which waited for: 0 -> 3; matrix products, arithmetic and copies ran while one was open for 25% -> 15% of each run, Pallas kernels for 0% -> 33%
where the time goes in v3:
time: 74.4 us; the launch traced here: 73.9 us
  Pallas kernels  33.9 us (46%)
  starting transfers between devices  14.5 us (19%)
  local copies, waits for them, and re-layouts  10.1 us (14%)
  other arithmetic  7.83 us (11%)
  waiting for transfers between devices  7.31 us (10%)
    ppermute x10, starting transfers between devices, swapped(): lax.ppermute(array, axis, [(i, i ^ 1 << bit) for i in range(lax.axis_size...  14.5 us
    pallas_call x2, Pallas kernels, backproject(): pl.pallas_call(functools.partial(image_kernel, (leaf, each, half, beams,...  12.7 us
    pallas_call x6, Pallas kernels, fold(): pl.pallas_call(fold_kernel, in_specs=[SCALARS] + [pl.BlockSpec(memory_spa...  11.8 us
    pallas_call x1, Pallas kernels, compress(): pl.pallas_call(functools.partial(compress_kernel, (each, pulses, half)),...  7.61 us
    ppermute x10, waiting for transfers between devices, swapped(): lax.ppermute(array, axis, [(i, i ^ 1 << bit) for i in range(lax.axis_size...  7.31 us
    unnamed x26, local copies, waits for them, and re-layouts  6.57 us
    cos x2, other arithmetic, unit(): return (jnp.cos(angle), jnp.sin(angle))  2.27 us
    add x1, other arithmetic, steering(): 2 * slot + 1  1.97 us
  transfers between devices with their start and end apart: 10, of which 3 were waited for; matrix products, arithmetic and copies ran while one was open for 15% of the time, Pallas kernels for 33%

profile of v3, /device:TPU:0, one launch (start us, length us, event | category | flops | bytes accessed | tf_op | source)
XLA Modules:
  0.0 73.9 jit_solution(7298634115005242102)
XLA Ops:
  0.6 7.6 %compress.1 = (bf16[2,2,1,4,64,256]{5,4,3,2,1,0:T(8,128)(2,1)}, bf16[2,2,1,4,64,256]{5,4,3,2,1,0:T(8,128)(2,1)}, bf16[2,1,2,4,64,256]{5,4,3,2,1,0:T(8,128)(2,1)}, bf16[2,1,2,4,64,256]{5,4,3,2,1,0:T(8,128)(2,1)}) custom-call(s32[2]{0:T(128)} %get-tuple-element.65.own_ref, bf16[2,128]{1,0:T(2,128)(2,1)} %chirp_ref.1, bf16[64,64,256]{2,1,0:T(8,128)(2,1)} %echo_ref.1), custom_call_target="tpu_custom_call" | custom-call | flops 1073741824 | bytes 4194304 | tf_op jit(solution)/shard_map/compress/pallas_call | solution.py:104
  8.2 3.0 %collective-permute-start = (bf16[2,2,1,4,64,256]{5,4,3,2,1,0:T(8,128)(2,1)}, bf16[2,2,1,4,64,256]{5,4,3,2,1,0:T(8,128)(2,1)S(1)}, u32[]{:S(2)}, u32[]{:S(2)}) collective-permute-start(bf16[2,2,1,4,64,256]{5,4,3,2,1,0:T(8,128)(2,1)} %get-tuple-element.26), channel_id=1, source_target_pairs={{0,1},{1,0},{2,3},{3,2},{4,5},{5,4},{6,7},{7,6},{8,9},{9,8},{10,11... | collective-permute-start | bytes 1572872 | tf_op jit(solution)/shard_map/ppermute | solution.py:22
  11.2 1.6 %collective-permute-start.5 = (bf16[2,1,2,4,64,256]{5,4,3,2,1,0:T(8,128)(2,1)}, bf16[2,1,2,4,64,256]{5,4,3,2,1,0:T(8,128)(2,1)S(1)}, u32[]{:S(2)}, u32[]{:S(2)}) collective-permute-start(bf16[2,1,2,4,64,256]{5,4,3,2,1,0:T(8,128)(2,1)} %get-tuple-element.36), channel_id=1, source_target_pairs={{0,2},{1,3},{2,0},{3,1},{4,6},{5,7},{6,4},{7,5},{8,10},{9,11},{10,... | collective-permute-start | bytes 1572872 | tf_op jit(solution)/shard_map/ppermute | solution.py:22
  14.9 2.0 %fusion.27 = s32[3]{0:T(128)S(1)} fusion(s32[1]{0:T(128)} %bitcast.13, s32[1]{0:T(128)} %bitcast.12, s32[1]{0:T(128)} %bitcast.11), kind=kLoop, calls=%fused_computation.70 | loop fusion | flops 12 | bytes 24 | tf_op jit(solution)/shard_map/add | solution.py:301
  19.1 0.8 %copy.20.steer_ref = bf16[256,256]{1,0:T(8,128)(2,1)} copy(bf16[256,256]{0,1:T(8,128)(2,1)S(1)} %bitcast.59) | data formatting | bytes 262144 | tf_op jit(solution)/shard_map/reshape | solution.py:358
  19.9 0.8 %copy.19.steer_ref = bf16[256,256]{1,0:T(8,128)(2,1)} copy(bf16[256,256]{0,1:T(8,128)(2,1)S(1)} %bitcast.60) | data formatting | bytes 262144 | tf_op jit(solution)/shard_map/reshape | solution.py:357
  20.6 2.1 %fusion.4 = (f32[2,1,128,512]{3,2,1,0:T(8,128)S(1)}, f32[2,1,128,512]{3,2,1,0:T(8,128)S(1)}) fusion(s32[512]{0:T(512)S(1)} %iota_add_fusion, s32[2,128]{1,0:T(2,128)S(1)} %broadcast_multiply_fusion.2), kind=kLoop, calls=%fused_computation.12 | loop fusion | flops 1835008 | bytes 1051648 | tf_op jit(solution)/shard_map/cos | solution.py:27
  22.8 1.0 %pad_maximum_fusion.step_ref = f32[2,2,128,512]{3,2,1,0:T(8,128)} fusion(f32[2,1,128,512]{3,2,1,0:T(8,128)S(1)} %get-tuple-element.55, f32[2,1,128,512]{3,2,1,0:T(8,128)S(1)} %get-tuple-element.54), kind=kLoop, calls=%fused_computation | loop fusion | flops 262144 | bytes 2097152 | tf_op jit(solution)/shard_map/stack | solution.py:365
  23.8 0.8 %copy-done.1 = bf16[2,2,1,4,64,256]{5,4,3,2,1,0:T(8,128)(2,1)} copy-done((bf16[2,2,1,4,64,256]{5,4,3,2,1,0:T(8,128)(2,1)}, bf16[2,2,1,4,64,256]{5,4,3,2,1,0:T(8,128)(2,1)S(1)}, u32[]{:S(2)}) %copy-start.1) | copy-done | bytes 524312
  24.6 6.3 %image.2 = (f32[2,4,4,32,256]{4,3,2,1,0:T(8,128)}, bf16[2,4,4,32,256]{4,3,2,1,0:T(8,128)(2,1)}) custom-call(s32[1]{0:T(128)} %bitcast.3.own_ref, bf16[4,4,64,256]{3,2,1,0:T(8,128)(2,1)} %bitcast.53, bf16[4,4,64,256]{3,2,1,0:T(8,128)(2,1)} %bitcast.54, bf16[256,256]{1,0:T(8,128)(2,1)} %copy.19.steer_ref, bf16[1,128,256]{2,1,0:T(8,128)(2,1)} %pad_maximum_fusion.2.interp_ref, ...), custom_call_target="tpu_custom_call" | custom-call | flops 402653184 | bytes 2621440 | tf_op jit(solution)/shard_map/image/pallas_call | solution.py:210
  31.0 0.8 %copy-done = bf16[2,1,2,4,64,256]{5,4,3,2,1,0:T(8,128)(2,1)} copy-done((bf16[2,1,2,4,64,256]{5,4,3,2,1,0:T(8,128)(2,1)}, bf16[2,1,2,4,64,256]{5,4,3,2,1,0:T(8,128)(2,1)S(1)}, u32[]{:S(2)}) %copy-start) | copy-done | bytes 524312
  31.8 6.3 %image.3 = (f32[2,4,4,32,256]{4,3,2,1,0:T(8,128)}, bf16[2,4,4,32,256]{4,3,2,1,0:T(8,128)(2,1)}) custom-call(s32[1]{0:T(128)} %bitcast.3.own_ref, bf16[4,4,64,256]{3,2,1,0:T(8,128)(2,1)} %bitcast.51, bf16[4,4,64,256]{3,2,1,0:T(8,128)(2,1)} %bitcast.52, bf16[256,256]{1,0:T(8,128)(2,1)} %copy.20.steer_ref, bf16[1,128,256]{2,1,0:T(8,128)(2,1)} %pad_maximum_fusion.2.interp_ref, ...), custom_call_target="tpu_custom_call" | custom-call | flops 402653184 | bytes 2621440 | tf_op jit(solution)/shard_map/image/pallas_call | solution.py:210
  38.6 0.8 %copy-done.2 = bf16[2,4,4,32,256]{4,3,2,1,0:T(8,128)(2,1)} copy-done((bf16[2,4,4,32,256]{4,3,2,1,0:T(8,128)(2,1)}, bf16[2,4,4,32,256]{4,3,2,1,0:T(8,128)(2,1)S(1)}, u32[]{:S(2)}) %copy-start.2) | copy-done | bytes 524312
  39.4 2.3 %fold.6 = (f32[1,16,32,256]{3,2,1,0:T(8,128)}, bf16[1,16,32,256]{3,2,1,0:T(8,128)(2,1)}) custom-call(s32[1]{0:T(128)} %bitcast.2.own_ref, f32[1,2,16,32,256]{4,3,2,1,0:T(8,128)} %bitcast.49, bf16[1,2,16,32,256]{4,3,2,1,0:T(8,128)(2,1)} %bitcast.57), custom_call_target="tpu_custom_call" | custom-call | flops 262144 | bytes 2359296 | tf_op jit(solution)/shard_map/fold/pallas_call | solution.py:248
  41.8 1.5 %collective-permute-start.2 = (bf16[1,16,32,256]{3,2,1,0:T(8,128)(2,1)}, bf16[1,16,32,256]{3,2,1,0:T(8,128)(2,1)S(1)}, u32[]{:S(2)}, u32[]{:S(2)}) collective-permute-start(bf16[1,16,32,256]{3,2,1,0:T(8,128)(2,1)} %get-tuple-element.30), channel_id=1, source_target_pairs={{0,16},{8,24},{16,0},{24,8},{1,17},{9,25},{17,1},{25,9},{2,18},{10... | collective-permute-start | bytes 786440 | tf_op jit(solution)/shard_map/ppermute | solution.py:22
  43.2 0.8 %copy-done.3 = bf16[2,4,4,32,256]{4,3,2,1,0:T(8,128)(2,1)} copy-done((bf16[2,4,4,32,256]{4,3,2,1,0:T(8,128)(2,1)}, bf16[2,4,4,32,256]{4,3,2,1,0:T(8,128)(2,1)S(1)}, u32[]{:S(2)}) %copy-start.3) | copy-done | bytes 524312
  44.1 2.3 %fold.9 = (f32[4,4,32,256]{3,2,1,0:T(8,128)}, bf16[4,4,32,256]{3,2,1,0:T(8,128)(2,1)}) custom-call(s32[1]{0:T(128)} %bitcast.4.own_ref, f32[4,2,4,32,256]{4,3,2,1,0:T(8,128)} %bitcast.50, bf16[4,2,4,32,256]{4,3,2,1,0:T(8,128)(2,1)} %bitcast.58), custom_call_target="tpu_custom_call" | custom-call | flops 262144 | bytes 2359296 | tf_op jit(solution)/shard_map/fold/pallas_call | solution.py:248
  46.4 1.2 %collective-permute-start.7 = (bf16[4,4,32,256]{3,2,1,0:T(8,128)(2,1)}, bf16[4,4,32,256]{3,2,1,0:T(8,128)(2,1)S(1)}, u32[]{:S(2)}, u32[]{:S(2)}) collective-permute-start(bf16[4,4,32,256]{3,2,1,0:T(8,128)(2,1)} %get-tuple-element.40), channel_id=1, source_target_pairs={{0,1},{1,0},{2,3},{3,2},{4,5},{5,4},{6,7},{7,6},{8,9},{9,8},{10,11... | collective-permute-start | bytes 786440 | tf_op jit(solution)/shard_map/ppermute | solution.py:22
  47.6 2.6 %collective-permute-done.2 = bf16[1,16,32,256]{3,2,1,0:T(8,128)(2,1)S(1)} collective-permute-done((bf16[1,16,32,256]{3,2,1,0:T(8,128)(2,1)}, bf16[1,16,32,256]{3,2,1,0:T(8,128)(2,1)S(1)}, u32[]{:S(2)}, u32[]{:S(2)}) %collective-permute-start.2) | collective-permute-done | bytes 262176 | tf_op jit(solution)/shard_map/ppermute | solution.py:22
  50.2 0.7 copy-done.4
  50.9 1.9 %fold.7 = (f32[2,4,32,256]{3,2,1,0:T(8,128)}, bf16[2,4,32,256]{3,2,1,0:T(8,128)(2,1)}) custom-call(s32[1]{0:T(128)} %bitcast.1.own_ref, f32[2,2,4,32,256]{4,3,2,1,0:T(8,128)} %bitcast.56, bf16[2,2,4,32,256]{4,3,2,1,0:T(8,128)(2,1)} %bitcast.63), custom_call_target="tpu_custom_call" | custom-call | flops 131072 | bytes 1179648 | tf_op jit(solution)/shard_map/fold/pallas_call | solution.py:248
  52.8 1.3 %collective-permute-start.3 = (bf16[2,4,32,256]{3,2,1,0:T(8,128)(2,1)}, bf16[2,4,32,256]{3,2,1,0:T(8,128)(2,1)S(1)}, u32[]{:S(2)}, u32[]{:S(2)}) collective-permute-start(bf16[2,4,32,256]{3,2,1,0:T(8,128)(2,1)} %get-tuple-element.32), channel_id=1, source_target_pairs={{0,2},{1,3},{2,0},{3,1},{4,6},{5,7},{6,4},{7,5},{8,10},{9,11},{10,... | collective-permute-start | bytes 393224 | tf_op jit(solution)/shard_map/ppermute | solution.py:22
  54.5 0.7 copy-done.5
  55.2 1.9 %fold.10 = (f32[1,8,32,256]{3,2,1,0:T(8,128)}, bf16[1,8,32,256]{3,2,1,0:T(8,128)(2,1)}) custom-call(s32[1]{0:T(128)} %bitcast.2.own_ref, f32[1,2,8,32,256]{4,3,2,1,0:T(8,128)} %bitcast.55, bf16[1,2,8,32,256]{4,3,2,1,0:T(8,128)(2,1)} %bitcast.64), custom_call_target="tpu_custom_call" | custom-call | flops 131072 | bytes 1179648 | tf_op jit(solution)/shard_map/fold/pallas_call | solution.py:248
  57.1 1.1 %collective-permute-start.8 = (bf16[1,8,32,256]{3,2,1,0:T(8,128)(2,1)}, bf16[1,8,32,256]{3,2,1,0:T(8,128)(2,1)S(1)}, u32[]{:S(2)}, u32[]{:S(2)}) collective-permute-start(bf16[1,8,32,256]{3,2,1,0:T(8,128)(2,1)} %get-tuple-element.42), channel_id=1, source_target_pairs={{0,16},{8,24},{16,0},{24,8},{1,17},{9,25},{17,1},{25,9},{2,18},{10... | collective-permute-start | bytes 393224 | tf_op jit(solution)/shard_map/ppermute | solution.py:22
  58.2 0.7 copy-done.6
  58.8 1.7 %fold.8 = (f32[1,4,32,256]{3,2,1,0:T(8,128)}, bf16[1,4,32,256]{3,2,1,0:T(8,128)(2,1)}) custom-call(s32[1]{0:T(128)} %bitcast.own_ref, f32[1,2,4,32,256]{4,3,2,1,0:T(8,128)} %bitcast.61, bf16[1,2,4,32,256]{4,3,2,1,0:T(8,128)(2,1)} %bitcast.65), custom_call_target="tpu_custom_call" | custom-call | flops 65536 | bytes 589824 | tf_op jit(solution)/shard_map/fold/pallas_call | solution.py:248
  60.5 2.6 %collective-permute-start.4 = (bf16[1,4,32,256]{3,2,1,0:T(8,128)(2,1)}, bf16[1,4,32,256]{3,2,1,0:T(8,128)(2,1)S(1)}, u32[]{:S(2)}, u32[]{:S(2)}) collective-permute-start(bf16[1,4,32,256]{3,2,1,0:T(8,128)(2,1)} %get-tuple-element.34), channel_id=1, source_target_pairs={{0,4},{1,5},{2,6},{3,7},{4,0},{5,1},{6,2},{7,3},{8,12},{9,13},{10,... | collective-permute-start | bytes 196616 | tf_op jit(solution)/shard_map/ppermute | solution.py:22
  63.8 1.7 %fold.11 = (f32[1,4,32,256]{3,2,1,0:T(8,128)}, bf16[1,4,32,256]{3,2,1,0:T(8,128)(2,1)}) custom-call(s32[1]{0:T(128)} %bitcast.own_ref, f32[1,2,4,32,256]{4,3,2,1,0:T(8,128)} %bitcast.62, bf16[1,2,4,32,256]{4,3,2,1,0:T(8,128)(2,1)} %bitcast.66), custom_call_target="tpu_custom_call" | custom-call | flops 65536 | bytes 589824 | tf_op jit(solution)/shard_map/fold/pallas_call | solution.py:248
  65.5 1.8 %collective-permute-start.9 = (bf16[1,4,32,256]{3,2,1,0:T(8,128)(2,1)}, bf16[1,4,32,256]{3,2,1,0:T(8,128)(2,1)S(1)}, u32[]{:S(2)}, u32[]{:S(2)}) collective-permute-start(bf16[1,4,32,256]{3,2,1,0:T(8,128)(2,1)} %get-tuple-element.44), channel_id=1, source_target_pairs={{0,4},{1,5},{2,6},{3,7},{4,0},{5,1},{6,2},{7,3},{8,12},{9,13},{10,... | collective-permute-start | bytes 196616 | tf_op jit(solution)/shard_map/ppermute | solution.py:22
  67.2 4.3 %collective-permute-done.9 = bf16[1,4,32,256]{3,2,1,0:T(8,128)(2,1)S(1)} collective-permute-done((bf16[1,4,32,256]{3,2,1,0:T(8,128)(2,1)}, bf16[1,4,32,256]{3,2,1,0:T(8,128)(2,1)S(1)}, u32[]{:S(2)}, u32[]{:S(2)}) %collective-permute-start.9) | collective-permute-done | bytes 65568 | tf_op jit(solution)/shard_map/ppermute | solution.py:22
  72.2 1.7 %last_sum.1 = bf16[32,8,256]{2,1,0:T(8,128)(2,1)} custom-call(f32[4,32,256]{2,1,0:T(8,128)} %bitcast.67, bf16[4,32,256]{2,1,0:T(8,128)(2,1)} %bitcast.69, f32[4,32,256]{2,1,0:T(8,128)} %bitcast.68, bf16[4,32,256]{2,1,0:T(8,128)(2,1)} %bitcast.70), custom_call_target="tpu_custom_call" | custom-call | tf_op jit(solution)/shard_map/last_sum/pallas_call | solution.py:279
  (62 shorter events, 7.1 us)
Async XLA Ops:
  0.0 12.9 %copy-start.10 = (s32[2,2,128,8]{2,3,1,0:T(8,128)S(1)}, s32[2,2,128,8]{2,3,1,0:T(8,128)}, u32[]{:S(2)}) copy-start(s32[2,2,128,8]{2,3,1,0:T(8,128)} %param.7) | copy-start | bytes 49156
  0.6 12.6 %copy-start.12 = (f32[8]{0:T(128)S(1)}, f32[8]{0:T(128)}, u32[]{:S(2)}) copy-start(f32[8]{0:T(128)} %constant.131.clone) | copy-start | bytes 100
  0.6 13.7 %copy-start.11 = (s32[1,8]{1,0:T(1,128)S(1)}, s32[1,8]{1,0:T(1,128)}, u32[]{:S(2)}) copy-start(s32[1,8]{1,0:T(1,128)} %param.8) | copy-start | bytes 100
  8.2 15.6 %collective-permute-start = (bf16[2,2,1,4,64,256]{5,4,3,2,1,0:T(8,128)(2,1)}, bf16[2,2,1,4,64,256]{5,4,3,2,1,0:T(8,128)(2,1)S(1)}, u32[]{:S(2)}, u32[]{:S(2)}) collective-permute-start(bf16[2,2,1,4,64,256]{5,4,3,2,1,0:T(8,128)(2,1)} %get-tuple-element.26), channel_id=1, source_target_pairs={{0,1},{1,0},{2,3},{3,2},{4,5},{5,4},{6,7},{7,6},{8,9},{9,8},{10,11... | collective-permute-start | bytes 1572872 | tf_op jit(solution)/shard_map/ppermute | solution.py:22
  11.2 19.8 %collective-permute-start.5 = (bf16[2,1,2,4,64,256]{5,4,3,2,1,0:T(8,128)(2,1)}, bf16[2,1,2,4,64,256]{5,4,3,2,1,0:T(8,128)(2,1)S(1)}, u32[]{:S(2)}, u32[]{:S(2)}) collective-permute-start(bf16[2,1,2,4,64,256]{5,4,3,2,1,0:T(8,128)(2,1)} %get-tuple-element.36), channel_id=1, source_target_pairs={{0,2},{1,3},{2,0},{3,1},{4,6},{5,7},{6,4},{7,5},{8,10},{9,11},{10,... | collective-permute-start | bytes 1572872 | tf_op jit(solution)/shard_map/ppermute | solution.py:22
  23.8 0.8 %copy-start.1 = (bf16[2,2,1,4,64,256]{5,4,3,2,1,0:T(8,128)(2,1)}, bf16[2,2,1,4,64,256]{5,4,3,2,1,0:T(8,128)(2,1)S(1)}, u32[]{:S(2)}) copy-start(bf16[2,2,1,4,64,256]{5,4,3,2,1,0:T(8,128)(2,1)S(1)} %collective-permute-done) | copy-start | bytes 1572868
  31.0 7.7 %collective-permute-start.1 = (bf16[2,4,4,32,256]{4,3,2,1,0:T(8,128)(2,1)}, bf16[2,4,4,32,256]{4,3,2,1,0:T(8,128)(2,1)S(1)}, u32[]{:S(2)}, u32[]{:S(2)}) collective-permute-start(bf16[2,4,4,32,256]{4,3,2,1,0:T(8,128)(2,1)} %get-tuple-element.28), channel_id=1, source_target_pairs={{0,8},{8,0},{16,24},{24,16},{1,9},{9,1},{17,25},{25,17},{2,10},{10... | collective-permute-start | bytes 1572872 | tf_op jit(solution)/shard_map/ppermute | solution.py:22
  31.0 0.8 %copy-start = (bf16[2,1,2,4,64,256]{5,4,3,2,1,0:T(8,128)(2,1)}, bf16[2,1,2,4,64,256]{5,4,3,2,1,0:T(8,128)(2,1)S(1)}, u32[]{:S(2)}) copy-start(bf16[2,1,2,4,64,256]{5,4,3,2,1,0:T(8,128)(2,1)S(1)} %collective-permute-done.5) | copy-start | bytes 1572868
  38.1 5.1 %collective-permute-start.6 = (bf16[2,4,4,32,256]{4,3,2,1,0:T(8,128)(2,1)}, bf16[2,4,4,32,256]{4,3,2,1,0:T(8,128)(2,1)S(1)}, u32[]{:S(2)}, u32[]{:S(2)}) collective-permute-start(bf16[2,4,4,32,256]{4,3,2,1,0:T(8,128)(2,1)} %get-tuple-element.38), channel_id=1, source_target_pairs={{0,8},{8,0},{16,24},{24,16},{1,9},{9,1},{17,25},{25,17},{2,10},{10... | collective-permute-start | bytes 1572872 | tf_op jit(solution)/shard_map/ppermute | solution.py:22
  38.6 0.8 %copy-start.2 = (bf16[2,4,4,32,256]{4,3,2,1,0:T(8,128)(2,1)}, bf16[2,4,4,32,256]{4,3,2,1,0:T(8,128)(2,1)S(1)}, u32[]{:S(2)}) copy-start(bf16[2,4,4,32,256]{4,3,2,1,0:T(8,128)(2,1)S(1)} %collective-permute-done.1) | copy-start | bytes 1572868
  41.8 8.4 %collective-permute-start.2 = (bf16[1,16,32,256]{3,2,1,0:T(8,128)(2,1)}, bf16[1,16,32,256]{3,2,1,0:T(8,128)(2,1)S(1)}, u32[]{:S(2)}, u32[]{:S(2)}) collective-permute-start(bf16[1,16,32,256]{3,2,1,0:T(8,128)(2,1)} %get-tuple-element.30), channel_id=1, source_target_pairs={{0,16},{8,24},{16,0},{24,8},{1,17},{9,25},{17,1},{25,9},{2,18},{10... | collective-permute-start | bytes 786440 | tf_op jit(solution)/shard_map/ppermute | solution.py:22
  43.2 0.8 %copy-start.3 = (bf16[2,4,4,32,256]{4,3,2,1,0:T(8,128)(2,1)}, bf16[2,4,4,32,256]{4,3,2,1,0:T(8,128)(2,1)S(1)}, u32[]{:S(2)}) copy-start(bf16[2,4,4,32,256]{4,3,2,1,0:T(8,128)(2,1)S(1)} %collective-permute-done.6) | copy-start | bytes 1572868
  46.4 8.2 %collective-permute-start.7 = (bf16[4,4,32,256]{3,2,1,0:T(8,128)(2,1)}, bf16[4,4,32,256]{3,2,1,0:T(8,128)(2,1)S(1)}, u32[]{:S(2)}, u32[]{:S(2)}) collective-permute-start(bf16[4,4,32,256]{3,2,1,0:T(8,128)(2,1)} %get-tuple-element.40), channel_id=1, source_target_pairs={{0,1},{1,0},{2,3},{3,2},{4,5},{5,4},{6,7},{7,6},{8,9},{9,8},{10,11... | collective-permute-start | bytes 786440 | tf_op jit(solution)/shard_map/ppermute | solution.py:22
  50.2 0.7 copy-start.4
  52.8 5.4 %collective-permute-start.3 = (bf16[2,4,32,256]{3,2,1,0:T(8,128)(2,1)}, bf16[2,4,32,256]{3,2,1,0:T(8,128)(2,1)S(1)}, u32[]{:S(2)}, u32[]{:S(2)}) collective-permute-start(bf16[2,4,32,256]{3,2,1,0:T(8,128)(2,1)} %get-tuple-element.32), channel_id=1, source_target_pairs={{0,2},{1,3},{2,0},{3,1},{4,6},{5,7},{6,4},{7,5},{8,10},{9,11},{10,... | collective-permute-start | bytes 393224 | tf_op jit(solution)/shard_map/ppermute | solution.py:22
  54.5 0.7 copy-start.5
  57.1 6.0 %collective-permute-start.8 = (bf16[1,8,32,256]{3,2,1,0:T(8,128)(2,1)}, bf16[1,8,32,256]{3,2,1,0:T(8,128)(2,1)S(1)}, u32[]{:S(2)}, u32[]{:S(2)}) collective-permute-start(bf16[1,8,32,256]{3,2,1,0:T(8,128)(2,1)} %get-tuple-element.42), channel_id=1, source_target_pairs={{0,16},{8,24},{16,0},{24,8},{1,17},{9,25},{17,1},{25,9},{2,18},{10... | collective-permute-start | bytes 393224 | tf_op jit(solution)/shard_map/ppermute | solution.py:22
  58.2 0.7 copy-start.6
  60.5 6.7 %collective-permute-start.4 = (bf16[1,4,32,256]{3,2,1,0:T(8,128)(2,1)}, bf16[1,4,32,256]{3,2,1,0:T(8,128)(2,1)S(1)}, u32[]{:S(2)}, u32[]{:S(2)}) collective-permute-start(bf16[1,4,32,256]{3,2,1,0:T(8,128)(2,1)} %get-tuple-element.34), channel_id=1, source_target_pairs={{0,4},{1,5},{2,6},{3,7},{4,0},{5,1},{6,2},{7,3},{8,12},{9,13},{10,... | collective-permute-start | bytes 196616 | tf_op jit(solution)/shard_map/ppermute | solution.py:22
  63.1 0.7 copy-start.7
  65.5 6.1 %collective-permute-start.9 = (bf16[1,4,32,256]{3,2,1,0:T(8,128)(2,1)}, bf16[1,4,32,256]{3,2,1,0:T(8,128)(2,1)S(1)}, u32[]{:S(2)}, u32[]{:S(2)}) collective-permute-start(bf16[1,4,32,256]{3,2,1,0:T(8,128)(2,1)} %get-tuple-element.44), channel_id=1, source_target_pairs={{0,4},{1,5},{2,6},{3,7},{4,0},{5,1},{6,2},{7,3},{8,12},{9,13},{10,... | collective-permute-start | bytes 196616 | tf_op jit(solution)/shard_map/ppermute | solution.py:22
  67.2 4.3 %copy-start.8 = (bf16[1,4,32,256]{3,2,1,0:T(8,128)(2,1)}, bf16[1,4,32,256]{3,2,1,0:T(8,128)(2,1)S(1)}, u32[]{:S(2)}) copy-start(bf16[1,4,32,256]{3,2,1,0:T(8,128)(2,1)S(1)} %collective-permute-done.4) | copy-start | bytes 196612
  71.5 0.6 copy-start.9

commit v4 on v3

--- a/solution.py
+++ b/solution.py
@@ -224,7 +224,7 @@
             jax.ShapeDtypeStruct(shape, jnp.float32),
             jax.ShapeDtypeStruct(shape, jnp.bfloat16),
         ],
-        compiler_params=pltpu.CompilerParams(vmem_limit_bytes=VMEM_BYTES),
+        compiler_params=pltpu.CompilerParams(vmem_limit_bytes=16 * 2**20),
         cost_estimate=pl.CostEstimate(
             flops=12 * beams * pulses * keep.shape[0] * each * width,
             bytes_accessed=4 * keep.size + 6 * shape[0] * count * each * rows * width,
@@ -234,31 +234,12 @@
     )(own, keep, got, steer, interp, base, step)
 
 
-def fold_kernel(own_ref, keep_ref, got_ref, out_keep, out_send):
-    own = own_ref[0]
-    for a in range(keep_ref.shape[0]):
-        out_send[a] = (
-            keep_ref[a, 1 - own] + got_ref[a, 1 - own].astype(jnp.float32)
-        ).astype(jnp.bfloat16)
-        out_keep[a] = keep_ref[a, own] + got_ref[a, own].astype(jnp.float32)
-
-
 def fold(own, keep, got):
-    shape = keep.shape[:1] + keep.shape[2:]
-    return pl.pallas_call(
-        fold_kernel,
-        in_specs=[SCALARS] + [pl.BlockSpec(memory_space=pltpu.VMEM)] * 2,
-        out_specs=[pl.BlockSpec(memory_space=pltpu.VMEM)] * 2,
-        out_shape=[
-            jax.ShapeDtypeStruct(shape, jnp.float32),
-            jax.ShapeDtypeStruct(shape, jnp.bfloat16),
-        ],
-        compiler_params=pltpu.CompilerParams(vmem_limit_bytes=VMEM_BYTES),
-        cost_estimate=pl.CostEstimate(
-            flops=keep.size, bytes_accessed=9 * keep.size, transcendentals=0
-        ),
-        name="fold",
-    )(own, keep, got)
+    def half(at):
+        kept, came = (lax.dynamic_index_in_dim(a, at, 1, False) for a in (keep, got))
+        return kept + came.astype(jnp.float32)
+
+    return half(own), half(1 - own).astype(jnp.bfloat16)
 
 
 def last_kernel(keep_y, got_y, keep_z, got_z, out_ref, rows_ref):
@@ -280,6 +261,7 @@
         last_kernel,
         out_shape=jax.ShapeDtypeStruct((rows, 2 * each, width), jnp.bfloat16),
         scratch_shapes=[pltpu.VMEM((2, rows * 2 * each, width // 2), jnp.float32)],
+        compiler_params=pltpu.CompilerParams(vmem_limit_bytes=8 * 2**20),
         name="last_sum",
     )(keep_y, got_y, keep_z, got_z)
 
@@ -401,7 +383,7 @@
             before, after = 1 << at, (1 << len(leading) - at - 1) * each
             leading.pop(at)
             split = (before, 2, after, rows, width)
-            own = scalar(bit(own_leaf if axis == "leaf" else own_turn, b))
+            own = bit(own_leaf if axis == "leaf" else own_turn, b)
             kept, sent = fold(own, kept.reshape(split), arrived.reshape(split))
             arrived = swapped(sent, axis, b)
         final += [kept.reshape(each, rows, width), arrived.reshape(each, rows, width)]

time: 74.4 us -> 61.8 us (0.83)
  Pallas kernels: 33.9 us -> 17.6 us
  local copies, waits for them, and re-layouts: 10.1 us -> 5.79 us
  other arithmetic: 7.83 us -> 11 us
  starting transfers between devices: 14.5 us -> 17 us
  waiting for transfers between devices: 7.31 us -> 9.65 us
    pallas_call x6 -> x0, Pallas kernels: 11.8 us -> none  [fold(): pl.pallas_call(fold_kernel, in_specs=[SCALARS] + [pl.BlockSpec(memory_spa...]
    pallas_call x2, Pallas kernels: 12.7 us -> 9.23 us  [backproject(): pl.pallas_call(functools.partial(image_kernel, (leaf, each, half, beams,...]
    convert_element_type x0 -> x6, other arithmetic: none -> 2.53 us  [fold(): return (half(own), half(1 - own).astype(jnp.bfloat16))]
    ppermute x10, starting transfers between devices: 14.5 us -> 17 us  [swapped(): lax.ppermute(array, axis, [(i, i ^ 1 << bit) for i in range(lax.axis_size...]
    ppermute x10, waiting for transfers between devices: 7.31 us -> 9.65 us  [swapped(): lax.ppermute(array, axis, [(i, i ^ 1 << bit) for i in range(lax.axis_size...]
    unnamed x26 -> x18, local copies, waits for them, and re-layouts: 6.57 us -> 4.74 us
    another operation x2, local copies, waits for them, and re-layouts: 1.2 us -> 0.01 us  [bases(): jnp.stack(unit(slopes[:, None] * lean * start + squares, PERIOD), axis=2)]
    cos x2, other arithmetic: 2.27 us -> 3.29 us  [unit(): return (jnp.cos(angle), jnp.sin(angle))]
  transfers between devices with their start and end apart: 10 -> 10, of which waited for: 3 -> 6; matrix products, arithmetic and copies ran while one was open for 15% -> 19% of each run, Pallas kernels for 33% -> 15%
where the time goes in v4:
time: 61.8 us; the launch traced here: 61.4 us
  Pallas kernels  17.6 us (28%)
  starting transfers between devices  17 us (28%)
  other arithmetic  11 us (18%)
  waiting for transfers between devices  9.65 us (16%)
  local copies, waits for them, and re-layouts  5.79 us (9%)
    ppermute x10, starting transfers between devices, swapped(): lax.ppermute(array, axis, [(i, i ^ 1 << bit) for i in range(lax.axis_size...  17 us
    ppermute x10, waiting for transfers between devices, swapped(): lax.ppermute(array, axis, [(i, i ^ 1 << bit) for i in range(lax.axis_size...  9.65 us
    pallas_call x2, Pallas kernels, backproject(): pl.pallas_call(functools.partial(image_kernel, (leaf, each, half, beams,...  9.23 us
    pallas_call x1, Pallas kernels, compress(): pl.pallas_call(functools.partial(compress_kernel, (each, pulses, half)),...  7.6 us
    unnamed x18, local copies, waits for them, and re-layouts  4.74 us
    cos x2, other arithmetic, unit(): return (jnp.cos(angle), jnp.sin(angle))  3.29 us
    convert_element_type x6, other arithmetic, fold(): return (half(own), half(1 - own).astype(jnp.bfloat16))  2.53 us
    add x1, other arithmetic, steering(): 2 * slot + 1  2.08 us
  transfers between devices with their start and end apart: 10, of which 6 were waited for; matrix products, arithmetic and copies ran while one was open for 19% of the time, Pallas kernels for 15%

profile of v4, /device:TPU:0, one launch (start us, length us, event | category | flops | bytes accessed | tf_op | source)
XLA Modules:
  0.0 61.4 jit_solution(11194725587868184726)
XLA Ops:
  0.0 0.7 %pad_add_fusion.1 = (s32[2]{0:T(128)}, s32[2]{0:T(128)S(1)}) fusion(s32[1]{0:T(128)} %bitcast.2, s32[1]{0:T(128)} %bitcast.1, s32[1]{0:T(128)} %bitcast.17, s32[1]{0:T(128)} %bitcast.16), kind=kLoop, calls=%fused_computation.90 | loop fusion | flops 4 | bytes 32 | tf_op jit(solution)/shard_map/concatenate | solution.py:321
  0.7 7.6 %compress.1 = (bf16[2,2,1,4,64,256]{5,4,3,2,1,0:T(8,128)(2,1)}, bf16[2,2,1,4,64,256]{5,4,3,2,1,0:T(8,128)(2,1)}, bf16[2,1,2,4,64,256]{5,4,3,2,1,0:T(8,128)(2,1)}, bf16[2,1,2,4,64,256]{5,4,3,2,1,0:T(8,128)(2,1)}) custom-call(s32[2]{0:T(128)} %get-tuple-element.51.own_ref, bf16[2,128]{1,0:T(2,128)(2,1)} %chirp_ref.1, bf16[64,64,256]{2,1,0:T(8,128)(2,1)} %echo_ref.1), custom_call_target="tpu_custom_call" | custom-call | flops 1073741824 | bytes 4194304 | tf_op jit(solution)/shard_map/compress/pallas_call | solution.py:104
  8.3 3.0 %collective-permute-start = (bf16[2,2,1,4,64,256]{5,4,3,2,1,0:T(8,128)(2,1)}, bf16[2,2,1,4,64,256]{5,4,3,2,1,0:T(8,128)(2,1)S(1)}, u32[]{:S(2)}, u32[]{:S(2)}) collective-permute-start(bf16[2,2,1,4,64,256]{5,4,3,2,1,0:T(8,128)(2,1)} %get-tuple-element.14), channel_id=1, source_target_pairs={{0,1},{1,0},{2,3},{3,2},{4,5},{5,4},{6,7},{7,6},{8,9},{9,8},{10,11... | collective-permute-start | bytes 1572872 | tf_op jit(solution)/shard_map/ppermute | solution.py:22
  11.2 1.6 %collective-permute-start.5 = (bf16[2,1,2,4,64,256]{5,4,3,2,1,0:T(8,128)(2,1)}, bf16[2,1,2,4,64,256]{5,4,3,2,1,0:T(8,128)(2,1)S(1)}, u32[]{:S(2)}, u32[]{:S(2)}) collective-permute-start(bf16[2,1,2,4,64,256]{5,4,3,2,1,0:T(8,128)(2,1)} %get-tuple-element.18), channel_id=1, source_target_pairs={{0,2},{1,3},{2,0},{3,1},{4,6},{5,7},{6,4},{7,5},{8,10},{9,11},{10,... | collective-permute-start | bytes 1572872 | tf_op jit(solution)/shard_map/ppermute | solution.py:22
  13.7 0.7 %constant_dynamic-slice_fusion.2 = (s32[1,1]{1,0:T(1,128)}, s32[1,1]{1,0:T(1,128)}, s32[1,1]{1,0:T(1,128)}) fusion(s32[1,8]{1,0:T(1,128)S(1)} %copy-done.7, s32[]{:T(128)S(6)} %select_n.142, s32[]{:T(128)S(6)} %select_n.144, s32[]{:T(128)S(6)} %select_n.143), kind=kLoop, calls=%fused_computation.61 | loop fusion | bytes 36 | tf_op jit(solution)/shard_map/jit(dynamic_index_in_dim)/dynamic_slice | solution.py:334
  14.4 2.1 %fusion.37 = s32[3]{0:T(128)S(1)} fusion(s32[1]{0:T(128)} %bitcast.11, s32[1]{0:T(128)} %bitcast.10, s32[1]{0:T(128)} %bitcast.9), kind=kLoop, calls=%fused_computation.92 | loop fusion | flops 12 | bytes 24 | tf_op jit(solution)/shard_map/add | solution.py:283
  16.6 0.5 multiply_convert_fusion.1
  17.2 3.1 %fusion.7 = (f32[2,1,128,512]{3,2,1,0:T(8,128)S(1)}, f32[2,1,128,512]{3,2,1,0:T(8,128)}) fusion(s32[512]{0:T(512)S(1)} %iota_add_fusion, s32[2,128]{1,0:T(2,128)S(1)} %broadcast_multiply_fusion.2), kind=kLoop, calls=%fused_computation.23 | loop fusion | flops 1835008 | bytes 1051648 | tf_op jit(solution)/shard_map/cos | solution.py:27
  20.8 1.1 %pad_maximum_fusion.step_ref = f32[2,2,128,512]{3,2,1,0:T(8,128)S(1)} fusion(f32[2,1,128,512]{3,2,1,0:T(8,128)} %get-tuple-element.41, f32[2,1,128,512]{3,2,1,0:T(8,128)S(1)} %get-tuple-element.40), kind=kLoop, calls=%fused_computation | loop fusion | flops 262144 | bytes 2097152 | tf_op jit(solution)/shard_map/stack | solution.py:347
  21.9 1.4 %collective-permute-done = bf16[2,2,1,4,64,256]{5,4,3,2,1,0:T(8,128)(2,1)S(1)} collective-permute-done((bf16[2,2,1,4,64,256]{5,4,3,2,1,0:T(8,128)(2,1)}, bf16[2,2,1,4,64,256]{5,4,3,2,1,0:T(8,128)(2,1)S(1)}, u32[]{:S(2)}, u32[]{:S(2)}) %collective-permute-start) | collective-permute-done | bytes 524320 | tf_op jit(solution)/shard_map/ppermute | solution.py:22
  23.4 0.8 %copy-done.4 = bf16[2,2,1,4,64,256]{5,4,3,2,1,0:T(8,128)(2,1)} copy-done((bf16[2,2,1,4,64,256]{5,4,3,2,1,0:T(8,128)(2,1)}, bf16[2,2,1,4,64,256]{5,4,3,2,1,0:T(8,128)(2,1)S(1)}, u32[]{:S(2)}) %copy-start.4) | copy-done | bytes 524312
  24.2 1.0 %copy-done.5 = bf16[2,2,1,4,64,256]{5,4,3,2,1,0:T(8,128)(2,1)S(1)} copy-done((bf16[2,2,1,4,64,256]{5,4,3,2,1,0:T(8,128)(2,1)S(1)}, bf16[2,2,1,4,64,256]{5,4,3,2,1,0:T(8,128)(2,1)}, u32[]{:S(2)}) %copy-start.5) | copy-done | bytes 524312
  25.2 4.6 %image.2 = (f32[2,4,4,32,256]{4,3,2,1,0:T(8,128)S(1)}, bf16[2,4,4,32,256]{4,3,2,1,0:T(8,128)(2,1)}) custom-call(s32[1]{0:T(128)} %bitcast.own_ref, bf16[4,4,64,256]{3,2,1,0:T(8,128)(2,1)S(1)} %bitcast.77, bf16[4,4,64,256]{3,2,1,0:T(8,128)(2,1)S(1)} %bitcast.78, bf16[256,256]{1,0:T(8,128)(2,1)S(1)} %copy.25.steer_ref, ...), custom_call_target="tpu_custom_call" | custom-call | flops 402653184 | bytes 2621440 | tf_op jit(solution)/shard_map/image/pallas_call | solution.py:210
  30.0 0.8 %copy-done.1 = bf16[2,1,2,4,64,256]{5,4,3,2,1,0:T(8,128)(2,1)} copy-done((bf16[2,1,2,4,64,256]{5,4,3,2,1,0:T(8,128)(2,1)}, bf16[2,1,2,4,64,256]{5,4,3,2,1,0:T(8,128)(2,1)S(1)}, u32[]{:S(2)}) %copy-start.1) | copy-done | bytes 524312
  30.8 1.0 %copy-done = bf16[2,1,2,4,64,256]{5,4,3,2,1,0:T(8,128)(2,1)S(1)} copy-done((bf16[2,1,2,4,64,256]{5,4,3,2,1,0:T(8,128)(2,1)S(1)}, bf16[2,1,2,4,64,256]{5,4,3,2,1,0:T(8,128)(2,1)}, u32[]{:S(2)}) %copy-start) | copy-done | bytes 524312
  31.8 1.0 %copy-done.2 = bf16[2,1,2,4,64,256]{5,4,3,2,1,0:T(8,128)(2,1)S(1)} copy-done((bf16[2,1,2,4,64,256]{5,4,3,2,1,0:T(8,128)(2,1)S(1)}, bf16[2,1,2,4,64,256]{5,4,3,2,1,0:T(8,128)(2,1)}, u32[]{:S(2)}) %copy-start.2) | copy-done | bytes 524312
  32.9 4.6 %image.3 = (f32[2,4,4,32,256]{4,3,2,1,0:T(8,128)S(1)}, bf16[2,4,4,32,256]{4,3,2,1,0:T(8,128)(2,1)}) custom-call(s32[1]{0:T(128)} %bitcast.own_ref, bf16[4,4,64,256]{3,2,1,0:T(8,128)(2,1)S(1)} %bitcast.75, bf16[4,4,64,256]{3,2,1,0:T(8,128)(2,1)S(1)} %bitcast.76, bf16[256,256]{1,0:T(8,128)(2,1)S(1)} %copy.26.steer_ref, ...), custom_call_target="tpu_custom_call" | custom-call | flops 402653184 | bytes 2621440 | tf_op jit(solution)/shard_map/image/pallas_call | solution.py:210
  37.5 0.5 collective-permute-start.6
  38.0 1.2 %fusion.3 = (bf16[1,16,32,256]{3,2,1,0:T(8,128)(2,1)S(1)}, f32[1,1,16,32,256]{4,3,2,1,0:T(8,128)S(1)}) fusion(f32[1,2,16,32,256]{4,3,2,1,0:T(8,128)S(1)} %bitcast.73, s32[]{:T(128)S(6)} %select_n.149, bf16[1,2,16,32,256]{4,3,2,1,0:T(8,128)(2,1)} %bitcast.20, s32[]{:T(128)S(6)} %select_n.140), kind=kLoop, calls=%fused_computation.15 | loop fusion | flops 655360 | bytes 2359304 | tf_op jit(solution)/shard_map/convert_element_type | solution.py:242
  39.2 1.8 %collective-permute-start.2 = (bf16[1,16,32,256]{3,2,1,0:T(8,128)(2,1)S(1)}, bf16[1,16,32,256]{3,2,1,0:T(8,128)(2,1)S(1)}, u32[]{:S(2)}, u32[]{:S(2)}) collective-permute-start(bf16[1,16,32,256]{3,2,1,0:T(8,128)(2,1)S(1)} %get-tuple-element.23), channel_id=1, source_target_pairs={{0,16},{8,24},{16,0},{24,8},{1,17},{9,25},{17,1},{25,9},{2,18},{10... | collective-permute-start | bytes 786440 | tf_op jit(solution)/shard_map/ppermute | solution.py:22
  41.0 1.2 %fusion.4 = (bf16[4,4,32,256]{3,2,1,0:T(8,128)(2,1)S(1)}, f32[4,1,4,32,256]{4,3,2,1,0:T(8,128)S(1)}) fusion(f32[4,2,4,32,256]{4,3,2,1,0:T(8,128)S(1)} %bitcast.74, s32[]{:T(128)S(6)} %select_n.155, bf16[4,2,4,32,256]{4,3,2,1,0:T(8,128)(2,1)} %bitcast.34, s32[]{:T(128)S(6)} %select_n.154), kind=kLoop, calls=%fused_computation.16 | loop fusion | flops 655360 | bytes 2359304 | tf_op jit(solution)/shard_map/convert_element_type | solution.py:242
  42.2 1.6 %collective-permute-start.7 = (bf16[4,4,32,256]{3,2,1,0:T(8,128)(2,1)S(1)}, bf16[4,4,32,256]{3,2,1,0:T(8,128)(2,1)S(1)}, u32[]{:S(2)}, u32[]{:S(2)}) collective-permute-start(bf16[4,4,32,256]{3,2,1,0:T(8,128)(2,1)S(1)} %get-tuple-element.21), channel_id=1, source_target_pairs={{0,1},{1,0},{2,3},{3,2},{4,5},{5,4},{6,7},{7,6},{8,9},{9,8},{10,11... | collective-permute-start | bytes 786440 | tf_op jit(solution)/shard_map/ppermute | solution.py:22
  43.7 3.7 %collective-permute-done.2 = bf16[1,16,32,256]{3,2,1,0:T(8,128)(2,1)S(1)} collective-permute-done((bf16[1,16,32,256]{3,2,1,0:T(8,128)(2,1)S(1)}, bf16[1,16,32,256]{3,2,1,0:T(8,128)(2,1)S(1)}, u32[]{:S(2)}, u32[]{:S(2)}) %collective-permute-start.2) | collective-permute-done | bytes 262176 | tf_op jit(solution)/shard_map/ppermute | solution.py:22
  47.5 1.9 %collective-permute-start.3 = (bf16[2,4,32,256]{3,2,1,0:T(8,128)(2,1)S(1)}, bf16[2,4,32,256]{3,2,1,0:T(8,128)(2,1)S(1)}, u32[]{:S(2)}, u32[]{:S(2)}) collective-permute-start(bf16[2,4,32,256]{3,2,1,0:T(8,128)(2,1)S(1)} %fusion.9), channel_id=1, source_target_pairs={{0,2},{1,3},{2,0},{3,1},{4,6},{5,7},{6,4},{7,5},{8,10},{9,11},{10,... | collective-permute-start | bytes 393224 | tf_op jit(solution)/shard_map/ppermute | solution.py:22
  49.4 0.8 %collective-permute-done.7 = bf16[4,4,32,256]{3,2,1,0:T(8,128)(2,1)S(1)} collective-permute-done((bf16[4,4,32,256]{3,2,1,0:T(8,128)(2,1)S(1)}, bf16[4,4,32,256]{3,2,1,0:T(8,128)(2,1)S(1)}, u32[]{:S(2)}, u32[]{:S(2)}) %collective-permute-start.7) | collective-permute-done | bytes 262176 | tf_op jit(solution)/shard_map/ppermute | solution.py:22
  50.2 1.3 %collective-permute-start.8 = (bf16[1,8,32,256]{3,2,1,0:T(8,128)(2,1)S(1)}, bf16[1,8,32,256]{3,2,1,0:T(8,128)(2,1)S(1)}, u32[]{:S(2)}, u32[]{:S(2)}) collective-permute-start(bf16[1,8,32,256]{3,2,1,0:T(8,128)(2,1)S(1)} %get-tuple-element.25), channel_id=1, source_target_pairs={{0,16},{8,24},{16,0},{24,8},{1,17},{9,25},{17,1},{25,9},{2,18},{10... | collective-permute-start | bytes 393224 | tf_op jit(solution)/shard_map/ppermute | solution.py:22
  51.6 0.9 %collective-permute-done.3 = bf16[2,4,32,256]{3,2,1,0:T(8,128)(2,1)S(1)} collective-permute-done((bf16[2,4,32,256]{3,2,1,0:T(8,128)(2,1)S(1)}, bf16[2,4,32,256]{3,2,1,0:T(8,128)(2,1)S(1)}, u32[]{:S(2)}, u32[]{:S(2)}) %collective-permute-start.3) | collective-permute-done | bytes 131104 | tf_op jit(solution)/shard_map/ppermute | solution.py:22
  52.6 2.9 %collective-permute-start.4 = (bf16[1,4,32,256]{3,2,1,0:T(8,128)(2,1)S(1)}, bf16[1,4,32,256]{3,2,1,0:T(8,128)(2,1)S(1)}, u32[]{:S(2)}, u32[]{:S(2)}) collective-permute-start(bf16[1,4,32,256]{3,2,1,0:T(8,128)(2,1)S(1)} %get-tuple-element.29), channel_id=1, source_target_pairs={{0,4},{1,5},{2,6},{3,7},{4,0},{5,1},{6,2},{7,3},{8,12},{9,13},{10,... | collective-permute-start | bytes 196616 | tf_op jit(solution)/shard_map/ppermute | solution.py:22
  55.5 2.5 %collective-permute-start.9 = (bf16[1,4,32,256]{3,2,1,0:T(8,128)(2,1)S(1)}, bf16[1,4,32,256]{3,2,1,0:T(8,128)(2,1)S(1)}, u32[]{:S(2)}, u32[]{:S(2)}) collective-permute-start(bf16[1,4,32,256]{3,2,1,0:T(8,128)(2,1)S(1)} %get-tuple-element.27), channel_id=1, source_target_pairs={{0,4},{1,5},{2,6},{3,7},{4,0},{5,1},{6,2},{7,3},{8,12},{9,13},{10,... | collective-permute-start | bytes 196616 | tf_op jit(solution)/shard_map/ppermute | solution.py:22
  58.0 1.7 %collective-permute-done.4 = bf16[1,4,32,256]{3,2,1,0:T(8,128)(2,1)S(1)} collective-permute-done((bf16[1,4,32,256]{3,2,1,0:T(8,128)(2,1)S(1)}, bf16[1,4,32,256]{3,2,1,0:T(8,128)(2,1)S(1)}, u32[]{:S(2)}, u32[]{:S(2)}) %collective-permute-start.4) | collective-permute-done | bytes 65568 | tf_op jit(solution)/shard_map/ppermute | solution.py:22
  59.7 1.0 %collective-permute-done.9 = bf16[1,4,32,256]{3,2,1,0:T(8,128)(2,1)S(1)} collective-permute-done((bf16[1,4,32,256]{3,2,1,0:T(8,128)(2,1)S(1)}, bf16[1,4,32,256]{3,2,1,0:T(8,128)(2,1)S(1)}, u32[]{:S(2)}, u32[]{:S(2)}) %collective-permute-start.9) | collective-permute-done | bytes 65568 | tf_op jit(solution)/shard_map/ppermute | solution.py:22
  60.7 0.7 %last_sum.1 = bf16[32,8,256]{2,1,0:T(8,128)(2,1)} custom-call(f32[4,32,256]{2,1,0:T(8,128)S(1)} %get-tuple-element.30.keep_y, bf16[4,32,256]{2,1,0:T(8,128)(2,1)S(1)} %bitcast.79, f32[4,32,256]{2,1,0:T(8,128)S(1)} %get-tuple-element.28.keep_z, bf16[4,32,256]{2,1,0:T(8,128)(2,1)S(1)} %bitcast.80), custom_call_target="tpu_custom_call" | custom-call | tf_op jit(solution)/shard_map/last_sum/pallas_call | solution.py:260
  (55 shorter events, 1.7 us)
Async XLA Ops:
  0.0 13.0 %copy-start.6 = (s32[2,2,128,8]{2,3,1,0:T(8,128)S(1)}, s32[2,2,128,8]{2,3,1,0:T(8,128)}, u32[]{:S(2)}) copy-start(s32[2,2,128,8]{2,3,1,0:T(8,128)} %param.7) | copy-start | bytes 49156
  0.7 12.6 %copy-start.8 = (f32[8]{0:T(128)S(1)}, f32[8]{0:T(128)}, u32[]{:S(2)}) copy-start(f32[8]{0:T(128)} %constant.205.clone) | copy-start | bytes 100
  0.7 13.1 %copy-start.7 = (s32[1,8]{1,0:T(1,128)S(1)}, s32[1,8]{1,0:T(1,128)}, u32[]{:S(2)}) copy-start(s32[1,8]{1,0:T(1,128)} %param.8) | copy-start | bytes 100
  8.3 15.1 %collective-permute-start = (bf16[2,2,1,4,64,256]{5,4,3,2,1,0:T(8,128)(2,1)}, bf16[2,2,1,4,64,256]{5,4,3,2,1,0:T(8,128)(2,1)S(1)}, u32[]{:S(2)}, u32[]{:S(2)}) collective-permute-start(bf16[2,2,1,4,64,256]{5,4,3,2,1,0:T(8,128)(2,1)} %get-tuple-element.14), channel_id=1, source_target_pairs={{0,1},{1,0},{2,3},{3,2},{4,5},{5,4},{6,7},{7,6},{8,9},{9,8},{10,11... | collective-permute-start | bytes 1572872 | tf_op jit(solution)/shard_map/ppermute | solution.py:22
  11.2 18.7 %collective-permute-start.5 = (bf16[2,1,2,4,64,256]{5,4,3,2,1,0:T(8,128)(2,1)}, bf16[2,1,2,4,64,256]{5,4,3,2,1,0:T(8,128)(2,1)S(1)}, u32[]{:S(2)}, u32[]{:S(2)}) collective-permute-start(bf16[2,1,2,4,64,256]{5,4,3,2,1,0:T(8,128)(2,1)} %get-tuple-element.18), channel_id=1, source_target_pairs={{0,2},{1,3},{2,0},{3,1},{4,6},{5,7},{6,4},{7,5},{8,10},{9,11},{10,... | collective-permute-start | bytes 1572872 | tf_op jit(solution)/shard_map/ppermute | solution.py:22
  20.4 3.8 %copy-start.3 = (bf16[2,2,1,4,64,256]{5,4,3,2,1,0:T(8,128)(2,1)S(1)}, bf16[2,2,1,4,64,256]{5,4,3,2,1,0:T(8,128)(2,1)}, u32[]{:S(2)}) copy-start(bf16[2,2,1,4,64,256]{5,4,3,2,1,0:T(8,128)(2,1)} %get-tuple-element.13) | copy-start | bytes 1572868
  23.4 0.8 %copy-start.4 = (bf16[2,2,1,4,64,256]{5,4,3,2,1,0:T(8,128)(2,1)}, bf16[2,2,1,4,64,256]{5,4,3,2,1,0:T(8,128)(2,1)S(1)}, u32[]{:S(2)}) copy-start(bf16[2,2,1,4,64,256]{5,4,3,2,1,0:T(8,128)(2,1)S(1)} %collective-permute-done) | copy-start | bytes 1572868
  24.2 1.0 %copy-start.5 = (bf16[2,2,1,4,64,256]{5,4,3,2,1,0:T(8,128)(2,1)S(1)}, bf16[2,2,1,4,64,256]{5,4,3,2,1,0:T(8,128)(2,1)}, u32[]{:S(2)}) copy-start(bf16[2,2,1,4,64,256]{5,4,3,2,1,0:T(8,128)(2,1)} %copy-done.4) | copy-start | bytes 1572868
  29.8 8.2 %collective-permute-start.1 = (bf16[2,4,4,32,256]{4,3,2,1,0:T(8,128)(2,1)}, bf16[2,4,4,32,256]{4,3,2,1,0:T(8,128)(2,1)}, u32[]{:S(2)}, u32[]{:S(2)}) collective-permute-start(bf16[2,4,4,32,256]{4,3,2,1,0:T(8,128)(2,1)} %get-tuple-element.16), channel_id=1, source_target_pairs={{0,8},{8,0},{16,24},{24,16},{1,9},{9,1},{17,25},{25,17},{2,10},{10... | collective-permute-start | bytes 1572872 | tf_op jit(solution)/shard_map/ppermute | solution.py:22
  30.0 0.8 %copy-start.1 = (bf16[2,1,2,4,64,256]{5,4,3,2,1,0:T(8,128)(2,1)}, bf16[2,1,2,4,64,256]{5,4,3,2,1,0:T(8,128)(2,1)S(1)}, u32[]{:S(2)}) copy-start(bf16[2,1,2,4,64,256]{5,4,3,2,1,0:T(8,128)(2,1)S(1)} %collective-permute-done.5) | copy-start | bytes 1572868
  30.8 1.0 %copy-start = (bf16[2,1,2,4,64,256]{5,4,3,2,1,0:T(8,128)(2,1)S(1)}, bf16[2,1,2,4,64,256]{5,4,3,2,1,0:T(8,128)(2,1)}, u32[]{:S(2)}) copy-start(bf16[2,1,2,4,64,256]{5,4,3,2,1,0:T(8,128)(2,1)} %get-tuple-element.17) | copy-start | bytes 1572868
  31.8 1.0 %copy-start.2 = (bf16[2,1,2,4,64,256]{5,4,3,2,1,0:T(8,128)(2,1)S(1)}, bf16[2,1,2,4,64,256]{5,4,3,2,1,0:T(8,128)(2,1)}, u32[]{:S(2)}) copy-start(bf16[2,1,2,4,64,256]{5,4,3,2,1,0:T(8,128)(2,1)} %copy-done.1) | copy-start | bytes 1572868
  37.5 3.5 %collective-permute-start.6 = (bf16[2,4,4,32,256]{4,3,2,1,0:T(8,128)(2,1)}, bf16[2,4,4,32,256]{4,3,2,1,0:T(8,128)(2,1)}, u32[]{:S(2)}, u32[]{:S(2)}) collective-permute-start(bf16[2,4,4,32,256]{4,3,2,1,0:T(8,128)(2,1)} %get-tuple-element.20), channel_id=1, source_target_pairs={{0,8},{8,0},{16,24},{24,16},{1,9},{9,1},{17,25},{25,17},{2,10},{10... | collective-permute-start | bytes 1572872 | tf_op jit(solution)/shard_map/ppermute | solution.py:22
  39.2 8.3 %collective-permute-start.2 = (bf16[1,16,32,256]{3,2,1,0:T(8,128)(2,1)S(1)}, bf16[1,16,32,256]{3,2,1,0:T(8,128)(2,1)S(1)}, u32[]{:S(2)}, u32[]{:S(2)}) collective-permute-start(bf16[1,16,32,256]{3,2,1,0:T(8,128)(2,1)S(1)} %get-tuple-element.23), channel_id=1, source_target_pairs={{0,16},{8,24},{16,0},{24,8},{1,17},{9,25},{17,1},{25,9},{2,18},{10... | collective-permute-start | bytes 786440 | tf_op jit(solution)/shard_map/ppermute | solution.py:22
  42.2 8.0 %collective-permute-start.7 = (bf16[4,4,32,256]{3,2,1,0:T(8,128)(2,1)S(1)}, bf16[4,4,32,256]{3,2,1,0:T(8,128)(2,1)S(1)}, u32[]{:S(2)}, u32[]{:S(2)}) collective-permute-start(bf16[4,4,32,256]{3,2,1,0:T(8,128)(2,1)S(1)} %get-tuple-element.21), channel_id=1, source_target_pairs={{0,1},{1,0},{2,3},{3,2},{4,5},{5,4},{6,7},{7,6},{8,9},{9,8},{10,11... | collective-permute-start | bytes 786440 | tf_op jit(solution)/shard_map/ppermute | solution.py:22
  47.5 5.0 %collective-permute-start.3 = (bf16[2,4,32,256]{3,2,1,0:T(8,128)(2,1)S(1)}, bf16[2,4,32,256]{3,2,1,0:T(8,128)(2,1)S(1)}, u32[]{:S(2)}, u32[]{:S(2)}) collective-permute-start(bf16[2,4,32,256]{3,2,1,0:T(8,128)(2,1)S(1)} %fusion.9), channel_id=1, source_target_pairs={{0,2},{1,3},{2,0},{3,1},{4,6},{5,7},{6,4},{7,5},{8,10},{9,11},{10,... | collective-permute-start | bytes 393224 | tf_op jit(solution)/shard_map/ppermute | solution.py:22
  50.2 5.2 %collective-permute-start.8 = (bf16[1,8,32,256]{3,2,1,0:T(8,128)(2,1)S(1)}, bf16[1,8,32,256]{3,2,1,0:T(8,128)(2,1)S(1)}, u32[]{:S(2)}, u32[]{:S(2)}) collective-permute-start(bf16[1,8,32,256]{3,2,1,0:T(8,128)(2,1)S(1)} %get-tuple-element.25), channel_id=1, source_target_pairs={{0,16},{8,24},{16,0},{24,8},{1,17},{9,25},{17,1},{25,9},{2,18},{10... | collective-permute-start | bytes 393224 | tf_op jit(solution)/shard_map/ppermute | solution.py:22
  52.6 7.1 %collective-permute-start.4 = (bf16[1,4,32,256]{3,2,1,0:T(8,128)(2,1)S(1)}, bf16[1,4,32,256]{3,2,1,0:T(8,128)(2,1)S(1)}, u32[]{:S(2)}, u32[]{:S(2)}) collective-permute-start(bf16[1,4,32,256]{3,2,1,0:T(8,128)(2,1)S(1)} %get-tuple-element.29), channel_id=1, source_target_pairs={{0,4},{1,5},{2,6},{3,7},{4,0},{5,1},{6,2},{7,3},{8,12},{9,13},{10,... | collective-permute-start | bytes 196616 | tf_op jit(solution)/shard_map/ppermute | solution.py:22
  55.5 5.2 %collective-permute-start.9 = (bf16[1,4,32,256]{3,2,1,0:T(8,128)(2,1)S(1)}, bf16[1,4,32,256]{3,2,1,0:T(8,128)(2,1)S(1)}, u32[]{:S(2)}, u32[]{:S(2)}) collective-permute-start(bf16[1,4,32,256]{3,2,1,0:T(8,128)(2,1)S(1)} %get-tuple-element.27), channel_id=1, source_target_pairs={{0,4},{1,5},{2,6},{3,7},{4,0},{5,1},{6,2},{7,3},{8,12},{9,13},{10,... | collective-permute-start | bytes 196616 | tf_op jit(solution)/shard_map/ppermute | solution.py:22

commit v5 on v4

v5 whole, which is shorter than its diff:
```python
import functools
import math

import jax
import jax.numpy as jnp
from jax import lax
from jax.experimental import pallas as pl
from jax.experimental.pallas import tpu as pltpu
from jax.sharding import PartitionSpec as P

WEIGHTS = (-1.0 / 32, 3.0 / 32, -7.0 / 32, 21.0 / 32, 21.0 / 32, -7.0 / 32, 3.0 / 32, -1.0 / 32)
PERIOD = 4096
VMEM_BYTES = 56 * 2**20


def bits_of(count):
    return count.bit_length() - 1


def swapped(array, axis, bit):
    return lax.ppermute(array, axis, [(i, i ^ 1 << bit) for i in range(lax.axis_size(axis))])


def unit(phase_int, period):
    angle = jnp.remainder(phase_int, period).astype(jnp.float32) * (2.0 * math.pi / period)
    return jnp.cos(angle), jnp.sin(angle)


def own_bit(axis, at):
    return lax.axis_index(axis) >> at & 1


def compress_kernel(
    dims, chirp_ref, edge_ref, echo_ref, keep_ref, send_ref, edge_out, weights, rows_ref, carry
):
    tile, pulses, half, near_chain, axis_bit = dims
    blocks = 2 * tile
    pitch = blocks + 1
    mid = pl.num_programs(2) - 1 - pl.program_id(2)
    near = 1 - pl.program_id(1)
    own = own_bit("turn", axis_bit)

    @pl.when((pl.program_id(0) == 0) & (pl.program_id(1) == 0) & (pl.program_id(2) == 0))
    def _():
        rows = lax.broadcasted_iota(jnp.int32, (half, half), 0)
        cols = lax.broadcasted_iota(jnp.int32, (half, half), 1)
        taps = chirp_ref[...].astype(jnp.float32)
        tables = []
        for c in range(2):
            wide = jnp.broadcast_to(taps[c : c + 1], (half, half))
            tables.append(pltpu.roll(wide, 0, 1, stride=1, stride_axis=0).T)
        for m, mask in enumerate((rows >= cols, rows < cols)):
            re, im = (jnp.where(mask, t, 0.0) for t in tables)
            top = jnp.concatenate([re, im], axis=1)
            low = jnp.concatenate([-im, re], axis=1)
            full = jnp.concatenate([top, low], axis=0)
            weights[m * 2 * half : (m + 1) * 2 * half, :] = full.astype(jnp.bfloat16)
        carry[...] = edge_ref[...]

    for p in range(pulses):
        for c in range(2):
            rows_ref[c, p * pitch : p * pitch + blocks, :] = echo_ref[
                p, :, c * half : (c + 1) * half
            ].astype(jnp.float32)
    turned = []
    for b in range(blocks):
        parts = [rows_ref[c, pl.ds(b, pulses, stride=pitch), :] for c in range(2)]
        turned.append(jnp.concatenate(parts, axis=1).astype(jnp.bfloat16))
    turned.append(carry[...])
    current = jnp.concatenate(turned[:-1], axis=0)
    after = jnp.concatenate(turned[1:], axis=0)
    total = jnp.dot(
        jnp.concatenate([current, after], axis=1),
        weights[...],
        preferred_element_type=jnp.float32,
    ).astype(jnp.bfloat16)
    carry[...] = turned[0]
    edge_out[...] = turned[0]

    if near_chain:
        for side in range(2):

            @pl.when(own == side)
            def _(side=side):
                for b in range(blocks):
                    ref = keep_ref if b // tile == side else send_ref
                    ref[0, 0, 0, b % tile] = total[b * pulses : (b + 1) * pulses]
    else:
        for ref, mine in ((keep_ref, True), (send_ref, False)):

            @pl.when((near == own) == mine)
            def _(ref=ref):
                for b in range(blocks):
                    ref[0, mid, b // tile, b % tile] = total[b * pulses : (b + 1) * pulses]


def compress(chirp, edge, echoes, high, mids, near_chain, axis_bit, first_high):
    pulses, blocks, width = echoes.shape
    half = width // 2
    tile = blocks // lax.axis_size("turn")
    if near_chain:
        shape = (high, 2, mids, tile, pulses, width)
        spec = pl.BlockSpec(
            (1, 1, 1) + shape[3:], lambda h, v, m: (high - 1 - h, 1 - v, mids - 1 - m, 0, 0, 0)
        )
    else:
        shape = (high, mids, 2, tile, pulses, width)
        spec = pl.BlockSpec((1,) + shape[1:], lambda h, v, m: (high - 1 - h, 0, 0, 0, 0, 0))
    edge_spec = pl.BlockSpec((pulses, width), lambda h, v, m: (0, 0))

    def chunk(h, v, m):
        return 0, ((first_high + high - 1 - h) * 2 + 1 - v) * mids + mids - 1 - m, 0

    return pl.pallas_call(
        functools.partial(compress_kernel, (tile, pulses, half, near_chain, axis_bit)),
        grid=(high, 2, mids),
        in_specs=[
            pl.BlockSpec((2, half), lambda h, v, m: (0, 0)),
            edge_spec,
            pl.BlockSpec((pulses, 2 * tile, width), chunk),
        ],
        out_specs=[spec, spec, edge_spec],
        out_shape=[
            jax.ShapeDtypeStruct(s, jnp.bfloat16) for s in (shape, shape, (pulses, width))
        ],
        scratch_shapes=[
            pltpu.VMEM((2 * width, width), jnp.bfloat16),
            pltpu.VMEM((2, pulses * (2 * tile + 1), half), jnp.float32),
            pltpu.VMEM((pulses, width), jnp.bfloat16),
        ],
        compiler_params=pltpu.CompilerParams(vmem_limit_bytes=VMEM_BYTES),
        cost_estimate=pl.CostEstimate(
            flops=2 * pulses * blocks * width * width,
            bytes_accessed=2 * pulses * blocks * width,
            transcendentals=0,
        ),
        name="compress",
    )(chirp, edge, echoes)


def image_kernel(dims, data_ref, steer_ref, interp_ref, base_ref, step_ref, out_keep, out_send):
    leaf, each, half, beams, levels = dims
    rows = beams // leaf
    pair = 2
    piece = rows

    def turned(phase, re, im):
        c, s = phase
        return c * re - s * im, c * im + s * re

    bases = []
    for n in range(2 * levels):
        bases.append(jnp.broadcast_to(base_ref[0, n : n + 1, :], (half, beams)).T)

    def phased(level, block, first, re, im):
        cut = slice(first, first + piece)
        lanes = slice(block * half, (block + 1) * half)
        phase = turned(
            (bases[2 * level][cut], bases[2 * level + 1][cut]),
            step_ref[level, 0, cut, lanes],
            step_ref[level, 1, cut, lanes],
        )
        return turned(phase, re, im)

    for at in range(0, each, pair):
        parts = []
        for n in range(2):
            for c in range(2):
                cols = slice(c * half, (c + 1) * half)
                parts.append(
                    jnp.concatenate([data_ref[n, 0, at + i, :, cols] for i in range(pair)], axis=1)
                )
        raw = jnp.dot(
            steer_ref[...], jnp.concatenate(parts, axis=0), preferred_element_type=jnp.float32
        )
        re, im = raw[:beams], raw[beams:]
        for level in range(levels):
            columns = []
            for i in range(pair):
                lanes = slice(i * half, (i + 1) * half)
                pieces = []
                for first in range(0, beams, piece):
                    cut = slice(first, first + piece)
                    both = phased(level, at + i, first, re[cut, lanes], im[cut, lanes])
                    if level == levels - 1:
                        both = jnp.concatenate(both, axis=1)
                        g = first // rows
                        if g < leaf // 2:
                            out_keep[g, 0, at + i] = both
                        else:
                            out_send[g - leaf // 2, 0, at + i] = both.astype(jnp.bfloat16)
                        continue
                    both = jnp.concatenate(both, axis=1)
                    big = both.astype(jnp.bfloat16)
                    low = (both - big.astype(jnp.float32)).astype(jnp.bfloat16)
                    pieces.append((big, low))
                if pieces:
                    columns.append(
                        jnp.concatenate([p[0] for p in pieces] + [p[1] for p in pieces], axis=0)
                    )
            if columns:
                moved = jnp.dot(
                    interp_ref[level],
                    jnp.concatenate(columns, axis=1),
                    preferred_element_type=jnp.float32,
                )
                cuts = [moved[:, n * half : (n + 1) * half] for n in range(2 * pair)]
                re = jnp.concatenate(cuts[0::2], axis=1)
                im = jnp.concatenate(cuts[1::2], axis=1)


def backproject(data, steer, interp, base, step, leaf):
    _, count, each, pulses, width = data.shape
    half = width // 2
    beams = steer.shape[0] // 2
    rows = beams // leaf
    shape = (leaf // 2, count, each, rows, width)
    out_spec = pl.BlockSpec((leaf // 2, 1) + shape[2:], lambda n: (0, n, 0, 0, 0))
    return pl.pallas_call(
        functools.partial(image_kernel, (leaf, each, half, beams, bits_of(leaf))),
        grid=(count,),
        in_specs=[
            pl.BlockSpec((2, 1, each, pulses, width), lambda n: (0, n, 0, 0, 0)),
            pl.BlockSpec(steer.shape, lambda n: (0, 0)),
            pl.BlockSpec(interp.shape, lambda n: (0, 0, 0)),
            pl.BlockSpec((1,) + base.shape[1:], lambda n: (n, 0, 0)),
            pl.BlockSpec(step.shape, lambda n: (0, 0, 0, 0)),
        ],
        out_specs=[out_spec, out_spec],
        out_shape=[
            jax.ShapeDtypeStruct(shape, jnp.float32),
            jax.ShapeDtypeStruct(shape, jnp.bfloat16),
        ],
        compiler_params=pltpu.CompilerParams(vmem_limit_bytes=16 * 2**20),
        cost_estimate=pl.CostEstimate(
            flops=12 * beams * pulses * count * each * width,
            bytes_accessed=2 * data.size + 6 * count * each * beams * width // 2,
            transcendentals=0,
        ),
        name="image",
    )(data, steer, interp, base, step)


def fold(own, keep, got):
    def half(at):
        kept, came = (lax.dynamic_index_in_dim(a, at, 1, False) for a in (keep, got))
        return kept + came.astype(jnp.float32)

    return half(own), half(1 - own).astype(jnp.bfloat16)


def last_kernel(keep_ref, got_ref, out_ref, rows_ref):
    blocks, rows, width = keep_ref.shape
    for i in range(blocks):
        value = keep_ref[i] + got_ref[i].astype(jnp.float32)
        for c in range(2):
            cols = slice(c * width // 2, (c + 1) * width // 2)
            rows_ref[c, pl.ds(i, rows, stride=blocks), :] = value[:, cols]
    both = jnp.concatenate([rows_ref[0], rows_ref[1]], axis=1)
    out_ref[...] = both.reshape(rows, blocks, width).astype(jnp.bfloat16)


def last_sum(keep, got):
    blocks, rows, width = keep.shape
    return pl.pallas_call(
        last_kernel,
        out_shape=jax.ShapeDtypeStruct((rows, blocks, width), jnp.bfloat16),
        scratch_shapes=[pltpu.VMEM((2, rows * blocks, width // 2), jnp.float32)],
        compiler_params=pltpu.CompilerParams(vmem_limit_bytes=8 * 2**20),
        name="last_sum",
    )(keep, got)


def interpolation(taps, beams):
    cells = jnp.arange(beams, dtype=jnp.int32)
    weights = jnp.array(WEIGHTS, jnp.float32)
    picks = taps[..., None] == cells
    return jnp.where(picks, weights[:, None], 0.0).sum(axis=-2)


def steering(slots, matrix, side, beams, pulses, scale):
    count = slots.shape[0]
    beam = jnp.arange(beams, dtype=jnp.int32)[:, None, None]
    place = jnp.arange(pulses, dtype=jnp.int32)
    slot = slots[None, :, None]
    cos, sin = unit(
        (2 * beam + 1 - beams) * (2 * place + 1 - pulses)
        + 3 * (beam + 1) * (2 * slot + 1) * (2 * place + 1),
        8 * pulses,
    )
    pair = jnp.concatenate([cos * scale, sin * scale], axis=2).astype(jnp.bfloat16)
    moved = jnp.dot(
        matrix.astype(jnp.bfloat16),
        pair.reshape(beams, count * 2 * pulses),
        preferred_element_type=jnp.float32,
    ).reshape(beams, count, 2 * pulses)
    re, im = moved[:, :, :pulses], moved[:, :, pulses:]
    row = jnp.arange(beams, dtype=jnp.int32)
    c, s = (t[:, None, None] for t in unit(row * row * (side + 1), PERIOD))
    re, im = c * re - s * im, c * im + s * re
    top = jnp.concatenate([re, -im], axis=2)
    low = jnp.concatenate([im, re], axis=2)
    return jnp.concatenate([top, low], axis=0).astype(jnp.bfloat16)


def bit(value, at):
    return value >> at & 1


def per_device(echoes, chirp, taps, slots):
    leaf, turn = lax.axis_size("leaf"), lax.axis_size("turn")
    pulses, blocks, width = echoes.shape
    half = width // 2
    beams = taps.shape[2]
    levels = bits_of(leaf)
    far = (bits_of(turn) + 1) // 2 - 1
    top = bits_of(turn) - 1
    mids = 1 << far - 1
    high = turn >> far + 2
    tile = blocks // turn
    each = tile // 2
    rows = beams // leaf
    own_leaf, own_turn = lax.axis_index("leaf"), lax.axis_index("turn")

    edge = jnp.zeros((pulses, width), jnp.bfloat16)
    keep_y, send_y, edge = compress(chirp, edge, echoes, high, mids, True, 0, high)
    got_y = swapped(send_y, "turn", 0)
    keep_z, send_z, _ = compress(chirp, edge, echoes, high, mids, False, far, 0)
    got_z = swapped(send_z, "turn", far)

    own_sides = [bit(own_leaf, level) for level in range(levels)]
    row = jnp.arange(beams, dtype=jnp.int32)
    part, place = row // rows, row % rows
    group = 2 * (part % (leaf // 2)) + (part // (leaf // 2) ^ own_sides[0])
    orders = [row] * (levels - 1) + [group * rows + place]
    own_taps = [
        lax.dynamic_index_in_dim(taps[n], own_sides[n], 0, False) for n in range(levels)
    ]
    cores = own_taps[-1].reshape(leaf // 2, 2, rows, -1)
    cores = [
        lax.dynamic_index_in_dim(cores, own_sides[0] ^ n, 1, False).reshape(beams // 2, -1)
        for n in range(2)
    ]
    own_taps[-1] = jnp.concatenate(cores, axis=0)
    matrices = interpolation(jnp.stack(own_taps), beams)
    interp = jnp.concatenate([matrices[1:]] * 2, axis=-1).astype(jnp.bfloat16)
    scale = 1.0 / math.sqrt(2.0 * slots.shape[1] * pulses)
    wanted = own_turn ^ jnp.array([0, 1, 1 << far], jnp.int32)
    picked = jnp.arange(slots.shape[1], dtype=jnp.int32) == wanted[:, None]
    own_slots = jnp.where(picked, slots, 0).sum(axis=1)
    steer = steering(own_slots, matrices[0], own_sides[0], beams, pulses, scale)
    steer_y = steer[:, :2].reshape(2 * beams, 4 * pulses)
    steer_z = jnp.concatenate([steer[:, :1], steer[:, 2:]], axis=1).reshape(2 * beams, 4 * pulses)

    leans = jnp.stack([2 * order + 1 - beams for order in orders])
    bins = jnp.arange(each * half, dtype=jnp.int32) + 1
    slopes = jnp.stack([(2 * own_sides[n] - 1) * (n + 2) for n in range(levels)])[:, None] * leans
    step = jnp.stack(unit(slopes[:, :, None] * bins, PERIOD), axis=1)
    squares = jnp.stack(
        [orders[n] * orders[n] * (own_sides[n] + 1) * (1 if n else 0) for n in range(levels)]
    )

    def bases(tiles):
        parts = (2 * tiles[:, None] + jnp.arange(2, dtype=jnp.int32)).reshape(-1)
        start = (parts * each * half)[:, None, None]
        both = jnp.stack(unit(slopes * start + squares, PERIOD), axis=2)
        return both.reshape(parts.shape[0], 2 * levels, beams)

    index = jnp.arange(turn // 4, dtype=jnp.int32)
    tiles_y = turn // 2 + 2 * index + bit(own_turn, 0)
    low_part = index & (1 << far) - 1
    tiles_z = ((index >> far) * 2 + bit(own_turn, far)) * (1 << far) + low_part

    final = []
    for name, keep, got, steer_own, tiles in (
        ("y", keep_y, got_y, steer_y, tiles_y),
        ("z", keep_z, got_z, steer_z, tiles_z),
    ):
        shape = (turn // 2, each, pulses, width)
        data = jnp.stack([keep.reshape(shape), got.reshape(shape)])
        kept, sent = backproject(data, steer_own, interp, bases(tiles), step, leaf)
        gone = 0 if name == "y" else far
        leading = [("leaf", b) for b in range(levels - 1, 0, -1)]
        leading += [("turn", b) for b in range(top - 1, -1, -1) if b != gone]
        order = [("leaf", b) for b in range(1, levels)]
        rest = [("turn", b) for b in range(top) if b not in (0, far)]
        order = order + [("turn", far)] if name == "y" else [("turn", 0)] + order
        arrived = swapped(sent, "leaf", 0)
        for axis, b in order + rest:
            at = leading.index((axis, b))
            before, after = 1 << at, (1 << len(leading) - at - 1) * tile
            leading.pop(at)
            split = (before, 2, after, rows, width)
            own = bit(own_leaf if axis == "leaf" else own_turn, b)
            kept, sent = fold(own, kept.reshape(split), arrived.reshape(split))
            arrived = swapped(sent, axis, b)
        shape = (tile, rows, width)
        final.append(kept.reshape(shape) + arrived.reshape(shape).astype(jnp.float32))
    upper = bit(own_turn, top) == 1
    kept = jnp.where(upper, final[0], final[1])
    sent = jnp.where(upper, final[1], final[0]).astype(jnp.bfloat16)
    return last_sum(kept, swapped(sent, "turn", top))


def solution(mesh):
    placed = (P(("leaf", "turn"), None, None), P(), P(), P("leaf", None))
    return jax.shard_map(
        per_device, mesh=mesh, in_specs=placed, out_specs=P("leaf", "turn", None), check_vma=False
    )
```

time: 61.8 us -> 52 us (0.84)
  waiting for transfers between devices: 9.65 us -> 18.2 us
  Pallas kernels: 17.6 us -> 11.6 us
  starting transfers between devices: 17 us -> 12.1 us
  local copies, waits for them, and re-layouts: 5.79 us -> 1.49 us
  other arithmetic: 11 us -> 7.77 us
    ppermute x10 -> x9, waiting for transfers between devices: 9.65 us -> 18.2 us  [swapped(): lax.ppermute(array, axis, [(i, i ^ 1 << bit) for i in range(lax.axis_size...]
    ppermute x10 -> x9, starting transfers between devices: 17 us -> 12.1 us  [swapped(): lax.ppermute(array, axis, [(i, i ^ 1 << bit) for i in range(lax.axis_size...]
    pallas_call x2, Pallas kernels: 9.23 us -> 4.48 us  [backproject(): pl.pallas_call(functools.partial(image_kernel, (leaf, each, half, beams,...]
    unnamed x18 -> x10, local copies, waits for them, and re-layouts: 4.74 us -> 0.02 us
    add x1, other arithmetic: 2.08 us -> 0.01 us  [steering(): 2 * slot + 1]
    pallas_call x2 -> x3, Pallas kernels: 8.34 us -> 7.17 us  [the longest x2 6.43 us: compress(): pl.pallas_call(functools.partial(compress_kernel, (tile, pulses, half, ne...]
    cos x2, other arithmetic: 3.29 us -> 2.27 us  [unit(): return (jnp.cos(angle), jnp.sin(angle))]
    add x1, other arithmetic: 0.03 us -> 1.02 us  [half(): return kept + came.astype(jnp.float32)]
  transfers between devices with their start and end apart: 10 -> 9, of which waited for: 6 -> 7; matrix products, arithmetic and copies ran while one was open for 19% -> 17% of each run, Pallas kernels for 15% -> 15%
where the time goes in v5:
time: 52 us; the launch traced here: 51.7 us
  waiting for transfers between devices  18.2 us (35%)
  starting transfers between devices  12.1 us (23%)
  Pallas kernels  11.6 us (22%)
  other arithmetic  7.77 us (15%)
  local copies, waits for them, and re-layouts  1.49 us (3%)
    ppermute x9, waiting for transfers between devices, swapped(): lax.ppermute(array, axis, [(i, i ^ 1 << bit) for i in range(lax.axis_size...  18.2 us
    ppermute x9, starting transfers between devices, swapped(): lax.ppermute(array, axis, [(i, i ^ 1 << bit) for i in range(lax.axis_size...  12.1 us
    pallas_call x2, Pallas kernels, compress(): pl.pallas_call(functools.partial(compress_kernel, (tile, pulses, half, ne...  6.43 us
    pallas_call x2, Pallas kernels, backproject(): pl.pallas_call(functools.partial(image_kernel, (leaf, each, half, beams,...  4.48 us
    convert_element_type x4, other arithmetic, fold(): return (half(own), half(1 - own).astype(jnp.bfloat16))  2.28 us
    cos x2, other arithmetic, unit(): return (jnp.cos(angle), jnp.sin(angle))  2.27 us
  transfers between devices with their start and end apart: 9, of which 7 were waited for; matrix products, arithmetic and copies ran while one was open for 17% of the time, Pallas kernels for 15%

profile of v5, /device:TPU:0, one launch (start us, length us, event | category | flops | bytes accessed | tf_op | source)
XLA Modules:
  0.0 51.7 jit_solution(10810636179362726927)
XLA Ops:
  0.0 0.6 %broadcast_in_dim.28.edge_ref = bf16[64,256]{1,0:T(8,128)(2,1)} broadcast(bf16[]{:T(256)} %constant.205.clone.1), dimensions={} | broadcast | bytes 32770 | tf_op jit(solution)/shard_map/broadcast_in_dim | solution.py:325
  0.6 3.2 %compress.2 = (bf16[1,2,1,8,64,256]{5,4,3,2,1,0:T(8,128)(2,1)}, bf16[1,2,1,8,64,256]{5,4,3,2,1,0:T(8,128)(2,1)}, bf16[64,256]{1,0:T(8,128)(2,1)}) custom-call(bf16[2,128]{1,0:T(2,128)(2,1)} %chirp_ref.3, bf16[64,256]{1,0:T(8,128)(2,1)} %broadcast_in_dim.28.edge_ref, bf16[64,64,256]{2,1,0:T(8,128)(2,1)} %echo_ref.3), custom_call_target="tpu_custom_call" | custom-call | flops 536870912 | bytes 2097152 | tf_op jit(solution)/shard_map/compress/pallas_call | solution.py:114
  3.8 3.0 %collective-permute-start = (bf16[1,2,1,8,64,256]{5,4,3,2,1,0:T(8,128)(2,1)}, bf16[1,2,1,8,64,256]{5,4,3,2,1,0:T(8,128)(2,1)S(1)}, u32[]{:S(2)}, u32[]{:S(2)}) collective-permute-start(bf16[1,2,1,8,64,256]{5,4,3,2,1,0:T(8,128)(2,1)} %get-tuple-element.15), channel_id=1, source_target_pairs={{0,1},{1,0},{2,3},{3,2},{4,5},{5,4},{6,7},{7,6},{8,9},{9,8},{10,11... | collective-permute-start | bytes 1572872 | tf_op jit(solution)/shard_map/ppermute | solution.py:21
  6.8 3.3 %compress.3 = (bf16[1,1,2,8,64,256]{5,4,3,2,1,0:T(8,128)(2,1)}, bf16[1,1,2,8,64,256]{5,4,3,2,1,0:T(8,128)(2,1)}, bf16[64,256]{1,0:T(8,128)(2,1)}) custom-call(bf16[2,128]{1,0:T(2,128)(2,1)} %chirp_ref.3, bf16[64,256]{1,0:T(8,128)(2,1)} %get-tuple-element.18.edge_ref, bf16[64,64,256]{2,1,0:T(8,128)(2,1)} %echo_ref.3), custom_call_target="tpu_custom_call" | custom-call | flops 536870912 | bytes 2097152 | tf_op jit(solution)/shard_map/compress/pallas_call | solution.py:114
  10.1 1.6 %collective-permute-start.4 = (bf16[1,1,2,8,64,256]{5,4,3,2,1,0:T(8,128)(2,1)}, bf16[1,1,2,8,64,256]{5,4,3,2,1,0:T(8,128)(2,1)S(1)}, u32[]{:S(2)}, u32[]{:S(2)}) collective-permute-start(bf16[1,1,2,8,64,256]{5,4,3,2,1,0:T(8,128)(2,1)} %get-tuple-element.20), channel_id=1, source_target_pairs={{0,2},{1,3},{2,0},{3,1},{4,6},{5,7},{6,4},{7,5},{8,10},{9,11},{10,... | collective-permute-start | bytes 1572872 | tf_op jit(solution)/shard_map/ppermute | solution.py:21
  12.2 0.1 copy.25
  12.3 0.2 select_reduce_fusion.1
  12.9 0.4 select_reduce_fusion
  13.5 0.5 multiply_convert_fusion.1
  14.0 0.2 fusion.15
  14.4 0.2 fusion.31
  14.7 0.1 copy.32.steer_ref
  14.9 2.1 %fusion.10 = (f32[2,1,128,512]{3,2,1,0:T(8,128)S(1)}, f32[2,1,128,512]{3,2,1,0:T(8,128)S(1)}) fusion(s32[512]{0:T(512)S(1)} %iota_add_fusion, s32[2,128]{1,0:T(2,128)S(1)} %add_multiply_fusion), kind=kLoop, calls=%fused_computation.30 | loop fusion | flops 1835008 | bytes 1051648 | tf_op jit(solution)/shard_map/cos | solution.py:26
  17.1 1.8 %collective-permute-done = bf16[1,2,1,8,64,256]{5,4,3,2,1,0:T(8,128)(2,1)S(1)} collective-permute-done((bf16[1,2,1,8,64,256]{5,4,3,2,1,0:T(8,128)(2,1)}, bf16[1,2,1,8,64,256]{5,4,3,2,1,0:T(8,128)(2,1)S(1)}, u32[]{:S(2)}, u32[]{:S(2)}) %collective-permute-start) | collective-permute-done | bytes 524320 | tf_op jit(solution)/shard_map/ppermute | solution.py:21
  19.1 2.2 %image.2 = (f32[2,4,4,32,256]{4,3,2,1,0:T(8,128)S(1)}, bf16[2,4,4,32,256]{4,3,2,1,0:T(8,128)(2,1)S(1)}) custom-call(bf16[2,4,4,64,256]{4,3,2,1,0:T(8,128)(2,1)S(1)} %pad_maximum_fusion.data_ref, bf16[256,256]{1,0:T(8,128)(2,1)S(1)} %copy.32.steer_ref, bf16[1,128,256]{2,1,0:T(8,128)(2,1)S(1)} %pad_maximum_fusion.4.interp_ref, f32[4,4,128]{2,1,0:T(4,128)S(1)} %bitcast.88, ...), custom_call_target="tpu_custom_call" | custom-call | flops 402653184 | bytes 2621440 | tf_op jit(solution)/shard_map/image/pallas_call | solution.py:219
  21.4 2.3 %collective-permute-done.4 = bf16[1,1,2,8,64,256]{5,4,3,2,1,0:T(8,128)(2,1)S(1)} collective-permute-done((bf16[1,1,2,8,64,256]{5,4,3,2,1,0:T(8,128)(2,1)}, bf16[1,1,2,8,64,256]{5,4,3,2,1,0:T(8,128)(2,1)S(1)}, u32[]{:S(2)}, u32[]{:S(2)}) %collective-permute-start.4) | collective-permute-done | bytes 524320 | tf_op jit(solution)/shard_map/ppermute | solution.py:21
  23.8 2.2 %image.3 = (f32[2,4,4,32,256]{4,3,2,1,0:T(8,128)S(1)}, bf16[2,4,4,32,256]{4,3,2,1,0:T(8,128)(2,1)S(1)}) custom-call(bf16[2,4,4,64,256]{4,3,2,1,0:T(8,128)(2,1)S(1)} %pad_maximum_fusion.2.data_ref, bf16[256,256]{1,0:T(8,128)(2,1)S(1)} %copy.33.steer_ref, bf16[1,128,256]{2,1,0:T(8,128)(2,1)S(1)} %pad_maximum_fusion.4.interp_ref, f32[4,4,128]{2,1,0:T(4,128)S(1)} %bitcast.87, ...), custom_call_target="tpu_custom_call" | custom-call | flops 402653184 | bytes 2621440 | tf_op jit(solution)/shard_map/image/pallas_call | solution.py:219
  26.1 1.2 %fusion.4 = (bf16[1,16,32,256]{3,2,1,0:T(8,128)(2,1)S(1)}, f32[1,1,16,32,256]{4,3,2,1,0:T(8,128)S(1)}) fusion(f32[1,2,16,32,256]{4,3,2,1,0:T(8,128)S(1)} %bitcast.86, s32[]{:T(128)S(6)} %select_n.226, bf16[1,2,16,32,256]{4,3,2,1,0:T(8,128)(2,1)} %bitcast.15, s32[]{:T(128)S(6)} %select_n.214), kind=kLoop, calls=%fused_computation.18 | loop fusion | flops 655360 | bytes 2359304 | tf_op jit(solution)/shard_map/convert_element_type | solution.py:249
  27.3 1.6 %collective-permute-start.2 = (bf16[1,16,32,256]{3,2,1,0:T(8,128)(2,1)S(1)}, bf16[1,16,32,256]{3,2,1,0:T(8,128)(2,1)S(1)}, u32[]{:S(2)}, u32[]{:S(2)}) collective-permute-start(bf16[1,16,32,256]{3,2,1,0:T(8,128)(2,1)S(1)} %get-tuple-element.27), channel_id=1, source_target_pairs={{0,16},{8,24},{16,0},{24,8},{1,17},{9,25},{17,1},{25,9},{2,18},{10... | collective-permute-start | bytes 786440 | tf_op jit(solution)/shard_map/ppermute | solution.py:21
  28.9 1.0 %fusion.5 = bf16[2,8,32,256]{3,2,1,0:T(8,128)(2,1)S(1)} fusion(f32[2,2,8,32,256]{4,3,2,1,0:T(8,128)S(1)} %bitcast.84, s32[]{:T(128)S(6)} %select_n.230, bf16[2,2,8,32,256]{4,3,2,1,0:T(8,128)(2,1)} %bitcast.27), kind=kLoop, calls=%fused_computation.19 | loop fusion | flops 393216 | bytes 1048580 | tf_op jit(solution)/shard_map/convert_element_type | solution.py:249
  29.9 0.6 %collective-permute-start.6 = (bf16[2,8,32,256]{3,2,1,0:T(8,128)(2,1)S(1)}, bf16[2,8,32,256]{3,2,1,0:T(8,128)(2,1)S(1)}, u32[]{:S(2)}, u32[]{:S(2)}) collective-permute-start(bf16[2,8,32,256]{3,2,1,0:T(8,128)(2,1)S(1)} %fusion.5), channel_id=1, source_target_pairs={{0,1},{1,0},{2,3},{3,2},{4,5},{5,4},{6,7},{7,6},{8,9},{9,8},{10,11... | collective-permute-start | bytes 786440 | tf_op jit(solution)/shard_map/ppermute | solution.py:21
  30.5 1.0 %convert_add_fusion = f32[2,1,8,32,256]{4,3,2,1,0:T(8,128)S(1)} fusion(f32[2,2,8,32,256]{4,3,2,1,0:T(8,128)S(1)} %bitcast.85, s32[]{:T(128)S(6)} %select_n.229, bf16[2,2,8,32,256]{4,3,2,1,0:T(8,128)(2,1)} %bitcast.27), kind=kLoop, calls=%fused_computation.15 | loop fusion | flops 262144 | bytes 1310724 | tf_op jit(solution)/shard_map/add | solution.py:247
  31.5 4.6 %collective-permute-done.2 = bf16[1,16,32,256]{3,2,1,0:T(8,128)(2,1)S(1)} collective-permute-done((bf16[1,16,32,256]{3,2,1,0:T(8,128)(2,1)S(1)}, bf16[1,16,32,256]{3,2,1,0:T(8,128)(2,1)S(1)}, u32[]{:S(2)}, u32[]{:S(2)}) %collective-permute-start.2) | collective-permute-done | bytes 262176 | tf_op jit(solution)/shard_map/ppermute | solution.py:21
  36.1 1.6 %collective-permute-start.3 = (bf16[1,8,32,256]{3,2,1,0:T(8,128)(2,1)S(1)}, bf16[1,8,32,256]{3,2,1,0:T(8,128)(2,1)S(1)}, u32[]{:S(2)}, u32[]{:S(2)}) collective-permute-start(bf16[1,8,32,256]{3,2,1,0:T(8,128)(2,1)S(1)} %fusion.11), channel_id=1, source_target_pairs={{0,2},{1,3},{2,0},{3,1},{4,6},{5,7},{6,4},{7,5},{8,10},{9,11},{10,... | collective-permute-start | bytes 393224 | tf_op jit(solution)/shard_map/ppermute | solution.py:21
  37.8 0.6 %collective-permute-done.6 = bf16[2,8,32,256]{3,2,1,0:T(8,128)(2,1)S(1)} collective-permute-done((bf16[2,8,32,256]{3,2,1,0:T(8,128)(2,1)S(1)}, bf16[2,8,32,256]{3,2,1,0:T(8,128)(2,1)S(1)}, u32[]{:S(2)}, u32[]{:S(2)}) %collective-permute-start.6) | collective-permute-done | bytes 262176 | tf_op jit(solution)/shard_map/ppermute | solution.py:21
  38.4 0.9 %collective-permute-start.7 = (bf16[1,8,32,256]{3,2,1,0:T(8,128)(2,1)S(1)}, bf16[1,8,32,256]{3,2,1,0:T(8,128)(2,1)S(1)}, u32[]{:S(2)}, u32[]{:S(2)}) collective-permute-start(bf16[1,8,32,256]{3,2,1,0:T(8,128)(2,1)S(1)} %fusion.7), channel_id=1, source_target_pairs={{0,16},{8,24},{16,0},{24,8},{1,17},{9,25},{17,1},{25,9},{2,18},{10... | collective-permute-start | bytes 393224 | tf_op jit(solution)/shard_map/ppermute | solution.py:21
  39.4 1.9 %collective-permute-done.3 = bf16[1,8,32,256]{3,2,1,0:T(8,128)(2,1)S(1)} collective-permute-done((bf16[1,8,32,256]{3,2,1,0:T(8,128)(2,1)S(1)}, bf16[1,8,32,256]{3,2,1,0:T(8,128)(2,1)S(1)}, u32[]{:S(2)}, u32[]{:S(2)}) %collective-permute-start.3) | collective-permute-done | bytes 131104 | tf_op jit(solution)/shard_map/ppermute | solution.py:21
  41.3 2.2 %collective-permute-done.7 = bf16[1,8,32,256]{3,2,1,0:T(8,128)(2,1)S(1)} collective-permute-done((bf16[1,8,32,256]{3,2,1,0:T(8,128)(2,1)S(1)}, bf16[1,8,32,256]{3,2,1,0:T(8,128)(2,1)S(1)}, u32[]{:S(2)}, u32[]{:S(2)}) %collective-permute-start.7) | collective-permute-done | bytes 131104 | tf_op jit(solution)/shard_map/ppermute | solution.py:21
  43.5 0.1 fusion.6
  43.6 2.7 %collective-permute-start.8 = (bf16[8,32,256]{2,1,0:T(8,128)(2,1)S(1)}, bf16[8,32,256]{2,1,0:T(8,128)(2,1)S(1)}, u32[]{:S(2)}, u32[]{:S(2)}) collective-permute-start(bf16[8,32,256]{2,1,0:T(8,128)(2,1)S(1)} %get-tuple-element.25), channel_id=1, source_target_pairs={{0,4},{1,5},{2,6},{3,7},{4,0},{5,1},{6,2},{7,3},{8,12},{9,13},{10,... | collective-permute-start | bytes 393224 | tf_op jit(solution)/shard_map/ppermute | solution.py:21
  46.2 4.8 %collective-permute-done.8.got_ref = bf16[8,32,256]{2,1,0:T(8,128)(2,1)S(1)} collective-permute-done((bf16[8,32,256]{2,1,0:T(8,128)(2,1)S(1)}, bf16[8,32,256]{2,1,0:T(8,128)(2,1)S(1)}, u32[]{:S(2)}, u32[]{:S(2)}) %collective-permute-start.8) | collective-permute-done | bytes 131104 | tf_op jit(solution)/shard_map/ppermute | solution.py:21
  51.0 0.7 %last_sum.1 = bf16[32,8,256]{2,1,0:T(8,128)(2,1)} custom-call(f32[8,32,256]{2,1,0:T(8,128)S(1)} %get-tuple-element.26.keep_ref, bf16[8,32,256]{2,1,0:T(8,128)(2,1)S(1)} %collective-permute-done.8.got_ref), custom_call_target="tpu_custom_call" | custom-call | tf_op jit(solution)/shard_map/last_sum/pallas_call | solution.py:265
  (61 shorter events, 1.9 us)
Async XLA Ops:
  0.6 11.1 %copy-start.2 = (s32[2,2,128,8]{2,3,1,0:T(8,128)S(1)}, s32[2,2,128,8]{2,3,1,0:T(8,128)}, u32[]{:S(2)}) copy-start(s32[2,2,128,8]{2,3,1,0:T(8,128)} %param.8) | copy-start | bytes 49156
  0.6 11.7 %copy-start.4 = (s32[1,8]{1,0:T(1,128)S(1)}, s32[1,8]{1,0:T(1,128)}, u32[]{:S(2)}) copy-start(s32[1,8]{1,0:T(1,128)} %param.9) | copy-start | bytes 100
  0.6 12.3 %copy-start.3 = (f32[8]{0:T(128)S(1)}, f32[8]{0:T(128)}, u32[]{:S(2)}) copy-start(f32[8]{0:T(128)} %constant.224.clone) | copy-start | bytes 100
  3.8 15.2 %collective-permute-start = (bf16[1,2,1,8,64,256]{5,4,3,2,1,0:T(8,128)(2,1)}, bf16[1,2,1,8,64,256]{5,4,3,2,1,0:T(8,128)(2,1)S(1)}, u32[]{:S(2)}, u32[]{:S(2)}) collective-permute-start(bf16[1,2,1,8,64,256]{5,4,3,2,1,0:T(8,128)(2,1)} %get-tuple-element.15), channel_id=1, source_target_pairs={{0,1},{1,0},{2,3},{3,2},{4,5},{5,4},{6,7},{7,6},{8,9},{9,8},{10,11... | collective-permute-start | bytes 1572872 | tf_op jit(solution)/shard_map/ppermute | solution.py:21
  10.1 13.6 %collective-permute-start.4 = (bf16[1,1,2,8,64,256]{5,4,3,2,1,0:T(8,128)(2,1)}, bf16[1,1,2,8,64,256]{5,4,3,2,1,0:T(8,128)(2,1)S(1)}, u32[]{:S(2)}, u32[]{:S(2)}) collective-permute-start(bf16[1,1,2,8,64,256]{5,4,3,2,1,0:T(8,128)(2,1)} %get-tuple-element.20), channel_id=1, source_target_pairs={{0,2},{1,3},{2,0},{3,1},{4,6},{5,7},{6,4},{7,5},{8,10},{9,11},{10,... | collective-permute-start | bytes 1572872 | tf_op jit(solution)/shard_map/ppermute | solution.py:21
  14.6 4.3 %copy-start.1 = (bf16[1,2,1,8,64,256]{5,4,3,2,1,0:T(8,128)(2,1)S(1)}, bf16[1,2,1,8,64,256]{5,4,3,2,1,0:T(8,128)(2,1)}, u32[]{:S(2)}) copy-start(bf16[1,2,1,8,64,256]{5,4,3,2,1,0:T(8,128)(2,1)} %get-tuple-element.14) | copy-start | bytes 1572868
  18.9 4.7 %copy-start = (bf16[1,1,2,8,64,256]{5,4,3,2,1,0:T(8,128)(2,1)S(1)}, bf16[1,1,2,8,64,256]{5,4,3,2,1,0:T(8,128)(2,1)}, u32[]{:S(2)}) copy-start(bf16[1,1,2,8,64,256]{5,4,3,2,1,0:T(8,128)(2,1)} %get-tuple-element.19) | copy-start | bytes 1572868
  21.3 4.8 %collective-permute-start.1 = (bf16[2,4,4,32,256]{4,3,2,1,0:T(8,128)(2,1)S(1)}, bf16[2,4,4,32,256]{4,3,2,1,0:T(8,128)(2,1)}, u32[]{:S(2)}, u32[]{:S(2)}) collective-permute-start(bf16[2,4,4,32,256]{4,3,2,1,0:T(8,128)(2,1)S(1)} %get-tuple-element.17), channel_id=1, source_target_pairs={{0,8},{8,0},{16,24},{24,16},{1,9},{9,1},{17,25},{25,17},{2,10},{10... | collective-permute-start | bytes 1572872 | tf_op jit(solution)/shard_map/ppermute | solution.py:21
  26.0 2.9 %collective-permute-start.5 = (bf16[2,4,4,32,256]{4,3,2,1,0:T(8,128)(2,1)S(1)}, bf16[2,4,4,32,256]{4,3,2,1,0:T(8,128)(2,1)}, u32[]{:S(2)}, u32[]{:S(2)}) collective-permute-start(bf16[2,4,4,32,256]{4,3,2,1,0:T(8,128)(2,1)S(1)} %get-tuple-element.22), channel_id=1, source_target_pairs={{0,8},{8,0},{16,24},{24,16},{1,9},{9,1},{17,25},{25,17},{2,10},{10... | collective-permute-start | bytes 1572872 | tf_op jit(solution)/shard_map/ppermute | solution.py:21
  27.3 8.8 %collective-permute-start.2 = (bf16[1,16,32,256]{3,2,1,0:T(8,128)(2,1)S(1)}, bf16[1,16,32,256]{3,2,1,0:T(8,128)(2,1)S(1)}, u32[]{:S(2)}, u32[]{:S(2)}) collective-permute-start(bf16[1,16,32,256]{3,2,1,0:T(8,128)(2,1)S(1)} %get-tuple-element.27), channel_id=1, source_target_pairs={{0,16},{8,24},{16,0},{24,8},{1,17},{9,25},{17,1},{25,9},{2,18},{10... | collective-permute-start | bytes 786440 | tf_op jit(solution)/shard_map/ppermute | solution.py:21
  29.9 8.5 %collective-permute-start.6 = (bf16[2,8,32,256]{3,2,1,0:T(8,128)(2,1)S(1)}, bf16[2,8,32,256]{3,2,1,0:T(8,128)(2,1)S(1)}, u32[]{:S(2)}, u32[]{:S(2)}) collective-permute-start(bf16[2,8,32,256]{3,2,1,0:T(8,128)(2,1)S(1)} %fusion.5), channel_id=1, source_target_pairs={{0,1},{1,0},{2,3},{3,2},{4,5},{5,4},{6,7},{7,6},{8,9},{9,8},{10,11... | collective-permute-start | bytes 786440 | tf_op jit(solution)/shard_map/ppermute | solution.py:21
  36.1 5.2 %collective-permute-start.3 = (bf16[1,8,32,256]{3,2,1,0:T(8,128)(2,1)S(1)}, bf16[1,8,32,256]{3,2,1,0:T(8,128)(2,1)S(1)}, u32[]{:S(2)}, u32[]{:S(2)}) collective-permute-start(bf16[1,8,32,256]{3,2,1,0:T(8,128)(2,1)S(1)} %fusion.11), channel_id=1, source_target_pairs={{0,2},{1,3},{2,0},{3,1},{4,6},{5,7},{6,4},{7,5},{8,10},{9,11},{10,... | collective-permute-start | bytes 393224 | tf_op jit(solution)/shard_map/ppermute | solution.py:21
  38.4 5.0 %collective-permute-start.7 = (bf16[1,8,32,256]{3,2,1,0:T(8,128)(2,1)S(1)}, bf16[1,8,32,256]{3,2,1,0:T(8,128)(2,1)S(1)}, u32[]{:S(2)}, u32[]{:S(2)}) collective-permute-start(bf16[1,8,32,256]{3,2,1,0:T(8,128)(2,1)S(1)} %fusion.7), channel_id=1, source_target_pairs={{0,16},{8,24},{16,0},{24,8},{1,17},{9,25},{17,1},{25,9},{2,18},{10... | collective-permute-start | bytes 393224 | tf_op jit(solution)/shard_map/ppermute | solution.py:21
  43.6 7.4 %collective-permute-start.8 = (bf16[8,32,256]{2,1,0:T(8,128)(2,1)S(1)}, bf16[8,32,256]{2,1,0:T(8,128)(2,1)S(1)}, u32[]{:S(2)}, u32[]{:S(2)}) collective-permute-start(bf16[8,32,256]{2,1,0:T(8,128)(2,1)S(1)} %get-tuple-element.25), channel_id=1, source_target_pairs={{0,4},{1,5},{2,6},{3,7},{4,0},{5,1},{6,2},{7,3},{8,12},{9,13},{10,... | collective-permute-start | bytes 393224 | tf_op jit(solution)/shard_map/ppermute | solution.py:21

commit v6 on v5

--- a/solution.py
+++ b/solution.py
@@ -30,9 +30,9 @@
     return lax.axis_index(axis) >> at & 1
 
 
-def compress_kernel(
-    dims, chirp_ref, edge_ref, echo_ref, keep_ref, send_ref, edge_out, weights, rows_ref, carry
-):
+def compress_kernel(dims, has_edge, chirp_ref, echo_ref, *refs):
+    edge_ref, refs = (refs[0], refs[1:]) if has_edge else (None, refs)
+    keep_ref, send_ref, edge_out, weights, rows_ref, carry = refs
     tile, pulses, half, near_chain, axis_bit = dims
     blocks = 2 * tile
     pitch = blocks + 1
@@ -40,7 +40,14 @@
     near = 1 - pl.program_id(1)
     own = own_bit("turn", axis_bit)
 
-    @pl.when((pl.program_id(0) == 0) & (pl.program_id(1) == 0) & (pl.program_id(2) == 0))
+    set_of_pulses = pl.program_id(3)
+    start = (pl.program_id(0) == 0) & (pl.program_id(1) == 0) & (pl.program_id(2) == 0)
+
+    @pl.when(start)
+    def _():
+        carry[set_of_pulses] = edge_ref[...] if has_edge else jnp.zeros_like(carry[0])
+
+    @pl.when(start & (set_of_pulses == 0))
     def _():
         rows = lax.broadcasted_iota(jnp.int32, (half, half), 0)
         cols = lax.broadcasted_iota(jnp.int32, (half, half), 1)
@@ -55,7 +62,6 @@
             low = jnp.concatenate([-im, re], axis=1)
             full = jnp.concatenate([top, low], axis=0)
             weights[m * 2 * half : (m + 1) * 2 * half, :] = full.astype(jnp.bfloat16)
-        carry[...] = edge_ref[...]
 
     for p in range(pulses):
         for c in range(2):
@@ -66,7 +72,7 @@
     for b in range(blocks):
         parts = [rows_ref[c, pl.ds(b, pulses, stride=pitch), :] for c in range(2)]
         turned.append(jnp.concatenate(parts, axis=1).astype(jnp.bfloat16))
-    turned.append(carry[...])
+    turned.append(carry[set_of_pulses])
     current = jnp.concatenate(turned[:-1], axis=0)
     after = jnp.concatenate(turned[1:], axis=0)
     total = jnp.dot(
@@ -74,7 +80,7 @@
         weights[...],
         preferred_element_type=jnp.float32,
     ).astype(jnp.bfloat16)
-    carry[...] = turned[0]
+    carry[set_of_pulses] = turned[0]
     edge_out[...] = turned[0]
 
     if near_chain:
@@ -91,42 +97,53 @@
             @pl.when((near == own) == mine)
             def _(ref=ref):
                 for b in range(blocks):
-                    ref[0, mid, b // tile, b % tile] = total[b * pulses : (b + 1) * pulses]
+                    span = pl.ds(pl.multiple_of(set_of_pulses * pulses, pulses), pulses)
+                    ref[0, mid, b // tile, b % tile, span] = total[b * pulses : (b + 1) * pulses]
 
 
 def compress(chirp, edge, echoes, high, mids, near_chain, axis_bit, first_high):
     pulses, blocks, width = echoes.shape
     half = width // 2
     tile = blocks // lax.axis_size("turn")
+    cuts = 2
+    some = pulses // cuts
     if near_chain:
         shape = (high, 2, mids, tile, pulses, width)
         spec = pl.BlockSpec(
-            (1, 1, 1) + shape[3:], lambda h, v, m: (high - 1 - h, 1 - v, mids - 1 - m, 0, 0, 0)
+            (1, 1, 1, tile, some, width),
+            lambda h, v, m, p: (high - 1 - h, 1 - v, mids - 1 - m, 0, p, 0),
         )
     else:
         shape = (high, mids, 2, tile, pulses, width)
-        spec = pl.BlockSpec((1,) + shape[1:], lambda h, v, m: (high - 1 - h, 0, 0, 0, 0, 0))
-    edge_spec = pl.BlockSpec((pulses, width), lambda h, v, m: (0, 0))
-
-    def chunk(h, v, m):
-        return 0, ((first_high + high - 1 - h) * 2 + 1 - v) * mids + mids - 1 - m, 0
-
+        spec = pl.BlockSpec(
+            (1, mids, 2, tile, pulses, width), lambda h, v, m, p: (high - 1 - h, 0, 0, 0, 0, 0)
+        )
+    edge_spec = pl.BlockSpec((some, width), lambda h, v, m, p: (p, 0))
+
+    def chunk(h, v, m, p):
+        return p, ((first_high + high - 1 - h) * 2 + 1 - v) * mids + mids - 1 - m, 0
+
+    in_specs = [
+        pl.BlockSpec((2, half), lambda h, v, m, p: (0, 0)),
+        pl.BlockSpec((some, 2 * tile, width), chunk),
+    ]
+    operands = [chirp, echoes]
+    if edge is not None:
+        in_specs.append(edge_spec)
+        operands.append(edge)
+    dims = (tile, some, half, near_chain, axis_bit)
     return pl.pallas_call(
-        functools.partial(compress_kernel, (tile, pulses, half, near_chain, axis_bit)),
-        grid=(high, 2, mids),
-        in_specs=[
-            pl.BlockSpec((2, half), lambda h, v, m: (0, 0)),
-            edge_spec,
-            pl.BlockSpec((pulses, 2 * tile, width), chunk),
-        ],
+        functools.partial(compress_kernel, dims, edge is not None),
+        grid=(high, 2, mids, cuts),
+        in_specs=in_specs,
         out_specs=[spec, spec, edge_spec],
         out_shape=[
             jax.ShapeDtypeStruct(s, jnp.bfloat16) for s in (shape, shape, (pulses, width))
         ],
         scratch_shapes=[
             pltpu.VMEM((2 * width, width), jnp.bfloat16),
-            pltpu.VMEM((2, pulses * (2 * tile + 1), half), jnp.float32),
-            pltpu.VMEM((pulses, width), jnp.bfloat16),
+            pltpu.VMEM((2, some * (2 * tile + 1), half), jnp.float32),
+            pltpu.VMEM((cuts, some, width), jnp.bfloat16),
         ],
         compiler_params=pltpu.CompilerParams(vmem_limit_bytes=VMEM_BYTES),
         cost_estimate=pl.CostEstimate(
@@ -135,7 +152,7 @@
             transcendentals=0,
         ),
         name="compress",
-    )(chirp, edge, echoes)
+    )(*operands)
 
 
 def image_kernel(dims, data_ref, steer_ref, interp_ref, base_ref, step_ref, out_keep, out_send):
@@ -241,12 +258,18 @@
     )(data, steer, interp, base, step)
 
 
-def fold(own, keep, got):
+def total_of(terms):
+    total = terms[0]
+    for term in terms[1:]:
+        total = total + term.astype(jnp.float32)
+    return total
+
+
+def fold(own, terms, split):
     def half(at):
-        kept, came = (lax.dynamic_index_in_dim(a, at, 1, False) for a in (keep, got))
-        return kept + came.astype(jnp.float32)
-
-    return half(own), half(1 - own).astype(jnp.bfloat16)
+        return [lax.dynamic_index_in_dim(t.reshape(split), at, 1, False) for t in terms]
+
+    return half(own), total_of(half(1 - own)).astype(jnp.bfloat16)
 
 
 def last_kernel(keep_ref, got_ref, out_ref, rows_ref):
@@ -322,8 +345,7 @@
     rows = beams // leaf
     own_leaf, own_turn = lax.axis_index("leaf"), lax.axis_index("turn")
 
-    edge = jnp.zeros((pulses, width), jnp.bfloat16)
-    keep_y, send_y, edge = compress(chirp, edge, echoes, high, mids, True, 0, high)
+    keep_y, send_y, edge = compress(chirp, None, echoes, high, mids, True, 0, high)
     got_y = swapped(send_y, "turn", 0)
     keep_z, send_z, _ = compress(chirp, edge, echoes, high, mids, False, far, 0)
     got_z = swapped(send_z, "turn", far)
@@ -385,17 +407,15 @@
         order = [("leaf", b) for b in range(1, levels)]
         rest = [("turn", b) for b in range(top) if b not in (0, far)]
         order = order + [("turn", far)] if name == "y" else [("turn", 0)] + order
-        arrived = swapped(sent, "leaf", 0)
+        terms = [kept, swapped(sent, "leaf", 0)]
         for axis, b in order + rest:
             at = leading.index((axis, b))
             before, after = 1 << at, (1 << len(leading) - at - 1) * tile
             leading.pop(at)
-            split = (before, 2, after, rows, width)
             own = bit(own_leaf if axis == "leaf" else own_turn, b)
-            kept, sent = fold(own, kept.reshape(split), arrived.reshape(split))
-            arrived = swapped(sent, axis, b)
-        shape = (tile, rows, width)
-        final.append(kept.reshape(shape) + arrived.reshape(shape).astype(jnp.float32))
+            terms, sent = fold(own, terms, (before, 2, after, rows, width))
+            terms.append(swapped(sent, axis, b))
+        final.append(total_of([t.reshape(tile, rows, width) for t in terms]))
     upper = bit(own_turn, top) == 1
     kept = jnp.where(upper, final[0], final[1])
     sent = jnp.where(upper, final[1], final[0]).astype(jnp.bfloat16)

time: 52 us -> 55.3 us (1.063)
  Pallas kernels: 11.6 us -> 13.8 us
  other arithmetic: 7.77 us -> 8.54 us
    pallas_call x2, Pallas kernels: 6.43 us -> 8.62 us  [compress(): pl.pallas_call(functools.partial(compress_kernel, dims, edge is not None)...]
    add x1 -> x0, other arithmetic: 1.02 us -> none  [half(): return kept + came.astype(jnp.float32)]
    dynamic_slice x0 -> x1, local copies, waits for them, and re-layouts: none -> 0.97 us  [half(): lax.dynamic_index_in_dim(t.reshape(split), at, 1, False)]
    convert_element_type x1, other arithmetic: 0.11 us -> 1.06 us  [per_device(): sent = jnp.where(upper, final[1], final[0]).astype(jnp.bfloat16)]
    convert_element_type x4, other arithmetic: 2.28 us -> 3.11 us  [fold(): return (half(own), total_of(half(1 - own)).astype(jnp.bfloat16))]
    broadcast_in_dim x1 -> x0, local copies, waits for them, and re-layouts: 0.62 us -> none  [per_device(): edge = jnp.zeros((pulses, width), jnp.bfloat16)]
  transfers between devices with their start and end apart: 9 -> 9, of which waited for: 7 -> 7; matrix products, arithmetic and copies ran while one was open for 17% -> 17% of each run, Pallas kernels for 15% -> 16%
where the time goes in v6:
time: 55.3 us; the launch traced here: 55 us
  waiting for transfers between devices  18.2 us (33%)
  Pallas kernels  13.8 us (25%)
  starting transfers between devices  12.1 us (22%)
  other arithmetic  8.54 us (15%)
  local copies, waits for them, and re-layouts  1.85 us (3%)
    ppermute x9, waiting for transfers between devices, swapped(): lax.ppermute(array, axis, [(i, i ^ 1 << bit) for i in range(lax.axis_size...  18.2 us
    ppermute x9, starting transfers between devices, swapped(): lax.ppermute(array, axis, [(i, i ^ 1 << bit) for i in range(lax.axis_size...  12.1 us
    pallas_call x2, Pallas kernels, compress(): pl.pallas_call(functools.partial(compress_kernel, dims, edge is not None)...  8.62 us
    pallas_call x2, Pallas kernels, backproject(): pl.pallas_call(functools.partial(image_kernel, (leaf, each, half, beams,...  4.46 us
    convert_element_type x4, other arithmetic, fold(): return (half(own), total_of(half(1 - own)).astype(jnp.bfloat16))  3.11 us
    cos x2, other arithmetic, unit(): return (jnp.cos(angle), jnp.sin(angle))  2.27 us
  transfers between devices with their start and end apart: 9, of which 7 were waited for; matrix products, arithmetic and copies ran while one was open for 17% of the time, Pallas kernels for 16%

profile of v6, /device:TPU:0, one launch (start us, length us, event | category | flops | bytes accessed | tf_op | source)
XLA Modules:
  0.0 55.0 jit_solution(17895044380059216784)
XLA Ops:
  0.0 4.2 %compress.2 = (bf16[1,2,1,8,64,256]{5,4,3,2,1,0:T(8,128)(2,1)}, bf16[1,2,1,8,64,256]{5,4,3,2,1,0:T(8,128)(2,1)}, bf16[64,256]{1,0:T(8,128)(2,1)}) custom-call(bf16[2,128]{1,0:T(2,128)(2,1)} %chirp_ref.3, bf16[64,64,256]{2,1,0:T(8,128)(2,1)} %echo_ref.3), custom_call_target="tpu_custom_call" | custom-call | flops 536870912 | bytes 2097152 | tf_op jit(solution)/shard_map/compress/pallas_call | solution.py:135
  4.3 3.0 %collective-permute-start = (bf16[1,2,1,8,64,256]{5,4,3,2,1,0:T(8,128)(2,1)}, bf16[1,2,1,8,64,256]{5,4,3,2,1,0:T(8,128)(2,1)S(1)}, u32[]{:S(2)}, u32[]{:S(2)}) collective-permute-start(bf16[1,2,1,8,64,256]{5,4,3,2,1,0:T(8,128)(2,1)} %get-tuple-element.15), channel_id=1, source_target_pairs={{0,1},{1,0},{2,3},{3,2},{4,5},{5,4},{6,7},{7,6},{8,9},{9,8},{10,11... | collective-permute-start | bytes 1572872 | tf_op jit(solution)/shard_map/ppermute | solution.py:21
  7.2 4.4 %compress.3 = (bf16[1,1,2,8,64,256]{5,4,3,2,1,0:T(8,128)(2,1)}, bf16[1,1,2,8,64,256]{5,4,3,2,1,0:T(8,128)(2,1)}, bf16[64,256]{1,0:T(8,128)(2,1)}) custom-call(bf16[2,128]{1,0:T(2,128)(2,1)} %chirp_ref.3, bf16[64,64,256]{2,1,0:T(8,128)(2,1)} %echo_ref.3, bf16[64,256]{1,0:T(8,128)(2,1)} %get-tuple-element.18.refs_0_), custom_call_target="tpu_custom_call" | custom-call | flops 536870912 | bytes 2097152 | tf_op jit(solution)/shard_map/compress/pallas_call | solution.py:135
  11.6 1.6 %collective-permute-start.4 = (bf16[1,1,2,8,64,256]{5,4,3,2,1,0:T(8,128)(2,1)}, bf16[1,1,2,8,64,256]{5,4,3,2,1,0:T(8,128)(2,1)S(1)}, u32[]{:S(2)}, u32[]{:S(2)}) collective-permute-start(bf16[1,1,2,8,64,256]{5,4,3,2,1,0:T(8,128)(2,1)} %get-tuple-element.20), channel_id=1, source_target_pairs={{0,2},{1,3},{2,0},{3,1},{4,6},{5,7},{6,4},{7,5},{8,10},{9,11},{10,... | collective-permute-start | bytes 1572872 | tf_op jit(solution)/shard_map/ppermute | solution.py:21
  13.2 0.2 select_reduce_fusion.1
  13.9 0.1 copy.19
  14.6 0.4 select_reduce_fusion
  15.0 0.5 multiply_convert_fusion.1
  15.5 0.2 fusion.12
  15.9 0.2 fusion.26
  16.2 0.1 copy.24.steer_ref
  16.4 2.1 %fusion.7 = (f32[2,1,128,512]{3,2,1,0:T(8,128)S(1)}, f32[2,1,128,512]{3,2,1,0:T(8,128)S(1)}) fusion(s32[512]{0:T(512)S(1)} %iota_add_fusion, s32[2,128]{1,0:T(2,128)S(1)} %add_multiply_fusion), kind=kLoop, calls=%fused_computation.25 | loop fusion | flops 1835008 | bytes 1051648 | tf_op jit(solution)/shard_map/cos | solution.py:26
  18.6 0.7 %collective-permute-done = bf16[1,2,1,8,64,256]{5,4,3,2,1,0:T(8,128)(2,1)S(1)} collective-permute-done((bf16[1,2,1,8,64,256]{5,4,3,2,1,0:T(8,128)(2,1)}, bf16[1,2,1,8,64,256]{5,4,3,2,1,0:T(8,128)(2,1)S(1)}, u32[]{:S(2)}, u32[]{:S(2)}) %collective-permute-start) | collective-permute-done | bytes 524320 | tf_op jit(solution)/shard_map/ppermute | solution.py:21
  19.5 2.2 %image.2 = (f32[2,4,4,32,256]{4,3,2,1,0:T(8,128)S(1)}, bf16[2,4,4,32,256]{4,3,2,1,0:T(8,128)(2,1)S(1)}) custom-call(bf16[2,4,4,64,256]{4,3,2,1,0:T(8,128)(2,1)S(1)} %pad_maximum_fusion.data_ref, bf16[256,256]{1,0:T(8,128)(2,1)S(1)} %copy.24.steer_ref, bf16[1,128,256]{2,1,0:T(8,128)(2,1)S(1)} %pad_maximum_fusion.4.interp_ref, f32[4,4,128]{2,1,0:T(4,128)S(1)} %bitcast.89, ...), custom_call_target="tpu_custom_call" | custom-call | flops 402653184 | bytes 2621440 | tf_op jit(solution)/shard_map/image/pallas_call | solution.py:236
  21.8 3.4 %collective-permute-done.4 = bf16[1,1,2,8,64,256]{5,4,3,2,1,0:T(8,128)(2,1)S(1)} collective-permute-done((bf16[1,1,2,8,64,256]{5,4,3,2,1,0:T(8,128)(2,1)}, bf16[1,1,2,8,64,256]{5,4,3,2,1,0:T(8,128)(2,1)S(1)}, u32[]{:S(2)}, u32[]{:S(2)}) %collective-permute-start.4) | collective-permute-done | bytes 524320 | tf_op jit(solution)/shard_map/ppermute | solution.py:21
  25.3 2.2 %image.3 = (f32[2,4,4,32,256]{4,3,2,1,0:T(8,128)S(1)}, bf16[2,4,4,32,256]{4,3,2,1,0:T(8,128)(2,1)S(1)}) custom-call(bf16[2,4,4,64,256]{4,3,2,1,0:T(8,128)(2,1)S(1)} %pad_maximum_fusion.2.data_ref, bf16[256,256]{1,0:T(8,128)(2,1)S(1)} %copy.25.steer_ref, bf16[1,128,256]{2,1,0:T(8,128)(2,1)S(1)} %pad_maximum_fusion.4.interp_ref, f32[4,4,128]{2,1,0:T(4,128)S(1)} %bitcast.88, ...), custom_call_target="tpu_custom_call" | custom-call | flops 402653184 | bytes 2621440 | tf_op jit(solution)/shard_map/image/pallas_call | solution.py:236
  27.6 1.1 %fusion.3 = (bf16[1,16,32,256]{3,2,1,0:T(8,128)(2,1)S(1)}, f32[1,1,16,32,256]{4,3,2,1,0:T(8,128)S(1)}) fusion(f32[1,2,16,32,256]{4,3,2,1,0:T(8,128)S(1)} %bitcast.87, s32[]{:T(128)S(6)} %select_n.236, bf16[1,2,16,32,256]{4,3,2,1,0:T(8,128)(2,1)} %bitcast.16, s32[]{:T(128)S(6)} %select_n.224), kind=kLoop, calls=%fused_computation.15 | loop fusion | flops 393216 | bytes 2097160 | tf_op jit(solution)/shard_map/convert_element_type | solution.py:272
  28.7 1.6 %collective-permute-start.2 = (bf16[1,16,32,256]{3,2,1,0:T(8,128)(2,1)S(1)}, bf16[1,16,32,256]{3,2,1,0:T(8,128)(2,1)S(1)}, u32[]{:S(2)}, u32[]{:S(2)}) collective-permute-start(bf16[1,16,32,256]{3,2,1,0:T(8,128)(2,1)S(1)} %get-tuple-element.27), channel_id=1, source_target_pairs={{0,16},{8,24},{16,0},{24,8},{1,17},{9,25},{17,1},{25,9},{2,18},{10... | collective-permute-start | bytes 786440 | tf_op jit(solution)/shard_map/ppermute | solution.py:21
  30.3 1.0 %fusion.4 = bf16[2,8,32,256]{3,2,1,0:T(8,128)(2,1)S(1)} fusion(f32[2,2,8,32,256]{4,3,2,1,0:T(8,128)S(1)} %bitcast.84, s32[]{:T(128)S(6)} %select_n.242, bf16[2,2,8,32,256]{4,3,2,1,0:T(8,128)(2,1)} %bitcast.28), kind=kLoop, calls=%fused_computation.16 | loop fusion | flops 393216 | bytes 1048580 | tf_op jit(solution)/shard_map/convert_element_type | solution.py:272
  31.3 0.6 %collective-permute-start.6 = (bf16[2,8,32,256]{3,2,1,0:T(8,128)(2,1)S(1)}, bf16[2,8,32,256]{3,2,1,0:T(8,128)(2,1)S(1)}, u32[]{:S(2)}, u32[]{:S(2)}) collective-permute-start(bf16[2,8,32,256]{3,2,1,0:T(8,128)(2,1)S(1)} %fusion.4), channel_id=1, source_target_pairs={{0,1},{1,0},{2,3},{3,2},{4,5},{5,4},{6,7},{7,6},{8,9},{9,8},{10,11... | collective-permute-start | bytes 786440 | tf_op jit(solution)/shard_map/ppermute | solution.py:21
  31.9 1.0 %constant_dynamic-slice_fusion = bf16[1,1,16,32,256]{4,3,2,1,0:T(8,128)(2,1)S(1)} fusion(bf16[1,2,16,32,256]{4,3,2,1,0:T(8,128)(2,1)} %bitcast.16, s32[]{:T(128)S(6)} %select_n.224), kind=kLoop, calls=%fused_computation.62 | loop fusion | bytes 524292 | tf_op jit(solution)/shard_map/jit(dynamic_index_in_dim)/dynamic_slice | solution.py:270
  32.8 4.6 %collective-permute-done.2 = bf16[1,16,32,256]{3,2,1,0:T(8,128)(2,1)S(1)} collective-permute-done((bf16[1,16,32,256]{3,2,1,0:T(8,128)(2,1)S(1)}, bf16[1,16,32,256]{3,2,1,0:T(8,128)(2,1)S(1)}, u32[]{:S(2)}, u32[]{:S(2)}) %collective-permute-start.2) | collective-permute-done | bytes 262176 | tf_op jit(solution)/shard_map/ppermute | solution.py:21
  37.5 1.6 %collective-permute-start.3 = (bf16[1,8,32,256]{3,2,1,0:T(8,128)(2,1)S(1)}, bf16[1,8,32,256]{3,2,1,0:T(8,128)(2,1)S(1)}, u32[]{:S(2)}, u32[]{:S(2)}) collective-permute-start(bf16[1,8,32,256]{3,2,1,0:T(8,128)(2,1)S(1)} %fusion.8), channel_id=1, source_target_pairs={{0,2},{1,3},{2,0},{3,1},{4,6},{5,7},{6,4},{7,5},{8,10},{9,11},{10,... | collective-permute-start | bytes 393224 | tf_op jit(solution)/shard_map/ppermute | solution.py:21
  39.2 0.6 %collective-permute-done.6 = bf16[2,8,32,256]{3,2,1,0:T(8,128)(2,1)S(1)} collective-permute-done((bf16[2,8,32,256]{3,2,1,0:T(8,128)(2,1)S(1)}, bf16[2,8,32,256]{3,2,1,0:T(8,128)(2,1)S(1)}, u32[]{:S(2)}, u32[]{:S(2)}) %collective-permute-start.6) | collective-permute-done | bytes 262176 | tf_op jit(solution)/shard_map/ppermute | solution.py:21
  39.8 1.0 %fusion.5 = bf16[1,8,32,256]{3,2,1,0:T(8,128)(2,1)S(1)} fusion(f32[2,2,8,32,256]{4,3,2,1,0:T(8,128)S(1)} %bitcast.85, s32[]{:T(128)S(6)} %select_n.243, s32[]{:T(128)S(6)} %select_n.241, bf16[2,8,32,256]{3,2,1,0:T(8,128)(2,1)S(1)} %collective-permute-done.6, s32[]{:T(128)S(6)} %select_n.236, bf16[2,2,8,32,256]{4,3,2,1,0:T(8,128)(2,1)} %bitcast.28), kind=kLoop, calls=%fused_computation.21 | loop fusion | flops 327680 | bytes 655372 | tf_op jit(solution)/shard_map/convert_element_type | solution.py:272
  40.7 0.9 %collective-permute-start.7 = (bf16[1,8,32,256]{3,2,1,0:T(8,128)(2,1)S(1)}, bf16[1,8,32,256]{3,2,1,0:T(8,128)(2,1)S(1)}, u32[]{:S(2)}, u32[]{:S(2)}) collective-permute-start(bf16[1,8,32,256]{3,2,1,0:T(8,128)(2,1)S(1)} %fusion.5), channel_id=1, source_target_pairs={{0,16},{8,24},{16,0},{24,8},{1,17},{9,25},{17,1},{25,9},{2,18},{10... | collective-permute-start | bytes 393224 | tf_op jit(solution)/shard_map/ppermute | solution.py:21
  41.7 1.0 %collective-permute-done.3 = bf16[1,8,32,256]{3,2,1,0:T(8,128)(2,1)S(1)} collective-permute-done((bf16[1,8,32,256]{3,2,1,0:T(8,128)(2,1)S(1)}, bf16[1,8,32,256]{3,2,1,0:T(8,128)(2,1)S(1)}, u32[]{:S(2)}, u32[]{:S(2)}) %collective-permute-start.3) | collective-permute-done | bytes 131104 | tf_op jit(solution)/shard_map/ppermute | solution.py:21
  42.7 3.1 %collective-permute-done.7 = bf16[1,8,32,256]{3,2,1,0:T(8,128)(2,1)S(1)} collective-permute-done((bf16[1,8,32,256]{3,2,1,0:T(8,128)(2,1)S(1)}, bf16[1,8,32,256]{3,2,1,0:T(8,128)(2,1)S(1)}, u32[]{:S(2)}, u32[]{:S(2)}) %collective-permute-start.7) | collective-permute-done | bytes 131104 | tf_op jit(solution)/shard_map/ppermute | solution.py:21
  45.8 1.1 %select_convert_fusion = (bf16[8,32,256]{2,1,0:T(8,128)(2,1)S(1)}, f32[8,32,256]{2,1,0:T(8,128)S(1)}) fusion(pred[]{:T(512)S(6)} %eq.40, bf16[1,8,32,256]{3,2,1,0:T(8,128)(2,1)S(1)} %collective-permute-done.3, bf16[1,2,8,32,256]{4,3,2,1,0:T(8,128)(2,1)S(1)} %bitcast.101, s32[]{:T(128)S(6)} %select_n.235, bf16[1,2,8,32,256]{4,3,2,1,0:T(8,128)(2,1)S(1)} %bitcast.93, ...), kind=kLoop, calls=%fused_computation.22 | loop fusion | flops 983040 | bytes 1703953 | tf_op jit(solution)/shard_map/convert_element_type | solution.py:421
  46.8 2.7 %collective-permute-start.8 = (bf16[8,32,256]{2,1,0:T(8,128)(2,1)S(1)}, bf16[8,32,256]{2,1,0:T(8,128)(2,1)S(1)}, u32[]{:S(2)}, u32[]{:S(2)}) collective-permute-start(bf16[8,32,256]{2,1,0:T(8,128)(2,1)S(1)} %get-tuple-element.25), channel_id=1, source_target_pairs={{0,4},{1,5},{2,6},{3,7},{4,0},{5,1},{6,2},{7,3},{8,12},{9,13},{10,... | collective-permute-start | bytes 393224 | tf_op jit(solution)/shard_map/ppermute | solution.py:21
  49.5 4.7 %collective-permute-done.8.got_ref = bf16[8,32,256]{2,1,0:T(8,128)(2,1)S(1)} collective-permute-done((bf16[8,32,256]{2,1,0:T(8,128)(2,1)S(1)}, bf16[8,32,256]{2,1,0:T(8,128)(2,1)S(1)}, u32[]{:S(2)}, u32[]{:S(2)}) %collective-permute-start.8) | collective-permute-done | bytes 131104 | tf_op jit(solution)/shard_map/ppermute | solution.py:21
  54.2 0.7 %last_sum.1 = bf16[32,8,256]{2,1,0:T(8,128)(2,1)} custom-call(f32[8,32,256]{2,1,0:T(8,128)S(1)} %get-tuple-element.26.keep_ref, bf16[8,32,256]{2,1,0:T(8,128)(2,1)S(1)} %collective-permute-done.8.got_ref), custom_call_target="tpu_custom_call" | custom-call | tf_op jit(solution)/shard_map/last_sum/pallas_call | solution.py:288
  (60 shorter events, 1.9 us)
Async XLA Ops:
  0.0 14.6 %copy-start.3 = (f32[8]{0:T(128)S(1)}, f32[8]{0:T(128)}, u32[]{:S(2)}) copy-start(f32[8]{0:T(128)} %constant.324.clone) | copy-start | bytes 100
  0.0 13.2 %copy-start.4 = (s32[1,8]{1,0:T(1,128)S(1)}, s32[1,8]{1,0:T(1,128)}, u32[]{:S(2)}) copy-start(s32[1,8]{1,0:T(1,128)} %param.9) | copy-start | bytes 100
  0.0 13.4 %copy-start.2 = (s32[2,2,128,8]{2,3,1,0:T(8,128)S(1)}, s32[2,2,128,8]{2,3,1,0:T(8,128)}, u32[]{:S(2)}) copy-start(s32[2,2,128,8]{2,3,1,0:T(8,128)} %param.8) | copy-start | bytes 49156
  4.3 15.1 %collective-permute-start = (bf16[1,2,1,8,64,256]{5,4,3,2,1,0:T(8,128)(2,1)}, bf16[1,2,1,8,64,256]{5,4,3,2,1,0:T(8,128)(2,1)S(1)}, u32[]{:S(2)}, u32[]{:S(2)}) collective-permute-start(bf16[1,2,1,8,64,256]{5,4,3,2,1,0:T(8,128)(2,1)} %get-tuple-element.15), channel_id=1, source_target_pairs={{0,1},{1,0},{2,3},{3,2},{4,5},{5,4},{6,7},{7,6},{8,9},{9,8},{10,11... | collective-permute-start | bytes 1572872 | tf_op jit(solution)/shard_map/ppermute | solution.py:21
  11.6 13.6 %collective-permute-start.4 = (bf16[1,1,2,8,64,256]{5,4,3,2,1,0:T(8,128)(2,1)}, bf16[1,1,2,8,64,256]{5,4,3,2,1,0:T(8,128)(2,1)S(1)}, u32[]{:S(2)}, u32[]{:S(2)}) collective-permute-start(bf16[1,1,2,8,64,256]{5,4,3,2,1,0:T(8,128)(2,1)} %get-tuple-element.20), channel_id=1, source_target_pairs={{0,2},{1,3},{2,0},{3,1},{4,6},{5,7},{6,4},{7,5},{8,10},{9,11},{10,... | collective-permute-start | bytes 1572872 | tf_op jit(solution)/shard_map/ppermute | solution.py:21
  16.1 3.2 %copy-start.1 = (bf16[1,2,1,8,64,256]{5,4,3,2,1,0:T(8,128)(2,1)S(1)}, bf16[1,2,1,8,64,256]{5,4,3,2,1,0:T(8,128)(2,1)}, u32[]{:S(2)}) copy-start(bf16[1,2,1,8,64,256]{5,4,3,2,1,0:T(8,128)(2,1)} %get-tuple-element.14) | copy-start | bytes 1572868
  19.4 5.8 %copy-start = (bf16[1,1,2,8,64,256]{5,4,3,2,1,0:T(8,128)(2,1)S(1)}, bf16[1,1,2,8,64,256]{5,4,3,2,1,0:T(8,128)(2,1)}, u32[]{:S(2)}) copy-start(bf16[1,1,2,8,64,256]{5,4,3,2,1,0:T(8,128)(2,1)} %get-tuple-element.19) | copy-start | bytes 1572868
  21.7 5.9 %collective-permute-start.1 = (bf16[2,4,4,32,256]{4,3,2,1,0:T(8,128)(2,1)S(1)}, bf16[2,4,4,32,256]{4,3,2,1,0:T(8,128)(2,1)}, u32[]{:S(2)}, u32[]{:S(2)}) collective-permute-start(bf16[2,4,4,32,256]{4,3,2,1,0:T(8,128)(2,1)S(1)} %get-tuple-element.17), channel_id=1, source_target_pairs={{0,8},{8,0},{16,24},{24,16},{1,9},{9,1},{17,25},{25,17},{2,10},{10... | collective-permute-start | bytes 1572872 | tf_op jit(solution)/shard_map/ppermute | solution.py:21
  27.5 2.7 %collective-permute-start.5 = (bf16[2,4,4,32,256]{4,3,2,1,0:T(8,128)(2,1)S(1)}, bf16[2,4,4,32,256]{4,3,2,1,0:T(8,128)(2,1)}, u32[]{:S(2)}, u32[]{:S(2)}) collective-permute-start(bf16[2,4,4,32,256]{4,3,2,1,0:T(8,128)(2,1)S(1)} %get-tuple-element.22), channel_id=1, source_target_pairs={{0,8},{8,0},{16,24},{24,16},{1,9},{9,1},{17,25},{25,17},{2,10},{10... | collective-permute-start | bytes 1572872 | tf_op jit(solution)/shard_map/ppermute | solution.py:21
  28.7 8.8 %collective-permute-start.2 = (bf16[1,16,32,256]{3,2,1,0:T(8,128)(2,1)S(1)}, bf16[1,16,32,256]{3,2,1,0:T(8,128)(2,1)S(1)}, u32[]{:S(2)}, u32[]{:S(2)}) collective-permute-start(bf16[1,16,32,256]{3,2,1,0:T(8,128)(2,1)S(1)} %get-tuple-element.27), channel_id=1, source_target_pairs={{0,16},{8,24},{16,0},{24,8},{1,17},{9,25},{17,1},{25,9},{2,18},{10... | collective-permute-start | bytes 786440 | tf_op jit(solution)/shard_map/ppermute | solution.py:21
  31.3 8.5 %collective-permute-start.6 = (bf16[2,8,32,256]{3,2,1,0:T(8,128)(2,1)S(1)}, bf16[2,8,32,256]{3,2,1,0:T(8,128)(2,1)S(1)}, u32[]{:S(2)}, u32[]{:S(2)}) collective-permute-start(bf16[2,8,32,256]{3,2,1,0:T(8,128)(2,1)S(1)} %fusion.4), channel_id=1, source_target_pairs={{0,1},{1,0},{2,3},{3,2},{4,5},{5,4},{6,7},{7,6},{8,9},{9,8},{10,11... | collective-permute-start | bytes 786440 | tf_op jit(solution)/shard_map/ppermute | solution.py:21
  37.5 5.2 %collective-permute-start.3 = (bf16[1,8,32,256]{3,2,1,0:T(8,128)(2,1)S(1)}, bf16[1,8,32,256]{3,2,1,0:T(8,128)(2,1)S(1)}, u32[]{:S(2)}, u32[]{:S(2)}) collective-permute-start(bf16[1,8,32,256]{3,2,1,0:T(8,128)(2,1)S(1)} %fusion.8), channel_id=1, source_target_pairs={{0,2},{1,3},{2,0},{3,1},{4,6},{5,7},{6,4},{7,5},{8,10},{9,11},{10,... | collective-permute-start | bytes 393224 | tf_op jit(solution)/shard_map/ppermute | solution.py:21
  40.7 5.0 %collective-permute-start.7 = (bf16[1,8,32,256]{3,2,1,0:T(8,128)(2,1)S(1)}, bf16[1,8,32,256]{3,2,1,0:T(8,128)(2,1)S(1)}, u32[]{:S(2)}, u32[]{:S(2)}) collective-permute-start(bf16[1,8,32,256]{3,2,1,0:T(8,128)(2,1)S(1)} %fusion.5), channel_id=1, source_target_pairs={{0,16},{8,24},{16,0},{24,8},{1,17},{9,25},{17,1},{25,9},{2,18},{10... | collective-permute-start | bytes 393224 | tf_op jit(solution)/shard_map/ppermute | solution.py:21
  46.8 7.4 %collective-permute-start.8 = (bf16[8,32,256]{2,1,0:T(8,128)(2,1)S(1)}, bf16[8,32,256]{2,1,0:T(8,128)(2,1)S(1)}, u32[]{:S(2)}, u32[]{:S(2)}) collective-permute-start(bf16[8,32,256]{2,1,0:T(8,128)(2,1)S(1)} %get-tuple-element.25), channel_id=1, source_target_pairs={{0,4},{1,5},{2,6},{3,7},{4,0},{5,1},{6,2},{7,3},{8,12},{9,13},{10,... | collective-permute-start | bytes 393224 | tf_op jit(solution)/shard_map/ppermute | solution.py:21

commit v7 on v5

--- a/solution.py
+++ b/solution.py
@@ -30,15 +30,15 @@
     return lax.axis_index(axis) >> at & 1
 
 
-def compress_kernel(
-    dims, chirp_ref, edge_ref, echo_ref, keep_ref, send_ref, edge_out, weights, rows_ref, carry
-):
-    tile, pulses, half, near_chain, axis_bit = dims
+def compress_kernel(dims, chirp_ref, echo_ref, *refs):
+    tile, pulses, half, far = dims
+    keep_y, send_y, keep_z, send_z, weights, rows_ref, carry = refs
     blocks = 2 * tile
     pitch = blocks + 1
+    high = pl.num_programs(0)
     mid = pl.num_programs(2) - 1 - pl.program_id(2)
     near = 1 - pl.program_id(1)
-    own = own_bit("turn", axis_bit)
+    upper = pl.program_id(0) < high // 2
 
     @pl.when((pl.program_id(0) == 0) & (pl.program_id(1) == 0) & (pl.program_id(2) == 0))
     def _():
@@ -55,7 +55,7 @@
             low = jnp.concatenate([-im, re], axis=1)
             full = jnp.concatenate([top, low], axis=0)
             weights[m * 2 * half : (m + 1) * 2 * half, :] = full.astype(jnp.bfloat16)
-        carry[...] = edge_ref[...]
+        carry[...] = jnp.zeros_like(carry)
 
     for p in range(pulses):
         for c in range(2):
@@ -75,53 +75,55 @@
         preferred_element_type=jnp.float32,
     ).astype(jnp.bfloat16)
     carry[...] = turned[0]
-    edge_out[...] = turned[0]
-
-    if near_chain:
-        for side in range(2):
-
-            @pl.when(own == side)
-            def _(side=side):
-                for b in range(blocks):
-                    ref = keep_ref if b // tile == side else send_ref
-                    ref[0, 0, 0, b % tile] = total[b * pulses : (b + 1) * pulses]
-    else:
-        for ref, mine in ((keep_ref, True), (send_ref, False)):
-
-            @pl.when((near == own) == mine)
-            def _(ref=ref):
-                for b in range(blocks):
-                    ref[0, mid, b // tile, b % tile] = total[b * pulses : (b + 1) * pulses]
-
-
-def compress(chirp, edge, echoes, high, mids, near_chain, axis_bit, first_high):
+
+    for side in range(2):
+
+        @pl.when(upper & (own_bit("turn", 0) == side))
+        def _(side=side):
+            for b in range(blocks):
+                ref = keep_y if b // tile == side else send_y
+                ref[0, 0, 0, b % tile] = total[b * pulses : (b + 1) * pulses]
+
+    for ref, mine in ((keep_z, True), (send_z, False)):
+
+        @pl.when(jnp.logical_not(upper) & ((near == own_bit("turn", far)) == mine))
+        def _(ref=ref):
+            for b in range(blocks):
+                ref[0, mid, b // tile, b % tile] = total[b * pulses : (b + 1) * pulses]
+
+
+def compress(chirp, echoes, high, mids, far):
     pulses, blocks, width = echoes.shape
     half = width // 2
     tile = blocks // lax.axis_size("turn")
-    if near_chain:
-        shape = (high, 2, mids, tile, pulses, width)
-        spec = pl.BlockSpec(
-            (1, 1, 1) + shape[3:], lambda h, v, m: (high - 1 - h, 1 - v, mids - 1 - m, 0, 0, 0)
-        )
-    else:
-        shape = (high, mids, 2, tile, pulses, width)
-        spec = pl.BlockSpec((1,) + shape[1:], lambda h, v, m: (high - 1 - h, 0, 0, 0, 0, 0))
-    edge_spec = pl.BlockSpec((pulses, width), lambda h, v, m: (0, 0))
+    each = high // 2
+    shape_y = (each, 2, mids, tile, pulses, width)
+    shape_z = (each, mids, 2, tile, pulses, width)
+
+    def place_y(h, v, m):
+        over = h >= each
+        spot = (each - 1 - h, 1 - v, mids - 1 - m)
+        return tuple(jnp.where(over, 0, x) for x in spot) + (0, 0, 0)
+
+    def place_z(h, v, m):
+        return jnp.minimum(high - 1 - h, each - 1), 0, 0, 0, 0, 0
+
+    spec_y = pl.BlockSpec((1, 1, 1) + shape_y[3:], place_y)
+    spec_z = pl.BlockSpec((1,) + shape_z[1:], place_z)
 
     def chunk(h, v, m):
-        return 0, ((first_high + high - 1 - h) * 2 + 1 - v) * mids + mids - 1 - m, 0
+        return 0, ((high - 1 - h) * 2 + 1 - v) * mids + mids - 1 - m, 0
 
     return pl.pallas_call(
-        functools.partial(compress_kernel, (tile, pulses, half, near_chain, axis_bit)),
+        functools.partial(compress_kernel, (tile, pulses, half, far)),
         grid=(high, 2, mids),
         in_specs=[
             pl.BlockSpec((2, half), lambda h, v, m: (0, 0)),
-            edge_spec,
             pl.BlockSpec((pulses, 2 * tile, width), chunk),
         ],
-        out_specs=[spec, spec, edge_spec],
+        out_specs=[spec_y, spec_y, spec_z, spec_z],
         out_shape=[
-            jax.ShapeDtypeStruct(s, jnp.bfloat16) for s in (shape, shape, (pulses, width))
+            jax.ShapeDtypeStruct(s, jnp.bfloat16) for s in (shape_y, shape_y, shape_z, shape_z)
         ],
         scratch_shapes=[
             pltpu.VMEM((2 * width, width), jnp.bfloat16),
@@ -130,12 +132,12 @@
         ],
         compiler_params=pltpu.CompilerParams(vmem_limit_bytes=VMEM_BYTES),
         cost_estimate=pl.CostEstimate(
-            flops=2 * pulses * blocks * width * width,
-            bytes_accessed=2 * pulses * blocks * width,
+            flops=4 * pulses * blocks * width * width,
+            bytes_accessed=4 * pulses * blocks * width,
             transcendentals=0,
         ),
         name="compress",
-    )(chirp, edge, echoes)
+    )(chirp, echoes)
 
 
 def image_kernel(dims, data_ref, steer_ref, interp_ref, base_ref, step_ref, out_keep, out_send):
@@ -242,11 +244,10 @@
 
 
 def fold(own, keep, got):
-    def half(at):
-        kept, came = (lax.dynamic_index_in_dim(a, at, 1, False) for a in (keep, got))
-        return kept + came.astype(jnp.float32)
-
-    return half(own), half(1 - own).astype(jnp.bfloat16)
+    sums = [keep[:, n] + got[:, n].astype(jnp.float32) for n in range(2)]
+    upper = own == 1
+    sent = jnp.where(upper, sums[0], sums[1]).astype(jnp.bfloat16)
+    return jnp.where(upper, sums[1], sums[0]), sent
 
 
 def last_kernel(keep_ref, got_ref, out_ref, rows_ref):
@@ -316,16 +317,14 @@
     far = (bits_of(turn) + 1) // 2 - 1
     top = bits_of(turn) - 1
     mids = 1 << far - 1
-    high = turn >> far + 2
+    high = turn >> far + 1
     tile = blocks // turn
     each = tile // 2
     rows = beams // leaf
     own_leaf, own_turn = lax.axis_index("leaf"), lax.axis_index("turn")
 
-    edge = jnp.zeros((pulses, width), jnp.bfloat16)
-    keep_y, send_y, edge = compress(chirp, edge, echoes, high, mids, True, 0, high)
+    keep_y, send_y, keep_z, send_z = compress(chirp, echoes, high, mids, far)
     got_y = swapped(send_y, "turn", 0)
-    keep_z, send_z, _ = compress(chirp, edge, echoes, high, mids, False, far, 0)
     got_z = swapped(send_z, "turn", far)
 
     own_sides = [bit(own_leaf, level) for level in range(levels)]

time: 52 us -> 54.2 us (1.042)
  starting transfers between devices: 12.1 us -> 14.2 us
  local copies, waits for them, and re-layouts: 1.49 us -> 0.89 us
    ppermute x9, starting transfers between devices: 12.1 us -> 14.2 us  [swapped(): lax.ppermute(array, axis, [(i, i ^ 1 << bit) for i in range(lax.axis_size...]
    pallas_call x2, Pallas kernels: 4.48 us -> 5.85 us  [backproject(): pl.pallas_call(functools.partial(image_kernel, (leaf, each, half, beams,...]
    another operation x2, other arithmetic: 0.2 us -> 1.24 us  [per_device(): data = jnp.stack([keep.reshape(shape), got.reshape(shape)])]
    pallas_call x2 -> x1, Pallas kernels: 6.43 us -> 5.41 us  [compress(): pl.pallas_call(functools.partial(compress_kernel, (tile, pulses, half, fa...]
    add x1 -> x0, other arithmetic: 1.02 us -> none  [half(): return kept + came.astype(jnp.float32)]
    broadcast_in_dim x1 -> x0, local copies, waits for them, and re-layouts: 0.62 us -> none  [per_device(): edge = jnp.zeros((pulses, width), jnp.bfloat16)]
  transfers between devices with their start and end apart: 9 -> 9, of which waited for: 7 -> 6; matrix products, arithmetic and copies ran while one was open for 17% -> 17% of each run, Pallas kernels for 15% -> 11%
where the time goes in v7:
time: 54.2 us; the launch traced here: 53.9 us
  waiting for transfers between devices  18.1 us (33%)
  starting transfers between devices  14.2 us (26%)
  Pallas kernels  12 us (22%)
  other arithmetic  8.24 us (15%)
  local copies, waits for them, and re-layouts  0.89 us (2%)
    ppermute x9, waiting for transfers between devices, swapped(): lax.ppermute(array, axis, [(i, i ^ 1 << bit) for i in range(lax.axis_size...  18.1 us
    ppermute x9, starting transfers between devices, swapped(): lax.ppermute(array, axis, [(i, i ^ 1 << bit) for i in range(lax.axis_size...  14.2 us
    pallas_call x2, Pallas kernels, backproject(): pl.pallas_call(functools.partial(image_kernel, (leaf, each, half, beams,...  5.85 us
    pallas_call x1, Pallas kernels, compress(): pl.pallas_call(functools.partial(compress_kernel, (tile, pulses, half, fa...  5.41 us
    convert_element_type x4, other arithmetic, fold(): sent = jnp.where(upper, sums[0], sums[1]).astype(jnp.bfloat16)  2.6 us
    cos x2, other arithmetic, unit(): return (jnp.cos(angle), jnp.sin(angle))  2.28 us
    another operation x2, other arithmetic, per_device(): data = jnp.stack([keep.reshape(shape), got.reshape(shape)])  1.24 us
  transfers between devices with their start and end apart: 9, of which 6 were waited for; matrix products, arithmetic and copies ran while one was open for 17% of the time, Pallas kernels for 11%

profile of v7, /device:TPU:0, one launch (start us, length us, event | category | flops | bytes accessed | tf_op | source)
XLA Modules:
  0.0 53.9 jit_solution(299273237908546804)
XLA Ops:
  0.0 5.4 %compress.1 = (bf16[1,2,1,8,64,256]{5,4,3,2,1,0:T(8,128)(2,1)}, bf16[1,2,1,8,64,256]{5,4,3,2,1,0:T(8,128)(2,1)}, bf16[1,1,2,8,64,256]{5,4,3,2,1,0:T(8,128)(2,1)}, bf16[1,1,2,8,64,256]{5,4,3,2,1,0:T(8,128)(2,1)}) custom-call(bf16[2,128]{1,0:T(2,128)(2,1)} %chirp_ref.1, bf16[64,64,256]{2,1,0:T(8,128)(2,1)} %echo_ref.1), custom_call_target="tpu_custom_call" | custom-call | flops 1073741824 | bytes 4194304 | tf_op jit(solution)/shard_map/compress/pallas_call | solution.py:117
  5.4 3.0 %collective-permute-start = (bf16[1,2,1,8,64,256]{5,4,3,2,1,0:T(8,128)(2,1)}, bf16[1,2,1,8,64,256]{5,4,3,2,1,0:T(8,128)(2,1)S(1)}, u32[]{:S(2)}, u32[]{:S(2)}) collective-permute-start(bf16[1,2,1,8,64,256]{5,4,3,2,1,0:T(8,128)(2,1)} %get-tuple-element.14), channel_id=1, source_target_pairs={{0,1},{1,0},{2,3},{3,2},{4,5},{5,4},{6,7},{7,6},{8,9},{9,8},{10,11... | collective-permute-start | bytes 1572872 | tf_op jit(solution)/shard_map/ppermute | solution.py:21
  8.4 1.6 %collective-permute-start.4 = (bf16[1,1,2,8,64,256]{5,4,3,2,1,0:T(8,128)(2,1)}, bf16[1,1,2,8,64,256]{5,4,3,2,1,0:T(8,128)(2,1)}, u32[]{:S(2)}, u32[]{:S(2)}) collective-permute-start(bf16[1,1,2,8,64,256]{5,4,3,2,1,0:T(8,128)(2,1)} %get-tuple-element.18), channel_id=1, source_target_pairs={{0,2},{1,3},{2,0},{3,1},{4,6},{5,7},{6,4},{7,5},{8,10},{9,11},{10,... | collective-permute-start | bytes 1572872 | tf_op jit(solution)/shard_map/ppermute | solution.py:21
  10.1 0.2 select_reduce_fusion.1
  11.1 0.1 copy.31
  11.3 0.4 select_reduce_fusion
  11.9 0.5 multiply_convert_fusion.1
  12.4 0.2 fusion.15
  12.7 2.1 %fusion.9 = (f32[2,1,128,512]{3,2,1,0:T(8,128)S(1)}, f32[2,1,128,512]{3,2,1,0:T(8,128)S(1)}) fusion(s32[512]{0:T(512)S(1)} %iota_add_fusion, s32[2,128]{1,0:T(2,128)S(1)} %add_multiply_fusion), kind=kLoop, calls=%fused_computation.37 | loop fusion | flops 1835008 | bytes 1051648 | tf_op jit(solution)/shard_map/cos | solution.py:26
  14.8 0.2 fusion.30
  15.2 0.1 copy.40.steer_ref
  15.3 5.2 %collective-permute-done = bf16[1,2,1,8,64,256]{5,4,3,2,1,0:T(8,128)(2,1)S(1)} collective-permute-done((bf16[1,2,1,8,64,256]{5,4,3,2,1,0:T(8,128)(2,1)}, bf16[1,2,1,8,64,256]{5,4,3,2,1,0:T(8,128)(2,1)S(1)}, u32[]{:S(2)}, u32[]{:S(2)}) %collective-permute-start) | collective-permute-done | bytes 524320 | tf_op jit(solution)/shard_map/ppermute | solution.py:21
  20.5 0.1 pad_maximum_fusion.data_ref
  20.6 2.9 %image.2 = (f32[2,4,4,32,256]{4,3,2,1,0:T(8,128)S(1)}, bf16[2,4,4,32,256]{4,3,2,1,0:T(8,128)(2,1)}) custom-call(bf16[2,4,4,64,256]{4,3,2,1,0:T(8,128)(2,1)S(1)} %pad_maximum_fusion.data_ref, bf16[256,256]{1,0:T(8,128)(2,1)S(1)} %copy.40.steer_ref, bf16[1,128,256]{2,1,0:T(8,128)(2,1)S(1)} %pad_maximum_fusion.4.interp_ref, f32[4,4,128]{2,1,0:T(4,128)S(1)} %bitcast.100, ...), custom_call_target="tpu_custom_call" | custom-call | flops 402653184 | bytes 2621440 | tf_op jit(solution)/shard_map/image/pallas_call | solution.py:221
  23.6 0.1 copy.41.steer_ref
  23.7 1.1 %pad_maximum_fusion.2.data_ref = bf16[2,4,4,64,256]{4,3,2,1,0:T(8,128)(2,1)S(1)} fusion(bf16[1,4,4,64,256]{4,3,2,1,0:T(8,128)(2,1)} %bitcast.23, bf16[1,4,4,64,256]{4,3,2,1,0:T(8,128)(2,1)S(1)} %bitcast.109), kind=kLoop, calls=%fused_computation.2 | loop fusion | flops 524288 | bytes 2097152 | tf_op jit(solution)/shard_map/stack | solution.py:379
  24.8 2.9 %image.3 = (f32[2,4,4,32,256]{4,3,2,1,0:T(8,128)S(1)}, bf16[2,4,4,32,256]{4,3,2,1,0:T(8,128)(2,1)}) custom-call(bf16[2,4,4,64,256]{4,3,2,1,0:T(8,128)(2,1)S(1)} %pad_maximum_fusion.2.data_ref, bf16[256,256]{1,0:T(8,128)(2,1)S(1)} %copy.41.steer_ref, bf16[1,128,256]{2,1,0:T(8,128)(2,1)S(1)} %pad_maximum_fusion.4.interp_ref, f32[4,4,128]{2,1,0:T(4,128)S(1)} %bitcast.99, ...), custom_call_target="tpu_custom_call" | custom-call | flops 402653184 | bytes 2621440 | tf_op jit(solution)/shard_map/image/pallas_call | solution.py:221
  27.8 0.5 collective-permute-start.5
  28.3 1.2 %fusion.6 = (bf16[1,16,32,256]{3,2,1,0:T(8,128)(2,1)S(1)}, f32[1,1,16,32,256]{4,3,2,1,0:T(8,128)S(1)}) fusion(f32[1,2,16,32,256]{4,3,2,1,0:T(8,128)S(1)} %bitcast.97, pred[]{:T(512)S(6)} %eq.52, bf16[1,2,16,32,256]{4,3,2,1,0:T(8,128)(2,1)} %bitcast.15), kind=kLoop, calls=%fused_computation.23 | loop fusion | flops 917504 | bytes 2359297 | tf_op jit(solution)/shard_map/convert_element_type | solution.py:249
  29.5 1.8 %collective-permute-start.2 = (bf16[1,16,32,256]{3,2,1,0:T(8,128)(2,1)S(1)}, bf16[1,16,32,256]{3,2,1,0:T(8,128)(2,1)S(1)}, u32[]{:S(2)}, u32[]{:S(2)}) collective-permute-start(bf16[1,16,32,256]{3,2,1,0:T(8,128)(2,1)S(1)} %get-tuple-element.26), channel_id=1, source_target_pairs={{0,16},{8,24},{16,0},{24,8},{1,17},{9,25},{17,1},{25,9},{2,18},{10... | collective-permute-start | bytes 786440 | tf_op jit(solution)/shard_map/ppermute | solution.py:21
  31.3 1.2 %fusion.7 = (bf16[2,8,32,256]{3,2,1,0:T(8,128)(2,1)S(1)}, f32[1,2,8,32,256]{4,3,2,1,0:T(8,128)S(1)}) fusion(f32[2,2,8,32,256]{4,3,2,1,0:T(8,128)S(1)} %bitcast.98, pred[]{:T(512)S(6)} %eq.59, bf16[2,2,8,32,256]{4,3,2,1,0:T(8,128)(2,1)} %bitcast.27), kind=kLoop, calls=%fused_computation.24 | loop fusion | flops 917504 | bytes 2359297 | tf_op jit(solution)/shard_map/convert_element_type | solution.py:249
  32.5 1.6 %collective-permute-start.6 = (bf16[2,8,32,256]{3,2,1,0:T(8,128)(2,1)S(1)}, bf16[2,8,32,256]{3,2,1,0:T(8,128)(2,1)S(1)}, u32[]{:S(2)}, u32[]{:S(2)}) collective-permute-start(bf16[2,8,32,256]{3,2,1,0:T(8,128)(2,1)S(1)} %get-tuple-element.28), channel_id=1, source_target_pairs={{0,1},{1,0},{2,3},{3,2},{4,5},{5,4},{6,7},{7,6},{8,9},{9,8},{10,11... | collective-permute-start | bytes 786440 | tf_op jit(solution)/shard_map/ppermute | solution.py:21
  34.1 3.7 %collective-permute-done.2 = bf16[1,16,32,256]{3,2,1,0:T(8,128)(2,1)S(1)} collective-permute-done((bf16[1,16,32,256]{3,2,1,0:T(8,128)(2,1)S(1)}, bf16[1,16,32,256]{3,2,1,0:T(8,128)(2,1)S(1)}, u32[]{:S(2)}, u32[]{:S(2)}) %collective-permute-start.2) | collective-permute-done | bytes 262176 | tf_op jit(solution)/shard_map/ppermute | solution.py:21
  37.9 1.9 %collective-permute-start.3 = (bf16[1,8,32,256]{3,2,1,0:T(8,128)(2,1)S(1)}, bf16[1,8,32,256]{3,2,1,0:T(8,128)(2,1)S(1)}, u32[]{:S(2)}, u32[]{:S(2)}) collective-permute-start(bf16[1,8,32,256]{3,2,1,0:T(8,128)(2,1)S(1)} %fusion.10), channel_id=1, source_target_pairs={{0,2},{1,3},{2,0},{3,1},{4,6},{5,7},{6,4},{7,5},{8,10},{9,11},{10,... | collective-permute-start | bytes 393224 | tf_op jit(solution)/shard_map/ppermute | solution.py:21
  39.7 0.8 %collective-permute-done.6 = bf16[2,8,32,256]{3,2,1,0:T(8,128)(2,1)S(1)} collective-permute-done((bf16[2,8,32,256]{3,2,1,0:T(8,128)(2,1)S(1)}, bf16[2,8,32,256]{3,2,1,0:T(8,128)(2,1)S(1)}, u32[]{:S(2)}, u32[]{:S(2)}) %collective-permute-start.6) | collective-permute-done | bytes 262176 | tf_op jit(solution)/shard_map/ppermute | solution.py:21
  40.6 1.3 %collective-permute-start.7 = (bf16[1,8,32,256]{3,2,1,0:T(8,128)(2,1)S(1)}, bf16[1,8,32,256]{3,2,1,0:T(8,128)(2,1)S(1)}, u32[]{:S(2)}, u32[]{:S(2)}) collective-permute-start(bf16[1,8,32,256]{3,2,1,0:T(8,128)(2,1)S(1)} %fusion.11), channel_id=1, source_target_pairs={{0,16},{8,24},{16,0},{24,8},{1,17},{9,25},{17,1},{25,9},{2,18},{10... | collective-permute-start | bytes 393224 | tf_op jit(solution)/shard_map/ppermute | solution.py:21
  41.9 1.0 %collective-permute-done.3 = bf16[1,8,32,256]{3,2,1,0:T(8,128)(2,1)S(1)} collective-permute-done((bf16[1,8,32,256]{3,2,1,0:T(8,128)(2,1)S(1)}, bf16[1,8,32,256]{3,2,1,0:T(8,128)(2,1)S(1)}, u32[]{:S(2)}, u32[]{:S(2)}) %collective-permute-start.3) | collective-permute-done | bytes 131104 | tf_op jit(solution)/shard_map/ppermute | solution.py:21
  42.9 2.7 %collective-permute-done.7 = bf16[1,8,32,256]{3,2,1,0:T(8,128)(2,1)S(1)} collective-permute-done((bf16[1,8,32,256]{3,2,1,0:T(8,128)(2,1)S(1)}, bf16[1,8,32,256]{3,2,1,0:T(8,128)(2,1)S(1)}, u32[]{:S(2)}, u32[]{:S(2)}) %collective-permute-start.7) | collective-permute-done | bytes 131104 | tf_op jit(solution)/shard_map/ppermute | solution.py:21
  45.6 0.2 select_convert_fusion.2
  45.9 2.6 %collective-permute-start.8 = (bf16[8,32,256]{2,1,0:T(8,128)(2,1)S(1)}, bf16[8,32,256]{2,1,0:T(8,128)(2,1)S(1)}, u32[]{:S(2)}, u32[]{:S(2)}) collective-permute-start(bf16[8,32,256]{2,1,0:T(8,128)(2,1)S(1)} %get-tuple-element.23), channel_id=1, source_target_pairs={{0,4},{1,5},{2,6},{3,7},{4,0},{5,1},{6,2},{7,3},{8,12},{9,13},{10,... | collective-permute-start | bytes 393224 | tf_op jit(solution)/shard_map/ppermute | solution.py:21
  48.5 4.7 %collective-permute-done.8.got_ref = bf16[8,32,256]{2,1,0:T(8,128)(2,1)S(1)} collective-permute-done((bf16[8,32,256]{2,1,0:T(8,128)(2,1)S(1)}, bf16[8,32,256]{2,1,0:T(8,128)(2,1)S(1)}, u32[]{:S(2)}, u32[]{:S(2)}) %collective-permute-start.8) | collective-permute-done | bytes 131104 | tf_op jit(solution)/shard_map/ppermute | solution.py:21
  53.2 0.7 %last_sum.1 = bf16[32,8,256]{2,1,0:T(8,128)(2,1)} custom-call(f32[8,32,256]{2,1,0:T(8,128)S(1)} %broadcast_select_fusion.keep_ref, bf16[8,32,256]{2,1,0:T(8,128)(2,1)S(1)} %collective-permute-done.8.got_ref), custom_call_target="tpu_custom_call" | custom-call | tf_op jit(solution)/shard_map/last_sum/pallas_call | solution.py:266
  (59 shorter events, 1.6 us)
Async XLA Ops:
  0.0 11.3 %copy-start.3 = (f32[8]{0:T(128)S(1)}, f32[8]{0:T(128)}, u32[]{:S(2)}) copy-start(f32[8]{0:T(128)} %constant.173.clone) | copy-start | bytes 100
  0.0 10.1 %copy-start.4 = (s32[1,8]{1,0:T(1,128)S(1)}, s32[1,8]{1,0:T(1,128)}, u32[]{:S(2)}) copy-start(s32[1,8]{1,0:T(1,128)} %param.9) | copy-start | bytes 100
  0.0 10.7 %copy-start.2 = (s32[2,2,128,8]{2,3,1,0:T(8,128)S(1)}, s32[2,2,128,8]{2,3,1,0:T(8,128)}, u32[]{:S(2)}) copy-start(s32[2,2,128,8]{2,3,1,0:T(8,128)} %param.8) | copy-start | bytes 49156
  5.4 15.1 %collective-permute-start = (bf16[1,2,1,8,64,256]{5,4,3,2,1,0:T(8,128)(2,1)}, bf16[1,2,1,8,64,256]{5,4,3,2,1,0:T(8,128)(2,1)S(1)}, u32[]{:S(2)}, u32[]{:S(2)}) collective-permute-start(bf16[1,2,1,8,64,256]{5,4,3,2,1,0:T(8,128)(2,1)} %get-tuple-element.14), channel_id=1, source_target_pairs={{0,1},{1,0},{2,3},{3,2},{4,5},{5,4},{6,7},{7,6},{8,9},{9,8},{10,11... | collective-permute-start | bytes 1572872 | tf_op jit(solution)/shard_map/ppermute | solution.py:21
  8.4 15.3 %collective-permute-start.4 = (bf16[1,1,2,8,64,256]{5,4,3,2,1,0:T(8,128)(2,1)}, bf16[1,1,2,8,64,256]{5,4,3,2,1,0:T(8,128)(2,1)}, u32[]{:S(2)}, u32[]{:S(2)}) collective-permute-start(bf16[1,1,2,8,64,256]{5,4,3,2,1,0:T(8,128)(2,1)} %get-tuple-element.18), channel_id=1, source_target_pairs={{0,2},{1,3},{2,0},{3,1},{4,6},{5,7},{6,4},{7,5},{8,10},{9,11},{10,... | collective-permute-start | bytes 1572872 | tf_op jit(solution)/shard_map/ppermute | solution.py:21
  14.8 5.7 %copy-start.1 = (bf16[1,2,1,8,64,256]{5,4,3,2,1,0:T(8,128)(2,1)S(1)}, bf16[1,2,1,8,64,256]{5,4,3,2,1,0:T(8,128)(2,1)}, u32[]{:S(2)}) copy-start(bf16[1,2,1,8,64,256]{5,4,3,2,1,0:T(8,128)(2,1)} %get-tuple-element.13) | copy-start | bytes 1572868
  20.5 3.2 %copy-start = (bf16[1,1,2,8,64,256]{5,4,3,2,1,0:T(8,128)(2,1)S(1)}, bf16[1,1,2,8,64,256]{5,4,3,2,1,0:T(8,128)(2,1)}, u32[]{:S(2)}) copy-start(bf16[1,1,2,8,64,256]{5,4,3,2,1,0:T(8,128)(2,1)} %get-tuple-element.17) | copy-start | bytes 1572868
  23.6 4.7 %collective-permute-start.1 = (bf16[2,4,4,32,256]{4,3,2,1,0:T(8,128)(2,1)}, bf16[2,4,4,32,256]{4,3,2,1,0:T(8,128)(2,1)}, u32[]{:S(2)}, u32[]{:S(2)}) collective-permute-start(bf16[2,4,4,32,256]{4,3,2,1,0:T(8,128)(2,1)} %get-tuple-element.16), channel_id=1, source_target_pairs={{0,8},{8,0},{16,24},{24,16},{1,9},{9,1},{17,25},{25,17},{2,10},{10... | collective-permute-start | bytes 1572872 | tf_op jit(solution)/shard_map/ppermute | solution.py:21
  27.8 3.5 %collective-permute-start.5 = (bf16[2,4,4,32,256]{4,3,2,1,0:T(8,128)(2,1)}, bf16[2,4,4,32,256]{4,3,2,1,0:T(8,128)(2,1)}, u32[]{:S(2)}, u32[]{:S(2)}) collective-permute-start(bf16[2,4,4,32,256]{4,3,2,1,0:T(8,128)(2,1)} %get-tuple-element.20), channel_id=1, source_target_pairs={{0,8},{8,0},{16,24},{24,16},{1,9},{9,1},{17,25},{25,17},{2,10},{10... | collective-permute-start | bytes 1572872 | tf_op jit(solution)/shard_map/ppermute | solution.py:21
  29.5 8.3 %collective-permute-start.2 = (bf16[1,16,32,256]{3,2,1,0:T(8,128)(2,1)S(1)}, bf16[1,16,32,256]{3,2,1,0:T(8,128)(2,1)S(1)}, u32[]{:S(2)}, u32[]{:S(2)}) collective-permute-start(bf16[1,16,32,256]{3,2,1,0:T(8,128)(2,1)S(1)} %get-tuple-element.26), channel_id=1, source_target_pairs={{0,16},{8,24},{16,0},{24,8},{1,17},{9,25},{17,1},{25,9},{2,18},{10... | collective-permute-start | bytes 786440 | tf_op jit(solution)/shard_map/ppermute | solution.py:21
  32.5 8.0 %collective-permute-start.6 = (bf16[2,8,32,256]{3,2,1,0:T(8,128)(2,1)S(1)}, bf16[2,8,32,256]{3,2,1,0:T(8,128)(2,1)S(1)}, u32[]{:S(2)}, u32[]{:S(2)}) collective-permute-start(bf16[2,8,32,256]{3,2,1,0:T(8,128)(2,1)S(1)} %get-tuple-element.28), channel_id=1, source_target_pairs={{0,1},{1,0},{2,3},{3,2},{4,5},{5,4},{6,7},{7,6},{8,9},{9,8},{10,11... | collective-permute-start | bytes 786440 | tf_op jit(solution)/shard_map/ppermute | solution.py:21
  37.9 5.0 %collective-permute-start.3 = (bf16[1,8,32,256]{3,2,1,0:T(8,128)(2,1)S(1)}, bf16[1,8,32,256]{3,2,1,0:T(8,128)(2,1)S(1)}, u32[]{:S(2)}, u32[]{:S(2)}) collective-permute-start(bf16[1,8,32,256]{3,2,1,0:T(8,128)(2,1)S(1)} %fusion.10), channel_id=1, source_target_pairs={{0,2},{1,3},{2,0},{3,1},{4,6},{5,7},{6,4},{7,5},{8,10},{9,11},{10,... | collective-permute-start | bytes 393224 | tf_op jit(solution)/shard_map/ppermute | solution.py:21
  40.6 5.0 %collective-permute-start.7 = (bf16[1,8,32,256]{3,2,1,0:T(8,128)(2,1)S(1)}, bf16[1,8,32,256]{3,2,1,0:T(8,128)(2,1)S(1)}, u32[]{:S(2)}, u32[]{:S(2)}) collective-permute-start(bf16[1,8,32,256]{3,2,1,0:T(8,128)(2,1)S(1)} %fusion.11), channel_id=1, source_target_pairs={{0,16},{8,24},{16,0},{24,8},{1,17},{9,25},{17,1},{25,9},{2,18},{10... | collective-permute-start | bytes 393224 | tf_op jit(solution)/shard_map/ppermute | solution.py:21
  45.9 7.3 %collective-permute-start.8 = (bf16[8,32,256]{2,1,0:T(8,128)(2,1)S(1)}, bf16[8,32,256]{2,1,0:T(8,128)(2,1)S(1)}, u32[]{:S(2)}, u32[]{:S(2)}) collective-permute-start(bf16[8,32,256]{2,1,0:T(8,128)(2,1)S(1)} %get-tuple-element.23), channel_id=1, source_target_pairs={{0,4},{1,5},{2,6},{3,7},{4,0},{5,1},{6,2},{7,3},{8,12},{9,13},{10,... | collective-permute-start | bytes 393224 | tf_op jit(solution)/shard_map/ppermute | solution.py:21

commit v8 on v5

--- a/solution.py
+++ b/solution.py
@@ -17,6 +17,10 @@
     return count.bit_length() - 1
 
 
+def bit(value, at):
+    return value >> at & 1
+
+
 def swapped(array, axis, bit):
     return lax.ppermute(array, axis, [(i, i ^ 1 << bit) for i in range(lax.axis_size(axis))])
 
@@ -26,19 +30,19 @@
     return jnp.cos(angle), jnp.sin(angle)
 
 
-def own_bit(axis, at):
-    return lax.axis_index(axis) >> at & 1
-
-
-def compress_kernel(
-    dims, chirp_ref, edge_ref, echo_ref, keep_ref, send_ref, edge_out, weights, rows_ref, carry
-):
-    tile, pulses, half, near_chain, axis_bit = dims
+def compress_kernel(dims, has_edge, chirp_ref, echo_ref, *refs):
+    tile, pulses, half, near_chain, far = dims
+    edge_ref, refs = (refs[0], refs[1:]) if has_edge else (None, refs)
+    keep_ref, send_ref, edge_out, weights, rows_ref, carry = refs
     blocks = 2 * tile
     pitch = blocks + 1
-    mid = pl.num_programs(2) - 1 - pl.program_id(2)
-    near = 1 - pl.program_id(1)
-    own = own_bit("turn", axis_bit)
+    mids = pl.num_programs(2)
+    high = pl.num_programs(0)
+    turn = lax.axis_index("turn")
+    spot_h = (high - 1 - pl.program_id(0)) ^ (turn >> far + 1 & high - 1)
+    spot_m = (mids - 1 - pl.program_id(2)) ^ (turn >> 1 & mids - 1)
+    spot_v = (1 - pl.program_id(1)) ^ bit(turn, far)
+    own_u = bit(turn, 0)
 
     @pl.when((pl.program_id(0) == 0) & (pl.program_id(1) == 0) & (pl.program_id(2) == 0))
     def _():
@@ -55,7 +59,7 @@
             low = jnp.concatenate([-im, re], axis=1)
             full = jnp.concatenate([top, low], axis=0)
             weights[m * 2 * half : (m + 1) * 2 * half, :] = full.astype(jnp.bfloat16)
-        carry[...] = edge_ref[...]
+        carry[...] = edge_ref[...] if has_edge else jnp.zeros_like(carry)
 
     for p in range(pulses):
         for c in range(2):
@@ -77,48 +81,53 @@
     carry[...] = turned[0]
     edge_out[...] = turned[0]
 
+    def block(b):
+        return total[b * pulses : (b + 1) * pulses]
+
     if near_chain:
         for side in range(2):
 
-            @pl.when(own == side)
+            @pl.when(own_u == side)
             def _(side=side):
                 for b in range(blocks):
                     ref = keep_ref if b // tile == side else send_ref
-                    ref[0, 0, 0, b % tile] = total[b * pulses : (b + 1) * pulses]
+                    ref[spot_h, spot_v, spot_m, b % tile] = block(b)
     else:
-        for ref, mine in ((keep_ref, True), (send_ref, False)):
-
-            @pl.when((near == own) == mine)
+        for ref, mine in ((keep_ref, 0), (send_ref, 1)):
+
+            @pl.when(spot_v == mine)
             def _(ref=ref):
                 for b in range(blocks):
-                    ref[0, mid, b // tile, b % tile] = total[b * pulses : (b + 1) * pulses]
-
-
-def compress(chirp, edge, echoes, high, mids, near_chain, axis_bit, first_high):
+                    ref[spot_h, spot_m, b // tile ^ own_u, b % tile] = block(b)
+
+
+def compress(chirp, edge, echoes, high, mids, near_chain, far, first_high):
     pulses, blocks, width = echoes.shape
     half = width // 2
     tile = blocks // lax.axis_size("turn")
     if near_chain:
         shape = (high, 2, mids, tile, pulses, width)
-        spec = pl.BlockSpec(
-            (1, 1, 1) + shape[3:], lambda h, v, m: (high - 1 - h, 1 - v, mids - 1 - m, 0, 0, 0)
-        )
     else:
         shape = (high, mids, 2, tile, pulses, width)
-        spec = pl.BlockSpec((1,) + shape[1:], lambda h, v, m: (high - 1 - h, 0, 0, 0, 0, 0))
+    spec = pl.BlockSpec(shape, lambda h, v, m: (0, 0, 0, 0, 0, 0))
     edge_spec = pl.BlockSpec((pulses, width), lambda h, v, m: (0, 0))
 
     def chunk(h, v, m):
         return 0, ((first_high + high - 1 - h) * 2 + 1 - v) * mids + mids - 1 - m, 0
 
+    in_specs = [
+        pl.BlockSpec((2, half), lambda h, v, m: (0, 0)),
+        pl.BlockSpec((pulses, 2 * tile, width), chunk),
+    ]
+    operands = [chirp, echoes]
+    if edge is not None:
+        in_specs.append(edge_spec)
+        operands.append(edge)
+    dims = (tile, pulses, half, near_chain, far)
     return pl.pallas_call(
-        functools.partial(compress_kernel, (tile, pulses, half, near_chain, axis_bit)),
+        functools.partial(compress_kernel, dims, edge is not None),
         grid=(high, 2, mids),
-        in_specs=[
-            pl.BlockSpec((2, half), lambda h, v, m: (0, 0)),
-            edge_spec,
-            pl.BlockSpec((pulses, 2 * tile, width), chunk),
-        ],
+        in_specs=in_specs,
         out_specs=[spec, spec, edge_spec],
         out_shape=[
             jax.ShapeDtypeStruct(s, jnp.bfloat16) for s in (shape, shape, (pulses, width))
@@ -135,7 +144,7 @@
             transcendentals=0,
         ),
         name="compress",
-    )(chirp, edge, echoes)
+    )(*operands)
 
 
 def image_kernel(dims, data_ref, steer_ref, interp_ref, base_ref, step_ref, out_keep, out_send):
@@ -231,7 +240,7 @@
             jax.ShapeDtypeStruct(shape, jnp.float32),
             jax.ShapeDtypeStruct(shape, jnp.bfloat16),
         ],
-        compiler_params=pltpu.CompilerParams(vmem_limit_bytes=16 * 2**20),
+        compiler_params=pltpu.CompilerParams(vmem_limit_bytes=10 * 2**20),
         cost_estimate=pl.CostEstimate(
             flops=12 * beams * pulses * count * each * width,
             bytes_accessed=2 * data.size + 6 * count * each * beams * width // 2,
@@ -241,12 +250,9 @@
     )(data, steer, interp, base, step)
 
 
-def fold(own, keep, got):
-    def half(at):
-        kept, came = (lax.dynamic_index_in_dim(a, at, 1, False) for a in (keep, got))
-        return kept + came.astype(jnp.float32)
-
-    return half(own), half(1 - own).astype(jnp.bfloat16)
+def fold(keep, got):
+    stay, gone = (keep[:, n] + got[:, n].astype(jnp.float32) for n in range(2))
+    return stay, gone.astype(jnp.bfloat16)
 
 
 def last_kernel(keep_ref, got_ref, out_ref, rows_ref):
@@ -303,10 +309,6 @@
     return jnp.concatenate([top, low], axis=0).astype(jnp.bfloat16)
 
 
-def bit(value, at):
-    return value >> at & 1
-
-
 def per_device(echoes, chirp, taps, slots):
     leaf, turn = lax.axis_size("leaf"), lax.axis_size("turn")
     pulses, blocks, width = echoes.shape
@@ -322,8 +324,7 @@
     rows = beams // leaf
     own_leaf, own_turn = lax.axis_index("leaf"), lax.axis_index("turn")
 
-    edge = jnp.zeros((pulses, width), jnp.bfloat16)
-    keep_y, send_y, edge = compress(chirp, edge, echoes, high, mids, True, 0, high)
+    keep_y, send_y, edge = compress(chirp, None, echoes, high, mids, True, far, high)
     got_y = swapped(send_y, "turn", 0)
     keep_z, send_z, _ = compress(chirp, edge, echoes, high, mids, False, far, 0)
     got_z = swapped(send_z, "turn", far)
@@ -331,17 +332,20 @@
     own_sides = [bit(own_leaf, level) for level in range(levels)]
     row = jnp.arange(beams, dtype=jnp.int32)
     part, place = row // rows, row % rows
-    group = 2 * (part % (leaf // 2)) + (part // (leaf // 2) ^ own_sides[0])
+    group = own_leaf ^ (2 * (part % (leaf // 2)) + part // (leaf // 2))
     orders = [row] * (levels - 1) + [group * rows + place]
     own_taps = [
         lax.dynamic_index_in_dim(taps[n], own_sides[n], 0, False) for n in range(levels)
     ]
-    cores = own_taps[-1].reshape(leaf // 2, 2, rows, -1)
-    cores = [
-        lax.dynamic_index_in_dim(cores, own_sides[0] ^ n, 1, False).reshape(beams // 2, -1)
-        for n in range(2)
-    ]
-    own_taps[-1] = jnp.concatenate(cores, axis=0)
+    groups = own_taps[-1].reshape(leaf, rows, -1)
+    own_taps[-1] = jnp.concatenate(
+        [
+            lax.dynamic_index_in_dim(groups, own_leaf ^ (2 * g + side), 0, False)
+            for side in range(2)
+            for g in range(leaf // 2)
+        ],
+        axis=0,
+    )
     matrices = interpolation(jnp.stack(own_taps), beams)
     interp = jnp.concatenate([matrices[1:]] * 2, axis=-1).astype(jnp.bfloat16)
     scale = 1.0 / math.sqrt(2.0 * slots.shape[1] * pulses)
@@ -367,9 +371,10 @@
         return both.reshape(parts.shape[0], 2 * levels, beams)
 
     index = jnp.arange(turn // 4, dtype=jnp.int32)
-    tiles_y = turn // 2 + 2 * index + bit(own_turn, 0)
-    low_part = index & (1 << far) - 1
-    tiles_z = ((index >> far) * 2 + bit(own_turn, far)) * (1 << far) + low_part
+    tiles_y = turn // 2 + 2 * (index ^ (own_turn >> 1 & turn // 4 - 1)) + bit(own_turn, 0)
+    low_part = (index ^ own_turn) & (1 << far) - 1
+    high_part = index >> far ^ (own_turn >> far + 1 & high - 1)
+    tiles_z = (high_part * 2 + bit(own_turn, far)) * (1 << far) + low_part
 
     final = []
     for name, keep, got, steer_own, tiles in (
@@ -391,8 +396,7 @@
             before, after = 1 << at, (1 << len(leading) - at - 1) * tile
             leading.pop(at)
             split = (before, 2, after, rows, width)
-            own = bit(own_leaf if axis == "leaf" else own_turn, b)
-            kept, sent = fold(own, kept.reshape(split), arrived.reshape(split))
+            kept, sent = fold(kept.reshape(split), arrived.reshape(split))
             arrived = swapped(sent, axis, b)
         shape = (tile, rows, width)
         final.append(kept.reshape(shape) + arrived.reshape(shape).astype(jnp.float32))

time: 52 us -> 52.3 us (level)
  waiting for transfers between devices: 18.2 us -> 19.5 us
  other arithmetic: 7.77 us -> 6.94 us
  local copies, waits for them, and re-layouts: 1.49 us -> 0.67 us
  starting transfers between devices: 12.1 us -> 12.7 us
    ppermute x9, waiting for transfers between devices: 18.2 us -> 19.5 us  [swapped(): lax.ppermute(array, axis, [(i, i ^ 1 << bit) for i in range(lax.axis_size...]
    another operation x2, other arithmetic: 0.2 us -> 1.24 us  [per_device(): data = jnp.stack([keep.reshape(shape), got.reshape(shape)])]
    add x1 -> x0, other arithmetic: 1.02 us -> none  [half(): return kept + came.astype(jnp.float32)]
    convert_element_type x4, other arithmetic: 2.28 us -> 1.43 us  [fold(): return (stay, gone.astype(jnp.bfloat16))]
    broadcast_in_dim x1 -> x0, local copies, waits for them, and re-layouts: 0.62 us -> none  [per_device(): edge = jnp.zeros((pulses, width), jnp.bfloat16)]
    ppermute x9, starting transfers between devices: 12.1 us -> 12.7 us  [swapped(): lax.ppermute(array, axis, [(i, i ^ 1 << bit) for i in range(lax.axis_size...]
  transfers between devices with their start and end apart: 9 -> 9, of which waited for: 7 -> 6; matrix products, arithmetic and copies ran while one was open for 17% -> 15% of each run, Pallas kernels for 15% -> 15%
where the time goes in v8:
time: 52.3 us; the launch traced here: 52.1 us
  waiting for transfers between devices  19.5 us (37%)
  starting transfers between devices  12.7 us (24%)
  Pallas kernels  11.8 us (23%)
  other arithmetic  6.94 us (13%)
  local copies, waits for them, and re-layouts  0.67 us (1%)
    ppermute x9, waiting for transfers between devices, swapped(): lax.ppermute(array, axis, [(i, i ^ 1 << bit) for i in range(lax.axis_size...  19.5 us
    ppermute x9, starting transfers between devices, swapped(): lax.ppermute(array, axis, [(i, i ^ 1 << bit) for i in range(lax.axis_size...  12.7 us
    pallas_call x2, Pallas kernels, compress(): pl.pallas_call(functools.partial(compress_kernel, dims, edge is not None)...  6.62 us
    pallas_call x2, Pallas kernels, backproject(): pl.pallas_call(functools.partial(image_kernel, (leaf, each, half, beams,...  4.46 us
    cos x2, other arithmetic, unit(): return (jnp.cos(angle), jnp.sin(angle))  2.28 us
    convert_element_type x4, other arithmetic, fold(): return (stay, gone.astype(jnp.bfloat16))  1.43 us
    another operation x2, other arithmetic, per_device(): data = jnp.stack([keep.reshape(shape), got.reshape(shape)])  1.24 us
  transfers between devices with their start and end apart: 9, of which 6 were waited for; matrix products, arithmetic and copies ran while one was open for 15% of the time, Pallas kernels for 15%

profile of v8, /device:TPU:0, one launch (start us, length us, event | category | flops | bytes accessed | tf_op | source)
XLA Modules:
  0.0 52.1 jit_solution(9197559271572218871)
XLA Ops:
  0.0 3.3 %compress.2 = (bf16[1,2,1,8,64,256]{5,4,3,2,1,0:T(8,128)(2,1)}, bf16[1,2,1,8,64,256]{5,4,3,2,1,0:T(8,128)(2,1)}, bf16[64,256]{1,0:T(8,128)(2,1)}) custom-call(bf16[2,128]{1,0:T(2,128)(2,1)} %chirp_ref.3, bf16[64,64,256]{2,1,0:T(8,128)(2,1)} %echo_ref.3), custom_call_target="tpu_custom_call" | custom-call | flops 536870912 | bytes 2097152 | tf_op jit(solution)/shard_map/compress/pallas_call | solution.py:127
  3.3 3.0 %collective-permute-start = (bf16[1,2,1,8,64,256]{5,4,3,2,1,0:T(8,128)(2,1)}, bf16[1,2,1,8,64,256]{5,4,3,2,1,0:T(8,128)(2,1)S(1)}, u32[]{:S(2)}, u32[]{:S(2)}) collective-permute-start(bf16[1,2,1,8,64,256]{5,4,3,2,1,0:T(8,128)(2,1)} %get-tuple-element.15), channel_id=1, source_target_pairs={{0,1},{1,0},{2,3},{3,2},{4,5},{5,4},{6,7},{7,6},{8,9},{9,8},{10,11... | collective-permute-start | bytes 1572872 | tf_op jit(solution)/shard_map/ppermute | solution.py:25
  6.3 3.3 %compress.3 = (bf16[1,1,2,8,64,256]{5,4,3,2,1,0:T(8,128)(2,1)}, bf16[1,1,2,8,64,256]{5,4,3,2,1,0:T(8,128)(2,1)}, bf16[64,256]{1,0:T(8,128)(2,1)}) custom-call(bf16[2,128]{1,0:T(2,128)(2,1)} %chirp_ref.3, bf16[64,64,256]{2,1,0:T(8,128)(2,1)} %echo_ref.3, bf16[64,256]{1,0:T(8,128)(2,1)} %get-tuple-element.18.refs_0_), custom_call_target="tpu_custom_call" | custom-call | flops 536870912 | bytes 2097152 | tf_op jit(solution)/shard_map/compress/pallas_call | solution.py:127
  9.6 1.6 %collective-permute-start.4 = (bf16[1,1,2,8,64,256]{5,4,3,2,1,0:T(8,128)(2,1)}, bf16[1,1,2,8,64,256]{5,4,3,2,1,0:T(8,128)(2,1)}, u32[]{:S(2)}, u32[]{:S(2)}) collective-permute-start(bf16[1,1,2,8,64,256]{5,4,3,2,1,0:T(8,128)(2,1)} %get-tuple-element.20), channel_id=1, source_target_pairs={{0,2},{1,3},{2,0},{3,1},{4,6},{5,7},{6,4},{7,5},{8,10},{9,11},{10,... | collective-permute-start | bytes 1572872 | tf_op jit(solution)/shard_map/ppermute | solution.py:25
  11.3 0.2 select_reduce_fusion.1
  12.1 0.1 copy.31
  12.2 0.4 select_reduce_fusion
  12.9 0.5 multiply_convert_fusion.1
  13.4 0.2 fusion.23
  13.6 2.1 %fusion.17 = (f32[2,1,128,512]{3,2,1,0:T(8,128)S(1)}, f32[2,1,128,512]{3,2,1,0:T(8,128)S(1)}) fusion(s32[512]{0:T(512)S(1)} %iota_add_fusion, s32[2,128]{1,0:T(2,128)S(1)} %add_multiply_fusion), kind=kLoop, calls=%fused_computation.38 | loop fusion | flops 1835008 | bytes 1051648 | tf_op jit(solution)/shard_map/cos | solution.py:30
  15.7 0.2 fusion.36
  16.1 0.1 copy.40.steer_ref
  16.3 2.2 %collective-permute-done = bf16[1,2,1,8,64,256]{5,4,3,2,1,0:T(8,128)(2,1)S(1)} collective-permute-done((bf16[1,2,1,8,64,256]{5,4,3,2,1,0:T(8,128)(2,1)}, bf16[1,2,1,8,64,256]{5,4,3,2,1,0:T(8,128)(2,1)S(1)}, u32[]{:S(2)}, u32[]{:S(2)}) %collective-permute-start) | collective-permute-done | bytes 524320 | tf_op jit(solution)/shard_map/ppermute | solution.py:25
  18.4 0.1 pad_maximum_fusion.data_ref
  18.5 2.2 %image.2 = (f32[2,4,4,32,256]{4,3,2,1,0:T(8,128)S(1)}, bf16[2,4,4,32,256]{4,3,2,1,0:T(8,128)(2,1)S(1)}) custom-call(bf16[2,4,4,64,256]{4,3,2,1,0:T(8,128)(2,1)S(1)} %pad_maximum_fusion.data_ref, bf16[256,256]{1,0:T(8,128)(2,1)S(1)} %copy.40.steer_ref, bf16[1,128,256]{2,1,0:T(8,128)(2,1)S(1)} %pad_maximum_fusion.4.interp_ref, f32[4,4,128]{2,1,0:T(4,128)S(1)} %bitcast.106, ...), custom_call_target="tpu_custom_call" | custom-call | flops 402653184 | bytes 2621440 | tf_op jit(solution)/shard_map/image/pallas_call | solution.py:228
  20.9 0.1 copy.41.steer_ref
  21.0 2.3 %collective-permute-done.4 = bf16[1,1,2,8,64,256]{5,4,3,2,1,0:T(8,128)(2,1)} collective-permute-done((bf16[1,1,2,8,64,256]{5,4,3,2,1,0:T(8,128)(2,1)}, bf16[1,1,2,8,64,256]{5,4,3,2,1,0:T(8,128)(2,1)}, u32[]{:S(2)}, u32[]{:S(2)}) %collective-permute-start.4) | collective-permute-done | bytes 524320 | tf_op jit(solution)/shard_map/ppermute | solution.py:25
  23.3 1.1 %pad_maximum_fusion.2.data_ref = bf16[2,4,4,64,256]{4,3,2,1,0:T(8,128)(2,1)S(1)} fusion(bf16[1,4,4,64,256]{4,3,2,1,0:T(8,128)(2,1)} %bitcast.27, bf16[1,4,4,64,256]{4,3,2,1,0:T(8,128)(2,1)S(1)} %bitcast.111), kind=kLoop, calls=%fused_computation.2 | loop fusion | flops 524288 | bytes 2097152 | tf_op jit(solution)/shard_map/stack | solution.py:385
  24.4 2.2 %image.3 = (f32[2,4,4,32,256]{4,3,2,1,0:T(8,128)S(1)}, bf16[2,4,4,32,256]{4,3,2,1,0:T(8,128)(2,1)S(1)}) custom-call(bf16[2,4,4,64,256]{4,3,2,1,0:T(8,128)(2,1)S(1)} %pad_maximum_fusion.2.data_ref, bf16[256,256]{1,0:T(8,128)(2,1)S(1)} %copy.41.steer_ref, bf16[1,128,256]{2,1,0:T(8,128)(2,1)S(1)} %pad_maximum_fusion.4.interp_ref, f32[4,4,128]{2,1,0:T(4,128)S(1)} %bitcast.105, ...), custom_call_target="tpu_custom_call" | custom-call | flops 402653184 | bytes 2621440 | tf_op jit(solution)/shard_map/image/pallas_call | solution.py:228
  26.8 1.2 %fusion.8 = (bf16[1,16,32,256]{3,2,1,0:T(8,128)(2,1)S(1)}, f32[1,1,16,32,256]{4,3,2,1,0:T(8,128)S(1)}) fusion(f32[1,2,16,32,256]{4,3,2,1,0:T(8,128)S(1)} %bitcast.103, bf16[1,2,16,32,256]{4,3,2,1,0:T(8,128)(2,1)} %bitcast.19), kind=kLoop, calls=%fused_computation.22 | loop fusion | flops 655360 | bytes 2359296 | tf_op jit(solution)/shard_map/convert_element_type | solution.py:255
  28.0 1.6 %collective-permute-start.2 = (bf16[1,16,32,256]{3,2,1,0:T(8,128)(2,1)S(1)}, bf16[1,16,32,256]{3,2,1,0:T(8,128)(2,1)S(1)}, u32[]{:S(2)}, u32[]{:S(2)}) collective-permute-start(bf16[1,16,32,256]{3,2,1,0:T(8,128)(2,1)S(1)} %get-tuple-element.27), channel_id=1, source_target_pairs={{0,16},{8,24},{16,0},{24,8},{1,17},{9,25},{17,1},{25,9},{2,18},{10... | collective-permute-start | bytes 786440 | tf_op jit(solution)/shard_map/ppermute | solution.py:25
  29.5 0.1 fusion.9
  29.7 0.6 %collective-permute-start.6 = (bf16[2,8,32,256]{3,2,1,0:T(8,128)(2,1)S(1)}, bf16[2,8,32,256]{3,2,1,0:T(8,128)(2,1)S(1)}, u32[]{:S(2)}, u32[]{:S(2)}) collective-permute-start(bf16[2,8,32,256]{3,2,1,0:T(8,128)(2,1)S(1)} %get-tuple-element.25), channel_id=1, source_target_pairs={{0,1},{1,0},{2,3},{3,2},{4,5},{5,4},{6,7},{7,6},{8,9},{9,8},{10,11... | collective-permute-start | bytes 786440 | tf_op jit(solution)/shard_map/ppermute | solution.py:25
  30.3 6.5 %collective-permute-done.2 = bf16[1,16,32,256]{3,2,1,0:T(8,128)(2,1)S(1)} collective-permute-done((bf16[1,16,32,256]{3,2,1,0:T(8,128)(2,1)S(1)}, bf16[1,16,32,256]{3,2,1,0:T(8,128)(2,1)S(1)}, u32[]{:S(2)}, u32[]{:S(2)}) %collective-permute-start.2) | collective-permute-done | bytes 262176 | tf_op jit(solution)/shard_map/ppermute | solution.py:25
  36.8 1.6 %collective-permute-start.3 = (bf16[1,8,32,256]{3,2,1,0:T(8,128)(2,1)S(1)}, bf16[1,8,32,256]{3,2,1,0:T(8,128)(2,1)S(1)}, u32[]{:S(2)}, u32[]{:S(2)}) collective-permute-start(bf16[1,8,32,256]{3,2,1,0:T(8,128)(2,1)S(1)} %fusion.18), channel_id=1, source_target_pairs={{0,2},{1,3},{2,0},{3,1},{4,6},{5,7},{6,4},{7,5},{8,10},{9,11},{10,... | collective-permute-start | bytes 393224 | tf_op jit(solution)/shard_map/ppermute | solution.py:25
  38.5 1.6 %collective-permute-start.7 = (bf16[1,8,32,256]{3,2,1,0:T(8,128)(2,1)S(1)}, bf16[1,8,32,256]{3,2,1,0:T(8,128)(2,1)S(1)}, u32[]{:S(2)}, u32[]{:S(2)}) collective-permute-start(bf16[1,8,32,256]{3,2,1,0:T(8,128)(2,1)S(1)} %fusion.19), channel_id=1, source_target_pairs={{0,16},{8,24},{16,0},{24,8},{1,17},{9,25},{17,1},{25,9},{2,18},{10... | collective-permute-start | bytes 393224 | tf_op jit(solution)/shard_map/ppermute | solution.py:25
  40.0 1.9 %collective-permute-done.3 = bf16[1,8,32,256]{3,2,1,0:T(8,128)(2,1)S(1)} collective-permute-done((bf16[1,8,32,256]{3,2,1,0:T(8,128)(2,1)S(1)}, bf16[1,8,32,256]{3,2,1,0:T(8,128)(2,1)S(1)}, u32[]{:S(2)}, u32[]{:S(2)}) %collective-permute-start.3) | collective-permute-done | bytes 131104 | tf_op jit(solution)/shard_map/ppermute | solution.py:25
  42.0 1.5 %collective-permute-done.7 = bf16[1,8,32,256]{3,2,1,0:T(8,128)(2,1)S(1)} collective-permute-done((bf16[1,8,32,256]{3,2,1,0:T(8,128)(2,1)S(1)}, bf16[1,8,32,256]{3,2,1,0:T(8,128)(2,1)S(1)}, u32[]{:S(2)}, u32[]{:S(2)}) %collective-permute-start.7) | collective-permute-done | bytes 131104 | tf_op jit(solution)/shard_map/ppermute | solution.py:25
  43.5 0.1 select_convert_fusion
  43.6 2.7 %collective-permute-start.8 = (bf16[8,32,256]{2,1,0:T(8,128)(2,1)S(1)}, bf16[8,32,256]{2,1,0:T(8,128)(2,1)S(1)}, u32[]{:S(2)}, u32[]{:S(2)}) collective-permute-start(bf16[8,32,256]{2,1,0:T(8,128)(2,1)S(1)} %get-tuple-element.23), channel_id=1, source_target_pairs={{0,4},{1,5},{2,6},{3,7},{4,0},{5,1},{6,2},{7,3},{8,12},{9,13},{10,... | collective-permute-start | bytes 393224 | tf_op jit(solution)/shard_map/ppermute | solution.py:25
  46.3 5.1 %collective-permute-done.8.got_ref = bf16[8,32,256]{2,1,0:T(8,128)(2,1)S(1)} collective-permute-done((bf16[8,32,256]{2,1,0:T(8,128)(2,1)S(1)}, bf16[8,32,256]{2,1,0:T(8,128)(2,1)S(1)}, u32[]{:S(2)}, u32[]{:S(2)}) %collective-permute-start.8) | collective-permute-done | bytes 131104 | tf_op jit(solution)/shard_map/ppermute | solution.py:25
  51.4 0.7 %last_sum.1 = bf16[32,8,256]{2,1,0:T(8,128)(2,1)} custom-call(f32[8,32,256]{2,1,0:T(8,128)S(1)} %get-tuple-element.24.keep_ref, bf16[8,32,256]{2,1,0:T(8,128)(2,1)S(1)} %collective-permute-done.8.got_ref), custom_call_target="tpu_custom_call" | custom-call | tf_op jit(solution)/shard_map/last_sum/pallas_call | solution.py:271
  (56 shorter events, 1.4 us)
Async XLA Ops:
  0.0 12.2 %copy-start.3 = (f32[8]{0:T(128)S(1)}, f32[8]{0:T(128)}, u32[]{:S(2)}) copy-start(f32[8]{0:T(128)} %constant.177.clone) | copy-start | bytes 100
  0.0 11.2 %copy-start.4 = (s32[1,8]{1,0:T(1,128)S(1)}, s32[1,8]{1,0:T(1,128)}, u32[]{:S(2)}) copy-start(s32[1,8]{1,0:T(1,128)} %param.9) | copy-start | bytes 100
  0.0 11.9 %copy-start.2 = (s32[2,2,128,8]{2,3,1,0:T(8,128)S(1)}, s32[2,2,128,8]{2,3,1,0:T(8,128)}, u32[]{:S(2)}) copy-start(s32[2,2,128,8]{2,3,1,0:T(8,128)} %param.8) | copy-start | bytes 49156
  3.3 15.1 %collective-permute-start = (bf16[1,2,1,8,64,256]{5,4,3,2,1,0:T(8,128)(2,1)}, bf16[1,2,1,8,64,256]{5,4,3,2,1,0:T(8,128)(2,1)S(1)}, u32[]{:S(2)}, u32[]{:S(2)}) collective-permute-start(bf16[1,2,1,8,64,256]{5,4,3,2,1,0:T(8,128)(2,1)} %get-tuple-element.15), channel_id=1, source_target_pairs={{0,1},{1,0},{2,3},{3,2},{4,5},{5,4},{6,7},{7,6},{8,9},{9,8},{10,11... | collective-permute-start | bytes 1572872 | tf_op jit(solution)/shard_map/ppermute | solution.py:25
  9.6 13.7 %collective-permute-start.4 = (bf16[1,1,2,8,64,256]{5,4,3,2,1,0:T(8,128)(2,1)}, bf16[1,1,2,8,64,256]{5,4,3,2,1,0:T(8,128)(2,1)}, u32[]{:S(2)}, u32[]{:S(2)}) collective-permute-start(bf16[1,1,2,8,64,256]{5,4,3,2,1,0:T(8,128)(2,1)} %get-tuple-element.20), channel_id=1, source_target_pairs={{0,2},{1,3},{2,0},{3,1},{4,6},{5,7},{6,4},{7,5},{8,10},{9,11},{10,... | collective-permute-start | bytes 1572872 | tf_op jit(solution)/shard_map/ppermute | solution.py:25
  15.7 2.7 %copy-start.1 = (bf16[1,2,1,8,64,256]{5,4,3,2,1,0:T(8,128)(2,1)S(1)}, bf16[1,2,1,8,64,256]{5,4,3,2,1,0:T(8,128)(2,1)}, u32[]{:S(2)}) copy-start(bf16[1,2,1,8,64,256]{5,4,3,2,1,0:T(8,128)(2,1)} %get-tuple-element.14) | copy-start | bytes 1572868
  18.4 4.9 %copy-start = (bf16[1,1,2,8,64,256]{5,4,3,2,1,0:T(8,128)(2,1)S(1)}, bf16[1,1,2,8,64,256]{5,4,3,2,1,0:T(8,128)(2,1)}, u32[]{:S(2)}) copy-start(bf16[1,1,2,8,64,256]{5,4,3,2,1,0:T(8,128)(2,1)} %get-tuple-element.19) | copy-start | bytes 1572868
  20.8 6.0 %collective-permute-start.1 = (bf16[2,4,4,32,256]{4,3,2,1,0:T(8,128)(2,1)S(1)}, bf16[2,4,4,32,256]{4,3,2,1,0:T(8,128)(2,1)}, u32[]{:S(2)}, u32[]{:S(2)}) collective-permute-start(bf16[2,4,4,32,256]{4,3,2,1,0:T(8,128)(2,1)S(1)} %get-tuple-element.17), channel_id=1, source_target_pairs={{0,8},{8,0},{16,24},{24,16},{1,9},{9,1},{17,25},{25,17},{2,10},{10... | collective-permute-start | bytes 1572872 | tf_op jit(solution)/shard_map/ppermute | solution.py:25
  26.7 2.9 %collective-permute-start.5 = (bf16[2,4,4,32,256]{4,3,2,1,0:T(8,128)(2,1)S(1)}, bf16[2,4,4,32,256]{4,3,2,1,0:T(8,128)(2,1)S(1)}, u32[]{:S(2)}, u32[]{:S(2)}) collective-permute-start(bf16[2,4,4,32,256]{4,3,2,1,0:T(8,128)(2,1)S(1)} %get-tuple-element.22), channel_id=1, source_target_pairs={{0,8},{8,0},{16,24},{24,16},{1,9},{9,1},{17,25},{25,17},{2,10},{10... | collective-permute-start | bytes 1572872 | tf_op jit(solution)/shard_map/ppermute | solution.py:25
  28.0 8.8 %collective-permute-start.2 = (bf16[1,16,32,256]{3,2,1,0:T(8,128)(2,1)S(1)}, bf16[1,16,32,256]{3,2,1,0:T(8,128)(2,1)S(1)}, u32[]{:S(2)}, u32[]{:S(2)}) collective-permute-start(bf16[1,16,32,256]{3,2,1,0:T(8,128)(2,1)S(1)} %get-tuple-element.27), channel_id=1, source_target_pairs={{0,16},{8,24},{16,0},{24,8},{1,17},{9,25},{17,1},{25,9},{2,18},{10... | collective-permute-start | bytes 786440 | tf_op jit(solution)/shard_map/ppermute | solution.py:25
  29.7 8.7 %collective-permute-start.6 = (bf16[2,8,32,256]{3,2,1,0:T(8,128)(2,1)S(1)}, bf16[2,8,32,256]{3,2,1,0:T(8,128)(2,1)S(1)}, u32[]{:S(2)}, u32[]{:S(2)}) collective-permute-start(bf16[2,8,32,256]{3,2,1,0:T(8,128)(2,1)S(1)} %get-tuple-element.25), channel_id=1, source_target_pairs={{0,1},{1,0},{2,3},{3,2},{4,5},{5,4},{6,7},{7,6},{8,9},{9,8},{10,11... | collective-permute-start | bytes 786440 | tf_op jit(solution)/shard_map/ppermute | solution.py:25
  36.8 5.2 %collective-permute-start.3 = (bf16[1,8,32,256]{3,2,1,0:T(8,128)(2,1)S(1)}, bf16[1,8,32,256]{3,2,1,0:T(8,128)(2,1)S(1)}, u32[]{:S(2)}, u32[]{:S(2)}) collective-permute-start(bf16[1,8,32,256]{3,2,1,0:T(8,128)(2,1)S(1)} %fusion.18), channel_id=1, source_target_pairs={{0,2},{1,3},{2,0},{3,1},{4,6},{5,7},{6,4},{7,5},{8,10},{9,11},{10,... | collective-permute-start | bytes 393224 | tf_op jit(solution)/shard_map/ppermute | solution.py:25
  38.5 5.0 %collective-permute-start.7 = (bf16[1,8,32,256]{3,2,1,0:T(8,128)(2,1)S(1)}, bf16[1,8,32,256]{3,2,1,0:T(8,128)(2,1)S(1)}, u32[]{:S(2)}, u32[]{:S(2)}) collective-permute-start(bf16[1,8,32,256]{3,2,1,0:T(8,128)(2,1)S(1)} %fusion.19), channel_id=1, source_target_pairs={{0,16},{8,24},{16,0},{24,8},{1,17},{9,25},{17,1},{25,9},{2,18},{10... | collective-permute-start | bytes 393224 | tf_op jit(solution)/shard_map/ppermute | solution.py:25
  43.6 7.8 %collective-permute-start.8 = (bf16[8,32,256]{2,1,0:T(8,128)(2,1)S(1)}, bf16[8,32,256]{2,1,0:T(8,128)(2,1)S(1)}, u32[]{:S(2)}, u32[]{:S(2)}) collective-permute-start(bf16[8,32,256]{2,1,0:T(8,128)(2,1)S(1)} %get-tuple-element.23), channel_id=1, source_target_pairs={{0,4},{1,5},{2,6},{3,7},{4,0},{5,1},{6,2},{7,3},{8,12},{9,13},{10,... | collective-permute-start | bytes 393224 | tf_op jit(solution)/shard_map/ppermute | solution.py:25

commit v9 on v8

--- a/solution.py
+++ b/solution.py
@@ -137,7 +137,9 @@
             pltpu.VMEM((2, pulses * (2 * tile + 1), half), jnp.float32),
             pltpu.VMEM((pulses, width), jnp.bfloat16),
         ],
-        compiler_params=pltpu.CompilerParams(vmem_limit_bytes=VMEM_BYTES),
+        compiler_params=pltpu.CompilerParams(
+            vmem_limit_bytes=VMEM_BYTES if near_chain else 20 * 2**20
+        ),
         cost_estimate=pl.CostEstimate(
             flops=2 * pulses * blocks * width * width,
             bytes_accessed=2 * pulses * blocks * width,
@@ -224,15 +226,19 @@
     beams = steer.shape[0] // 2
     rows = beams // leaf
     shape = (leaf // 2, count, each, rows, width)
+
+    def block(n):
+        return n % (count // 2) * 2 + n // (count // 2)
+
     out_spec = pl.BlockSpec((leaf // 2, 1) + shape[2:], lambda n: (0, n, 0, 0, 0))
     return pl.pallas_call(
         functools.partial(image_kernel, (leaf, each, half, beams, bits_of(leaf))),
         grid=(count,),
         in_specs=[
-            pl.BlockSpec((2, 1, each, pulses, width), lambda n: (0, n, 0, 0, 0)),
+            pl.BlockSpec((2, 1, each, pulses, width), lambda n: (0, block(n), 0, 0, 0)),
             pl.BlockSpec(steer.shape, lambda n: (0, 0)),
             pl.BlockSpec(interp.shape, lambda n: (0, 0, 0)),
-            pl.BlockSpec((1,) + base.shape[1:], lambda n: (n, 0, 0)),
+            pl.BlockSpec((1,) + base.shape[1:], lambda n: (block(n), 0, 0)),
             pl.BlockSpec(step.shape, lambda n: (0, 0, 0, 0)),
         ],
         out_specs=[out_spec, out_spec],
@@ -255,26 +261,29 @@
     return stay, gone.astype(jnp.bfloat16)
 
 
-def last_kernel(keep_ref, got_ref, out_ref, rows_ref):
-    blocks, rows, width = keep_ref.shape
-    for i in range(blocks):
-        value = keep_ref[i] + got_ref[i].astype(jnp.float32)
-        for c in range(2):
-            cols = slice(c * width // 2, (c + 1) * width // 2)
-            rows_ref[c, pl.ds(i, rows, stride=blocks), :] = value[:, cols]
+def last_kernel(*refs):
+    out_ref, rows_ref = refs[-2:]
+    each, rows, width = refs[0].shape
+    blocks = 2 * each
+    for n in range(2):
+        for i in range(each):
+            value = refs[2 * n][i] + refs[2 * n + 1][i].astype(jnp.float32)
+            for c in range(2):
+                cols = slice(c * width // 2, (c + 1) * width // 2)
+                rows_ref[c, pl.ds(n * each + i, rows, stride=blocks), :] = value[:, cols]
     both = jnp.concatenate([rows_ref[0], rows_ref[1]], axis=1)
     out_ref[...] = both.reshape(rows, blocks, width).astype(jnp.bfloat16)
 
 
-def last_sum(keep, got):
-    blocks, rows, width = keep.shape
+def last_sum(*parts):
+    each, rows, width = parts[0].shape
     return pl.pallas_call(
         last_kernel,
-        out_shape=jax.ShapeDtypeStruct((rows, blocks, width), jnp.bfloat16),
-        scratch_shapes=[pltpu.VMEM((2, rows * blocks, width // 2), jnp.float32)],
+        out_shape=jax.ShapeDtypeStruct((rows, 2 * each, width), jnp.bfloat16),
+        scratch_shapes=[pltpu.VMEM((2, rows * 2 * each, width // 2), jnp.float32)],
         compiler_params=pltpu.CompilerParams(vmem_limit_bytes=8 * 2**20),
         name="last_sum",
-    )(keep, got)
+    )(*parts)
 
 
 def interpolation(taps, beams):
@@ -376,7 +385,7 @@
     high_part = index >> far ^ (own_turn >> far + 1 & high - 1)
     tiles_z = (high_part * 2 + bit(own_turn, far)) * (1 << far) + low_part
 
-    final = []
+    pieces = []
     for name, keep, got, steer_own, tiles in (
         ("y", keep_y, got_y, steer_y, tiles_y),
         ("z", keep_z, got_z, steer_z, tiles_z),
@@ -385,25 +394,36 @@
         data = jnp.stack([keep.reshape(shape), got.reshape(shape)])
         kept, sent = backproject(data, steer_own, interp, bases(tiles), step, leaf)
         gone = 0 if name == "y" else far
-        leading = [("leaf", b) for b in range(levels - 1, 0, -1)]
-        leading += [("turn", b) for b in range(top - 1, -1, -1) if b != gone]
-        order = [("leaf", b) for b in range(1, levels)]
-        rest = [("turn", b) for b in range(top) if b not in (0, far)]
-        order = order + [("turn", far)] if name == "y" else [("turn", 0)] + order
         arrived = swapped(sent, "leaf", 0)
-        for axis, b in order + rest:
-            at = leading.index((axis, b))
-            before, after = 1 << at, (1 << len(leading) - at - 1) * tile
-            leading.pop(at)
-            split = (before, 2, after, rows, width)
-            kept, sent = fold(kept.reshape(split), arrived.reshape(split))
-            arrived = swapped(sent, axis, b)
-        shape = (tile, rows, width)
-        final.append(kept.reshape(shape) + arrived.reshape(shape).astype(jnp.float32))
+        parts = (leaf // 2, 2, turn // 4, each, rows, width)
+        kept, arrived = kept.reshape(parts), arrived.reshape(parts)
+        pieces.append([(kept[:, n], arrived[:, n], gone) for n in range(2)])
+
+    final = [[], []]
+    for n in range(2):
+        for chain in range(2):
+            kept, arrived, gone = pieces[chain][n]
+            leading = [("leaf", b) for b in range(levels - 1, 0, -1)]
+            leading += [("turn", b) for b in range(top - 1, -1, -1) if b != gone]
+            order = [("leaf", b) for b in range(1, levels)]
+            rest = [("turn", b) for b in range(top) if b not in (0, far)]
+            order = [("turn", 0)] + order if gone else order + [("turn", far)]
+            for axis, b in order + rest:
+                at = leading.index((axis, b))
+                before, after = 1 << at, (1 << len(leading) - at - 1) * each
+                leading.pop(at)
+                split = (before, 2, after, rows, width)
+                kept, sent = fold(kept.reshape(split), arrived.reshape(split))
+                arrived = swapped(sent, axis, b)
+            shape = (each, rows, width)
+            total = kept.reshape(shape) + arrived.reshape(shape).astype(jnp.float32)
+            final[n].append(total)
     upper = bit(own_turn, top) == 1
-    kept = jnp.where(upper, final[0], final[1])
-    sent = jnp.where(upper, final[1], final[0]).astype(jnp.bfloat16)
-    return last_sum(kept, swapped(sent, "turn", top))
+    sums = []
+    for first, second in final:
+        sent = jnp.where(upper, second, first).astype(jnp.bfloat16)
+        sums += [jnp.where(upper, first, second), swapped(sent, "turn", top)]
+    return last_sum(*sums)
 
 
 def solution(mesh):

time: 52.3 us -> 50.2 us (0.960)
  waiting for transfers between devices: 19.5 us -> 13.9 us
  starting transfers between devices: 12.7 us -> 18.2 us
  other arithmetic: 6.94 us -> 4.87 us
  local copies, waits for them, and re-layouts: 0.67 us -> 1.85 us
  Pallas kernels: 11.8 us -> 10.7 us
    ppermute x9 -> x14, waiting for transfers between devices: 19.5 us -> 13.9 us  [swapped(): lax.ppermute(array, axis, [(i, i ^ 1 << bit) for i in range(lax.axis_size...]
    ppermute x9 -> x14, starting transfers between devices: 12.7 us -> 18.2 us  [swapped(): lax.ppermute(array, axis, [(i, i ^ 1 << bit) for i in range(lax.axis_size...]
    pallas_call x2, Pallas kernels: 6.62 us -> 5.35 us  [compress(): pl.pallas_call(functools.partial(compress_kernel, dims, edge is not None)...]
    another operation x2, other arithmetic: 1.24 us -> 0.19 us  [per_device(): data = jnp.stack([keep.reshape(shape), got.reshape(shape)])]
    convert_element_type x4 -> x8, other arithmetic: 1.43 us -> 0.39 us  [fold(): return (stay, gone.astype(jnp.bfloat16))]
    unnamed x10 -> x14, local copies, waits for them, and re-layouts: 0.02 us -> 0.78 us
  transfers between devices with their start and end apart: 9 -> 14, of which waited for: 6 -> 7; matrix products, arithmetic and copies ran while one was open for 15% -> 12% of each run, Pallas kernels for 15% -> 13%
where the time goes in v9:
time: 50.2 us; the launch traced here: 50.1 us
  starting transfers between devices  18.2 us (36%)
  waiting for transfers between devices  13.9 us (28%)
  Pallas kernels  10.7 us (21%)
  other arithmetic  4.87 us (10%)
  local copies, waits for them, and re-layouts  1.85 us (4%)
    ppermute x14, starting transfers between devices, swapped(): lax.ppermute(array, axis, [(i, i ^ 1 << bit) for i in range(lax.axis_size...  18.2 us
    ppermute x14, waiting for transfers between devices, swapped(): lax.ppermute(array, axis, [(i, i ^ 1 << bit) for i in range(lax.axis_size...  13.9 us
    pallas_call x2, Pallas kernels, compress(): pl.pallas_call(functools.partial(compress_kernel, dims, edge is not None)...  5.35 us
    pallas_call x2, Pallas kernels, backproject(): pl.pallas_call(functools.partial(image_kernel, (leaf, each, half, beams,...  4.61 us
    cos x2, other arithmetic, unit(): return (jnp.cos(angle), jnp.sin(angle))  2.27 us
  transfers between devices with their start and end apart: 14, of which 7 were waited for; matrix products, arithmetic and copies ran while one was open for 12% of the time, Pallas kernels for 13%

profile of v9, /device:TPU:0, one launch (start us, length us, event | category | flops | bytes accessed | tf_op | source)
XLA Modules:
  0.0 50.1 jit_solution(7156395230636005316)
XLA Ops:
  0.0 3.4 %compress.2 = (bf16[1,2,1,8,64,256]{5,4,3,2,1,0:T(8,128)(2,1)}, bf16[1,2,1,8,64,256]{5,4,3,2,1,0:T(8,128)(2,1)}, bf16[64,256]{1,0:T(8,128)(2,1)}) custom-call(bf16[2,128]{1,0:T(2,128)(2,1)} %chirp_ref.3, bf16[64,64,256]{2,1,0:T(8,128)(2,1)} %echo_ref.3), custom_call_target="tpu_custom_call" | custom-call | flops 536870912 | bytes 2097152 | tf_op jit(solution)/shard_map/compress/pallas_call | solution.py:127
  3.4 3.0 %collective-permute-start = (bf16[1,2,1,8,64,256]{5,4,3,2,1,0:T(8,128)(2,1)}, bf16[1,2,1,8,64,256]{5,4,3,2,1,0:T(8,128)(2,1)S(1)}, u32[]{:S(2)}, u32[]{:S(2)}) collective-permute-start(bf16[1,2,1,8,64,256]{5,4,3,2,1,0:T(8,128)(2,1)} %get-tuple-element.15), channel_id=1, source_target_pairs={{0,1},{1,0},{2,3},{3,2},{4,5},{5,4},{6,7},{7,6},{8,9},{9,8},{10,11... | collective-permute-start | bytes 1572872 | tf_op jit(solution)/shard_map/ppermute | solution.py:25
  6.4 0.8 %copy-done.1 = bf16[64,256]{1,0:T(8,128)(2,1)S(1)} copy-done((bf16[64,256]{1,0:T(8,128)(2,1)S(1)}, bf16[64,256]{1,0:T(8,128)(2,1)}, u32[]{:S(2)}) %copy-start.1) | copy-done | bytes 32792
  7.2 1.9 %compress.3 = (bf16[1,1,2,8,64,256]{5,4,3,2,1,0:T(8,128)(2,1)S(1)}, bf16[1,1,2,8,64,256]{5,4,3,2,1,0:T(8,128)(2,1)S(1)}, bf16[64,256]{1,0:T(8,128)(2,1)}) custom-call(bf16[2,128]{1,0:T(2,128)(2,1)S(1)} %copy-done.2, bf16[64,64,256]{2,1,0:T(8,128)(2,1)S(1)} %copy-done, bf16[64,256]{1,0:T(8,128)(2,1)S(1)} %copy-done.1), custom_call_target="tpu_custom_call" | custom-call | flops 536870912 | bytes 2097152 | tf_op jit(solution)/shard_map/compress/pallas_call | solution.py:127
  9.1 1.6 %collective-permute-start.4 = (bf16[1,1,2,8,64,256]{5,4,3,2,1,0:T(8,128)(2,1)S(1)}, bf16[1,1,2,8,64,256]{5,4,3,2,1,0:T(8,128)(2,1)S(1)}, u32[]{:S(2)}, u32[]{:S(2)}) collective-permute-start(bf16[1,1,2,8,64,256]{5,4,3,2,1,0:T(8,128)(2,1)S(1)} %get-tuple-element.20), channel_id=1, source_target_pairs={{0,2},{1,3},{2,0},{3,1},{4,6},{5,7},{6,4},{7,5},{8,10},{9,11},{10,... | collective-permute-start | bytes 1572872 | tf_op jit(solution)/shard_map/ppermute | solution.py:25
  10.8 0.2 select_reduce_fusion.1
  11.6 0.1 copy.27
  11.9 0.4 select_reduce_fusion
  12.3 0.5 multiply_convert_fusion.1
  12.8 0.2 fusion.30
  13.2 0.2 fusion.47
  13.7 2.1 %fusion.10 = (f32[2,1,128,512]{3,2,1,0:T(8,128)S(1)}, f32[2,1,128,512]{3,2,1,0:T(8,128)S(1)}) fusion(s32[512]{0:T(512)S(1)} %iota_add_fusion, s32[2,128]{1,0:T(2,128)S(1)} %add_multiply_fusion), kind=kLoop, calls=%fused_computation.32 | loop fusion | flops 1835008 | bytes 1051648 | tf_op jit(solution)/shard_map/cos | solution.py:30
  15.9 2.6 %collective-permute-done = bf16[1,2,1,8,64,256]{5,4,3,2,1,0:T(8,128)(2,1)S(1)} collective-permute-done((bf16[1,2,1,8,64,256]{5,4,3,2,1,0:T(8,128)(2,1)}, bf16[1,2,1,8,64,256]{5,4,3,2,1,0:T(8,128)(2,1)S(1)}, u32[]{:S(2)}, u32[]{:S(2)}) %collective-permute-start) | collective-permute-done | bytes 524320 | tf_op jit(solution)/shard_map/ppermute | solution.py:25
  18.6 2.3 %image.2 = (f32[2,4,4,32,256]{4,3,2,1,0:T(8,128)S(1)}, bf16[2,4,4,32,256]{4,3,2,1,0:T(8,128)(2,1)S(1)}) custom-call(bf16[2,4,4,64,256]{4,3,2,1,0:T(8,128)(2,1)S(1)} %pad_maximum_fusion.data_ref, bf16[256,256]{1,0:T(8,128)(2,1)S(1)} %copy.34.steer_ref, bf16[1,128,256]{2,1,0:T(8,128)(2,1)S(1)} %pad_maximum_fusion.4.interp_ref, f32[4,4,128]{2,1,0:T(4,128)S(1)} %bitcast.139, ...), custom_call_target="tpu_custom_call" | custom-call | flops 402653184 | bytes 2621440 | tf_op jit(solution)/shard_map/image/pallas_call | solution.py:234
  21.0 1.4 %collective-permute-done.4 = bf16[1,1,2,8,64,256]{5,4,3,2,1,0:T(8,128)(2,1)S(1)} collective-permute-done((bf16[1,1,2,8,64,256]{5,4,3,2,1,0:T(8,128)(2,1)S(1)}, bf16[1,1,2,8,64,256]{5,4,3,2,1,0:T(8,128)(2,1)S(1)}, u32[]{:S(2)}, u32[]{:S(2)}) %collective-permute-start.4) | collective-permute-done | bytes 524320 | tf_op jit(solution)/shard_map/ppermute | solution.py:25
  22.6 2.3 %image.3 = (f32[2,4,4,32,256]{4,3,2,1,0:T(8,128)S(1)}, bf16[2,4,4,32,256]{4,3,2,1,0:T(8,128)(2,1)S(1)}) custom-call(bf16[2,4,4,64,256]{4,3,2,1,0:T(8,128)(2,1)S(1)} %pad_maximum_fusion.2.data_ref, bf16[256,256]{1,0:T(8,128)(2,1)S(1)} %copy.35.steer_ref, bf16[1,128,256]{2,1,0:T(8,128)(2,1)S(1)} %pad_maximum_fusion.4.interp_ref, f32[4,4,128]{2,1,0:T(4,128)S(1)} %bitcast.138, ...), custom_call_target="tpu_custom_call" | custom-call | flops 402653184 | bytes 2621440 | tf_op jit(solution)/shard_map/image/pallas_call | solution.py:234
  25.5 1.6 %collective-permute-start.2 = (bf16[1,8,32,256]{3,2,1,0:T(8,128)(2,1)S(1)}, bf16[1,8,32,256]{3,2,1,0:T(8,128)(2,1)S(1)}, u32[]{:S(2)}, u32[]{:S(2)}) collective-permute-start(bf16[1,8,32,256]{3,2,1,0:T(8,128)(2,1)S(1)} %get-tuple-element.37), channel_id=1, source_target_pairs={{0,16},{8,24},{16,0},{24,8},{1,17},{9,25},{17,1},{25,9},{2,18},{10... | collective-permute-start | bytes 393224 | tf_op jit(solution)/shard_map/ppermute | solution.py:25
  27.1 0.6 %collective-permute-start.9 = (bf16[1,8,32,256]{3,2,1,0:T(8,128)(2,1)S(1)}, bf16[1,8,32,256]{3,2,1,0:T(8,128)(2,1)S(1)}, u32[]{:S(2)}, u32[]{:S(2)}) collective-permute-start(bf16[1,8,32,256]{3,2,1,0:T(8,128)(2,1)S(1)} %get-tuple-element.33), channel_id=1, source_target_pairs={{0,16},{8,24},{16,0},{24,8},{1,17},{9,25},{17,1},{25,9},{2,18},{10... | collective-permute-start | bytes 393224 | tf_op jit(solution)/shard_map/ppermute | solution.py:25
  27.9 0.8 %collective-permute-start.6 = (bf16[2,4,32,256]{3,2,1,0:T(8,128)(2,1)S(1)}, bf16[2,4,32,256]{3,2,1,0:T(8,128)(2,1)S(1)}, u32[]{:S(2)}, u32[]{:S(2)}) collective-permute-start(bf16[2,4,32,256]{3,2,1,0:T(8,128)(2,1)S(1)} %get-tuple-element.35), channel_id=1, source_target_pairs={{0,1},{1,0},{2,3},{3,2},{4,5},{5,4},{6,7},{7,6},{8,9},{9,8},{10,11... | collective-permute-start | bytes 393224 | tf_op jit(solution)/shard_map/ppermute | solution.py:25
  28.8 1.3 %collective-permute-start.11 = (bf16[2,4,32,256]{3,2,1,0:T(8,128)(2,1)S(1)}, bf16[2,4,32,256]{3,2,1,0:T(8,128)(2,1)S(1)}, u32[]{:S(2)}, u32[]{:S(2)}) collective-permute-start(bf16[2,4,32,256]{3,2,1,0:T(8,128)(2,1)S(1)} %get-tuple-element.31), channel_id=1, source_target_pairs={{0,1},{1,0},{2,3},{3,2},{4,5},{5,4},{6,7},{7,6},{8,9},{9,8},{10,11... | collective-permute-start | bytes 393224 | tf_op jit(solution)/shard_map/ppermute | solution.py:25
  30.1 1.7 %collective-permute-done.2 = bf16[1,8,32,256]{3,2,1,0:T(8,128)(2,1)S(1)} collective-permute-done((bf16[1,8,32,256]{3,2,1,0:T(8,128)(2,1)S(1)}, bf16[1,8,32,256]{3,2,1,0:T(8,128)(2,1)S(1)}, u32[]{:S(2)}, u32[]{:S(2)}) %collective-permute-start.2) | collective-permute-done | bytes 131104 | tf_op jit(solution)/shard_map/ppermute | solution.py:25
  31.8 1.6 %collective-permute-start.3 = (bf16[1,4,32,256]{3,2,1,0:T(8,128)(2,1)S(1)}, bf16[1,4,32,256]{3,2,1,0:T(8,128)(2,1)S(1)}, u32[]{:S(2)}, u32[]{:S(2)}) collective-permute-start(bf16[1,4,32,256]{3,2,1,0:T(8,128)(2,1)S(1)} %fusion.33), channel_id=1, source_target_pairs={{0,2},{1,3},{2,0},{3,1},{4,6},{5,7},{6,4},{7,5},{8,10},{9,11},{10,... | collective-permute-start | bytes 196616 | tf_op jit(solution)/shard_map/ppermute | solution.py:25
  33.5 0.7 %collective-permute-done.9 = bf16[1,8,32,256]{3,2,1,0:T(8,128)(2,1)S(1)} collective-permute-done((bf16[1,8,32,256]{3,2,1,0:T(8,128)(2,1)S(1)}, bf16[1,8,32,256]{3,2,1,0:T(8,128)(2,1)S(1)}, u32[]{:S(2)}, u32[]{:S(2)}) %collective-permute-start.9) | collective-permute-done | bytes 131104 | tf_op jit(solution)/shard_map/ppermute | solution.py:25
  34.3 1.6 %collective-permute-start.10 = (bf16[1,4,32,256]{3,2,1,0:T(8,128)(2,1)S(1)}, bf16[1,4,32,256]{3,2,1,0:T(8,128)(2,1)S(1)}, u32[]{:S(2)}, u32[]{:S(2)}) collective-permute-start(bf16[1,4,32,256]{3,2,1,0:T(8,128)(2,1)S(1)} %fusion.35), channel_id=1, source_target_pairs={{0,2},{1,3},{2,0},{3,1},{4,6},{5,7},{6,4},{7,5},{8,10},{9,11},{10,... | collective-permute-start | bytes 196616 | tf_op jit(solution)/shard_map/ppermute | solution.py:25
  35.9 1.6 %collective-permute-start.7 = (bf16[1,4,32,256]{3,2,1,0:T(8,128)(2,1)S(1)}, bf16[1,4,32,256]{3,2,1,0:T(8,128)(2,1)S(1)}, u32[]{:S(2)}, u32[]{:S(2)}) collective-permute-start(bf16[1,4,32,256]{3,2,1,0:T(8,128)(2,1)S(1)} %fusion.34), channel_id=1, source_target_pairs={{0,16},{8,24},{16,0},{24,8},{1,17},{9,25},{17,1},{25,9},{2,18},{10... | collective-permute-start | bytes 196616 | tf_op jit(solution)/shard_map/ppermute | solution.py:25
  37.5 0.6 %collective-permute-start.12 = (bf16[1,4,32,256]{3,2,1,0:T(8,128)(2,1)S(1)}, bf16[1,4,32,256]{3,2,1,0:T(8,128)(2,1)S(1)}, u32[]{:S(2)}, u32[]{:S(2)}) collective-permute-start(bf16[1,4,32,256]{3,2,1,0:T(8,128)(2,1)S(1)} %fusion.36), channel_id=1, source_target_pairs={{0,16},{8,24},{16,0},{24,8},{1,17},{9,25},{17,1},{25,9},{2,18},{10... | collective-permute-start | bytes 196616 | tf_op jit(solution)/shard_map/ppermute | solution.py:25
  38.1 2.6 %collective-permute-done.7 = bf16[1,4,32,256]{3,2,1,0:T(8,128)(2,1)S(1)} collective-permute-done((bf16[1,4,32,256]{3,2,1,0:T(8,128)(2,1)S(1)}, bf16[1,4,32,256]{3,2,1,0:T(8,128)(2,1)S(1)}, u32[]{:S(2)}, u32[]{:S(2)}) %collective-permute-start.7) | collective-permute-done | bytes 65568 | tf_op jit(solution)/shard_map/ppermute | solution.py:25
  40.8 2.7 %collective-permute-start.8 = (bf16[4,32,256]{2,1,0:T(8,128)(2,1)S(1)}, bf16[4,32,256]{2,1,0:T(8,128)(2,1)S(1)}, u32[]{:S(2)}, u32[]{:S(2)}) collective-permute-start(bf16[4,32,256]{2,1,0:T(8,128)(2,1)S(1)} %get-tuple-element.29), channel_id=1, source_target_pairs={{0,4},{1,5},{2,6},{3,7},{4,0},{5,1},{6,2},{7,3},{8,12},{9,13},{10,... | collective-permute-start | bytes 196616 | tf_op jit(solution)/shard_map/ppermute | solution.py:25
  43.5 1.0 %collective-permute-start.13 = (bf16[4,32,256]{2,1,0:T(8,128)(2,1)S(1)}, bf16[4,32,256]{2,1,0:T(8,128)(2,1)S(1)}, u32[]{:S(2)}, u32[]{:S(2)}) collective-permute-start(bf16[4,32,256]{2,1,0:T(8,128)(2,1)S(1)} %get-tuple-element.27), channel_id=1, source_target_pairs={{0,4},{1,5},{2,6},{3,7},{4,0},{5,1},{6,2},{7,3},{8,12},{9,13},{10,... | collective-permute-start | bytes 196616 | tf_op jit(solution)/shard_map/ppermute | solution.py:25
  44.6 2.7 %collective-permute-done.8.refs_1_ = bf16[4,32,256]{2,1,0:T(8,128)(2,1)S(1)} collective-permute-done((bf16[4,32,256]{2,1,0:T(8,128)(2,1)S(1)}, bf16[4,32,256]{2,1,0:T(8,128)(2,1)S(1)}, u32[]{:S(2)}, u32[]{:S(2)}) %collective-permute-start.8) | collective-permute-done | bytes 65568 | tf_op jit(solution)/shard_map/ppermute | solution.py:25
  47.3 2.0 %collective-permute-done.13.refs_3_ = bf16[4,32,256]{2,1,0:T(8,128)(2,1)S(1)} collective-permute-done((bf16[4,32,256]{2,1,0:T(8,128)(2,1)S(1)}, bf16[4,32,256]{2,1,0:T(8,128)(2,1)S(1)}, u32[]{:S(2)}, u32[]{:S(2)}) %collective-permute-start.13) | collective-permute-done | bytes 65568 | tf_op jit(solution)/shard_map/ppermute | solution.py:25
  49.3 0.7 %last_sum.1 = bf16[32,8,256]{2,1,0:T(8,128)(2,1)} custom-call(f32[4,32,256]{2,1,0:T(8,128)S(1)} %get-tuple-element.30.refs_0_, bf16[4,32,256]{2,1,0:T(8,128)(2,1)S(1)} %collective-permute-done.8.refs_1_, f32[4,32,256]{2,1,0:T(8,128)S(1)} %get-tuple-element.28.refs_2_, bf16[4,32,256]{2,1,0:T(8,128)(2,1)S(1)} %collective-permute-done.13.refs_3_), custom_call_target="tpu_custom_call" | custom-call | tf_op jit(solution)/shard_map/last_sum/pallas_call | solution.py:280
  (81 shorter events, 2.6 us)
Async XLA Ops:
  0.0 11.9 %copy-start.5 = (f32[8]{0:T(128)S(1)}, f32[8]{0:T(128)}, u32[]{:S(2)}) copy-start(f32[8]{0:T(128)} %constant.177.clone) | copy-start | bytes 100
  0.0 6.4 %copy-start.2 = (bf16[2,128]{1,0:T(2,128)(2,1)S(1)}, bf16[2,128]{1,0:T(2,128)(2,1)}, u32[]{:S(2)}) copy-start(bf16[2,128]{1,0:T(2,128)(2,1)} %chirp_ref.3) | copy-start | bytes 1540
  0.0 6.4 %copy-start = (bf16[64,64,256]{2,1,0:T(8,128)(2,1)S(1)}, bf16[64,64,256]{2,1,0:T(8,128)(2,1)}, u32[]{:S(2)}) copy-start(bf16[64,64,256]{2,1,0:T(8,128)(2,1)} %echo_ref.3) | copy-start | bytes 6291460
  0.0 10.7 %copy-start.6 = (s32[1,8]{1,0:T(1,128)S(1)}, s32[1,8]{1,0:T(1,128)}, u32[]{:S(2)}) copy-start(s32[1,8]{1,0:T(1,128)} %param.9) | copy-start | bytes 100
  3.4 15.1 %collective-permute-start = (bf16[1,2,1,8,64,256]{5,4,3,2,1,0:T(8,128)(2,1)}, bf16[1,2,1,8,64,256]{5,4,3,2,1,0:T(8,128)(2,1)S(1)}, u32[]{:S(2)}, u32[]{:S(2)}) collective-permute-start(bf16[1,2,1,8,64,256]{5,4,3,2,1,0:T(8,128)(2,1)} %get-tuple-element.15), channel_id=1, source_target_pairs={{0,1},{1,0},{2,3},{3,2},{4,5},{5,4},{6,7},{7,6},{8,9},{9,8},{10,11... | collective-permute-start | bytes 1572872 | tf_op jit(solution)/shard_map/ppermute | solution.py:25
  6.4 0.8 %copy-start.1 = (bf16[64,256]{1,0:T(8,128)(2,1)S(1)}, bf16[64,256]{1,0:T(8,128)(2,1)}, u32[]{:S(2)}) copy-start(bf16[64,256]{1,0:T(8,128)(2,1)} %get-tuple-element.18.refs_0_) | copy-start | bytes 98308
  7.2 4.2 %copy-start.4 = (s32[2,2,128,8]{2,3,1,0:T(8,128)S(1)}, s32[2,2,128,8]{2,3,1,0:T(8,128)}, u32[]{:S(2)}) copy-start(s32[2,2,128,8]{2,3,1,0:T(8,128)} %param.8) | copy-start | bytes 49156
  9.1 13.4 %collective-permute-start.4 = (bf16[1,1,2,8,64,256]{5,4,3,2,1,0:T(8,128)(2,1)S(1)}, bf16[1,1,2,8,64,256]{5,4,3,2,1,0:T(8,128)(2,1)S(1)}, u32[]{:S(2)}, u32[]{:S(2)}) collective-permute-start(bf16[1,1,2,8,64,256]{5,4,3,2,1,0:T(8,128)(2,1)S(1)} %get-tuple-element.20), channel_id=1, source_target_pairs={{0,2},{1,3},{2,0},{3,1},{4,6},{5,7},{6,4},{7,5},{8,10},{9,11},{10,... | collective-permute-start | bytes 1572872 | tf_op jit(solution)/shard_map/ppermute | solution.py:25
  13.4 5.2 %copy-start.3 = (bf16[1,2,1,8,64,256]{5,4,3,2,1,0:T(8,128)(2,1)S(1)}, bf16[1,2,1,8,64,256]{5,4,3,2,1,0:T(8,128)(2,1)}, u32[]{:S(2)}) copy-start(bf16[1,2,1,8,64,256]{5,4,3,2,1,0:T(8,128)(2,1)} %get-tuple-element.14) | copy-start | bytes 1572868
  21.0 4.4 %collective-permute-start.1 = (bf16[2,4,4,32,256]{4,3,2,1,0:T(8,128)(2,1)S(1)}, bf16[2,4,4,32,256]{4,3,2,1,0:T(8,128)(2,1)S(1)}, u32[]{:S(2)}, u32[]{:S(2)}) collective-permute-start(bf16[2,4,4,32,256]{4,3,2,1,0:T(8,128)(2,1)S(1)} %get-tuple-element.17), channel_id=1, source_target_pairs={{0,8},{8,0},{16,24},{24,16},{1,9},{9,1},{17,25},{25,17},{2,10},{10... | collective-permute-start | bytes 1572872 | tf_op jit(solution)/shard_map/ppermute | solution.py:25
  25.0 2.7 %collective-permute-start.5 = (bf16[2,4,4,32,256]{4,3,2,1,0:T(8,128)(2,1)S(1)}, bf16[2,4,4,32,256]{4,3,2,1,0:T(8,128)(2,1)S(1)}, u32[]{:S(2)}, u32[]{:S(2)}) collective-permute-start(bf16[2,4,4,32,256]{4,3,2,1,0:T(8,128)(2,1)S(1)} %get-tuple-element.22), channel_id=1, source_target_pairs={{0,8},{8,0},{16,24},{24,16},{1,9},{9,1},{17,25},{25,17},{2,10},{10... | collective-permute-start | bytes 1572872 | tf_op jit(solution)/shard_map/ppermute | solution.py:25
  25.5 6.4 %collective-permute-start.2 = (bf16[1,8,32,256]{3,2,1,0:T(8,128)(2,1)S(1)}, bf16[1,8,32,256]{3,2,1,0:T(8,128)(2,1)S(1)}, u32[]{:S(2)}, u32[]{:S(2)}) collective-permute-start(bf16[1,8,32,256]{3,2,1,0:T(8,128)(2,1)S(1)} %get-tuple-element.37), channel_id=1, source_target_pairs={{0,16},{8,24},{16,0},{24,8},{1,17},{9,25},{17,1},{25,9},{2,18},{10... | collective-permute-start | bytes 393224 | tf_op jit(solution)/shard_map/ppermute | solution.py:25
  27.1 7.1 %collective-permute-start.9 = (bf16[1,8,32,256]{3,2,1,0:T(8,128)(2,1)S(1)}, bf16[1,8,32,256]{3,2,1,0:T(8,128)(2,1)S(1)}, u32[]{:S(2)}, u32[]{:S(2)}) collective-permute-start(bf16[1,8,32,256]{3,2,1,0:T(8,128)(2,1)S(1)} %get-tuple-element.33), channel_id=1, source_target_pairs={{0,16},{8,24},{16,0},{24,8},{1,17},{9,25},{17,1},{25,9},{2,18},{10... | collective-permute-start | bytes 393224 | tf_op jit(solution)/shard_map/ppermute | solution.py:25
  27.9 8.0 %collective-permute-start.6 = (bf16[2,4,32,256]{3,2,1,0:T(8,128)(2,1)S(1)}, bf16[2,4,32,256]{3,2,1,0:T(8,128)(2,1)S(1)}, u32[]{:S(2)}, u32[]{:S(2)}) collective-permute-start(bf16[2,4,32,256]{3,2,1,0:T(8,128)(2,1)S(1)} %get-tuple-element.35), channel_id=1, source_target_pairs={{0,1},{1,0},{2,3},{3,2},{4,5},{5,4},{6,7},{7,6},{8,9},{9,8},{10,11... | collective-permute-start | bytes 393224 | tf_op jit(solution)/shard_map/ppermute | solution.py:25
  28.8 8.7 %collective-permute-start.11 = (bf16[2,4,32,256]{3,2,1,0:T(8,128)(2,1)S(1)}, bf16[2,4,32,256]{3,2,1,0:T(8,128)(2,1)S(1)}, u32[]{:S(2)}, u32[]{:S(2)}) collective-permute-start(bf16[2,4,32,256]{3,2,1,0:T(8,128)(2,1)S(1)} %get-tuple-element.31), channel_id=1, source_target_pairs={{0,1},{1,0},{2,3},{3,2},{4,5},{5,4},{6,7},{7,6},{8,9},{9,8},{10,11... | collective-permute-start | bytes 393224 | tf_op jit(solution)/shard_map/ppermute | solution.py:25
  31.8 6.3 %collective-permute-start.3 = (bf16[1,4,32,256]{3,2,1,0:T(8,128)(2,1)S(1)}, bf16[1,4,32,256]{3,2,1,0:T(8,128)(2,1)S(1)}, u32[]{:S(2)}, u32[]{:S(2)}) collective-permute-start(bf16[1,4,32,256]{3,2,1,0:T(8,128)(2,1)S(1)} %fusion.33), channel_id=1, source_target_pairs={{0,2},{1,3},{2,0},{3,1},{4,6},{5,7},{6,4},{7,5},{8,10},{9,11},{10,... | collective-permute-start | bytes 196616 | tf_op jit(solution)/shard_map/ppermute | solution.py:25
  34.3 9.2 %collective-permute-start.10 = (bf16[1,4,32,256]{3,2,1,0:T(8,128)(2,1)S(1)}, bf16[1,4,32,256]{3,2,1,0:T(8,128)(2,1)S(1)}, u32[]{:S(2)}, u32[]{:S(2)}) collective-permute-start(bf16[1,4,32,256]{3,2,1,0:T(8,128)(2,1)S(1)} %fusion.35), channel_id=1, source_target_pairs={{0,2},{1,3},{2,0},{3,1},{4,6},{5,7},{6,4},{7,5},{8,10},{9,11},{10,... | collective-permute-start | bytes 196616 | tf_op jit(solution)/shard_map/ppermute | solution.py:25
  35.9 4.8 %collective-permute-start.7 = (bf16[1,4,32,256]{3,2,1,0:T(8,128)(2,1)S(1)}, bf16[1,4,32,256]{3,2,1,0:T(8,128)(2,1)S(1)}, u32[]{:S(2)}, u32[]{:S(2)}) collective-permute-start(bf16[1,4,32,256]{3,2,1,0:T(8,128)(2,1)S(1)} %fusion.34), channel_id=1, source_target_pairs={{0,16},{8,24},{16,0},{24,8},{1,17},{9,25},{17,1},{25,9},{2,18},{10... | collective-permute-start | bytes 196616 | tf_op jit(solution)/shard_map/ppermute | solution.py:25
  37.5 5.9 %collective-permute-start.12 = (bf16[1,4,32,256]{3,2,1,0:T(8,128)(2,1)S(1)}, bf16[1,4,32,256]{3,2,1,0:T(8,128)(2,1)S(1)}, u32[]{:S(2)}, u32[]{:S(2)}) collective-permute-start(bf16[1,4,32,256]{3,2,1,0:T(8,128)(2,1)S(1)} %fusion.36), channel_id=1, source_target_pairs={{0,16},{8,24},{16,0},{24,8},{1,17},{9,25},{17,1},{25,9},{2,18},{10... | collective-permute-start | bytes 196616 | tf_op jit(solution)/shard_map/ppermute | solution.py:25
  40.8 6.5 %collective-permute-start.8 = (bf16[4,32,256]{2,1,0:T(8,128)(2,1)S(1)}, bf16[4,32,256]{2,1,0:T(8,128)(2,1)S(1)}, u32[]{:S(2)}, u32[]{:S(2)}) collective-permute-start(bf16[4,32,256]{2,1,0:T(8,128)(2,1)S(1)} %get-tuple-element.29), channel_id=1, source_target_pairs={{0,4},{1,5},{2,6},{3,7},{4,0},{5,1},{6,2},{7,3},{8,12},{9,13},{10,... | collective-permute-start | bytes 196616 | tf_op jit(solution)/shard_map/ppermute | solution.py:25
  43.5 5.8 %collective-permute-start.13 = (bf16[4,32,256]{2,1,0:T(8,128)(2,1)S(1)}, bf16[4,32,256]{2,1,0:T(8,128)(2,1)S(1)}, u32[]{:S(2)}, u32[]{:S(2)}) collective-permute-start(bf16[4,32,256]{2,1,0:T(8,128)(2,1)S(1)} %get-tuple-element.27), channel_id=1, source_target_pairs={{0,4},{1,5},{2,6},{3,7},{4,0},{5,1},{6,2},{7,3},{8,12},{9,13},{10,... | collective-permute-start | bytes 196616 | tf_op jit(solution)/shard_map/ppermute | solution.py:25

commit v10 on v9

--- a/solution.py
+++ b/solution.py
@@ -10,7 +10,7 @@
 
 WEIGHTS = (-1.0 / 32, 3.0 / 32, -7.0 / 32, 21.0 / 32, 21.0 / 32, -7.0 / 32, 3.0 / 32, -1.0 / 32)
 PERIOD = 4096
-VMEM_BYTES = 56 * 2**20
+VMEM_BYTES = 52 * 2**20
 
 
 def bits_of(count):
@@ -201,14 +201,9 @@
                         else:
                             out_send[g - leaf // 2, 0, at + i] = both.astype(jnp.bfloat16)
                         continue
-                    both = jnp.concatenate(both, axis=1)
-                    big = both.astype(jnp.bfloat16)
-                    low = (both - big.astype(jnp.float32)).astype(jnp.bfloat16)
-                    pieces.append((big, low))
+                    pieces.append(jnp.concatenate(both, axis=1).astype(jnp.bfloat16))
                 if pieces:
-                    columns.append(
-                        jnp.concatenate([p[0] for p in pieces] + [p[1] for p in pieces], axis=0)
-                    )
+                    columns.append(jnp.concatenate(pieces, axis=0))
             if columns:
                 moved = jnp.dot(
                     interp_ref[level],
@@ -261,29 +256,26 @@
     return stay, gone.astype(jnp.bfloat16)
 
 
-def last_kernel(*refs):
-    out_ref, rows_ref = refs[-2:]
-    each, rows, width = refs[0].shape
-    blocks = 2 * each
-    for n in range(2):
-        for i in range(each):
-            value = refs[2 * n][i] + refs[2 * n + 1][i].astype(jnp.float32)
-            for c in range(2):
-                cols = slice(c * width // 2, (c + 1) * width // 2)
-                rows_ref[c, pl.ds(n * each + i, rows, stride=blocks), :] = value[:, cols]
+def last_kernel(keep_ref, got_ref, out_ref, rows_ref):
+    blocks, rows, width = keep_ref.shape
+    for i in range(blocks):
+        value = keep_ref[i] + got_ref[i].astype(jnp.float32)
+        for c in range(2):
+            cols = slice(c * width // 2, (c + 1) * width // 2)
+            rows_ref[c, pl.ds(i, rows, stride=blocks), :] = value[:, cols]
     both = jnp.concatenate([rows_ref[0], rows_ref[1]], axis=1)
     out_ref[...] = both.reshape(rows, blocks, width).astype(jnp.bfloat16)
 
 
-def last_sum(*parts):
-    each, rows, width = parts[0].shape
+def last_sum(keep, got):
+    blocks, rows, width = keep.shape
     return pl.pallas_call(
         last_kernel,
-        out_shape=jax.ShapeDtypeStruct((rows, 2 * each, width), jnp.bfloat16),
-        scratch_shapes=[pltpu.VMEM((2, rows * 2 * each, width // 2), jnp.float32)],
+        out_shape=jax.ShapeDtypeStruct((rows, blocks, width), jnp.bfloat16),
+        scratch_shapes=[pltpu.VMEM((2, rows * blocks, width // 2), jnp.float32)],
         compiler_params=pltpu.CompilerParams(vmem_limit_bytes=8 * 2**20),
         name="last_sum",
-    )(*parts)
+    )(keep, got)
 
 
 def interpolation(taps, beams):
@@ -356,7 +348,7 @@
         axis=0,
     )
     matrices = interpolation(jnp.stack(own_taps), beams)
-    interp = jnp.concatenate([matrices[1:]] * 2, axis=-1).astype(jnp.bfloat16)
+    interp = matrices[1:].astype(jnp.bfloat16)
     scale = 1.0 / math.sqrt(2.0 * slots.shape[1] * pulses)
     wanted = own_turn ^ jnp.array([0, 1, 1 << far], jnp.int32)
     picked = jnp.arange(slots.shape[1], dtype=jnp.int32) == wanted[:, None]
@@ -419,11 +411,11 @@
             total = kept.reshape(shape) + arrived.reshape(shape).astype(jnp.float32)
             final[n].append(total)
     upper = bit(own_turn, top) == 1
-    sums = []
-    for first, second in final:
-        sent = jnp.where(upper, second, first).astype(jnp.bfloat16)
-        sums += [jnp.where(upper, first, second), swapped(sent, "turn", top)]
-    return last_sum(*sums)
+    sent = jnp.stack([jnp.where(upper, second, first) for first, second in final])
+    kept = jnp.stack([jnp.where(upper, first, second) for first, second in final])
+    shape = (tile, rows, width)
+    got = swapped(sent.astype(jnp.bfloat16), "turn", top)
+    return last_sum(kept.reshape(shape), got.reshape(shape))
 
 
 def solution(mesh):

time: 50.2 us -> 50.7 us (level)
  other arithmetic: 4.87 us -> 5.93 us
  waiting for transfers between devices: 13.9 us -> 13.3 us
    pallas_call x2, Pallas kernels: 4.61 us -> 5.84 us  [backproject(): pl.pallas_call(functools.partial(image_kernel, (leaf, each, half, beams,...]
    pallas_call x2, Pallas kernels: 5.35 us -> 4.27 us  [compress(): pl.pallas_call(functools.partial(compress_kernel, dims, edge is not None)...]
    another operation x2, other arithmetic: 0.19 us -> 1.24 us  [per_device(): data = jnp.stack([keep.reshape(shape), got.reshape(shape)])]
    ppermute x14 -> x13, waiting for transfers between devices: 13.9 us -> 13.3 us  [swapped(): lax.ppermute(array, axis, [(i, i ^ 1 << bit) for i in range(lax.axis_size...]
    ppermute x14 -> x13, starting transfers between devices: 18.2 us -> 18.1 us  [swapped(): lax.ppermute(array, axis, [(i, i ^ 1 << bit) for i in range(lax.axis_size...]
  transfers between devices with their start and end apart: 14 -> 13, of which waited for: 7 -> 6; matrix products, arithmetic and copies ran while one was open for 12% -> 14% of each run, Pallas kernels for 13% -> 15%
where the time goes in v10:
time: 50.7 us; the launch traced here: 50.6 us
  starting transfers between devices  18.1 us (36%)
  waiting for transfers between devices  13.3 us (26%)
  Pallas kernels  10.8 us (21%)
  other arithmetic  5.93 us (12%)
  local copies, waits for them, and re-layouts  1.84 us (4%)
    ppermute x13, starting transfers between devices, swapped(): lax.ppermute(array, axis, [(i, i ^ 1 << bit) for i in range(lax.axis_size...  18.1 us
    ppermute x13, waiting for transfers between devices, swapped(): lax.ppermute(array, axis, [(i, i ^ 1 << bit) for i in range(lax.axis_size...  13.3 us
    pallas_call x2, Pallas kernels, backproject(): pl.pallas_call(functools.partial(image_kernel, (leaf, each, half, beams,...  5.84 us
    pallas_call x2, Pallas kernels, compress(): pl.pallas_call(functools.partial(compress_kernel, dims, edge is not None)...  4.27 us
    cos x2, other arithmetic, unit(): return (jnp.cos(angle), jnp.sin(angle))  2.27 us
    another operation x2, other arithmetic, per_device(): data = jnp.stack([keep.reshape(shape), got.reshape(shape)])  1.24 us
  transfers between devices with their start and end apart: 13, of which 6 were waited for; matrix products, arithmetic and copies ran while one was open for 14% of the time, Pallas kernels for 15%

profile of v10, /device:TPU:0, one launch (start us, length us, event | category | flops | bytes accessed | tf_op | source)
XLA Modules:
  0.0 50.6 jit_solution(3600520619611971370)
XLA Ops:
  0.0 0.8 %copy-done.1 = bf16[2,128]{1,0:T(2,128)(2,1)S(1)} copy-done((bf16[2,128]{1,0:T(2,128)(2,1)S(1)}, bf16[2,128]{1,0:T(2,128)(2,1)}, u32[]{:S(2)}) %copy-start.1) | copy-done | bytes 536
  0.8 2.3 %compress.2 = (bf16[1,2,1,8,64,256]{5,4,3,2,1,0:T(8,128)(2,1)S(1)}, bf16[1,2,1,8,64,256]{5,4,3,2,1,0:T(8,128)(2,1)S(1)}, bf16[64,256]{1,0:T(8,128)(2,1)S(1)}) custom-call(bf16[2,128]{1,0:T(2,128)(2,1)S(1)} %copy-done.1, bf16[64,64,256]{2,1,0:T(8,128)(2,1)} %echo_ref.3), custom_call_target="tpu_custom_call" | custom-call | flops 536870912 | bytes 2097152 | tf_op jit(solution)/shard_map/compress/pallas_call | solution.py:127
  3.2 3.0 %collective-permute-start = (bf16[1,2,1,8,64,256]{5,4,3,2,1,0:T(8,128)(2,1)S(1)}, bf16[1,2,1,8,64,256]{5,4,3,2,1,0:T(8,128)(2,1)}, u32[]{:S(2)}, u32[]{:S(2)}) collective-permute-start(bf16[1,2,1,8,64,256]{5,4,3,2,1,0:T(8,128)(2,1)S(1)} %get-tuple-element.15), channel_id=1, source_target_pairs={{0,1},{1,0},{2,3},{3,2},{4,5},{5,4},{6,7},{7,6},{8,9},{9,8},{10,11... | collective-permute-start | bytes 1572872 | tf_op jit(solution)/shard_map/ppermute | solution.py:25
  6.2 1.9 %compress.3 = (bf16[1,1,2,8,64,256]{5,4,3,2,1,0:T(8,128)(2,1)S(1)}, bf16[1,1,2,8,64,256]{5,4,3,2,1,0:T(8,128)(2,1)S(1)}, bf16[64,256]{1,0:T(8,128)(2,1)}) custom-call(bf16[2,128]{1,0:T(2,128)(2,1)S(1)} %copy-done.1, bf16[64,64,256]{2,1,0:T(8,128)(2,1)S(1)} %copy-done, bf16[64,256]{1,0:T(8,128)(2,1)S(1)} %get-tuple-element.18.refs_0_), custom_call_target="tpu_custom_call" | custom-call | flops 536870912 | bytes 2097152 | tf_op jit(solution)/shard_map/compress/pallas_call | solution.py:127
  8.1 1.6 %collective-permute-start.4 = (bf16[1,1,2,8,64,256]{5,4,3,2,1,0:T(8,128)(2,1)S(1)}, bf16[1,1,2,8,64,256]{5,4,3,2,1,0:T(8,128)(2,1)S(1)}, u32[]{:S(2)}, u32[]{:S(2)}) collective-permute-start(bf16[1,1,2,8,64,256]{5,4,3,2,1,0:T(8,128)(2,1)S(1)} %get-tuple-element.20), channel_id=1, source_target_pairs={{0,2},{1,3},{2,0},{3,1},{4,6},{5,7},{6,4},{7,5},{8,10},{9,11},{10,... | collective-permute-start | bytes 1572872 | tf_op jit(solution)/shard_map/ppermute | solution.py:25
  9.8 0.2 select_reduce_fusion.1
  10.6 0.1 copy.35
  10.9 0.4 select_reduce_fusion
  11.3 0.5 multiply_convert_fusion.1
  11.8 0.2 fusion.30
  12.2 0.2 fusion.45
  12.7 2.1 %fusion.10 = (f32[2,1,128,512]{3,2,1,0:T(8,128)S(1)}, f32[2,1,128,512]{3,2,1,0:T(8,128)S(1)}) fusion(s32[512]{0:T(512)S(1)} %iota_add_fusion, s32[2,128]{1,0:T(2,128)S(1)} %add_multiply_fusion), kind=kLoop, calls=%fused_computation.33 | loop fusion | flops 1835008 | bytes 1051648 | tf_op jit(solution)/shard_map/cos | solution.py:30
  14.9 3.3 %collective-permute-done = bf16[1,2,1,8,64,256]{5,4,3,2,1,0:T(8,128)(2,1)} collective-permute-done((bf16[1,2,1,8,64,256]{5,4,3,2,1,0:T(8,128)(2,1)S(1)}, bf16[1,2,1,8,64,256]{5,4,3,2,1,0:T(8,128)(2,1)}, u32[]{:S(2)}, u32[]{:S(2)}) %collective-permute-start) | collective-permute-done | bytes 524320 | tf_op jit(solution)/shard_map/ppermute | solution.py:25
  18.2 1.1 %pad_maximum_fusion.data_ref = bf16[2,4,4,64,256]{4,3,2,1,0:T(8,128)(2,1)S(1)} fusion(bf16[1,4,4,64,256]{4,3,2,1,0:T(8,128)(2,1)} %bitcast.1, bf16[1,4,4,64,256]{4,3,2,1,0:T(8,128)(2,1)S(1)} %bitcast.118), kind=kLoop, calls=%fused_computation | loop fusion | flops 524288 | bytes 2097152 | tf_op jit(solution)/shard_map/stack | solution.py:386
  19.4 2.9 %image.2 = (f32[2,4,4,32,256]{4,3,2,1,0:T(8,128)S(1)}, bf16[2,4,4,32,256]{4,3,2,1,0:T(8,128)(2,1)S(1)}) custom-call(bf16[2,4,4,64,256]{4,3,2,1,0:T(8,128)(2,1)S(1)} %pad_maximum_fusion.data_ref, bf16[256,256]{1,0:T(8,128)(2,1)S(1)} %copy.44.steer_ref, bf16[1,128,128]{2,1,0:T(8,128)(2,1)S(1)} %slice.202.interp_ref, f32[4,4,128]{2,1,0:T(4,128)S(1)} %bitcast.121, ...), custom_call_target="tpu_custom_call" | custom-call | flops 402653184 | bytes 2621440 | tf_op jit(solution)/shard_map/image/pallas_call | solution.py:229
  22.5 2.9 %image.3 = (f32[2,4,4,32,256]{4,3,2,1,0:T(8,128)S(1)}, bf16[2,4,4,32,256]{4,3,2,1,0:T(8,128)(2,1)S(1)}) custom-call(bf16[2,4,4,64,256]{4,3,2,1,0:T(8,128)(2,1)S(1)} %pad_maximum_fusion.2.data_ref, bf16[256,256]{1,0:T(8,128)(2,1)S(1)} %copy.45.steer_ref, bf16[1,128,128]{2,1,0:T(8,128)(2,1)S(1)} %slice.202.interp_ref, f32[4,4,128]{2,1,0:T(4,128)S(1)} %bitcast.120, ...), custom_call_target="tpu_custom_call" | custom-call | flops 402653184 | bytes 2621440 | tf_op jit(solution)/shard_map/image/pallas_call | solution.py:229
  25.6 0.6 %collective-permute-start.5 = (bf16[2,4,4,32,256]{4,3,2,1,0:T(8,128)(2,1)S(1)}, bf16[2,4,4,32,256]{4,3,2,1,0:T(8,128)(2,1)S(1)}, u32[]{:S(2)}, u32[]{:S(2)}) collective-permute-start(bf16[2,4,4,32,256]{4,3,2,1,0:T(8,128)(2,1)S(1)} %get-tuple-element.22), channel_id=1, source_target_pairs={{0,8},{8,0},{16,24},{24,16},{1,9},{9,1},{17,25},{25,17},{2,10},{10... | collective-permute-start | bytes 1572872 | tf_op jit(solution)/shard_map/ppermute | solution.py:25
  26.4 1.8 %collective-permute-start.8 = (bf16[1,8,32,256]{3,2,1,0:T(8,128)(2,1)S(1)}, bf16[1,8,32,256]{3,2,1,0:T(8,128)(2,1)S(1)}, u32[]{:S(2)}, u32[]{:S(2)}) collective-permute-start(bf16[1,8,32,256]{3,2,1,0:T(8,128)(2,1)S(1)} %get-tuple-element.37), channel_id=1, source_target_pairs={{0,16},{8,24},{16,0},{24,8},{1,17},{9,25},{17,1},{25,9},{2,18},{10... | collective-permute-start | bytes 393224 | tf_op jit(solution)/shard_map/ppermute | solution.py:25
  28.3 0.4 collective-permute-start.2
  28.8 1.8 %collective-permute-start.6 = (bf16[2,4,32,256]{3,2,1,0:T(8,128)(2,1)S(1)}, bf16[2,4,32,256]{3,2,1,0:T(8,128)(2,1)S(1)}, u32[]{:S(2)}, u32[]{:S(2)}) collective-permute-start(bf16[2,4,32,256]{3,2,1,0:T(8,128)(2,1)S(1)} %get-tuple-element.31), channel_id=1, source_target_pairs={{0,1},{1,0},{2,3},{3,2},{4,5},{5,4},{6,7},{7,6},{8,9},{9,8},{10,11... | collective-permute-start | bytes 393224 | tf_op jit(solution)/shard_map/ppermute | solution.py:25
  30.7 0.4 collective-permute-start.10
  31.1 1.8 %collective-permute-done.8 = bf16[1,8,32,256]{3,2,1,0:T(8,128)(2,1)S(1)} collective-permute-done((bf16[1,8,32,256]{3,2,1,0:T(8,128)(2,1)S(1)}, bf16[1,8,32,256]{3,2,1,0:T(8,128)(2,1)S(1)}, u32[]{:S(2)}, u32[]{:S(2)}) %collective-permute-start.8) | collective-permute-done | bytes 131104 | tf_op jit(solution)/shard_map/ppermute | solution.py:25
  32.8 1.9 %collective-permute-start.9 = (bf16[1,4,32,256]{3,2,1,0:T(8,128)(2,1)S(1)}, bf16[1,4,32,256]{3,2,1,0:T(8,128)(2,1)S(1)}, u32[]{:S(2)}, u32[]{:S(2)}) collective-permute-start(bf16[1,4,32,256]{3,2,1,0:T(8,128)(2,1)S(1)} %fusion.35), channel_id=1, source_target_pairs={{0,2},{1,3},{2,0},{3,1},{4,6},{5,7},{6,4},{7,5},{8,10},{9,11},{10,... | collective-permute-start | bytes 196616 | tf_op jit(solution)/shard_map/ppermute | solution.py:25
  34.7 1.9 %collective-permute-start.3 = (bf16[1,4,32,256]{3,2,1,0:T(8,128)(2,1)S(1)}, bf16[1,4,32,256]{3,2,1,0:T(8,128)(2,1)S(1)}, u32[]{:S(2)}, u32[]{:S(2)}) collective-permute-start(bf16[1,4,32,256]{3,2,1,0:T(8,128)(2,1)S(1)} %fusion.33), channel_id=1, source_target_pairs={{0,2},{1,3},{2,0},{3,1},{4,6},{5,7},{6,4},{7,5},{8,10},{9,11},{10,... | collective-permute-start | bytes 196616 | tf_op jit(solution)/shard_map/ppermute | solution.py:25
  36.6 1.6 %collective-permute-start.7 = (bf16[1,4,32,256]{3,2,1,0:T(8,128)(2,1)S(1)}, bf16[1,4,32,256]{3,2,1,0:T(8,128)(2,1)S(1)}, u32[]{:S(2)}, u32[]{:S(2)}) collective-permute-start(bf16[1,4,32,256]{3,2,1,0:T(8,128)(2,1)S(1)} %fusion.34), channel_id=1, source_target_pairs={{0,16},{8,24},{16,0},{24,8},{1,17},{9,25},{17,1},{25,9},{2,18},{10... | collective-permute-start | bytes 196616 | tf_op jit(solution)/shard_map/ppermute | solution.py:25
  38.2 0.6 %collective-permute-start.11 = (bf16[1,4,32,256]{3,2,1,0:T(8,128)(2,1)S(1)}, bf16[1,4,32,256]{3,2,1,0:T(8,128)(2,1)S(1)}, u32[]{:S(2)}, u32[]{:S(2)}) collective-permute-start(bf16[1,4,32,256]{3,2,1,0:T(8,128)(2,1)S(1)} %fusion.36), channel_id=1, source_target_pairs={{0,16},{8,24},{16,0},{24,8},{1,17},{9,25},{17,1},{25,9},{2,18},{10... | collective-permute-start | bytes 196616 | tf_op jit(solution)/shard_map/ppermute | solution.py:25
  38.8 0.3 collective-permute-done.3
  39.1 1.9 %collective-permute-done.7 = bf16[1,4,32,256]{3,2,1,0:T(8,128)(2,1)S(1)} collective-permute-done((bf16[1,4,32,256]{3,2,1,0:T(8,128)(2,1)S(1)}, bf16[1,4,32,256]{3,2,1,0:T(8,128)(2,1)S(1)}, u32[]{:S(2)}, u32[]{:S(2)}) %collective-permute-start.7) | collective-permute-done | bytes 65568 | tf_op jit(solution)/shard_map/ppermute | solution.py:25
  41.0 1.5 %collective-permute-done.11 = bf16[1,4,32,256]{3,2,1,0:T(8,128)(2,1)S(1)} collective-permute-done((bf16[1,4,32,256]{3,2,1,0:T(8,128)(2,1)S(1)}, bf16[1,4,32,256]{3,2,1,0:T(8,128)(2,1)S(1)}, u32[]{:S(2)}, u32[]{:S(2)}) %collective-permute-start.11) | collective-permute-done | bytes 65568 | tf_op jit(solution)/shard_map/ppermute | solution.py:25
  42.6 2.7 %collective-permute-start.12 = (bf16[2,4,32,256]{3,2,1,0:T(8,128)(2,1)S(1)}, bf16[2,4,32,256]{3,2,1,0:T(8,128)(2,1)S(1)}, u32[]{:S(2)}, u32[]{:S(2)}) collective-permute-start(bf16[2,4,32,256]{3,2,1,0:T(8,128)(2,1)S(1)} %pad_maximum_fusion.5), channel_id=1, source_target_pairs={{0,4},{1,5},{2,6},{3,7},{4,0},{5,1},{6,2},{7,3},{8,12},{9,13},{10,... | collective-permute-start | bytes 393224 | tf_op jit(solution)/shard_map/ppermute | solution.py:25
  45.3 4.5 %collective-permute-done.12 = bf16[2,4,32,256]{3,2,1,0:T(8,128)(2,1)S(1)} collective-permute-done((bf16[2,4,32,256]{3,2,1,0:T(8,128)(2,1)S(1)}, bf16[2,4,32,256]{3,2,1,0:T(8,128)(2,1)S(1)}, u32[]{:S(2)}, u32[]{:S(2)}) %collective-permute-start.12) | collective-permute-done | bytes 131104 | tf_op jit(solution)/shard_map/ppermute | solution.py:25
  49.8 0.7 %last_sum.1 = bf16[32,8,256]{2,1,0:T(8,128)(2,1)} custom-call(f32[8,32,256]{2,1,0:T(8,128)S(1)} %bitcast.116, bf16[8,32,256]{2,1,0:T(8,128)(2,1)S(1)} %bitcast.119), custom_call_target="tpu_custom_call" | custom-call | tf_op jit(solution)/shard_map/last_sum/pallas_call | solution.py:272
  (78 shorter events, 2.4 us)
Async XLA Ops:
  0.0 6.2 %copy-start = (bf16[64,64,256]{2,1,0:T(8,128)(2,1)S(1)}, bf16[64,64,256]{2,1,0:T(8,128)(2,1)}, u32[]{:S(2)}) copy-start(bf16[64,64,256]{2,1,0:T(8,128)(2,1)} %echo_ref.3) | copy-start | bytes 6291460
  0.0 0.8 %copy-start.1 = (bf16[2,128]{1,0:T(2,128)(2,1)S(1)}, bf16[2,128]{1,0:T(2,128)(2,1)}, u32[]{:S(2)}) copy-start(bf16[2,128]{1,0:T(2,128)(2,1)} %chirp_ref.3) | copy-start | bytes 1540
  0.8 9.0 %copy-start.4 = (s32[1,8]{1,0:T(1,128)S(1)}, s32[1,8]{1,0:T(1,128)}, u32[]{:S(2)}) copy-start(s32[1,8]{1,0:T(1,128)} %param.9) | copy-start | bytes 100
  0.8 9.6 %copy-start.2 = (s32[2,2,128,8]{2,3,1,0:T(8,128)S(1)}, s32[2,2,128,8]{2,3,1,0:T(8,128)}, u32[]{:S(2)}) copy-start(s32[2,2,128,8]{2,3,1,0:T(8,128)} %param.8) | copy-start | bytes 49156
  0.8 10.1 %copy-start.3 = (f32[8]{0:T(128)S(1)}, f32[8]{0:T(128)}, u32[]{:S(2)}) copy-start(f32[8]{0:T(128)} %constant.177.clone) | copy-start | bytes 100
  3.2 15.1 %collective-permute-start = (bf16[1,2,1,8,64,256]{5,4,3,2,1,0:T(8,128)(2,1)S(1)}, bf16[1,2,1,8,64,256]{5,4,3,2,1,0:T(8,128)(2,1)}, u32[]{:S(2)}, u32[]{:S(2)}) collective-permute-start(bf16[1,2,1,8,64,256]{5,4,3,2,1,0:T(8,128)(2,1)S(1)} %get-tuple-element.15), channel_id=1, source_target_pairs={{0,1},{1,0},{2,3},{3,2},{4,5},{5,4},{6,7},{7,6},{8,9},{9,8},{10,11... | collective-permute-start | bytes 1572872 | tf_op jit(solution)/shard_map/ppermute | solution.py:25
  8.1 14.3 %collective-permute-start.4 = (bf16[1,1,2,8,64,256]{5,4,3,2,1,0:T(8,128)(2,1)S(1)}, bf16[1,1,2,8,64,256]{5,4,3,2,1,0:T(8,128)(2,1)S(1)}, u32[]{:S(2)}, u32[]{:S(2)}) collective-permute-start(bf16[1,1,2,8,64,256]{5,4,3,2,1,0:T(8,128)(2,1)S(1)} %get-tuple-element.20), channel_id=1, source_target_pairs={{0,2},{1,3},{2,0},{3,1},{4,6},{5,7},{6,4},{7,5},{8,10},{9,11},{10,... | collective-permute-start | bytes 1572872 | tf_op jit(solution)/shard_map/ppermute | solution.py:25
  22.3 4.0 %collective-permute-start.1 = (bf16[2,4,4,32,256]{4,3,2,1,0:T(8,128)(2,1)S(1)}, bf16[2,4,4,32,256]{4,3,2,1,0:T(8,128)(2,1)S(1)}, u32[]{:S(2)}, u32[]{:S(2)}) collective-permute-start(bf16[2,4,4,32,256]{4,3,2,1,0:T(8,128)(2,1)S(1)} %get-tuple-element.17), channel_id=1, source_target_pairs={{0,8},{8,0},{16,24},{24,16},{1,9},{9,1},{17,25},{25,17},{2,10},{10... | collective-permute-start | bytes 1572872 | tf_op jit(solution)/shard_map/ppermute | solution.py:25
  25.6 3.0 %collective-permute-start.5 = (bf16[2,4,4,32,256]{4,3,2,1,0:T(8,128)(2,1)S(1)}, bf16[2,4,4,32,256]{4,3,2,1,0:T(8,128)(2,1)S(1)}, u32[]{:S(2)}, u32[]{:S(2)}) collective-permute-start(bf16[2,4,4,32,256]{4,3,2,1,0:T(8,128)(2,1)S(1)} %get-tuple-element.22), channel_id=1, source_target_pairs={{0,8},{8,0},{16,24},{24,16},{1,9},{9,1},{17,25},{25,17},{2,10},{10... | collective-permute-start | bytes 1572872 | tf_op jit(solution)/shard_map/ppermute | solution.py:25
  26.4 6.4 %collective-permute-start.8 = (bf16[1,8,32,256]{3,2,1,0:T(8,128)(2,1)S(1)}, bf16[1,8,32,256]{3,2,1,0:T(8,128)(2,1)S(1)}, u32[]{:S(2)}, u32[]{:S(2)}) collective-permute-start(bf16[1,8,32,256]{3,2,1,0:T(8,128)(2,1)S(1)} %get-tuple-element.37), channel_id=1, source_target_pairs={{0,16},{8,24},{16,0},{24,8},{1,17},{9,25},{17,1},{25,9},{2,18},{10... | collective-permute-start | bytes 393224 | tf_op jit(solution)/shard_map/ppermute | solution.py:25
  28.3 6.5 %collective-permute-start.2 = (bf16[1,8,32,256]{3,2,1,0:T(8,128)(2,1)S(1)}, bf16[1,8,32,256]{3,2,1,0:T(8,128)(2,1)S(1)}, u32[]{:S(2)}, u32[]{:S(2)}) collective-permute-start(bf16[1,8,32,256]{3,2,1,0:T(8,128)(2,1)S(1)} %get-tuple-element.33), channel_id=1, source_target_pairs={{0,16},{8,24},{16,0},{24,8},{1,17},{9,25},{17,1},{25,9},{2,18},{10... | collective-permute-start | bytes 393224 | tf_op jit(solution)/shard_map/ppermute | solution.py:25
  28.8 7.8 %collective-permute-start.6 = (bf16[2,4,32,256]{3,2,1,0:T(8,128)(2,1)S(1)}, bf16[2,4,32,256]{3,2,1,0:T(8,128)(2,1)S(1)}, u32[]{:S(2)}, u32[]{:S(2)}) collective-permute-start(bf16[2,4,32,256]{3,2,1,0:T(8,128)(2,1)S(1)} %get-tuple-element.31), channel_id=1, source_target_pairs={{0,1},{1,0},{2,3},{3,2},{4,5},{5,4},{6,7},{7,6},{8,9},{9,8},{10,11... | collective-permute-start | bytes 393224 | tf_op jit(solution)/shard_map/ppermute | solution.py:25
  30.7 7.5 %collective-permute-start.10 = (bf16[2,4,32,256]{3,2,1,0:T(8,128)(2,1)S(1)}, bf16[2,4,32,256]{3,2,1,0:T(8,128)(2,1)S(1)}, u32[]{:S(2)}, u32[]{:S(2)}) collective-permute-start(bf16[2,4,32,256]{3,2,1,0:T(8,128)(2,1)S(1)} %get-tuple-element.35), channel_id=1, source_target_pairs={{0,1},{1,0},{2,3},{3,2},{4,5},{5,4},{6,7},{7,6},{8,9},{9,8},{10,11... | collective-permute-start | bytes 393224 | tf_op jit(solution)/shard_map/ppermute | solution.py:25
  32.8 8.2 %collective-permute-start.9 = (bf16[1,4,32,256]{3,2,1,0:T(8,128)(2,1)S(1)}, bf16[1,4,32,256]{3,2,1,0:T(8,128)(2,1)S(1)}, u32[]{:S(2)}, u32[]{:S(2)}) collective-permute-start(bf16[1,4,32,256]{3,2,1,0:T(8,128)(2,1)S(1)} %fusion.35), channel_id=1, source_target_pairs={{0,2},{1,3},{2,0},{3,1},{4,6},{5,7},{6,4},{7,5},{8,10},{9,11},{10,... | collective-permute-start | bytes 196616 | tf_op jit(solution)/shard_map/ppermute | solution.py:25
  34.7 4.3 %collective-permute-start.3 = (bf16[1,4,32,256]{3,2,1,0:T(8,128)(2,1)S(1)}, bf16[1,4,32,256]{3,2,1,0:T(8,128)(2,1)S(1)}, u32[]{:S(2)}, u32[]{:S(2)}) collective-permute-start(bf16[1,4,32,256]{3,2,1,0:T(8,128)(2,1)S(1)} %fusion.33), channel_id=1, source_target_pairs={{0,2},{1,3},{2,0},{3,1},{4,6},{5,7},{6,4},{7,5},{8,10},{9,11},{10,... | collective-permute-start | bytes 196616 | tf_op jit(solution)/shard_map/ppermute | solution.py:25
  36.6 4.3 %collective-permute-start.7 = (bf16[1,4,32,256]{3,2,1,0:T(8,128)(2,1)S(1)}, bf16[1,4,32,256]{3,2,1,0:T(8,128)(2,1)S(1)}, u32[]{:S(2)}, u32[]{:S(2)}) collective-permute-start(bf16[1,4,32,256]{3,2,1,0:T(8,128)(2,1)S(1)} %fusion.34), channel_id=1, source_target_pairs={{0,16},{8,24},{16,0},{24,8},{1,17},{9,25},{17,1},{25,9},{2,18},{10... | collective-permute-start | bytes 196616 | tf_op jit(solution)/shard_map/ppermute | solution.py:25
  38.2 4.3 %collective-permute-start.11 = (bf16[1,4,32,256]{3,2,1,0:T(8,128)(2,1)S(1)}, bf16[1,4,32,256]{3,2,1,0:T(8,128)(2,1)S(1)}, u32[]{:S(2)}, u32[]{:S(2)}) collective-permute-start(bf16[1,4,32,256]{3,2,1,0:T(8,128)(2,1)S(1)} %fusion.36), channel_id=1, source_target_pairs={{0,16},{8,24},{16,0},{24,8},{1,17},{9,25},{17,1},{25,9},{2,18},{10... | collective-permute-start | bytes 196616 | tf_op jit(solution)/shard_map/ppermute | solution.py:25
  42.6 7.2 %collective-permute-start.12 = (bf16[2,4,32,256]{3,2,1,0:T(8,128)(2,1)S(1)}, bf16[2,4,32,256]{3,2,1,0:T(8,128)(2,1)S(1)}, u32[]{:S(2)}, u32[]{:S(2)}) collective-permute-start(bf16[2,4,32,256]{3,2,1,0:T(8,128)(2,1)S(1)} %pad_maximum_fusion.5), channel_id=1, source_target_pairs={{0,4},{1,5},{2,6},{3,7},{4,0},{5,1},{6,2},{7,3},{8,12},{9,13},{10,... | collective-permute-start | bytes 393224 | tf_op jit(solution)/shard_map/ppermute | solution.py:25

commit v11 on v10

--- a/solution.py
+++ b/solution.py
@@ -10,7 +10,7 @@
 
 WEIGHTS = (-1.0 / 32, 3.0 / 32, -7.0 / 32, 21.0 / 32, 21.0 / 32, -7.0 / 32, 3.0 / 32, -1.0 / 32)
 PERIOD = 4096
-VMEM_BYTES = 52 * 2**20
+VMEM_BYTES = 56 * 2**20
 
 
 def bits_of(count):
@@ -33,7 +33,7 @@
 def compress_kernel(dims, has_edge, chirp_ref, echo_ref, *refs):
     tile, pulses, half, near_chain, far = dims
     edge_ref, refs = (refs[0], refs[1:]) if has_edge else (None, refs)
-    keep_ref, send_ref, edge_out, weights, rows_ref, carry = refs
+    keep_ref, send_ref, weights, rows_ref, carry = refs
     blocks = 2 * tile
     pitch = blocks + 1
     mids = pl.num_programs(2)
@@ -59,7 +59,15 @@
             low = jnp.concatenate([-im, re], axis=1)
             full = jnp.concatenate([top, low], axis=0)
             weights[m * 2 * half : (m + 1) * 2 * half, :] = full.astype(jnp.bfloat16)
-        carry[...] = edge_ref[...] if has_edge else jnp.zeros_like(carry)
+        if has_edge:
+            for p in range(pulses):
+                for c in range(2):
+                    first = edge_ref[p, :, c * half : (c + 1) * half].astype(jnp.float32)
+                    rows_ref[c, p : p + 1, :] = first[:1]
+            edges = [rows_ref[c, :pulses, :] for c in range(2)]
+            carry[...] = jnp.concatenate(edges, axis=1).astype(jnp.bfloat16)
+        else:
+            carry[...] = jnp.zeros_like(carry)
 
     for p in range(pulses):
         for c in range(2):
@@ -79,7 +87,6 @@
         preferred_element_type=jnp.float32,
     ).astype(jnp.bfloat16)
     carry[...] = turned[0]
-    edge_out[...] = turned[0]
 
     def block(b):
         return total[b * pulses : (b + 1) * pulses]
@@ -91,7 +98,7 @@
             def _(side=side):
                 for b in range(blocks):
                     ref = keep_ref if b // tile == side else send_ref
-                    ref[spot_h, spot_v, spot_m, b % tile] = block(b)
+                    ref[0, 0, 0, b % tile] = block(b)
     else:
         for ref, mine in ((keep_ref, 0), (send_ref, 1)):
 
@@ -101,17 +108,23 @@
                     ref[spot_h, spot_m, b // tile ^ own_u, b % tile] = block(b)
 
 
-def compress(chirp, edge, echoes, high, mids, near_chain, far, first_high):
+def compress(chirp, echoes, high, mids, near_chain, far, first_high):
     pulses, blocks, width = echoes.shape
     half = width // 2
     tile = blocks // lax.axis_size("turn")
     if near_chain:
         shape = (high, 2, mids, tile, pulses, width)
+
+        def place(h, v, m):
+            turn = lax.axis_index("turn")
+            spot_h = (high - 1 - h) ^ (turn >> far + 1 & high - 1)
+            spot_m = (mids - 1 - m) ^ (turn >> 1 & mids - 1)
+            return spot_h, (1 - v) ^ bit(turn, far), spot_m, 0, 0, 0
+
+        spec = pl.BlockSpec((1, 1, 1) + shape[3:], place)
     else:
         shape = (high, mids, 2, tile, pulses, width)
-    spec = pl.BlockSpec(shape, lambda h, v, m: (0, 0, 0, 0, 0, 0))
-    edge_spec = pl.BlockSpec((pulses, width), lambda h, v, m: (0, 0))
-
+        spec = pl.BlockSpec(shape, lambda h, v, m: (0, 0, 0, 0, 0, 0))
     def chunk(h, v, m):
         return 0, ((first_high + high - 1 - h) * 2 + 1 - v) * mids + mids - 1 - m, 0
 
@@ -120,18 +133,18 @@
         pl.BlockSpec((pulses, 2 * tile, width), chunk),
     ]
     operands = [chirp, echoes]
-    if edge is not None:
-        in_specs.append(edge_spec)
-        operands.append(edge)
+    has_edge = not near_chain
+    if has_edge:
+        after = (first_high + high) * 2 * mids
+        in_specs.append(pl.BlockSpec((pulses, 2 * tile, width), lambda h, v, m: (0, after, 0)))
+        operands.append(echoes)
     dims = (tile, pulses, half, near_chain, far)
     return pl.pallas_call(
-        functools.partial(compress_kernel, dims, edge is not None),
+        functools.partial(compress_kernel, dims, has_edge),
         grid=(high, 2, mids),
         in_specs=in_specs,
-        out_specs=[spec, spec, edge_spec],
-        out_shape=[
-            jax.ShapeDtypeStruct(s, jnp.bfloat16) for s in (shape, shape, (pulses, width))
-        ],
+        out_specs=[spec, spec],
+        out_shape=[jax.ShapeDtypeStruct(shape, jnp.bfloat16)] * 2,
         scratch_shapes=[
             pltpu.VMEM((2 * width, width), jnp.bfloat16),
             pltpu.VMEM((2, pulses * (2 * tile + 1), half), jnp.float32),
@@ -201,9 +214,14 @@
                         else:
                             out_send[g - leaf // 2, 0, at + i] = both.astype(jnp.bfloat16)
                         continue
-                    pieces.append(jnp.concatenate(both, axis=1).astype(jnp.bfloat16))
+                    both = jnp.concatenate(both, axis=1)
+                    big = both.astype(jnp.bfloat16)
+                    low = (both - big.astype(jnp.float32)).astype(jnp.bfloat16)
+                    pieces.append((big, low))
                 if pieces:
-                    columns.append(jnp.concatenate(pieces, axis=0))
+                    columns.append(
+                        jnp.concatenate([p[0] for p in pieces] + [p[1] for p in pieces], axis=0)
+                    )
             if columns:
                 moved = jnp.dot(
                     interp_ref[level],
@@ -325,9 +343,9 @@
     rows = beams // leaf
     own_leaf, own_turn = lax.axis_index("leaf"), lax.axis_index("turn")
 
-    keep_y, send_y, edge = compress(chirp, None, echoes, high, mids, True, far, high)
+    keep_y, send_y = compress(chirp, echoes, high, mids, True, far, high)
     got_y = swapped(send_y, "turn", 0)
-    keep_z, send_z, _ = compress(chirp, edge, echoes, high, mids, False, far, 0)
+    keep_z, send_z = compress(chirp, echoes, high, mids, False, far, 0)
     got_z = swapped(send_z, "turn", far)
 
     own_sides = [bit(own_leaf, level) for level in range(levels)]
@@ -348,7 +366,7 @@
         axis=0,
     )
     matrices = interpolation(jnp.stack(own_taps), beams)
-    interp = matrices[1:].astype(jnp.bfloat16)
+    interp = jnp.concatenate([matrices[1:]] * 2, axis=-1).astype(jnp.bfloat16)
     scale = 1.0 / math.sqrt(2.0 * slots.shape[1] * pulses)
     wanted = own_turn ^ jnp.array([0, 1, 1 << far], jnp.int32)
     picked = jnp.arange(slots.shape[1], dtype=jnp.int32) == wanted[:, None]

time: 50.7 us -> 50.4 us (level)
  waiting for transfers between devices: 13.3 us -> 15 us
  starting transfers between devices: 18.1 us -> 16.5 us
  local copies, waits for them, and re-layouts: 1.84 us -> 3.33 us
  other arithmetic: 5.93 us -> 4.93 us
  Pallas kernels: 10.8 us -> 9.85 us
    ppermute x13, waiting for transfers between devices: 13.3 us -> 15 us  [swapped(): lax.ppermute(array, axis, [(i, i ^ 1 << bit) for i in range(lax.axis_size...]
    ppermute x13, starting transfers between devices: 18.1 us -> 16.5 us  [swapped(): lax.ppermute(array, axis, [(i, i ^ 1 << bit) for i in range(lax.axis_size...]
    unnamed x14 -> x16, local copies, waits for them, and re-layouts: 0.94 us -> 2.39 us
    pallas_call x2, Pallas kernels: 5.84 us -> 4.61 us  [backproject(): pl.pallas_call(functools.partial(image_kernel, (leaf, each, half, beams,...]
    another operation x2, other arithmetic: 1.24 us -> 0.19 us  [per_device(): data = jnp.stack([keep.reshape(shape), got.reshape(shape)])]
  transfers between devices with their start and end apart: 13 -> 13, of which waited for: 6 -> 9; matrix products, arithmetic and copies ran while one was open for 14% -> 12% of each run, Pallas kernels for 15% -> 15%
where the time goes in v11:
time: 50.4 us; the launch traced here: 50.2 us
  starting transfers between devices  16.5 us (33%)
  waiting for transfers between devices  15 us (30%)
  Pallas kernels  9.85 us (20%)
  other arithmetic  4.93 us (10%)
  local copies, waits for them, and re-layouts  3.33 us (7%)
    ppermute x13, starting transfers between devices, swapped(): lax.ppermute(array, axis, [(i, i ^ 1 << bit) for i in range(lax.axis_size...  16.5 us
    ppermute x13, waiting for transfers between devices, swapped(): lax.ppermute(array, axis, [(i, i ^ 1 << bit) for i in range(lax.axis_size...  15 us
    pallas_call x2, Pallas kernels, backproject(): pl.pallas_call(functools.partial(image_kernel, (leaf, each, half, beams,...  4.61 us
    pallas_call x2, Pallas kernels, compress(): pl.pallas_call(functools.partial(compress_kernel, dims, has_edge), grid=(...  4.5 us
    unnamed x16, local copies, waits for them, and re-layouts  2.39 us
    cos x2, other arithmetic, unit(): return (jnp.cos(angle), jnp.sin(angle))  2.27 us
  transfers between devices with their start and end apart: 13, of which 9 were waited for; matrix products, arithmetic and copies ran while one was open for 12% of the time, Pallas kernels for 15%

profile of v11, /device:TPU:0, one launch (start us, length us, event | category | flops | bytes accessed | tf_op | source)
XLA Modules:
  0.0 50.2 jit_solution(15833220681699286780)
XLA Ops:
  0.0 1.6 %copy-done = bf16[64,64,256]{2,1,0:T(8,128)(2,1)S(1)} copy-done((bf16[64,64,256]{2,1,0:T(8,128)(2,1)S(1)}, bf16[64,64,256]{2,1,0:T(8,128)(2,1)}, u32[]{:S(2)}) %copy-start) | copy-done | bytes 2097176
  1.6 0.7 %copy-done.1 = bf16[2,128]{1,0:T(2,128)(2,1)S(1)} copy-done((bf16[2,128]{1,0:T(2,128)(2,1)S(1)}, bf16[2,128]{1,0:T(2,128)(2,1)}, u32[]{:S(2)}) %copy-start.1) | copy-done | bytes 536
  2.2 1.4 %compress.3 = (bf16[1,1,2,8,64,256]{5,4,3,2,1,0:T(8,128)(2,1)S(1)}, bf16[1,1,2,8,64,256]{5,4,3,2,1,0:T(8,128)(2,1)S(1)}) custom-call(bf16[2,128]{1,0:T(2,128)(2,1)S(1)} %copy-done.1, bf16[64,64,256]{2,1,0:T(8,128)(2,1)S(1)} %copy-done, bf16[64,64,256]{2,1,0:T(8,128)(2,1)S(1)} %copy-done), custom_call_target="tpu_custom_call" | custom-call | flops 536870912 | bytes 2097152 | tf_op jit(solution)/shard_map/compress/pallas_call | solution.py:142
  3.7 3.1 %collective-permute-start.4 = (bf16[1,1,2,8,64,256]{5,4,3,2,1,0:T(8,128)(2,1)S(1)}, bf16[1,1,2,8,64,256]{5,4,3,2,1,0:T(8,128)(2,1)S(1)}, u32[]{:S(2)}, u32[]{:S(2)}) collective-permute-start(bf16[1,1,2,8,64,256]{5,4,3,2,1,0:T(8,128)(2,1)S(1)} %get-tuple-element.18), channel_id=1, source_target_pairs={{0,2},{1,3},{2,0},{3,1},{4,6},{5,7},{6,4},{7,5},{8,10},{9,11},{10,... | collective-permute-start | bytes 1572872 | tf_op jit(solution)/shard_map/ppermute | solution.py:25
  6.8 3.1 %compress.2 = (bf16[1,2,1,8,64,256]{5,4,3,2,1,0:T(8,128)(2,1)}, bf16[1,2,1,8,64,256]{5,4,3,2,1,0:T(8,128)(2,1)}) custom-call(bf16[2,128]{1,0:T(2,128)(2,1)} %chirp_ref.3, bf16[64,64,256]{2,1,0:T(8,128)(2,1)} %refs_0_.1), custom_call_target="tpu_custom_call" | custom-call | flops 536870912 | bytes 2097152 | tf_op jit(solution)/shard_map/compress/pallas_call | solution.py:142
  9.9 1.5 %collective-permute-start = (bf16[1,2,1,8,64,256]{5,4,3,2,1,0:T(8,128)(2,1)}, bf16[1,2,1,8,64,256]{5,4,3,2,1,0:T(8,128)(2,1)S(1)}, u32[]{:S(2)}, u32[]{:S(2)}) collective-permute-start(bf16[1,2,1,8,64,256]{5,4,3,2,1,0:T(8,128)(2,1)} %get-tuple-element.14), channel_id=1, source_target_pairs={{0,1},{1,0},{2,3},{3,2},{4,5},{5,4},{6,7},{7,6},{8,9},{9,8},{10,11... | collective-permute-start | bytes 1572872 | tf_op jit(solution)/shard_map/ppermute | solution.py:25
  11.5 0.2 select_reduce_fusion.1
  12.6 0.4 select_reduce_fusion
  13.0 0.5 multiply_convert_fusion.1
  13.5 0.2 fusion.30
  14.4 2.1 %fusion.10 = (f32[2,1,128,512]{3,2,1,0:T(8,128)S(1)}, f32[2,1,128,512]{3,2,1,0:T(8,128)S(1)}) fusion(s32[512]{0:T(512)S(1)} %iota_add_fusion, s32[2,128]{1,0:T(2,128)S(1)} %add_multiply_fusion), kind=kLoop, calls=%fused_computation.33 | loop fusion | flops 1835008 | bytes 1051648 | tf_op jit(solution)/shard_map/cos | solution.py:30
  16.6 2.1 %collective-permute-done.4 = bf16[1,1,2,8,64,256]{5,4,3,2,1,0:T(8,128)(2,1)S(1)} collective-permute-done((bf16[1,1,2,8,64,256]{5,4,3,2,1,0:T(8,128)(2,1)S(1)}, bf16[1,1,2,8,64,256]{5,4,3,2,1,0:T(8,128)(2,1)S(1)}, u32[]{:S(2)}, u32[]{:S(2)}) %collective-permute-start.4) | collective-permute-done | bytes 524320 | tf_op jit(solution)/shard_map/ppermute | solution.py:25
  18.8 2.3 %image.3 = (f32[2,4,4,32,256]{4,3,2,1,0:T(8,128)S(1)}, bf16[2,4,4,32,256]{4,3,2,1,0:T(8,128)(2,1)S(1)}) custom-call(bf16[2,4,4,64,256]{4,3,2,1,0:T(8,128)(2,1)S(1)} %pad_maximum_fusion.2.data_ref, bf16[256,256]{1,0:T(8,128)(2,1)S(1)} %copy.45.steer_ref, bf16[1,128,256]{2,1,0:T(8,128)(2,1)S(1)} %pad_maximum_fusion.6.interp_ref, f32[4,4,128]{2,1,0:T(4,128)S(1)} %bitcast.120, ...), custom_call_target="tpu_custom_call" | custom-call | flops 402653184 | bytes 2621440 | tf_op jit(solution)/shard_map/image/pallas_call | solution.py:247
  21.4 2.1 %collective-permute-done = bf16[1,2,1,8,64,256]{5,4,3,2,1,0:T(8,128)(2,1)S(1)} collective-permute-done((bf16[1,2,1,8,64,256]{5,4,3,2,1,0:T(8,128)(2,1)}, bf16[1,2,1,8,64,256]{5,4,3,2,1,0:T(8,128)(2,1)S(1)}, u32[]{:S(2)}, u32[]{:S(2)}) %collective-permute-start) | collective-permute-done | bytes 524320 | tf_op jit(solution)/shard_map/ppermute | solution.py:25
  23.6 2.3 %image.2 = (f32[2,4,4,32,256]{4,3,2,1,0:T(8,128)S(1)}, bf16[2,4,4,32,256]{4,3,2,1,0:T(8,128)(2,1)S(1)}) custom-call(bf16[2,4,4,64,256]{4,3,2,1,0:T(8,128)(2,1)S(1)} %pad_maximum_fusion.data_ref, bf16[256,256]{1,0:T(8,128)(2,1)S(1)} %copy.44.steer_ref, bf16[1,128,256]{2,1,0:T(8,128)(2,1)S(1)} %pad_maximum_fusion.6.interp_ref, f32[4,4,128]{2,1,0:T(4,128)S(1)} %bitcast.119, ...), custom_call_target="tpu_custom_call" | custom-call | flops 402653184 | bytes 2621440 | tf_op jit(solution)/shard_map/image/pallas_call | solution.py:247
  26.3 1.6 %collective-permute-start.6 = (bf16[2,4,32,256]{3,2,1,0:T(8,128)(2,1)S(1)}, bf16[2,4,32,256]{3,2,1,0:T(8,128)(2,1)S(1)}, u32[]{:S(2)}, u32[]{:S(2)}) collective-permute-start(bf16[2,4,32,256]{3,2,1,0:T(8,128)(2,1)S(1)} %get-tuple-element.29), channel_id=1, source_target_pairs={{0,1},{1,0},{2,3},{3,2},{4,5},{5,4},{6,7},{7,6},{8,9},{9,8},{10,11... | collective-permute-start | bytes 393224 | tf_op jit(solution)/shard_map/ppermute | solution.py:25
  28.0 0.6 %collective-permute-start.10 = (bf16[2,4,32,256]{3,2,1,0:T(8,128)(2,1)S(1)}, bf16[2,4,32,256]{3,2,1,0:T(8,128)(2,1)S(1)}, u32[]{:S(2)}, u32[]{:S(2)}) collective-permute-start(bf16[2,4,32,256]{3,2,1,0:T(8,128)(2,1)S(1)} %get-tuple-element.33), channel_id=1, source_target_pairs={{0,1},{1,0},{2,3},{3,2},{4,5},{5,4},{6,7},{7,6},{8,9},{9,8},{10,11... | collective-permute-start | bytes 393224 | tf_op jit(solution)/shard_map/ppermute | solution.py:25
  28.7 1.6 %collective-permute-start.8 = (bf16[1,8,32,256]{3,2,1,0:T(8,128)(2,1)S(1)}, bf16[1,8,32,256]{3,2,1,0:T(8,128)(2,1)S(1)}, u32[]{:S(2)}, u32[]{:S(2)}) collective-permute-start(bf16[1,8,32,256]{3,2,1,0:T(8,128)(2,1)S(1)} %get-tuple-element.35), channel_id=1, source_target_pairs={{0,16},{8,24},{16,0},{24,8},{1,17},{9,25},{17,1},{25,9},{2,18},{10... | collective-permute-start | bytes 393224 | tf_op jit(solution)/shard_map/ppermute | solution.py:25
  30.3 0.6 %collective-permute-start.2 = (bf16[1,8,32,256]{3,2,1,0:T(8,128)(2,1)S(1)}, bf16[1,8,32,256]{3,2,1,0:T(8,128)(2,1)S(1)}, u32[]{:S(2)}, u32[]{:S(2)}) collective-permute-start(bf16[1,8,32,256]{3,2,1,0:T(8,128)(2,1)S(1)} %get-tuple-element.31), channel_id=1, source_target_pairs={{0,16},{8,24},{16,0},{24,8},{1,17},{9,25},{17,1},{25,9},{2,18},{10... | collective-permute-start | bytes 393224 | tf_op jit(solution)/shard_map/ppermute | solution.py:25
  30.9 1.7 %collective-permute-done.6 = bf16[2,4,32,256]{3,2,1,0:T(8,128)(2,1)S(1)} collective-permute-done((bf16[2,4,32,256]{3,2,1,0:T(8,128)(2,1)S(1)}, bf16[2,4,32,256]{3,2,1,0:T(8,128)(2,1)S(1)}, u32[]{:S(2)}, u32[]{:S(2)}) %collective-permute-start.6) | collective-permute-done | bytes 131104 | tf_op jit(solution)/shard_map/ppermute | solution.py:25
  32.6 1.6 %collective-permute-start.7 = (bf16[1,4,32,256]{3,2,1,0:T(8,128)(2,1)S(1)}, bf16[1,4,32,256]{3,2,1,0:T(8,128)(2,1)S(1)}, u32[]{:S(2)}, u32[]{:S(2)}) collective-permute-start(bf16[1,4,32,256]{3,2,1,0:T(8,128)(2,1)S(1)} %fusion.34), channel_id=1, source_target_pairs={{0,16},{8,24},{16,0},{24,8},{1,17},{9,25},{17,1},{25,9},{2,18},{10... | collective-permute-start | bytes 196616 | tf_op jit(solution)/shard_map/ppermute | solution.py:25
  34.2 0.8 %collective-permute-done.10 = bf16[2,4,32,256]{3,2,1,0:T(8,128)(2,1)S(1)} collective-permute-done((bf16[2,4,32,256]{3,2,1,0:T(8,128)(2,1)S(1)}, bf16[2,4,32,256]{3,2,1,0:T(8,128)(2,1)S(1)}, u32[]{:S(2)}, u32[]{:S(2)}) %collective-permute-start.10) | collective-permute-done | bytes 131104 | tf_op jit(solution)/shard_map/ppermute | solution.py:25
  35.1 1.6 %collective-permute-start.11 = (bf16[1,4,32,256]{3,2,1,0:T(8,128)(2,1)S(1)}, bf16[1,4,32,256]{3,2,1,0:T(8,128)(2,1)S(1)}, u32[]{:S(2)}, u32[]{:S(2)}) collective-permute-start(bf16[1,4,32,256]{3,2,1,0:T(8,128)(2,1)S(1)} %fusion.36), channel_id=1, source_target_pairs={{0,16},{8,24},{16,0},{24,8},{1,17},{9,25},{17,1},{25,9},{2,18},{10... | collective-permute-start | bytes 196616 | tf_op jit(solution)/shard_map/ppermute | solution.py:25
  36.6 0.5 %collective-permute-start.9 = (bf16[1,4,32,256]{3,2,1,0:T(8,128)(2,1)S(1)}, bf16[1,4,32,256]{3,2,1,0:T(8,128)(2,1)S(1)}, u32[]{:S(2)}, u32[]{:S(2)}) collective-permute-start(bf16[1,4,32,256]{3,2,1,0:T(8,128)(2,1)S(1)} %fusion.35), channel_id=1, source_target_pairs={{0,2},{1,3},{2,0},{3,1},{4,6},{5,7},{6,4},{7,5},{8,10},{9,11},{10,... | collective-permute-start | bytes 196616 | tf_op jit(solution)/shard_map/ppermute | solution.py:25
  37.2 0.5 %collective-permute-done.2 = bf16[1,8,32,256]{3,2,1,0:T(8,128)(2,1)S(1)} collective-permute-done((bf16[1,8,32,256]{3,2,1,0:T(8,128)(2,1)S(1)}, bf16[1,8,32,256]{3,2,1,0:T(8,128)(2,1)S(1)}, u32[]{:S(2)}, u32[]{:S(2)}) %collective-permute-start.2) | collective-permute-done | bytes 131104 | tf_op jit(solution)/shard_map/ppermute | solution.py:25
  37.7 1.1 %collective-permute-start.3 = (bf16[1,4,32,256]{3,2,1,0:T(8,128)(2,1)S(1)}, bf16[1,4,32,256]{3,2,1,0:T(8,128)(2,1)S(1)}, u32[]{:S(2)}, u32[]{:S(2)}) collective-permute-start(bf16[1,4,32,256]{3,2,1,0:T(8,128)(2,1)S(1)} %fusion.33), channel_id=1, source_target_pairs={{0,2},{1,3},{2,0},{3,1},{4,6},{5,7},{6,4},{7,5},{8,10},{9,11},{10,... | collective-permute-start | bytes 196616 | tf_op jit(solution)/shard_map/ppermute | solution.py:25
  38.8 0.9 %collective-permute-done.11 = bf16[1,4,32,256]{3,2,1,0:T(8,128)(2,1)S(1)} collective-permute-done((bf16[1,4,32,256]{3,2,1,0:T(8,128)(2,1)S(1)}, bf16[1,4,32,256]{3,2,1,0:T(8,128)(2,1)S(1)}, u32[]{:S(2)}, u32[]{:S(2)}) %collective-permute-start.11) | collective-permute-done | bytes 65568 | tf_op jit(solution)/shard_map/ppermute | solution.py:25
  39.7 1.3 %collective-permute-done.9 = bf16[1,4,32,256]{3,2,1,0:T(8,128)(2,1)S(1)} collective-permute-done((bf16[1,4,32,256]{3,2,1,0:T(8,128)(2,1)S(1)}, bf16[1,4,32,256]{3,2,1,0:T(8,128)(2,1)S(1)}, u32[]{:S(2)}, u32[]{:S(2)}) %collective-permute-start.9) | collective-permute-done | bytes 65568 | tf_op jit(solution)/shard_map/ppermute | solution.py:25
  41.0 1.0 %collective-permute-done.3 = bf16[1,4,32,256]{3,2,1,0:T(8,128)(2,1)S(1)} collective-permute-done((bf16[1,4,32,256]{3,2,1,0:T(8,128)(2,1)S(1)}, bf16[1,4,32,256]{3,2,1,0:T(8,128)(2,1)S(1)}, u32[]{:S(2)}, u32[]{:S(2)}) %collective-permute-start.3) | collective-permute-done | bytes 65568 | tf_op jit(solution)/shard_map/ppermute | solution.py:25
  42.1 2.7 %collective-permute-start.12 = (bf16[2,4,32,256]{3,2,1,0:T(8,128)(2,1)S(1)}, bf16[2,4,32,256]{3,2,1,0:T(8,128)(2,1)S(1)}, u32[]{:S(2)}, u32[]{:S(2)}) collective-permute-start(bf16[2,4,32,256]{3,2,1,0:T(8,128)(2,1)S(1)} %pad_maximum_fusion.5), channel_id=1, source_target_pairs={{0,4},{1,5},{2,6},{3,7},{4,0},{5,1},{6,2},{7,3},{8,12},{9,13},{10,... | collective-permute-start | bytes 393224 | tf_op jit(solution)/shard_map/ppermute | solution.py:25
  44.8 4.7 %collective-permute-done.12 = bf16[2,4,32,256]{3,2,1,0:T(8,128)(2,1)S(1)} collective-permute-done((bf16[2,4,32,256]{3,2,1,0:T(8,128)(2,1)S(1)}, bf16[2,4,32,256]{3,2,1,0:T(8,128)(2,1)S(1)}, u32[]{:S(2)}, u32[]{:S(2)}) %collective-permute-start.12) | collective-permute-done | bytes 131104 | tf_op jit(solution)/shard_map/ppermute | solution.py:25
  49.5 0.7 %last_sum.1 = bf16[32,8,256]{2,1,0:T(8,128)(2,1)} custom-call(f32[8,32,256]{2,1,0:T(8,128)S(1)} %bitcast.116, bf16[8,32,256]{2,1,0:T(8,128)(2,1)S(1)} %bitcast.118), custom_call_target="tpu_custom_call" | custom-call | tf_op jit(solution)/shard_map/last_sum/pallas_call | solution.py:290
  (81 shorter events, 3.0 us)
Async XLA Ops:
  0.0 1.6 %copy-start = (bf16[64,64,256]{2,1,0:T(8,128)(2,1)S(1)}, bf16[64,64,256]{2,1,0:T(8,128)(2,1)}, u32[]{:S(2)}) copy-start(bf16[64,64,256]{2,1,0:T(8,128)(2,1)} %refs_0_.1) | copy-start | bytes 6291460
  1.6 0.7 %copy-start.1 = (bf16[2,128]{1,0:T(2,128)(2,1)S(1)}, bf16[2,128]{1,0:T(2,128)(2,1)}, u32[]{:S(2)}) copy-start(bf16[2,128]{1,0:T(2,128)(2,1)} %chirp_ref.3) | copy-start | bytes 1540
  3.6 7.8 %copy-start.5 = (s32[1,8]{1,0:T(1,128)S(1)}, s32[1,8]{1,0:T(1,128)}, u32[]{:S(2)}) copy-start(s32[1,8]{1,0:T(1,128)} %param.9) | copy-start | bytes 100
  3.7 8.4 %copy-start.3 = (s32[2,2,128,8]{2,3,1,0:T(8,128)S(1)}, s32[2,2,128,8]{2,3,1,0:T(8,128)}, u32[]{:S(2)}) copy-start(s32[2,2,128,8]{2,3,1,0:T(8,128)} %param.8) | copy-start | bytes 49156
  3.7 8.9 %copy-start.4 = (f32[8]{0:T(128)S(1)}, f32[8]{0:T(128)}, u32[]{:S(2)}) copy-start(f32[8]{0:T(128)} %constant.177.clone) | copy-start | bytes 100
  3.7 15.0 %collective-permute-start.4 = (bf16[1,1,2,8,64,256]{5,4,3,2,1,0:T(8,128)(2,1)S(1)}, bf16[1,1,2,8,64,256]{5,4,3,2,1,0:T(8,128)(2,1)S(1)}, u32[]{:S(2)}, u32[]{:S(2)}) collective-permute-start(bf16[1,1,2,8,64,256]{5,4,3,2,1,0:T(8,128)(2,1)S(1)} %get-tuple-element.18), channel_id=1, source_target_pairs={{0,2},{1,3},{2,0},{3,1},{4,6},{5,7},{6,4},{7,5},{8,10},{9,11},{10,... | collective-permute-start | bytes 1572872 | tf_op jit(solution)/shard_map/ppermute | solution.py:25
  9.9 13.6 %collective-permute-start = (bf16[1,2,1,8,64,256]{5,4,3,2,1,0:T(8,128)(2,1)}, bf16[1,2,1,8,64,256]{5,4,3,2,1,0:T(8,128)(2,1)S(1)}, u32[]{:S(2)}, u32[]{:S(2)}) collective-permute-start(bf16[1,2,1,8,64,256]{5,4,3,2,1,0:T(8,128)(2,1)} %get-tuple-element.14), channel_id=1, source_target_pairs={{0,1},{1,0},{2,3},{3,2},{4,5},{5,4},{6,7},{7,6},{8,9},{9,8},{10,11... | collective-permute-start | bytes 1572872 | tf_op jit(solution)/shard_map/ppermute | solution.py:25
  21.1 5.0 %collective-permute-start.5 = (bf16[2,4,4,32,256]{4,3,2,1,0:T(8,128)(2,1)S(1)}, bf16[2,4,4,32,256]{4,3,2,1,0:T(8,128)(2,1)S(1)}, u32[]{:S(2)}, u32[]{:S(2)}) collective-permute-start(bf16[2,4,4,32,256]{4,3,2,1,0:T(8,128)(2,1)S(1)} %get-tuple-element.20), channel_id=1, source_target_pairs={{0,8},{8,0},{16,24},{24,16},{1,9},{9,1},{17,25},{25,17},{2,10},{10... | collective-permute-start | bytes 1572872 | tf_op jit(solution)/shard_map/ppermute | solution.py:25
  21.2 2.3 %copy-start.2 = (bf16[1,2,1,8,64,256]{5,4,3,2,1,0:T(8,128)(2,1)S(1)}, bf16[1,2,1,8,64,256]{5,4,3,2,1,0:T(8,128)(2,1)}, u32[]{:S(2)}) copy-start(bf16[1,2,1,8,64,256]{5,4,3,2,1,0:T(8,128)(2,1)} %get-tuple-element.13) | copy-start | bytes 1572868
  25.9 2.6 %collective-permute-start.1 = (bf16[2,4,4,32,256]{4,3,2,1,0:T(8,128)(2,1)S(1)}, bf16[2,4,4,32,256]{4,3,2,1,0:T(8,128)(2,1)S(1)}, u32[]{:S(2)}, u32[]{:S(2)}) collective-permute-start(bf16[2,4,4,32,256]{4,3,2,1,0:T(8,128)(2,1)S(1)} %get-tuple-element.16), channel_id=1, source_target_pairs={{0,8},{8,0},{16,24},{24,16},{1,9},{9,1},{17,25},{25,17},{2,10},{10... | collective-permute-start | bytes 1572872 | tf_op jit(solution)/shard_map/ppermute | solution.py:25
  26.3 6.4 %collective-permute-start.6 = (bf16[2,4,32,256]{3,2,1,0:T(8,128)(2,1)S(1)}, bf16[2,4,32,256]{3,2,1,0:T(8,128)(2,1)S(1)}, u32[]{:S(2)}, u32[]{:S(2)}) collective-permute-start(bf16[2,4,32,256]{3,2,1,0:T(8,128)(2,1)S(1)} %get-tuple-element.29), channel_id=1, source_target_pairs={{0,1},{1,0},{2,3},{3,2},{4,5},{5,4},{6,7},{7,6},{8,9},{9,8},{10,11... | collective-permute-start | bytes 393224 | tf_op jit(solution)/shard_map/ppermute | solution.py:25
  28.0 7.1 %collective-permute-start.10 = (bf16[2,4,32,256]{3,2,1,0:T(8,128)(2,1)S(1)}, bf16[2,4,32,256]{3,2,1,0:T(8,128)(2,1)S(1)}, u32[]{:S(2)}, u32[]{:S(2)}) collective-permute-start(bf16[2,4,32,256]{3,2,1,0:T(8,128)(2,1)S(1)} %get-tuple-element.33), channel_id=1, source_target_pairs={{0,1},{1,0},{2,3},{3,2},{4,5},{5,4},{6,7},{7,6},{8,9},{9,8},{10,11... | collective-permute-start | bytes 393224 | tf_op jit(solution)/shard_map/ppermute | solution.py:25
  28.7 7.9 %collective-permute-start.8 = (bf16[1,8,32,256]{3,2,1,0:T(8,128)(2,1)S(1)}, bf16[1,8,32,256]{3,2,1,0:T(8,128)(2,1)S(1)}, u32[]{:S(2)}, u32[]{:S(2)}) collective-permute-start(bf16[1,8,32,256]{3,2,1,0:T(8,128)(2,1)S(1)} %get-tuple-element.35), channel_id=1, source_target_pairs={{0,16},{8,24},{16,0},{24,8},{1,17},{9,25},{17,1},{25,9},{2,18},{10... | collective-permute-start | bytes 393224 | tf_op jit(solution)/shard_map/ppermute | solution.py:25
  30.3 7.4 %collective-permute-start.2 = (bf16[1,8,32,256]{3,2,1,0:T(8,128)(2,1)S(1)}, bf16[1,8,32,256]{3,2,1,0:T(8,128)(2,1)S(1)}, u32[]{:S(2)}, u32[]{:S(2)}) collective-permute-start(bf16[1,8,32,256]{3,2,1,0:T(8,128)(2,1)S(1)} %get-tuple-element.31), channel_id=1, source_target_pairs={{0,16},{8,24},{16,0},{24,8},{1,17},{9,25},{17,1},{25,9},{2,18},{10... | collective-permute-start | bytes 393224 | tf_op jit(solution)/shard_map/ppermute | solution.py:25
  32.6 8.4 %collective-permute-start.7 = (bf16[1,4,32,256]{3,2,1,0:T(8,128)(2,1)S(1)}, bf16[1,4,32,256]{3,2,1,0:T(8,128)(2,1)S(1)}, u32[]{:S(2)}, u32[]{:S(2)}) collective-permute-start(bf16[1,4,32,256]{3,2,1,0:T(8,128)(2,1)S(1)} %fusion.34), channel_id=1, source_target_pairs={{0,16},{8,24},{16,0},{24,8},{1,17},{9,25},{17,1},{25,9},{2,18},{10... | collective-permute-start | bytes 196616 | tf_op jit(solution)/shard_map/ppermute | solution.py:25
  35.1 4.6 %collective-permute-start.11 = (bf16[1,4,32,256]{3,2,1,0:T(8,128)(2,1)S(1)}, bf16[1,4,32,256]{3,2,1,0:T(8,128)(2,1)S(1)}, u32[]{:S(2)}, u32[]{:S(2)}) collective-permute-start(bf16[1,4,32,256]{3,2,1,0:T(8,128)(2,1)S(1)} %fusion.36), channel_id=1, source_target_pairs={{0,16},{8,24},{16,0},{24,8},{1,17},{9,25},{17,1},{25,9},{2,18},{10... | collective-permute-start | bytes 196616 | tf_op jit(solution)/shard_map/ppermute | solution.py:25
  36.6 4.3 %collective-permute-start.9 = (bf16[1,4,32,256]{3,2,1,0:T(8,128)(2,1)S(1)}, bf16[1,4,32,256]{3,2,1,0:T(8,128)(2,1)S(1)}, u32[]{:S(2)}, u32[]{:S(2)}) collective-permute-start(bf16[1,4,32,256]{3,2,1,0:T(8,128)(2,1)S(1)} %fusion.35), channel_id=1, source_target_pairs={{0,2},{1,3},{2,0},{3,1},{4,6},{5,7},{6,4},{7,5},{8,10},{9,11},{10,... | collective-permute-start | bytes 196616 | tf_op jit(solution)/shard_map/ppermute | solution.py:25
  37.7 4.3 %collective-permute-start.3 = (bf16[1,4,32,256]{3,2,1,0:T(8,128)(2,1)S(1)}, bf16[1,4,32,256]{3,2,1,0:T(8,128)(2,1)S(1)}, u32[]{:S(2)}, u32[]{:S(2)}) collective-permute-start(bf16[1,4,32,256]{3,2,1,0:T(8,128)(2,1)S(1)} %fusion.33), channel_id=1, source_target_pairs={{0,2},{1,3},{2,0},{3,1},{4,6},{5,7},{6,4},{7,5},{8,10},{9,11},{10,... | collective-permute-start | bytes 196616 | tf_op jit(solution)/shard_map/ppermute | solution.py:25
  42.1 7.3 %collective-permute-start.12 = (bf16[2,4,32,256]{3,2,1,0:T(8,128)(2,1)S(1)}, bf16[2,4,32,256]{3,2,1,0:T(8,128)(2,1)S(1)}, u32[]{:S(2)}, u32[]{:S(2)}) collective-permute-start(bf16[2,4,32,256]{3,2,1,0:T(8,128)(2,1)S(1)} %pad_maximum_fusion.5), channel_id=1, source_target_pairs={{0,4},{1,5},{2,6},{3,7},{4,0},{5,1},{6,2},{7,3},{8,12},{9,13},{10,... | collective-permute-start | bytes 393224 | tf_op jit(solution)/shard_map/ppermute | solution.py:25

commit v12 on v11

--- a/solution.py
+++ b/solution.py
@@ -10,7 +10,7 @@
 
 WEIGHTS = (-1.0 / 32, 3.0 / 32, -7.0 / 32, 21.0 / 32, 21.0 / 32, -7.0 / 32, 3.0 / 32, -1.0 / 32)
 PERIOD = 4096
-VMEM_BYTES = 56 * 2**20
+VMEM_BYTES = 20 * 2**20
 
 
 def bits_of(count):
@@ -48,7 +48,7 @@
     def _():
         rows = lax.broadcasted_iota(jnp.int32, (half, half), 0)
         cols = lax.broadcasted_iota(jnp.int32, (half, half), 1)
-        taps = chirp_ref[...].astype(jnp.float32)
+        taps = chirp_ref[...]
         tables = []
         for c in range(2):
             wide = jnp.broadcast_to(taps[c : c + 1], (half, half))
@@ -150,9 +150,7 @@
             pltpu.VMEM((2, pulses * (2 * tile + 1), half), jnp.float32),
             pltpu.VMEM((pulses, width), jnp.bfloat16),
         ],
-        compiler_params=pltpu.CompilerParams(
-            vmem_limit_bytes=VMEM_BYTES if near_chain else 20 * 2**20
-        ),
+        compiler_params=pltpu.CompilerParams(vmem_limit_bytes=VMEM_BYTES),
         cost_estimate=pl.CostEstimate(
             flops=2 * pulses * blocks * width * width,
             bytes_accessed=2 * pulses * blocks * width,
@@ -343,6 +341,7 @@
     rows = beams // leaf
     own_leaf, own_turn = lax.axis_index("leaf"), lax.axis_index("turn")
 
+    chirp = chirp.astype(jnp.float32)
     keep_y, send_y = compress(chirp, echoes, high, mids, True, far, high)
     got_y = swapped(send_y, "turn", 0)
     keep_z, send_z = compress(chirp, echoes, high, mids, False, far, 0)

time: 50.4 us -> 50.3 us (level)
  starting transfers between devices: 16.5 us -> 19.4 us
  waiting for transfers between devices: 15 us -> 12.7 us
  Pallas kernels: 9.85 us -> 8.07 us
  other arithmetic: 4.93 us -> 6.64 us
  local copies, waits for them, and re-layouts: 3.33 us -> 2.67 us
    ppermute x13, starting transfers between devices: 16.5 us -> 19.4 us  [swapped(): lax.ppermute(array, axis, [(i, i ^ 1 << bit) for i in range(lax.axis_size...]
    ppermute x13, waiting for transfers between devices: 15 us -> 12.7 us  [swapped(): lax.ppermute(array, axis, [(i, i ^ 1 << bit) for i in range(lax.axis_size...]
    pallas_call x2, Pallas kernels: 4.5 us -> 2.72 us  [compress(): pl.pallas_call(functools.partial(compress_kernel, dims, has_edge), grid=(...]
    another operation x2, other arithmetic: 0.19 us -> 1.24 us  [per_device(): data = jnp.stack([keep.reshape(shape), got.reshape(shape)])]
    unnamed x16 -> x12, local copies, waits for them, and re-layouts: 2.39 us -> 1.73 us
    convert_element_type x0 -> x1, other arithmetic: none -> 0.66 us  [per_device(): chirp = chirp.astype(jnp.float32)]
  transfers between devices with their start and end apart: 13 -> 13, of which waited for: 9 -> 6; matrix products, arithmetic and copies ran while one was open for 12% -> 14% of each run, Pallas kernels for 15% -> 12%
where the time goes in v12:
time: 50.3 us; the launch traced here: 50.1 us
  starting transfers between devices  19.4 us (39%)
  waiting for transfers between devices  12.7 us (25%)
  Pallas kernels  8.07 us (16%)
  other arithmetic  6.64 us (13%)
  local copies, waits for them, and re-layouts  2.67 us (5%)
    ppermute x13, starting transfers between devices, swapped(): lax.ppermute(array, axis, [(i, i ^ 1 << bit) for i in range(lax.axis_size...  19.4 us
    ppermute x13, waiting for transfers between devices, swapped(): lax.ppermute(array, axis, [(i, i ^ 1 << bit) for i in range(lax.axis_size...  12.7 us
    pallas_call x2, Pallas kernels, backproject(): pl.pallas_call(functools.partial(image_kernel, (leaf, each, half, beams,...  4.61 us
    pallas_call x2, Pallas kernels, compress(): pl.pallas_call(functools.partial(compress_kernel, dims, has_edge), grid=(...  2.72 us
    cos x2, other arithmetic, unit(): return (jnp.cos(angle), jnp.sin(angle))  2.27 us
    unnamed x12, local copies, waits for them, and re-layouts  1.73 us
    another operation x2, other arithmetic, per_device(): data = jnp.stack([keep.reshape(shape), got.reshape(shape)])  1.24 us
  transfers between devices with their start and end apart: 13, of which 6 were waited for; matrix products, arithmetic and copies ran while one was open for 14% of the time, Pallas kernels for 12%

profile of v12, /device:TPU:0, one launch (start us, length us, event | category | flops | bytes accessed | tf_op | source)
XLA Modules:
  0.0 50.1 jit_solution(3818498046495384415)
XLA Ops:
  0.0 0.7 %convert_element_type.374.chirp_ref = f32[2,128]{1,0:T(2,128)S(1)} convert(bf16[2,128]{1,0:T(2,128)(2,1)} %param.7) | non-fusion elementwise | flops 256 | bytes 1536 | tf_op jit(solution)/shard_map/convert_element_type | solution.py:344
  0.7 1.6 %copy-done = bf16[64,64,256]{2,1,0:T(8,128)(2,1)S(1)} copy-done((bf16[64,64,256]{2,1,0:T(8,128)(2,1)S(1)}, bf16[64,64,256]{2,1,0:T(8,128)(2,1)}, u32[]{:S(2)}) %copy-start) | copy-done | bytes 2097176
  2.2 1.4 %compress.3 = (bf16[1,1,2,8,64,256]{5,4,3,2,1,0:T(8,128)(2,1)S(1)}, bf16[1,1,2,8,64,256]{5,4,3,2,1,0:T(8,128)(2,1)S(1)}) custom-call(f32[2,128]{1,0:T(2,128)S(1)} %convert_element_type.374.chirp_ref, bf16[64,64,256]{2,1,0:T(8,128)(2,1)S(1)} %copy-done, bf16[64,64,256]{2,1,0:T(8,128)(2,1)S(1)} %copy-done), custom_call_target="tpu_custom_call" | custom-call | flops 536870912 | bytes 2097152 | tf_op jit(solution)/shard_map/compress/pallas_call | solution.py:142
  3.7 3.1 %collective-permute-start.4 = (bf16[1,1,2,8,64,256]{5,4,3,2,1,0:T(8,128)(2,1)S(1)}, bf16[1,1,2,8,64,256]{5,4,3,2,1,0:T(8,128)(2,1)}, u32[]{:S(2)}, u32[]{:S(2)}) collective-permute-start(bf16[1,1,2,8,64,256]{5,4,3,2,1,0:T(8,128)(2,1)S(1)} %get-tuple-element.18), channel_id=1, source_target_pairs={{0,2},{1,3},{2,0},{3,1},{4,6},{5,7},{6,4},{7,5},{8,10},{9,11},{10,... | collective-permute-start | bytes 1572872 | tf_op jit(solution)/shard_map/ppermute | solution.py:25
  6.8 1.3 %compress.2 = (bf16[1,2,1,8,64,256]{5,4,3,2,1,0:T(8,128)(2,1)S(1)}, bf16[1,2,1,8,64,256]{5,4,3,2,1,0:T(8,128)(2,1)S(1)}) custom-call(f32[2,128]{1,0:T(2,128)S(1)} %convert_element_type.374.chirp_ref, bf16[64,64,256]{2,1,0:T(8,128)(2,1)S(1)} %copy-done), custom_call_target="tpu_custom_call" | custom-call | flops 536870912 | bytes 2097152 | tf_op jit(solution)/shard_map/compress/pallas_call | solution.py:142
  8.1 1.6 %collective-permute-start = (bf16[1,2,1,8,64,256]{5,4,3,2,1,0:T(8,128)(2,1)S(1)}, bf16[1,2,1,8,64,256]{5,4,3,2,1,0:T(8,128)(2,1)S(1)}, u32[]{:S(2)}, u32[]{:S(2)}) collective-permute-start(bf16[1,2,1,8,64,256]{5,4,3,2,1,0:T(8,128)(2,1)S(1)} %get-tuple-element.14), channel_id=1, source_target_pairs={{0,1},{1,0},{2,3},{3,2},{4,5},{5,4},{6,7},{7,6},{8,9},{9,8},{10,11... | collective-permute-start | bytes 1572872 | tf_op jit(solution)/shard_map/ppermute | solution.py:25
  9.8 0.2 select_reduce_fusion.1
  10.6 0.1 copy.35
  10.9 0.4 select_reduce_fusion
  11.3 0.5 multiply_convert_fusion.1
  11.8 0.2 fusion.30
  12.2 0.2 fusion.47
  12.7 2.1 %fusion.10 = (f32[2,1,128,512]{3,2,1,0:T(8,128)S(1)}, f32[2,1,128,512]{3,2,1,0:T(8,128)S(1)}) fusion(s32[512]{0:T(512)S(1)} %iota_add_fusion, s32[2,128]{1,0:T(2,128)S(1)} %add_multiply_fusion), kind=kLoop, calls=%fused_computation.33 | loop fusion | flops 1835008 | bytes 1051648 | tf_op jit(solution)/shard_map/cos | solution.py:30
  14.9 3.9 %collective-permute-done.4 = bf16[1,1,2,8,64,256]{5,4,3,2,1,0:T(8,128)(2,1)} collective-permute-done((bf16[1,1,2,8,64,256]{5,4,3,2,1,0:T(8,128)(2,1)S(1)}, bf16[1,1,2,8,64,256]{5,4,3,2,1,0:T(8,128)(2,1)}, u32[]{:S(2)}, u32[]{:S(2)}) %collective-permute-start.4) | collective-permute-done | bytes 524320 | tf_op jit(solution)/shard_map/ppermute | solution.py:25
  18.8 1.1 %pad_maximum_fusion.2.data_ref = bf16[2,4,4,64,256]{4,3,2,1,0:T(8,128)(2,1)S(1)} fusion(bf16[1,4,4,64,256]{4,3,2,1,0:T(8,128)(2,1)} %bitcast.28, bf16[1,4,4,64,256]{4,3,2,1,0:T(8,128)(2,1)S(1)} %bitcast.118), kind=kLoop, calls=%fused_computation.2 | loop fusion | flops 524288 | bytes 2097152 | tf_op jit(solution)/shard_map/stack | solution.py:403
  19.9 2.3 %image.3 = (f32[2,4,4,32,256]{4,3,2,1,0:T(8,128)S(1)}, bf16[2,4,4,32,256]{4,3,2,1,0:T(8,128)(2,1)S(1)}) custom-call(bf16[2,4,4,64,256]{4,3,2,1,0:T(8,128)(2,1)S(1)} %pad_maximum_fusion.2.data_ref, bf16[256,256]{1,0:T(8,128)(2,1)S(1)} %copy.45.steer_ref, bf16[1,128,256]{2,1,0:T(8,128)(2,1)S(1)} %pad_maximum_fusion.6.interp_ref, f32[4,4,128]{2,1,0:T(4,128)S(1)} %bitcast.121, ...), custom_call_target="tpu_custom_call" | custom-call | flops 402653184 | bytes 2621440 | tf_op jit(solution)/shard_map/image/pallas_call | solution.py:245
  22.7 2.3 %image.2 = (f32[2,4,4,32,256]{4,3,2,1,0:T(8,128)S(1)}, bf16[2,4,4,32,256]{4,3,2,1,0:T(8,128)(2,1)S(1)}) custom-call(bf16[2,4,4,64,256]{4,3,2,1,0:T(8,128)(2,1)S(1)} %pad_maximum_fusion.data_ref, bf16[256,256]{1,0:T(8,128)(2,1)S(1)} %copy.44.steer_ref, bf16[1,128,256]{2,1,0:T(8,128)(2,1)S(1)} %pad_maximum_fusion.6.interp_ref, f32[4,4,128]{2,1,0:T(4,128)S(1)} %bitcast.120, ...), custom_call_target="tpu_custom_call" | custom-call | flops 402653184 | bytes 2621440 | tf_op jit(solution)/shard_map/image/pallas_call | solution.py:245
  25.0 0.6 %collective-permute-start.1 = (bf16[2,4,4,32,256]{4,3,2,1,0:T(8,128)(2,1)S(1)}, bf16[2,4,4,32,256]{4,3,2,1,0:T(8,128)(2,1)S(1)}, u32[]{:S(2)}, u32[]{:S(2)}) collective-permute-start(bf16[2,4,4,32,256]{4,3,2,1,0:T(8,128)(2,1)S(1)} %get-tuple-element.16), channel_id=1, source_target_pairs={{0,8},{8,0},{16,24},{24,16},{1,9},{9,1},{17,25},{25,17},{2,10},{10... | collective-permute-start | bytes 1572872 | tf_op jit(solution)/shard_map/ppermute | solution.py:25
  25.8 1.8 %collective-permute-start.6 = (bf16[2,4,32,256]{3,2,1,0:T(8,128)(2,1)S(1)}, bf16[2,4,32,256]{3,2,1,0:T(8,128)(2,1)S(1)}, u32[]{:S(2)}, u32[]{:S(2)}) collective-permute-start(bf16[2,4,32,256]{3,2,1,0:T(8,128)(2,1)S(1)} %get-tuple-element.29), channel_id=1, source_target_pairs={{0,1},{1,0},{2,3},{3,2},{4,5},{5,4},{6,7},{7,6},{8,9},{9,8},{10,11... | collective-permute-start | bytes 393224 | tf_op jit(solution)/shard_map/ppermute | solution.py:25
  27.7 0.4 collective-permute-start.10
  28.2 1.7 %collective-permute-start.8 = (bf16[1,8,32,256]{3,2,1,0:T(8,128)(2,1)S(1)}, bf16[1,8,32,256]{3,2,1,0:T(8,128)(2,1)S(1)}, u32[]{:S(2)}, u32[]{:S(2)}) collective-permute-start(bf16[1,8,32,256]{3,2,1,0:T(8,128)(2,1)S(1)} %get-tuple-element.35), channel_id=1, source_target_pairs={{0,16},{8,24},{16,0},{24,8},{1,17},{9,25},{17,1},{25,9},{2,18},{10... | collective-permute-start | bytes 393224 | tf_op jit(solution)/shard_map/ppermute | solution.py:25
  30.1 0.4 collective-permute-start.2
  30.5 1.8 %collective-permute-done.6 = bf16[2,4,32,256]{3,2,1,0:T(8,128)(2,1)S(1)} collective-permute-done((bf16[2,4,32,256]{3,2,1,0:T(8,128)(2,1)S(1)}, bf16[2,4,32,256]{3,2,1,0:T(8,128)(2,1)S(1)}, u32[]{:S(2)}, u32[]{:S(2)}) %collective-permute-start.6) | collective-permute-done | bytes 131104 | tf_op jit(solution)/shard_map/ppermute | solution.py:25
  32.3 1.7 %collective-permute-start.7 = (bf16[1,4,32,256]{3,2,1,0:T(8,128)(2,1)S(1)}, bf16[1,4,32,256]{3,2,1,0:T(8,128)(2,1)S(1)}, u32[]{:S(2)}, u32[]{:S(2)}) collective-permute-start(bf16[1,4,32,256]{3,2,1,0:T(8,128)(2,1)S(1)} %fusion.34), channel_id=1, source_target_pairs={{0,16},{8,24},{16,0},{24,8},{1,17},{9,25},{17,1},{25,9},{2,18},{10... | collective-permute-start | bytes 196616 | tf_op jit(solution)/shard_map/ppermute | solution.py:25
  34.1 1.7 %collective-permute-start.11 = (bf16[1,4,32,256]{3,2,1,0:T(8,128)(2,1)S(1)}, bf16[1,4,32,256]{3,2,1,0:T(8,128)(2,1)S(1)}, u32[]{:S(2)}, u32[]{:S(2)}) collective-permute-start(bf16[1,4,32,256]{3,2,1,0:T(8,128)(2,1)S(1)} %fusion.36), channel_id=1, source_target_pairs={{0,16},{8,24},{16,0},{24,8},{1,17},{9,25},{17,1},{25,9},{2,18},{10... | collective-permute-start | bytes 196616 | tf_op jit(solution)/shard_map/ppermute | solution.py:25
  35.9 1.6 %collective-permute-start.9 = (bf16[1,4,32,256]{3,2,1,0:T(8,128)(2,1)S(1)}, bf16[1,4,32,256]{3,2,1,0:T(8,128)(2,1)S(1)}, u32[]{:S(2)}, u32[]{:S(2)}) collective-permute-start(bf16[1,4,32,256]{3,2,1,0:T(8,128)(2,1)S(1)} %fusion.35), channel_id=1, source_target_pairs={{0,2},{1,3},{2,0},{3,1},{4,6},{5,7},{6,4},{7,5},{8,10},{9,11},{10,... | collective-permute-start | bytes 196616 | tf_op jit(solution)/shard_map/ppermute | solution.py:25
  37.5 1.6 %collective-permute-start.3 = (bf16[1,4,32,256]{3,2,1,0:T(8,128)(2,1)S(1)}, bf16[1,4,32,256]{3,2,1,0:T(8,128)(2,1)S(1)}, u32[]{:S(2)}, u32[]{:S(2)}) collective-permute-start(bf16[1,4,32,256]{3,2,1,0:T(8,128)(2,1)S(1)} %fusion.33), channel_id=1, source_target_pairs={{0,2},{1,3},{2,0},{3,1},{4,6},{5,7},{6,4},{7,5},{8,10},{9,11},{10,... | collective-permute-start | bytes 196616 | tf_op jit(solution)/shard_map/ppermute | solution.py:25
  39.2 1.0 %collective-permute-done.9 = bf16[1,4,32,256]{3,2,1,0:T(8,128)(2,1)S(1)} collective-permute-done((bf16[1,4,32,256]{3,2,1,0:T(8,128)(2,1)S(1)}, bf16[1,4,32,256]{3,2,1,0:T(8,128)(2,1)S(1)}, u32[]{:S(2)}, u32[]{:S(2)}) %collective-permute-start.9) | collective-permute-done | bytes 65568 | tf_op jit(solution)/shard_map/ppermute | solution.py:25
  40.3 1.6 %collective-permute-done.3 = bf16[1,4,32,256]{3,2,1,0:T(8,128)(2,1)S(1)} collective-permute-done((bf16[1,4,32,256]{3,2,1,0:T(8,128)(2,1)S(1)}, bf16[1,4,32,256]{3,2,1,0:T(8,128)(2,1)S(1)}, u32[]{:S(2)}, u32[]{:S(2)}) %collective-permute-start.3) | collective-permute-done | bytes 65568 | tf_op jit(solution)/shard_map/ppermute | solution.py:25
  42.0 3.0 %collective-permute-start.12 = (bf16[2,4,32,256]{3,2,1,0:T(8,128)(2,1)S(1)}, bf16[2,4,32,256]{3,2,1,0:T(8,128)(2,1)S(1)}, u32[]{:S(2)}, u32[]{:S(2)}) collective-permute-start(bf16[2,4,32,256]{3,2,1,0:T(8,128)(2,1)S(1)} %pad_maximum_fusion.5), channel_id=1, source_target_pairs={{0,4},{1,5},{2,6},{3,7},{4,0},{5,1},{6,2},{7,3},{8,12},{9,13},{10,... | collective-permute-start | bytes 393224 | tf_op jit(solution)/shard_map/ppermute | solution.py:25
  45.0 4.3 %collective-permute-done.12 = bf16[2,4,32,256]{3,2,1,0:T(8,128)(2,1)S(1)} collective-permute-done((bf16[2,4,32,256]{3,2,1,0:T(8,128)(2,1)S(1)}, bf16[2,4,32,256]{3,2,1,0:T(8,128)(2,1)S(1)}, u32[]{:S(2)}, u32[]{:S(2)}) %collective-permute-start.12) | collective-permute-done | bytes 131104 | tf_op jit(solution)/shard_map/ppermute | solution.py:25
  49.3 0.7 %last_sum.1 = bf16[32,8,256]{2,1,0:T(8,128)(2,1)} custom-call(f32[8,32,256]{2,1,0:T(8,128)S(1)} %bitcast.116, bf16[8,32,256]{2,1,0:T(8,128)(2,1)S(1)} %bitcast.119), custom_call_target="tpu_custom_call" | custom-call | tf_op jit(solution)/shard_map/last_sum/pallas_call | solution.py:288
  (78 shorter events, 2.7 us)
Async XLA Ops:
  0.7 1.6 %copy-start = (bf16[64,64,256]{2,1,0:T(8,128)(2,1)S(1)}, bf16[64,64,256]{2,1,0:T(8,128)(2,1)}, u32[]{:S(2)}) copy-start(bf16[64,64,256]{2,1,0:T(8,128)(2,1)} %refs_0_.1) | copy-start | bytes 6291460
  3.6 6.1 %copy-start.3 = (s32[1,8]{1,0:T(1,128)S(1)}, s32[1,8]{1,0:T(1,128)}, u32[]{:S(2)}) copy-start(s32[1,8]{1,0:T(1,128)} %param.9) | copy-start | bytes 100
  3.7 6.7 %copy-start.1 = (s32[2,2,128,8]{2,3,1,0:T(8,128)S(1)}, s32[2,2,128,8]{2,3,1,0:T(8,128)}, u32[]{:S(2)}) copy-start(s32[2,2,128,8]{2,3,1,0:T(8,128)} %param.8) | copy-start | bytes 49156
  3.7 7.2 %copy-start.2 = (f32[8]{0:T(128)S(1)}, f32[8]{0:T(128)}, u32[]{:S(2)}) copy-start(f32[8]{0:T(128)} %constant.177.clone) | copy-start | bytes 100
  3.7 15.1 %collective-permute-start.4 = (bf16[1,1,2,8,64,256]{5,4,3,2,1,0:T(8,128)(2,1)S(1)}, bf16[1,1,2,8,64,256]{5,4,3,2,1,0:T(8,128)(2,1)}, u32[]{:S(2)}, u32[]{:S(2)}) collective-permute-start(bf16[1,1,2,8,64,256]{5,4,3,2,1,0:T(8,128)(2,1)S(1)} %get-tuple-element.18), channel_id=1, source_target_pairs={{0,2},{1,3},{2,0},{3,1},{4,6},{5,7},{6,4},{7,5},{8,10},{9,11},{10,... | collective-permute-start | bytes 1572872 | tf_op jit(solution)/shard_map/ppermute | solution.py:25
  8.1 14.4 %collective-permute-start = (bf16[1,2,1,8,64,256]{5,4,3,2,1,0:T(8,128)(2,1)S(1)}, bf16[1,2,1,8,64,256]{5,4,3,2,1,0:T(8,128)(2,1)S(1)}, u32[]{:S(2)}, u32[]{:S(2)}) collective-permute-start(bf16[1,2,1,8,64,256]{5,4,3,2,1,0:T(8,128)(2,1)S(1)} %get-tuple-element.14), channel_id=1, source_target_pairs={{0,1},{1,0},{2,3},{3,2},{4,5},{5,4},{6,7},{7,6},{8,9},{9,8},{10,11... | collective-permute-start | bytes 1572872 | tf_op jit(solution)/shard_map/ppermute | solution.py:25
  22.2 3.4 %collective-permute-start.5 = (bf16[2,4,4,32,256]{4,3,2,1,0:T(8,128)(2,1)S(1)}, bf16[2,4,4,32,256]{4,3,2,1,0:T(8,128)(2,1)S(1)}, u32[]{:S(2)}, u32[]{:S(2)}) collective-permute-start(bf16[2,4,4,32,256]{4,3,2,1,0:T(8,128)(2,1)S(1)} %get-tuple-element.20), channel_id=1, source_target_pairs={{0,8},{8,0},{16,24},{24,16},{1,9},{9,1},{17,25},{25,17},{2,10},{10... | collective-permute-start | bytes 1572872 | tf_op jit(solution)/shard_map/ppermute | solution.py:25
  25.0 3.1 %collective-permute-start.1 = (bf16[2,4,4,32,256]{4,3,2,1,0:T(8,128)(2,1)S(1)}, bf16[2,4,4,32,256]{4,3,2,1,0:T(8,128)(2,1)S(1)}, u32[]{:S(2)}, u32[]{:S(2)}) collective-permute-start(bf16[2,4,4,32,256]{4,3,2,1,0:T(8,128)(2,1)S(1)} %get-tuple-element.16), channel_id=1, source_target_pairs={{0,8},{8,0},{16,24},{24,16},{1,9},{9,1},{17,25},{25,17},{2,10},{10... | collective-permute-start | bytes 1572872 | tf_op jit(solution)/shard_map/ppermute | solution.py:25
  25.8 6.4 %collective-permute-start.6 = (bf16[2,4,32,256]{3,2,1,0:T(8,128)(2,1)S(1)}, bf16[2,4,32,256]{3,2,1,0:T(8,128)(2,1)S(1)}, u32[]{:S(2)}, u32[]{:S(2)}) collective-permute-start(bf16[2,4,32,256]{3,2,1,0:T(8,128)(2,1)S(1)} %get-tuple-element.29), channel_id=1, source_target_pairs={{0,1},{1,0},{2,3},{3,2},{4,5},{5,4},{6,7},{7,6},{8,9},{9,8},{10,11... | collective-permute-start | bytes 393224 | tf_op jit(solution)/shard_map/ppermute | solution.py:25
  27.7 6.4 %collective-permute-start.10 = (bf16[2,4,32,256]{3,2,1,0:T(8,128)(2,1)S(1)}, bf16[2,4,32,256]{3,2,1,0:T(8,128)(2,1)S(1)}, u32[]{:S(2)}, u32[]{:S(2)}) collective-permute-start(bf16[2,4,32,256]{3,2,1,0:T(8,128)(2,1)S(1)} %get-tuple-element.33), channel_id=1, source_target_pairs={{0,1},{1,0},{2,3},{3,2},{4,5},{5,4},{6,7},{7,6},{8,9},{9,8},{10,11... | collective-permute-start | bytes 393224 | tf_op jit(solution)/shard_map/ppermute | solution.py:25
  28.2 7.6 %collective-permute-start.8 = (bf16[1,8,32,256]{3,2,1,0:T(8,128)(2,1)S(1)}, bf16[1,8,32,256]{3,2,1,0:T(8,128)(2,1)S(1)}, u32[]{:S(2)}, u32[]{:S(2)}) collective-permute-start(bf16[1,8,32,256]{3,2,1,0:T(8,128)(2,1)S(1)} %get-tuple-element.35), channel_id=1, source_target_pairs={{0,16},{8,24},{16,0},{24,8},{1,17},{9,25},{17,1},{25,9},{2,18},{10... | collective-permute-start | bytes 393224 | tf_op jit(solution)/shard_map/ppermute | solution.py:25
  30.1 7.5 %collective-permute-start.2 = (bf16[1,8,32,256]{3,2,1,0:T(8,128)(2,1)S(1)}, bf16[1,8,32,256]{3,2,1,0:T(8,128)(2,1)S(1)}, u32[]{:S(2)}, u32[]{:S(2)}) collective-permute-start(bf16[1,8,32,256]{3,2,1,0:T(8,128)(2,1)S(1)} %get-tuple-element.31), channel_id=1, source_target_pairs={{0,16},{8,24},{16,0},{24,8},{1,17},{9,25},{17,1},{25,9},{2,18},{10... | collective-permute-start | bytes 393224 | tf_op jit(solution)/shard_map/ppermute | solution.py:25
  32.3 8.0 %collective-permute-start.7 = (bf16[1,4,32,256]{3,2,1,0:T(8,128)(2,1)S(1)}, bf16[1,4,32,256]{3,2,1,0:T(8,128)(2,1)S(1)}, u32[]{:S(2)}, u32[]{:S(2)}) collective-permute-start(bf16[1,4,32,256]{3,2,1,0:T(8,128)(2,1)S(1)} %fusion.34), channel_id=1, source_target_pairs={{0,16},{8,24},{16,0},{24,8},{1,17},{9,25},{17,1},{25,9},{2,18},{10... | collective-permute-start | bytes 196616 | tf_op jit(solution)/shard_map/ppermute | solution.py:25
  34.1 5.0 %collective-permute-start.11 = (bf16[1,4,32,256]{3,2,1,0:T(8,128)(2,1)S(1)}, bf16[1,4,32,256]{3,2,1,0:T(8,128)(2,1)S(1)}, u32[]{:S(2)}, u32[]{:S(2)}) collective-permute-start(bf16[1,4,32,256]{3,2,1,0:T(8,128)(2,1)S(1)} %fusion.36), channel_id=1, source_target_pairs={{0,16},{8,24},{16,0},{24,8},{1,17},{9,25},{17,1},{25,9},{2,18},{10... | collective-permute-start | bytes 196616 | tf_op jit(solution)/shard_map/ppermute | solution.py:25
  35.9 4.3 %collective-permute-start.9 = (bf16[1,4,32,256]{3,2,1,0:T(8,128)(2,1)S(1)}, bf16[1,4,32,256]{3,2,1,0:T(8,128)(2,1)S(1)}, u32[]{:S(2)}, u32[]{:S(2)}) collective-permute-start(bf16[1,4,32,256]{3,2,1,0:T(8,128)(2,1)S(1)} %fusion.35), channel_id=1, source_target_pairs={{0,2},{1,3},{2,0},{3,1},{4,6},{5,7},{6,4},{7,5},{8,10},{9,11},{10,... | collective-permute-start | bytes 196616 | tf_op jit(solution)/shard_map/ppermute | solution.py:25
  37.5 4.3 %collective-permute-start.3 = (bf16[1,4,32,256]{3,2,1,0:T(8,128)(2,1)S(1)}, bf16[1,4,32,256]{3,2,1,0:T(8,128)(2,1)S(1)}, u32[]{:S(2)}, u32[]{:S(2)}) collective-permute-start(bf16[1,4,32,256]{3,2,1,0:T(8,128)(2,1)S(1)} %fusion.33), channel_id=1, source_target_pairs={{0,2},{1,3},{2,0},{3,1},{4,6},{5,7},{6,4},{7,5},{8,10},{9,11},{10,... | collective-permute-start | bytes 196616 | tf_op jit(solution)/shard_map/ppermute | solution.py:25
  42.0 7.4 %collective-permute-start.12 = (bf16[2,4,32,256]{3,2,1,0:T(8,128)(2,1)S(1)}, bf16[2,4,32,256]{3,2,1,0:T(8,128)(2,1)S(1)}, u32[]{:S(2)}, u32[]{:S(2)}) collective-permute-start(bf16[2,4,32,256]{3,2,1,0:T(8,128)(2,1)S(1)} %pad_maximum_fusion.5), channel_id=1, source_target_pairs={{0,4},{1,5},{2,6},{3,7},{4,0},{5,1},{6,2},{7,3},{8,12},{9,13},{10,... | collective-permute-start | bytes 393224 | tf_op jit(solution)/shard_map/ppermute | solution.py:25

commit v13 on v11

--- a/solution.py
+++ b/solution.py
@@ -344,6 +344,7 @@
     own_leaf, own_turn = lax.axis_index("leaf"), lax.axis_index("turn")
 
     keep_y, send_y = compress(chirp, echoes, high, mids, True, far, high)
+    chirp, send_y = lax.optimization_barrier((chirp, send_y))
     got_y = swapped(send_y, "turn", 0)
     keep_z, send_z = compress(chirp, echoes, high, mids, False, far, 0)
     got_z = swapped(send_z, "turn", far)

time: 50.4 us -> 48.7 us (0.966)
  local copies, waits for them, and re-layouts: 3.33 us -> 1.05 us
  starting transfers between devices: 16.5 us -> 17.8 us
  waiting for transfers between devices: 15 us -> 14.2 us
    unnamed x16, local copies, waits for them, and re-layouts: 2.39 us -> 0.14 us
    ppermute x13, starting transfers between devices: 16.5 us -> 17.8 us  [swapped(): lax.ppermute(array, axis, [(i, i ^ 1 << bit) for i in range(lax.axis_size...]
    ppermute x13, waiting for transfers between devices: 15 us -> 14.2 us  [swapped(): lax.ppermute(array, axis, [(i, i ^ 1 << bit) for i in range(lax.axis_size...]
  transfers between devices with their start and end apart: 13 -> 13, of which waited for: 9 -> 8; matrix products, arithmetic and copies ran while one was open for 12% -> 12% of each run, Pallas kernels for 15% -> 12%
where the time goes in v13:
time: 48.7 us; the launch traced here: 48.6 us
  starting transfers between devices  17.8 us (37%)
  waiting for transfers between devices  14.2 us (29%)
  Pallas kernels  10 us (21%)
  other arithmetic  4.9 us (10%)
  local copies, waits for them, and re-layouts  1.05 us (2%)
    ppermute x13, starting transfers between devices, swapped(): lax.ppermute(array, axis, [(i, i ^ 1 << bit) for i in range(lax.axis_size...  17.8 us
    ppermute x13, waiting for transfers between devices, swapped(): lax.ppermute(array, axis, [(i, i ^ 1 << bit) for i in range(lax.axis_size...  14.2 us
    pallas_call x2, Pallas kernels, compress(): pl.pallas_call(functools.partial(compress_kernel, dims, has_edge), grid=(...  4.66 us
    pallas_call x2, Pallas kernels, backproject(): pl.pallas_call(functools.partial(image_kernel, (leaf, each, half, beams,...  4.61 us
    cos x2, other arithmetic, unit(): return (jnp.cos(angle), jnp.sin(angle))  2.27 us
  transfers between devices with their start and end apart: 13, of which 8 were waited for; matrix products, arithmetic and copies ran while one was open for 12% of the time, Pallas kernels for 12%

profile of v13, /device:TPU:0, one launch (start us, length us, event | category | flops | bytes accessed | tf_op | source)
XLA Modules:
  0.0 48.6 jit_solution(16596186728682819290)
XLA Ops:
  0.0 3.3 %compress.2 = (bf16[1,2,1,8,64,256]{5,4,3,2,1,0:T(8,128)(2,1)}, bf16[1,2,1,8,64,256]{5,4,3,2,1,0:T(8,128)(2,1)}) custom-call(bf16[2,128]{1,0:T(2,128)(2,1)} %chirp_ref.2, bf16[64,64,256]{2,1,0:T(8,128)(2,1)} %refs_0_.1), custom_call_target="tpu_custom_call" | custom-call | flops 536870912 | bytes 2097152 | tf_op jit(solution)/shard_map/compress/pallas_call | solution.py:142
  3.3 3.1 %collective-permute-start = (bf16[1,2,1,8,64,256]{5,4,3,2,1,0:T(8,128)(2,1)}, bf16[1,2,1,8,64,256]{5,4,3,2,1,0:T(8,128)(2,1)S(1)}, u32[]{:S(2)}, u32[]{:S(2)}) collective-permute-start(bf16[1,2,1,8,64,256]{5,4,3,2,1,0:T(8,128)(2,1)} %get-tuple-element.17), channel_id=1, source_target_pairs={{0,1},{1,0},{2,3},{3,2},{4,5},{5,4},{6,7},{7,6},{8,9},{9,8},{10,11... | collective-permute-start | bytes 1572872 | tf_op jit(solution)/shard_map/ppermute | solution.py:25
  6.4 1.4 %compress.3 = (bf16[1,1,2,8,64,256]{5,4,3,2,1,0:T(8,128)(2,1)S(1)}, bf16[1,1,2,8,64,256]{5,4,3,2,1,0:T(8,128)(2,1)S(1)}) custom-call(bf16[2,128]{1,0:T(2,128)(2,1)S(1)} %copy-done.1, bf16[64,64,256]{2,1,0:T(8,128)(2,1)S(1)} %copy-done, bf16[64,64,256]{2,1,0:T(8,128)(2,1)S(1)} %copy-done), custom_call_target="tpu_custom_call" | custom-call | flops 536870912 | bytes 2097152 | tf_op jit(solution)/shard_map/compress/pallas_call | solution.py:142
  7.8 1.6 %collective-permute-start.4 = (bf16[1,1,2,8,64,256]{5,4,3,2,1,0:T(8,128)(2,1)S(1)}, bf16[1,1,2,8,64,256]{5,4,3,2,1,0:T(8,128)(2,1)S(1)}, u32[]{:S(2)}, u32[]{:S(2)}) collective-permute-start(bf16[1,1,2,8,64,256]{5,4,3,2,1,0:T(8,128)(2,1)S(1)} %get-tuple-element.22), channel_id=1, source_target_pairs={{0,2},{1,3},{2,0},{3,1},{4,6},{5,7},{6,4},{7,5},{8,10},{9,11},{10,... | collective-permute-start | bytes 1572872 | tf_op jit(solution)/shard_map/ppermute | solution.py:25
  9.5 0.2 select_reduce_fusion.1
  10.3 0.1 copy.35
  10.6 0.4 select_reduce_fusion
  11.0 0.5 multiply_convert_fusion.1
  11.5 0.2 fusion.30
  11.9 0.2 fusion.47
  12.4 2.1 %fusion.10 = (f32[2,1,128,512]{3,2,1,0:T(8,128)S(1)}, f32[2,1,128,512]{3,2,1,0:T(8,128)S(1)}) fusion(s32[512]{0:T(512)S(1)} %iota_add_fusion, s32[2,128]{1,0:T(2,128)S(1)} %add_multiply_fusion), kind=kLoop, calls=%fused_computation.33 | loop fusion | flops 1835008 | bytes 1051648 | tf_op jit(solution)/shard_map/cos | solution.py:30
  14.6 3.9 %collective-permute-done = bf16[1,2,1,8,64,256]{5,4,3,2,1,0:T(8,128)(2,1)S(1)} collective-permute-done((bf16[1,2,1,8,64,256]{5,4,3,2,1,0:T(8,128)(2,1)}, bf16[1,2,1,8,64,256]{5,4,3,2,1,0:T(8,128)(2,1)S(1)}, u32[]{:S(2)}, u32[]{:S(2)}) %collective-permute-start) | collective-permute-done | bytes 524320 | tf_op jit(solution)/shard_map/ppermute | solution.py:25
  18.6 2.3 %image.2 = (f32[2,4,4,32,256]{4,3,2,1,0:T(8,128)S(1)}, bf16[2,4,4,32,256]{4,3,2,1,0:T(8,128)(2,1)S(1)}) custom-call(bf16[2,4,4,64,256]{4,3,2,1,0:T(8,128)(2,1)S(1)} %pad_maximum_fusion.data_ref, bf16[256,256]{1,0:T(8,128)(2,1)S(1)} %copy.44.steer_ref, bf16[1,128,256]{2,1,0:T(8,128)(2,1)S(1)} %pad_maximum_fusion.6.interp_ref, f32[4,4,128]{2,1,0:T(4,128)S(1)} %bitcast.120, ...), custom_call_target="tpu_custom_call" | custom-call | flops 402653184 | bytes 2621440 | tf_op jit(solution)/shard_map/image/pallas_call | solution.py:247
  21.0 0.2 collective-permute-done.4
  21.3 2.3 %image.3 = (f32[2,4,4,32,256]{4,3,2,1,0:T(8,128)S(1)}, bf16[2,4,4,32,256]{4,3,2,1,0:T(8,128)(2,1)S(1)}) custom-call(bf16[2,4,4,64,256]{4,3,2,1,0:T(8,128)(2,1)S(1)} %pad_maximum_fusion.2.data_ref, bf16[256,256]{1,0:T(8,128)(2,1)S(1)} %copy.45.steer_ref, bf16[1,128,256]{2,1,0:T(8,128)(2,1)S(1)} %pad_maximum_fusion.6.interp_ref, f32[4,4,128]{2,1,0:T(4,128)S(1)} %bitcast.119, ...), custom_call_target="tpu_custom_call" | custom-call | flops 402653184 | bytes 2621440 | tf_op jit(solution)/shard_map/image/pallas_call | solution.py:247
  23.8 0.4 collective-permute-start.5
  24.4 1.8 %collective-permute-start.8 = (bf16[1,8,32,256]{3,2,1,0:T(8,128)(2,1)S(1)}, bf16[1,8,32,256]{3,2,1,0:T(8,128)(2,1)S(1)}, u32[]{:S(2)}, u32[]{:S(2)}) collective-permute-start(bf16[1,8,32,256]{3,2,1,0:T(8,128)(2,1)S(1)} %get-tuple-element.39), channel_id=1, source_target_pairs={{0,16},{8,24},{16,0},{24,8},{1,17},{9,25},{17,1},{25,9},{2,18},{10... | collective-permute-start | bytes 393224 | tf_op jit(solution)/shard_map/ppermute | solution.py:25
  26.3 0.3 collective-permute-start.2
  26.8 1.8 %collective-permute-start.6 = (bf16[2,4,32,256]{3,2,1,0:T(8,128)(2,1)S(1)}, bf16[2,4,32,256]{3,2,1,0:T(8,128)(2,1)S(1)}, u32[]{:S(2)}, u32[]{:S(2)}) collective-permute-start(bf16[2,4,32,256]{3,2,1,0:T(8,128)(2,1)S(1)} %get-tuple-element.33), channel_id=1, source_target_pairs={{0,1},{1,0},{2,3},{3,2},{4,5},{5,4},{6,7},{7,6},{8,9},{9,8},{10,11... | collective-permute-start | bytes 393224 | tf_op jit(solution)/shard_map/ppermute | solution.py:25
  28.7 0.3 collective-permute-start.10
  29.0 1.7 %collective-permute-done.8 = bf16[1,8,32,256]{3,2,1,0:T(8,128)(2,1)S(1)} collective-permute-done((bf16[1,8,32,256]{3,2,1,0:T(8,128)(2,1)S(1)}, bf16[1,8,32,256]{3,2,1,0:T(8,128)(2,1)S(1)}, u32[]{:S(2)}, u32[]{:S(2)}) %collective-permute-start.8) | collective-permute-done | bytes 131104 | tf_op jit(solution)/shard_map/ppermute | solution.py:25
  30.8 1.9 %collective-permute-start.9 = (bf16[1,4,32,256]{3,2,1,0:T(8,128)(2,1)S(1)}, bf16[1,4,32,256]{3,2,1,0:T(8,128)(2,1)S(1)}, u32[]{:S(2)}, u32[]{:S(2)}) collective-permute-start(bf16[1,4,32,256]{3,2,1,0:T(8,128)(2,1)S(1)} %fusion.35), channel_id=1, source_target_pairs={{0,2},{1,3},{2,0},{3,1},{4,6},{5,7},{6,4},{7,5},{8,10},{9,11},{10,... | collective-permute-start | bytes 196616 | tf_op jit(solution)/shard_map/ppermute | solution.py:25
  32.7 0.2 collective-permute-done.2
  32.9 1.7 %collective-permute-start.3 = (bf16[1,4,32,256]{3,2,1,0:T(8,128)(2,1)S(1)}, bf16[1,4,32,256]{3,2,1,0:T(8,128)(2,1)S(1)}, u32[]{:S(2)}, u32[]{:S(2)}) collective-permute-start(bf16[1,4,32,256]{3,2,1,0:T(8,128)(2,1)S(1)} %fusion.33), channel_id=1, source_target_pairs={{0,2},{1,3},{2,0},{3,1},{4,6},{5,7},{6,4},{7,5},{8,10},{9,11},{10,... | collective-permute-start | bytes 196616 | tf_op jit(solution)/shard_map/ppermute | solution.py:25
  34.6 1.6 %collective-permute-start.7 = (bf16[1,4,32,256]{3,2,1,0:T(8,128)(2,1)S(1)}, bf16[1,4,32,256]{3,2,1,0:T(8,128)(2,1)S(1)}, u32[]{:S(2)}, u32[]{:S(2)}) collective-permute-start(bf16[1,4,32,256]{3,2,1,0:T(8,128)(2,1)S(1)} %fusion.34), channel_id=1, source_target_pairs={{0,16},{8,24},{16,0},{24,8},{1,17},{9,25},{17,1},{25,9},{2,18},{10... | collective-permute-start | bytes 196616 | tf_op jit(solution)/shard_map/ppermute | solution.py:25
  36.2 0.6 %collective-permute-start.11 = (bf16[1,4,32,256]{3,2,1,0:T(8,128)(2,1)S(1)}, bf16[1,4,32,256]{3,2,1,0:T(8,128)(2,1)S(1)}, u32[]{:S(2)}, u32[]{:S(2)}) collective-permute-start(bf16[1,4,32,256]{3,2,1,0:T(8,128)(2,1)S(1)} %fusion.36), channel_id=1, source_target_pairs={{0,16},{8,24},{16,0},{24,8},{1,17},{9,25},{17,1},{25,9},{2,18},{10... | collective-permute-start | bytes 196616 | tf_op jit(solution)/shard_map/ppermute | solution.py:25
  36.8 0.5 collective-permute-done.3
  37.2 1.7 %collective-permute-done.7 = bf16[1,4,32,256]{3,2,1,0:T(8,128)(2,1)S(1)} collective-permute-done((bf16[1,4,32,256]{3,2,1,0:T(8,128)(2,1)S(1)}, bf16[1,4,32,256]{3,2,1,0:T(8,128)(2,1)S(1)}, u32[]{:S(2)}, u32[]{:S(2)}) %collective-permute-start.7) | collective-permute-done | bytes 65568 | tf_op jit(solution)/shard_map/ppermute | solution.py:25
  39.0 1.5 %collective-permute-done.11 = bf16[1,4,32,256]{3,2,1,0:T(8,128)(2,1)S(1)} collective-permute-done((bf16[1,4,32,256]{3,2,1,0:T(8,128)(2,1)S(1)}, bf16[1,4,32,256]{3,2,1,0:T(8,128)(2,1)S(1)}, u32[]{:S(2)}, u32[]{:S(2)}) %collective-permute-start.11) | collective-permute-done | bytes 65568 | tf_op jit(solution)/shard_map/ppermute | solution.py:25
  40.6 2.7 %collective-permute-start.12 = (bf16[2,4,32,256]{3,2,1,0:T(8,128)(2,1)S(1)}, bf16[2,4,32,256]{3,2,1,0:T(8,128)(2,1)S(1)}, u32[]{:S(2)}, u32[]{:S(2)}) collective-permute-start(bf16[2,4,32,256]{3,2,1,0:T(8,128)(2,1)S(1)} %pad_maximum_fusion.5), channel_id=1, source_target_pairs={{0,4},{1,5},{2,6},{3,7},{4,0},{5,1},{6,2},{7,3},{8,12},{9,13},{10,... | collective-permute-start | bytes 393224 | tf_op jit(solution)/shard_map/ppermute | solution.py:25
  43.3 4.6 %collective-permute-done.12 = bf16[2,4,32,256]{3,2,1,0:T(8,128)(2,1)S(1)} collective-permute-done((bf16[2,4,32,256]{3,2,1,0:T(8,128)(2,1)S(1)}, bf16[2,4,32,256]{3,2,1,0:T(8,128)(2,1)S(1)}, u32[]{:S(2)}, u32[]{:S(2)}) %collective-permute-start.12) | collective-permute-done | bytes 131104 | tf_op jit(solution)/shard_map/ppermute | solution.py:25
  47.8 0.7 %last_sum.1 = bf16[32,8,256]{2,1,0:T(8,128)(2,1)} custom-call(f32[8,32,256]{2,1,0:T(8,128)S(1)} %bitcast.116, bf16[8,32,256]{2,1,0:T(8,128)(2,1)S(1)} %bitcast.118), custom_call_target="tpu_custom_call" | custom-call | tf_op jit(solution)/shard_map/last_sum/pallas_call | solution.py:290
  (81 shorter events, 2.6 us)
Async XLA Ops:
  0.0 6.4 %copy-start.1 = (bf16[2,128]{1,0:T(2,128)(2,1)S(1)}, bf16[2,128]{1,0:T(2,128)(2,1)}, u32[]{:S(2)}) copy-start(bf16[2,128]{1,0:T(2,128)(2,1)} %chirp_ref.2) | copy-start | bytes 1540
  0.0 6.4 %copy-start = (bf16[64,64,256]{2,1,0:T(8,128)(2,1)S(1)}, bf16[64,64,256]{2,1,0:T(8,128)(2,1)}, u32[]{:S(2)}) copy-start(bf16[64,64,256]{2,1,0:T(8,128)(2,1)} %refs_0_.1) | copy-start | bytes 6291460
  3.3 6.2 %copy-start.5 = (s32[1,8]{1,0:T(1,128)S(1)}, s32[1,8]{1,0:T(1,128)}, u32[]{:S(2)}) copy-start(s32[1,8]{1,0:T(1,128)} %param.9) | copy-start | bytes 100
  3.3 6.8 %copy-start.3 = (s32[2,2,128,8]{2,3,1,0:T(8,128)S(1)}, s32[2,2,128,8]{2,3,1,0:T(8,128)}, u32[]{:S(2)}) copy-start(s32[2,2,128,8]{2,3,1,0:T(8,128)} %param.8) | copy-start | bytes 49156
  3.3 7.3 %copy-start.4 = (f32[8]{0:T(128)S(1)}, f32[8]{0:T(128)}, u32[]{:S(2)}) copy-start(f32[8]{0:T(128)} %constant.177.clone) | copy-start | bytes 100
  3.3 15.2 %collective-permute-start = (bf16[1,2,1,8,64,256]{5,4,3,2,1,0:T(8,128)(2,1)}, bf16[1,2,1,8,64,256]{5,4,3,2,1,0:T(8,128)(2,1)S(1)}, u32[]{:S(2)}, u32[]{:S(2)}) collective-permute-start(bf16[1,2,1,8,64,256]{5,4,3,2,1,0:T(8,128)(2,1)} %get-tuple-element.17), channel_id=1, source_target_pairs={{0,1},{1,0},{2,3},{3,2},{4,5},{5,4},{6,7},{7,6},{8,9},{9,8},{10,11... | collective-permute-start | bytes 1572872 | tf_op jit(solution)/shard_map/ppermute | solution.py:25
  7.8 13.4 %collective-permute-start.4 = (bf16[1,1,2,8,64,256]{5,4,3,2,1,0:T(8,128)(2,1)S(1)}, bf16[1,1,2,8,64,256]{5,4,3,2,1,0:T(8,128)(2,1)S(1)}, u32[]{:S(2)}, u32[]{:S(2)}) collective-permute-start(bf16[1,1,2,8,64,256]{5,4,3,2,1,0:T(8,128)(2,1)S(1)} %get-tuple-element.22), channel_id=1, source_target_pairs={{0,2},{1,3},{2,0},{3,1},{4,6},{5,7},{6,4},{7,5},{8,10},{9,11},{10,... | collective-permute-start | bytes 1572872 | tf_op jit(solution)/shard_map/ppermute | solution.py:25
  12.1 6.4 %copy-start.2 = (bf16[1,2,1,8,64,256]{5,4,3,2,1,0:T(8,128)(2,1)S(1)}, bf16[1,2,1,8,64,256]{5,4,3,2,1,0:T(8,128)(2,1)}, u32[]{:S(2)}) copy-start(bf16[1,2,1,8,64,256]{5,4,3,2,1,0:T(8,128)(2,1)} %get-tuple-element.15) | copy-start | bytes 1572868
  20.9 3.4 %collective-permute-start.1 = (bf16[2,4,4,32,256]{4,3,2,1,0:T(8,128)(2,1)S(1)}, bf16[2,4,4,32,256]{4,3,2,1,0:T(8,128)(2,1)S(1)}, u32[]{:S(2)}, u32[]{:S(2)}) collective-permute-start(bf16[2,4,4,32,256]{4,3,2,1,0:T(8,128)(2,1)S(1)} %get-tuple-element.19), channel_id=1, source_target_pairs={{0,8},{8,0},{16,24},{24,16},{1,9},{9,1},{17,25},{25,17},{2,10},{10... | collective-permute-start | bytes 1572872 | tf_op jit(solution)/shard_map/ppermute | solution.py:25
  23.8 2.8 %collective-permute-start.5 = (bf16[2,4,4,32,256]{4,3,2,1,0:T(8,128)(2,1)S(1)}, bf16[2,4,4,32,256]{4,3,2,1,0:T(8,128)(2,1)S(1)}, u32[]{:S(2)}, u32[]{:S(2)}) collective-permute-start(bf16[2,4,4,32,256]{4,3,2,1,0:T(8,128)(2,1)S(1)} %get-tuple-element.24), channel_id=1, source_target_pairs={{0,8},{8,0},{16,24},{24,16},{1,9},{9,1},{17,25},{25,17},{2,10},{10... | collective-permute-start | bytes 1572872 | tf_op jit(solution)/shard_map/ppermute | solution.py:25
  24.4 6.4 %collective-permute-start.8 = (bf16[1,8,32,256]{3,2,1,0:T(8,128)(2,1)S(1)}, bf16[1,8,32,256]{3,2,1,0:T(8,128)(2,1)S(1)}, u32[]{:S(2)}, u32[]{:S(2)}) collective-permute-start(bf16[1,8,32,256]{3,2,1,0:T(8,128)(2,1)S(1)} %get-tuple-element.39), channel_id=1, source_target_pairs={{0,16},{8,24},{16,0},{24,8},{1,17},{9,25},{17,1},{25,9},{2,18},{10... | collective-permute-start | bytes 393224 | tf_op jit(solution)/shard_map/ppermute | solution.py:25
  26.3 6.6 %collective-permute-start.2 = (bf16[1,8,32,256]{3,2,1,0:T(8,128)(2,1)S(1)}, bf16[1,8,32,256]{3,2,1,0:T(8,128)(2,1)S(1)}, u32[]{:S(2)}, u32[]{:S(2)}) collective-permute-start(bf16[1,8,32,256]{3,2,1,0:T(8,128)(2,1)S(1)} %get-tuple-element.35), channel_id=1, source_target_pairs={{0,16},{8,24},{16,0},{24,8},{1,17},{9,25},{17,1},{25,9},{2,18},{10... | collective-permute-start | bytes 393224 | tf_op jit(solution)/shard_map/ppermute | solution.py:25
  26.8 7.8 %collective-permute-start.6 = (bf16[2,4,32,256]{3,2,1,0:T(8,128)(2,1)S(1)}, bf16[2,4,32,256]{3,2,1,0:T(8,128)(2,1)S(1)}, u32[]{:S(2)}, u32[]{:S(2)}) collective-permute-start(bf16[2,4,32,256]{3,2,1,0:T(8,128)(2,1)S(1)} %get-tuple-element.33), channel_id=1, source_target_pairs={{0,1},{1,0},{2,3},{3,2},{4,5},{5,4},{6,7},{7,6},{8,9},{9,8},{10,11... | collective-permute-start | bytes 393224 | tf_op jit(solution)/shard_map/ppermute | solution.py:25
  28.7 7.5 %collective-permute-start.10 = (bf16[2,4,32,256]{3,2,1,0:T(8,128)(2,1)S(1)}, bf16[2,4,32,256]{3,2,1,0:T(8,128)(2,1)S(1)}, u32[]{:S(2)}, u32[]{:S(2)}) collective-permute-start(bf16[2,4,32,256]{3,2,1,0:T(8,128)(2,1)S(1)} %get-tuple-element.37), channel_id=1, source_target_pairs={{0,1},{1,0},{2,3},{3,2},{4,5},{5,4},{6,7},{7,6},{8,9},{9,8},{10,11... | collective-permute-start | bytes 393224 | tf_op jit(solution)/shard_map/ppermute | solution.py:25
  30.8 8.2 %collective-permute-start.9 = (bf16[1,4,32,256]{3,2,1,0:T(8,128)(2,1)S(1)}, bf16[1,4,32,256]{3,2,1,0:T(8,128)(2,1)S(1)}, u32[]{:S(2)}, u32[]{:S(2)}) collective-permute-start(bf16[1,4,32,256]{3,2,1,0:T(8,128)(2,1)S(1)} %fusion.35), channel_id=1, source_target_pairs={{0,2},{1,3},{2,0},{3,1},{4,6},{5,7},{6,4},{7,5},{8,10},{9,11},{10,... | collective-permute-start | bytes 196616 | tf_op jit(solution)/shard_map/ppermute | solution.py:25
  32.9 4.3 %collective-permute-start.3 = (bf16[1,4,32,256]{3,2,1,0:T(8,128)(2,1)S(1)}, bf16[1,4,32,256]{3,2,1,0:T(8,128)(2,1)S(1)}, u32[]{:S(2)}, u32[]{:S(2)}) collective-permute-start(bf16[1,4,32,256]{3,2,1,0:T(8,128)(2,1)S(1)} %fusion.33), channel_id=1, source_target_pairs={{0,2},{1,3},{2,0},{3,1},{4,6},{5,7},{6,4},{7,5},{8,10},{9,11},{10,... | collective-permute-start | bytes 196616 | tf_op jit(solution)/shard_map/ppermute | solution.py:25
  34.6 4.3 %collective-permute-start.7 = (bf16[1,4,32,256]{3,2,1,0:T(8,128)(2,1)S(1)}, bf16[1,4,32,256]{3,2,1,0:T(8,128)(2,1)S(1)}, u32[]{:S(2)}, u32[]{:S(2)}) collective-permute-start(bf16[1,4,32,256]{3,2,1,0:T(8,128)(2,1)S(1)} %fusion.34), channel_id=1, source_target_pairs={{0,16},{8,24},{16,0},{24,8},{1,17},{9,25},{17,1},{25,9},{2,18},{10... | collective-permute-start | bytes 196616 | tf_op jit(solution)/shard_map/ppermute | solution.py:25
  36.2 4.3 %collective-permute-start.11 = (bf16[1,4,32,256]{3,2,1,0:T(8,128)(2,1)S(1)}, bf16[1,4,32,256]{3,2,1,0:T(8,128)(2,1)S(1)}, u32[]{:S(2)}, u32[]{:S(2)}) collective-permute-start(bf16[1,4,32,256]{3,2,1,0:T(8,128)(2,1)S(1)} %fusion.36), channel_id=1, source_target_pairs={{0,16},{8,24},{16,0},{24,8},{1,17},{9,25},{17,1},{25,9},{2,18},{10... | collective-permute-start | bytes 196616 | tf_op jit(solution)/shard_map/ppermute | solution.py:25
  40.6 7.2 %collective-permute-start.12 = (bf16[2,4,32,256]{3,2,1,0:T(8,128)(2,1)S(1)}, bf16[2,4,32,256]{3,2,1,0:T(8,128)(2,1)S(1)}, u32[]{:S(2)}, u32[]{:S(2)}) collective-permute-start(bf16[2,4,32,256]{3,2,1,0:T(8,128)(2,1)S(1)} %pad_maximum_fusion.5), channel_id=1, source_target_pairs={{0,4},{1,5},{2,6},{3,7},{4,0},{5,1},{6,2},{7,3},{8,12},{9,13},{10,... | collective-permute-start | bytes 393224 | tf_op jit(solution)/shard_map/ppermute | solution.py:25

commit v14 on v11

--- a/solution.py
+++ b/solution.py
@@ -33,13 +33,11 @@
 def compress_kernel(dims, has_edge, chirp_ref, echo_ref, *refs):
     tile, pulses, half, near_chain, far = dims
     edge_ref, refs = (refs[0], refs[1:]) if has_edge else (None, refs)
-    keep_ref, send_ref, weights, rows_ref, carry = refs
+    keeps, sends, (weights, rows_ref, carry) = refs[:2], refs[2:4], refs[4:]
     blocks = 2 * tile
     pitch = blocks + 1
     mids = pl.num_programs(2)
-    high = pl.num_programs(0)
     turn = lax.axis_index("turn")
-    spot_h = (high - 1 - pl.program_id(0)) ^ (turn >> far + 1 & high - 1)
     spot_m = (mids - 1 - pl.program_id(2)) ^ (turn >> 1 & mids - 1)
     spot_v = (1 - pl.program_id(1)) ^ bit(turn, far)
     own_u = bit(turn, 0)
@@ -91,40 +89,28 @@
     def block(b):
         return total[b * pulses : (b + 1) * pulses]
 
-    if near_chain:
-        for side in range(2):
-
-            @pl.when(own_u == side)
-            def _(side=side):
-                for b in range(blocks):
-                    ref = keep_ref if b // tile == side else send_ref
-                    ref[0, 0, 0, b % tile] = block(b)
-    else:
-        for ref, mine in ((keep_ref, 0), (send_ref, 1)):
-
-            @pl.when(spot_v == mine)
-            def _(ref=ref):
-                for b in range(blocks):
-                    ref[spot_h, spot_m, b // tile ^ own_u, b % tile] = block(b)
+    for spot, side in ((0, 0), (0, 1), (1, 0), (1, 1)):
+
+        @pl.when((spot_v == spot) & (own_u == side))
+        def _(spot=spot, side=side):
+            for b in range(blocks):
+                other = b // tile ^ side
+                swaps, part = (other, spot) if near_chain else (spot, other)
+                (sends if swaps else keeps)[part][0, spot_m, b % tile] = block(b)
 
 
 def compress(chirp, echoes, high, mids, near_chain, far, first_high):
     pulses, blocks, width = echoes.shape
     half = width // 2
     tile = blocks // lax.axis_size("turn")
-    if near_chain:
-        shape = (high, 2, mids, tile, pulses, width)
-
-        def place(h, v, m):
-            turn = lax.axis_index("turn")
-            spot_h = (high - 1 - h) ^ (turn >> far + 1 & high - 1)
-            spot_m = (mids - 1 - m) ^ (turn >> 1 & mids - 1)
-            return spot_h, (1 - v) ^ bit(turn, far), spot_m, 0, 0, 0
-
-        spec = pl.BlockSpec((1, 1, 1) + shape[3:], place)
-    else:
-        shape = (high, mids, 2, tile, pulses, width)
-        spec = pl.BlockSpec(shape, lambda h, v, m: (0, 0, 0, 0, 0, 0))
+    shape = (high, mids, tile, pulses, width)
+
+    def place(h, v, m):
+        turn = lax.axis_index("turn")
+        return (high - 1 - h) ^ (turn >> far + 1 & high - 1), 0, 0, 0, 0
+
+    spec = pl.BlockSpec((1,) + shape[1:], place)
+
     def chunk(h, v, m):
         return 0, ((first_high + high - 1 - h) * 2 + 1 - v) * mids + mids - 1 - m, 0
 
@@ -143,8 +129,8 @@
         functools.partial(compress_kernel, dims, has_edge),
         grid=(high, 2, mids),
         in_specs=in_specs,
-        out_specs=[spec, spec],
-        out_shape=[jax.ShapeDtypeStruct(shape, jnp.bfloat16)] * 2,
+        out_specs=[spec] * 4,
+        out_shape=[jax.ShapeDtypeStruct(shape, jnp.bfloat16)] * 4,
         scratch_shapes=[
             pltpu.VMEM((2 * width, width), jnp.bfloat16),
             pltpu.VMEM((2, pulses * (2 * tile + 1), half), jnp.float32),
@@ -162,8 +148,9 @@
     )(*operands)
 
 
-def image_kernel(dims, data_ref, steer_ref, interp_ref, base_ref, step_ref, out_keep, out_send):
+def image_kernel(dims, data_ref, steer_ref, interp_ref, base_ref, step_ref, *refs):
     leaf, each, half, beams, levels = dims
+    out_keep, out_send = refs[-2:]
     rows = beams // leaf
     pair = 2
     piece = rows
@@ -174,7 +161,7 @@
 
     bases = []
     for n in range(2 * levels):
-        bases.append(jnp.broadcast_to(base_ref[0, n : n + 1, :], (half, beams)).T)
+        bases.append(jnp.broadcast_to(base_ref[0, 0, 0, n : n + 1, :], (half, beams)).T)
 
     def phased(level, block, first, re, im):
         cut = slice(first, first + piece)
@@ -192,7 +179,7 @@
             for c in range(2):
                 cols = slice(c * half, (c + 1) * half)
                 parts.append(
-                    jnp.concatenate([data_ref[n, 0, at + i, :, cols] for i in range(pair)], axis=1)
+                    jnp.concatenate([data_ref[n, 0, 0, 0, at + i, :, cols] for i in range(pair)], axis=1)
                 )
         raw = jnp.dot(
             steer_ref[...], jnp.concatenate(parts, axis=0), preferred_element_type=jnp.float32
@@ -210,9 +197,9 @@
                         both = jnp.concatenate(both, axis=1)
                         g = first // rows
                         if g < leaf // 2:
-                            out_keep[g, 0, at + i] = both
+                            out_keep[g, 0, 0, 0, 0, at + i] = both
                         else:
-                            out_send[g - leaf // 2, 0, at + i] = both.astype(jnp.bfloat16)
+                            out_send[g - leaf // 2, 0, 0, 0, 0, at + i] = both.astype(jnp.bfloat16)
                         continue
                     both = jnp.concatenate(both, axis=1)
                     big = both.astype(jnp.bfloat16)
@@ -233,40 +220,45 @@
                 im = jnp.concatenate(cuts[1::2], axis=1)
 
 
-def backproject(data, steer, interp, base, step, leaf):
-    _, count, each, pulses, width = data.shape
+def backproject(data, steer, interp, base, step, leaf, near_chain, part, earlier):
+    _, high, mids, _, each, pulses, width = data.shape
     half = width // 2
     beams = steer.shape[0] // 2
     rows = beams // leaf
-    shape = (leaf // 2, count, each, rows, width)
-
-    def block(n):
-        return n % (count // 2) * 2 + n // (count // 2)
-
-    out_spec = pl.BlockSpec((leaf // 2, 1) + shape[2:], lambda n: (0, n, 0, 0, 0))
+    middle = (high, 2, mids) if near_chain else (high, mids, 2)
+    shape = (leaf // 2, 2) + middle + (each, rows, width)
+
+    def place(n, h, m):
+        return (0, n) + ((h, part, m) if near_chain else (h, m, part)) + (0, 0, 0)
+
+    out_spec = pl.BlockSpec((leaf // 2, 1, 1, 1, 1, each, rows, width), place)
     return pl.pallas_call(
         functools.partial(image_kernel, (leaf, each, half, beams, bits_of(leaf))),
-        grid=(count,),
+        grid=(2, high, mids),
         in_specs=[
-            pl.BlockSpec((2, 1, each, pulses, width), lambda n: (0, block(n), 0, 0, 0)),
-            pl.BlockSpec(steer.shape, lambda n: (0, 0)),
-            pl.BlockSpec(interp.shape, lambda n: (0, 0, 0)),
-            pl.BlockSpec((1,) + base.shape[1:], lambda n: (block(n), 0, 0)),
-            pl.BlockSpec(step.shape, lambda n: (0, 0, 0, 0)),
-        ],
+            pl.BlockSpec(
+                (2, 1, 1, 1, each, pulses, width), lambda n, h, m: (0, h, m, n, 0, 0, 0)
+            ),
+            pl.BlockSpec(steer.shape, lambda n, h, m: (0, 0)),
+            pl.BlockSpec(interp.shape, lambda n, h, m: (0, 0, 0)),
+            pl.BlockSpec((1, 1, 1) + base.shape[3:], lambda n, h, m: (h, m, n, 0, 0)),
+            pl.BlockSpec(step.shape, lambda n, h, m: (0, 0, 0, 0)),
+        ]
+        + [pl.BlockSpec(memory_space=pl.ANY)] * len(earlier),
         out_specs=[out_spec, out_spec],
         out_shape=[
             jax.ShapeDtypeStruct(shape, jnp.float32),
             jax.ShapeDtypeStruct(shape, jnp.bfloat16),
         ],
+        input_output_aliases={5 + n: n for n in range(len(earlier))},
         compiler_params=pltpu.CompilerParams(vmem_limit_bytes=10 * 2**20),
         cost_estimate=pl.CostEstimate(
-            flops=12 * beams * pulses * count * each * width,
-            bytes_accessed=2 * data.size + 6 * count * each * beams * width // 2,
+            flops=6 * beams * data.size,
+            bytes_accessed=2 * data.size + 3 * beams * 2 * high * mids * each * width,
             transcendentals=0,
         ),
         name="image",
-    )(data, steer, interp, base, step)
+    )(data, steer, interp, base, step, *earlier)
 
 
 def fold(keep, got):
@@ -343,10 +335,13 @@
     rows = beams // leaf
     own_leaf, own_turn = lax.axis_index("leaf"), lax.axis_index("turn")
 
-    keep_y, send_y = compress(chirp, echoes, high, mids, True, far, high)
-    got_y = swapped(send_y, "turn", 0)
-    keep_z, send_z = compress(chirp, echoes, high, mids, False, far, 0)
-    got_z = swapped(send_z, "turn", far)
+    swaps = ((True, 0, high), (False, far, 0))
+    keeps, gots = [], []
+    for near_chain, swap_bit, first_high in swaps:
+        *arrays, = compress(chirp, echoes, high, mids, near_chain, far, first_high)
+        chirp, *arrays = lax.optimization_barrier((chirp, *arrays))
+        keeps.append(arrays[:2])
+        gots.append([swapped(a, "turn", swap_bit) for a in arrays[2:]])
 
     own_sides = [bit(own_leaf, level) for level in range(levels)]
     row = jnp.arange(beams, dtype=jnp.int32)
@@ -383,31 +378,39 @@
         [orders[n] * orders[n] * (own_sides[n] + 1) * (1 if n else 0) for n in range(levels)]
     )
 
-    def bases(tiles):
-        parts = (2 * tiles[:, None] + jnp.arange(2, dtype=jnp.int32)).reshape(-1)
+    own_high, own_mid = own_turn >> far + 1 & high - 1, own_turn >> 1 & mids - 1
+    own_near, own_far = bit(own_turn, 0), bit(own_turn, far)
+
+    def bases(near_chain, part):
+        h = (jnp.arange(high, dtype=jnp.int32) ^ own_high)[:, None]
+        m = (jnp.arange(mids, dtype=jnp.int32) ^ own_mid)[None, :]
+        if near_chain:
+            h, u, v = h + high, own_near, own_far ^ part
+        else:
+            u, v = own_near ^ part, own_far
+        tiles = ((h * 2 + v) * mids + m) * 2 + u
+        parts = (2 * tiles[..., None] + jnp.arange(2, dtype=jnp.int32)).reshape(-1)
         start = (parts * each * half)[:, None, None]
         both = jnp.stack(unit(slopes * start + squares, PERIOD), axis=2)
-        return both.reshape(parts.shape[0], 2 * levels, beams)
-
-    index = jnp.arange(turn // 4, dtype=jnp.int32)
-    tiles_y = turn // 2 + 2 * (index ^ (own_turn >> 1 & turn // 4 - 1)) + bit(own_turn, 0)
-    low_part = (index ^ own_turn) & (1 << far) - 1
-    high_part = index >> far ^ (own_turn >> far + 1 & high - 1)
-    tiles_z = (high_part * 2 + bit(own_turn, far)) * (1 << far) + low_part
+        return both.reshape(high, mids, 2, 2 * levels, beams)
 
     pieces = []
-    for name, keep, got, steer_own, tiles in (
-        ("y", keep_y, got_y, steer_y, tiles_y),
-        ("z", keep_z, got_z, steer_z, tiles_z),
-    ):
-        shape = (turn // 2, each, pulses, width)
-        data = jnp.stack([keep.reshape(shape), got.reshape(shape)])
-        kept, sent = backproject(data, steer_own, interp, bases(tiles), step, leaf)
-        gone = 0 if name == "y" else far
+    results = [(), ()]
+    for part in range(2):
+        for n, steer_own in enumerate((steer_y, steer_z)):
+            shape = (high, mids, 2, each, pulses, width)
+            data = jnp.stack([keeps[n][part].reshape(shape), gots[n][part].reshape(shape)])
+            base = bases(n == 0, part)
+            results[n] = backproject(
+                data, steer_own, interp, base, step, leaf, n == 0, part, results[n]
+            )
+    for n in range(2):
+        kept, sent = results[n]
+        gone = swaps[n][1]
         arrived = swapped(sent, "leaf", 0)
         parts = (leaf // 2, 2, turn // 4, each, rows, width)
         kept, arrived = kept.reshape(parts), arrived.reshape(parts)
-        pieces.append([(kept[:, n], arrived[:, n], gone) for n in range(2)])
+        pieces.append([(kept[:, k], arrived[:, k], gone) for k in range(2)])
 
     final = [[], []]
     for n in range(2):

time: 50.4 us -> 51 us (1.012)
  starting transfers between devices: 16.5 us -> 18.7 us
  local copies, waits for them, and re-layouts: 3.33 us -> 1.18 us
  other arithmetic: 4.93 us -> 6.91 us
  waiting for transfers between devices: 15 us -> 13.2 us
    unnamed x16 -> x13, local copies, waits for them, and re-layouts: 2.39 us -> 0.04 us
    ppermute x13 -> x15, starting transfers between devices: 16.5 us -> 18.7 us  [swapped(): lax.ppermute(array, axis, [(i, i ^ 1 << bit) for i in range(lax.axis_size...]
    another operation x6 -> x8, other arithmetic: 0.84 us -> 2.83 us  [the longest x4 2.18 us: per_device(): jnp.stack([keeps[n][part].reshape(shape), gots[n][part].reshape(shape)])]
    ppermute x13 -> x15, waiting for transfers between devices: 15 us -> 13.2 us  [swapped(): lax.ppermute(array, axis, [(i, i ^ 1 << bit) for i in range(lax.axis_size...]
    pallas_call x2 -> x4, Pallas kernels: 4.61 us -> 4.58 us  [backproject(): pl.pallas_call(functools.partial(image_kernel, (leaf, each, half, beams,...]
  transfers between devices with their start and end apart: 13 -> 15, of which waited for: 9 -> 5; matrix products, arithmetic and copies ran while one was open for 12% -> 16% of each run, Pallas kernels for 15% -> 12%
where the time goes in v14:
time: 51 us; the launch traced here: 50.8 us
  starting transfers between devices  18.7 us (37%)
  waiting for transfers between devices  13.2 us (26%)
  Pallas kernels  10.1 us (20%)
  other arithmetic  6.91 us (14%)
  local copies, waits for them, and re-layouts  1.18 us (2%)
  between operations  0.51 us (1%)
    ppermute x15, starting transfers between devices, swapped(): lax.ppermute(array, axis, [(i, i ^ 1 << bit) for i in range(lax.axis_size...  18.7 us
    ppermute x15, waiting for transfers between devices, swapped(): lax.ppermute(array, axis, [(i, i ^ 1 << bit) for i in range(lax.axis_size...  13.2 us
    pallas_call x2, Pallas kernels, compress(): pl.pallas_call(functools.partial(compress_kernel, dims, has_edge), grid=(...  4.83 us
    pallas_call x4, Pallas kernels, backproject(): pl.pallas_call(functools.partial(image_kernel, (leaf, each, half, beams,...  4.58 us
    cos x2, other arithmetic, unit(): return (jnp.cos(angle), jnp.sin(angle))  2.44 us
    another operation x4, other arithmetic, per_device(): jnp.stack([keeps[n][part].reshape(shape), gots[n][part].reshape(shape)])  2.18 us
  transfers between devices with their start and end apart: 15, of which 5 were waited for; matrix products, arithmetic and copies ran while one was open for 16% of the time, Pallas kernels for 12%

profile of v14, /device:TPU:0, one launch (start us, length us, event | category | flops | bytes accessed | tf_op | source)
XLA Modules:
  0.0 50.8 jit_solution(6423570573978438691)
XLA Ops:
  0.0 3.4 %compress.2 = (bf16[1,1,8,64,256]{4,3,2,1,0:T(8,128)(2,1)}, bf16[1,1,8,64,256]{4,3,2,1,0:T(8,128)(2,1)}, bf16[1,1,8,64,256]{4,3,2,1,0:T(8,128)(2,1)}, bf16[1,1,8,64,256]{4,3,2,1,0:T(8,128)(2,1)}) custom-call(bf16[2,128]{1,0:T(2,128)(2,1)} %chirp_ref.2, bf16[64,64,256]{2,1,0:T(8,128)(2,1)} %refs_0_.1), custom_call_target="tpu_custom_call" | custom-call | flops 536870912 | bytes 2097152 | tf_op jit(solution)/shard_map/compress/pallas_call | solution.py:128
  3.4 3.0 %collective-permute-start = (bf16[1,1,8,64,256]{4,3,2,1,0:T(8,128)(2,1)}, bf16[1,1,8,64,256]{4,3,2,1,0:T(8,128)(2,1)}, u32[]{:S(2)}, u32[]{:S(2)}) collective-permute-start(bf16[1,1,8,64,256]{4,3,2,1,0:T(8,128)(2,1)} %get-tuple-element.35), channel_id=1, source_target_pairs={{0,1},{1,0},{2,3},{3,2},{4,5},{5,4},{6,7},{7,6},{8,9},{9,8},{10,11... | collective-permute-start | bytes 786440 | tf_op jit(solution)/shard_map/ppermute | solution.py:25
  6.6 1.4 %compress.3 = (bf16[1,1,8,64,256]{4,3,2,1,0:T(8,128)(2,1)S(1)}, bf16[1,1,8,64,256]{4,3,2,1,0:T(8,128)(2,1)S(1)}, bf16[1,1,8,64,256]{4,3,2,1,0:T(8,128)(2,1)S(1)}, bf16[1,1,8,64,256]{4,3,2,1,0:T(8,128)(2,1)S(1)}) custom-call(bf16[2,128]{1,0:T(2,128)(2,1)S(1)} %copy-done.1, bf16[64,64,256]{2,1,0:T(8,128)(2,1)S(1)} %copy-done, bf16[64,64,256]{2,1,0:T(8,128)(2,1)S(1)} %copy-done), custom_call_target="tpu_custom_call" | custom-call | flops 536870912 | bytes 2097152 | tf_op jit(solution)/shard_map/compress/pallas_call | solution.py:128
  8.0 2.1 %collective-permute-start.5 = (bf16[1,1,8,64,256]{4,3,2,1,0:T(8,128)(2,1)S(1)}, bf16[1,1,8,64,256]{4,3,2,1,0:T(8,128)(2,1)S(1)}, u32[]{:S(2)}, u32[]{:S(2)}) collective-permute-start(bf16[1,1,8,64,256]{4,3,2,1,0:T(8,128)(2,1)S(1)} %get-tuple-element.48), channel_id=1, source_target_pairs={{0,2},{1,3},{2,0},{3,1},{4,6},{5,7},{6,4},{7,5},{8,10},{9,11},{10,... | collective-permute-start | bytes 786440 | tf_op jit(solution)/shard_map/ppermute | solution.py:25
  10.2 0.2 select_reduce_fusion.1
  10.7 0.3 fusion.64
  11.7 0.4 select_reduce_fusion
  12.1 0.5 multiply_convert_fusion.1
  12.6 0.2 fusion.31
  12.9 2.1 %fusion.11 = (f32[2,1,128,512]{3,2,1,0:T(8,128)S(1)}, f32[2,1,128,512]{3,2,1,0:T(8,128)S(1)}) fusion(s32[512]{0:T(512)S(1)} %iota_add_fusion, s32[2,128]{1,0:T(2,128)S(1)} %add_multiply_fusion), kind=kLoop, calls=%fused_computation.37 | loop fusion | flops 1835008 | bytes 1051648 | tf_op jit(solution)/shard_map/cos | solution.py:30
  15.5 3.2 %collective-permute-done.1 = bf16[1,1,8,64,256]{4,3,2,1,0:T(8,128)(2,1)} collective-permute-done((bf16[1,1,8,64,256]{4,3,2,1,0:T(8,128)(2,1)}, bf16[1,1,8,64,256]{4,3,2,1,0:T(8,128)(2,1)}, u32[]{:S(2)}, u32[]{:S(2)}) %collective-permute-start.1) | collective-permute-done | bytes 262176 | tf_op jit(solution)/shard_map/ppermute | solution.py:25
  18.7 1.1 %pad_maximum_fusion.2.data_ref = bf16[2,1,1,2,4,64,256]{6,5,4,3,2,1,0:T(8,128)(2,1)S(1)} fusion(bf16[1,1,1,2,4,64,256]{6,5,4,3,2,1,0:T(8,128)(2,1)} %bitcast.19, bf16[1,1,1,2,4,64,256]{6,5,4,3,2,1,0:T(8,128)(2,1)} %bitcast.157), kind=kLoop, calls=%fused_computation.15 | loop fusion | flops 262144 | bytes 1048576 | tf_op jit(solution)/shard_map/stack | solution.py:402
  19.8 1.1 %image.4 = (f32[2,2,1,2,1,4,32,256]{7,6,5,4,3,2,1,0:T(8,128)S(1)}, bf16[2,2,1,2,1,4,32,256]{7,6,5,4,3,2,1,0:T(8,128)(2,1)S(1)}) custom-call(bf16[2,1,1,2,4,64,256]{6,5,4,3,2,1,0:T(8,128)(2,1)S(1)} %pad_maximum_fusion.2.data_ref, bf16[256,256]{1,0:T(8,128)(2,1)S(1)} %copy.39.steer_ref, bf16[1,128,256]{2,1,0:T(8,128)(2,1)S(1)} %pad_maximum_fusion.8.interp_ref, ...), custom_call_target="tpu_custom_call" | custom-call | flops 201326592 | bytes 1310720 | tf_op jit(solution)/shard_map/image/pallas_call | solution.py:235
  21.0 1.0 %pad_maximum_fusion.1.data_ref = bf16[2,1,1,2,4,64,256]{6,5,4,3,2,1,0:T(8,128)(2,1)S(1)} fusion(bf16[1,1,1,2,4,64,256]{6,5,4,3,2,1,0:T(8,128)(2,1)} %bitcast.1, bf16[1,1,1,2,4,64,256]{6,5,4,3,2,1,0:T(8,128)(2,1)S(1)} %bitcast.156), kind=kLoop, calls=%fused_computation.14 | loop fusion | flops 262144 | bytes 1048576 | tf_op jit(solution)/shard_map/stack | solution.py:402
  22.0 1.1 %image.5 = (f32[2,2,1,2,1,4,32,256]{7,6,5,4,3,2,1,0:T(8,128)S(1)}, bf16[2,2,1,2,1,4,32,256]{7,6,5,4,3,2,1,0:T(8,128)(2,1)S(1)}) custom-call(bf16[2,1,1,2,4,64,256]{6,5,4,3,2,1,0:T(8,128)(2,1)S(1)} %pad_maximum_fusion.1.data_ref, bf16[256,256]{1,0:T(8,128)(2,1)S(1)} %copy.39.steer_ref, ...), custom_call_target="tpu_custom_call", output_to_operand_aliasing={{0}: (5, {}), {1}: (6, {})} | custom-call | flops 201326592 | bytes 1310720 | tf_op jit(solution)/shard_map/image/pallas_call | solution.py:235
  23.3 1.1 %image.6 = (f32[2,2,1,1,2,4,32,256]{7,6,5,4,3,2,1,0:T(8,128)S(1)}, bf16[2,2,1,1,2,4,32,256]{7,6,5,4,3,2,1,0:T(8,128)(2,1)S(1)}) custom-call(bf16[2,1,1,2,4,64,256]{6,5,4,3,2,1,0:T(8,128)(2,1)S(1)} %pad_maximum_fusion.4.data_ref, bf16[256,256]{1,0:T(8,128)(2,1)S(1)} %copy.40.steer_ref, bf16[1,128,256]{2,1,0:T(8,128)(2,1)S(1)} %pad_maximum_fusion.8.interp_ref, ...), custom_call_target="tpu_custom_call" | custom-call | flops 201326592 | bytes 1310720 | tf_op jit(solution)/shard_map/image/pallas_call | solution.py:235
  24.5 1.1 %image.7 = (f32[2,2,1,1,2,4,32,256]{7,6,5,4,3,2,1,0:T(8,128)S(1)}, bf16[2,2,1,1,2,4,32,256]{7,6,5,4,3,2,1,0:T(8,128)(2,1)S(1)}) custom-call(bf16[2,1,1,2,4,64,256]{6,5,4,3,2,1,0:T(8,128)(2,1)S(1)} %pad_maximum_fusion.3.data_ref, bf16[256,256]{1,0:T(8,128)(2,1)S(1)} %copy.40.steer_ref, ...), custom_call_target="tpu_custom_call", output_to_operand_aliasing={{0}: (5, {}), {1}: (6, {})} | custom-call | flops 201326592 | bytes 1310720 | tf_op jit(solution)/shard_map/image/pallas_call | solution.py:235
  25.8 0.5 %collective-permute-start.7 = (bf16[2,2,1,1,2,4,32,256]{7,6,5,4,3,2,1,0:T(8,128)(2,1)S(1)}, bf16[2,2,1,1,2,4,32,256]{7,6,5,4,3,2,1,0:T(8,128)(2,1)S(1)}, u32[]{:S(2)}, u32[]{:S(2)}) collective-permute-start(bf16[2,2,1,1,2,4,32,256]{7,6,5,4,3,2,1,0:T(8,128)(2,1)S(1)} %get-tuple-element.54), channel_id=1, source_target_pairs={{0,8},{8,0},{16,24},{24,16},{1,9},{9,1},{17,25},{25,17},{2,10},{10... | collective-permute-start | bytes 1572872 | tf_op jit(solution)/shard_map/ppermute | solution.py:25
  26.7 1.8 %collective-permute-start.10 = (bf16[1,8,32,256]{3,2,1,0:T(8,128)(2,1)S(1)}, bf16[1,8,32,256]{3,2,1,0:T(8,128)(2,1)S(1)}, u32[]{:S(2)}, u32[]{:S(2)}) collective-permute-start(bf16[1,8,32,256]{3,2,1,0:T(8,128)(2,1)S(1)} %get-tuple-element.75), channel_id=1, source_target_pairs={{0,16},{8,24},{16,0},{24,8},{1,17},{9,25},{17,1},{25,9},{2,18},{10... | collective-permute-start | bytes 393224 | tf_op jit(solution)/shard_map/ppermute | solution.py:25
  28.5 0.4 collective-permute-start.3
  29.0 1.8 %collective-permute-start.12 = (bf16[2,4,32,256]{3,2,1,0:T(8,128)(2,1)S(1)}, bf16[2,4,32,256]{3,2,1,0:T(8,128)(2,1)S(1)}, u32[]{:S(2)}, u32[]{:S(2)}) collective-permute-start(bf16[2,4,32,256]{3,2,1,0:T(8,128)(2,1)S(1)} %fusion.15), channel_id=1, source_target_pairs={{0,1},{1,0},{2,3},{3,2},{4,5},{5,4},{6,7},{7,6},{8,9},{9,8},{10,11... | collective-permute-start | bytes 393224 | tf_op jit(solution)/shard_map/ppermute | solution.py:25
  30.9 0.4 collective-permute-start.8
  31.3 1.8 %collective-permute-done.10 = bf16[1,8,32,256]{3,2,1,0:T(8,128)(2,1)S(1)} collective-permute-done((bf16[1,8,32,256]{3,2,1,0:T(8,128)(2,1)S(1)}, bf16[1,8,32,256]{3,2,1,0:T(8,128)(2,1)S(1)}, u32[]{:S(2)}, u32[]{:S(2)}) %collective-permute-start.10) | collective-permute-done | bytes 131104 | tf_op jit(solution)/shard_map/ppermute | solution.py:25
  33.1 1.9 %collective-permute-start.11 = (bf16[1,4,32,256]{3,2,1,0:T(8,128)(2,1)S(1)}, bf16[1,4,32,256]{3,2,1,0:T(8,128)(2,1)S(1)}, u32[]{:S(2)}, u32[]{:S(2)}) collective-permute-start(bf16[1,4,32,256]{3,2,1,0:T(8,128)(2,1)S(1)} %fusion.36), channel_id=1, source_target_pairs={{0,2},{1,3},{2,0},{3,1},{4,6},{5,7},{6,4},{7,5},{8,10},{9,11},{10,... | collective-permute-start | bytes 196616 | tf_op jit(solution)/shard_map/ppermute | solution.py:25
  35.0 1.9 %collective-permute-start.4 = (bf16[1,4,32,256]{3,2,1,0:T(8,128)(2,1)S(1)}, bf16[1,4,32,256]{3,2,1,0:T(8,128)(2,1)S(1)}, u32[]{:S(2)}, u32[]{:S(2)}) collective-permute-start(bf16[1,4,32,256]{3,2,1,0:T(8,128)(2,1)S(1)} %fusion.34), channel_id=1, source_target_pairs={{0,2},{1,3},{2,0},{3,1},{4,6},{5,7},{6,4},{7,5},{8,10},{9,11},{10,... | collective-permute-start | bytes 196616 | tf_op jit(solution)/shard_map/ppermute | solution.py:25
  36.9 1.6 %collective-permute-start.13 = (bf16[1,4,32,256]{3,2,1,0:T(8,128)(2,1)S(1)}, bf16[1,4,32,256]{3,2,1,0:T(8,128)(2,1)S(1)}, u32[]{:S(2)}, u32[]{:S(2)}) collective-permute-start(bf16[1,4,32,256]{3,2,1,0:T(8,128)(2,1)S(1)} %fusion.37), channel_id=1, source_target_pairs={{0,16},{8,24},{16,0},{24,8},{1,17},{9,25},{17,1},{25,9},{2,18},{10... | collective-permute-start | bytes 196616 | tf_op jit(solution)/shard_map/ppermute | solution.py:25
  38.5 0.6 %collective-permute-start.9 = (bf16[1,4,32,256]{3,2,1,0:T(8,128)(2,1)S(1)}, bf16[1,4,32,256]{3,2,1,0:T(8,128)(2,1)S(1)}, u32[]{:S(2)}, u32[]{:S(2)}) collective-permute-start(bf16[1,4,32,256]{3,2,1,0:T(8,128)(2,1)S(1)} %fusion.35), channel_id=1, source_target_pairs={{0,16},{8,24},{16,0},{24,8},{1,17},{9,25},{17,1},{25,9},{2,18},{10... | collective-permute-start | bytes 196616 | tf_op jit(solution)/shard_map/ppermute | solution.py:25
  39.1 2.1 %collective-permute-done.13 = bf16[1,4,32,256]{3,2,1,0:T(8,128)(2,1)S(1)} collective-permute-done((bf16[1,4,32,256]{3,2,1,0:T(8,128)(2,1)S(1)}, bf16[1,4,32,256]{3,2,1,0:T(8,128)(2,1)S(1)}, u32[]{:S(2)}, u32[]{:S(2)}) %collective-permute-start.13) | collective-permute-done | bytes 65568 | tf_op jit(solution)/shard_map/ppermute | solution.py:25
  41.3 1.5 %collective-permute-done.9 = bf16[1,4,32,256]{3,2,1,0:T(8,128)(2,1)S(1)} collective-permute-done((bf16[1,4,32,256]{3,2,1,0:T(8,128)(2,1)S(1)}, bf16[1,4,32,256]{3,2,1,0:T(8,128)(2,1)S(1)}, u32[]{:S(2)}, u32[]{:S(2)}) %collective-permute-start.9) | collective-permute-done | bytes 65568 | tf_op jit(solution)/shard_map/ppermute | solution.py:25
  42.9 2.7 %collective-permute-start.14 = (bf16[2,4,32,256]{3,2,1,0:T(8,128)(2,1)S(1)}, bf16[2,4,32,256]{3,2,1,0:T(8,128)(2,1)S(1)}, u32[]{:S(2)}, u32[]{:S(2)}) collective-permute-start(bf16[2,4,32,256]{3,2,1,0:T(8,128)(2,1)S(1)} %pad_maximum_fusion.7), channel_id=1, source_target_pairs={{0,4},{1,5},{2,6},{3,7},{4,0},{5,1},{6,2},{7,3},{8,12},{9,13},{10,... | collective-permute-start | bytes 393224 | tf_op jit(solution)/shard_map/ppermute | solution.py:25
  45.6 4.5 %collective-permute-done.14 = bf16[2,4,32,256]{3,2,1,0:T(8,128)(2,1)S(1)} collective-permute-done((bf16[2,4,32,256]{3,2,1,0:T(8,128)(2,1)S(1)}, bf16[2,4,32,256]{3,2,1,0:T(8,128)(2,1)S(1)}, u32[]{:S(2)}, u32[]{:S(2)}) %collective-permute-start.14) | collective-permute-done | bytes 131104 | tf_op jit(solution)/shard_map/ppermute | solution.py:25
  50.1 0.7 %last_sum.1 = bf16[32,8,256]{2,1,0:T(8,128)(2,1)} custom-call(f32[8,32,256]{2,1,0:T(8,128)S(1)} %bitcast.132, bf16[8,32,256]{2,1,0:T(8,128)(2,1)S(1)} %bitcast.135), custom_call_target="tpu_custom_call" | custom-call | tf_op jit(solution)/shard_map/last_sum/pallas_call | solution.py:282
  (89 shorter events, 2.8 us)
Async XLA Ops:
  0.0 6.6 %copy-start.1 = (bf16[2,128]{1,0:T(2,128)(2,1)S(1)}, bf16[2,128]{1,0:T(2,128)(2,1)}, u32[]{:S(2)}) copy-start(bf16[2,128]{1,0:T(2,128)(2,1)} %chirp_ref.2) | copy-start | bytes 1540
  0.0 6.6 %copy-start = (bf16[64,64,256]{2,1,0:T(8,128)(2,1)S(1)}, bf16[64,64,256]{2,1,0:T(8,128)(2,1)}, u32[]{:S(2)}) copy-start(bf16[64,64,256]{2,1,0:T(8,128)(2,1)} %refs_0_.1) | copy-start | bytes 6291460
  3.4 6.8 %copy-start.5 = (s32[1,8]{1,0:T(1,128)S(1)}, s32[1,8]{1,0:T(1,128)}, u32[]{:S(2)}) copy-start(s32[1,8]{1,0:T(1,128)} %param.9) | copy-start | bytes 100
  3.4 7.8 %copy-start.3 = (s32[2,2,128,8]{2,3,1,0:T(8,128)S(1)}, s32[2,2,128,8]{2,3,1,0:T(8,128)}, u32[]{:S(2)}) copy-start(s32[2,2,128,8]{2,3,1,0:T(8,128)} %param.8) | copy-start | bytes 49156
  3.4 8.3 %copy-start.4 = (f32[8]{0:T(128)S(1)}, f32[8]{0:T(128)}, u32[]{:S(2)}) copy-start(f32[8]{0:T(128)} %constant.200.clone) | copy-start | bytes 100
  3.4 17.5 %collective-permute-start = (bf16[1,1,8,64,256]{4,3,2,1,0:T(8,128)(2,1)}, bf16[1,1,8,64,256]{4,3,2,1,0:T(8,128)(2,1)}, u32[]{:S(2)}, u32[]{:S(2)}) collective-permute-start(bf16[1,1,8,64,256]{4,3,2,1,0:T(8,128)(2,1)} %get-tuple-element.35), channel_id=1, source_target_pairs={{0,1},{1,0},{2,3},{3,2},{4,5},{5,4},{6,7},{7,6},{8,9},{9,8},{10,11... | collective-permute-start | bytes 786440 | tf_op jit(solution)/shard_map/ppermute | solution.py:25
  6.5 12.2 %collective-permute-start.1 = (bf16[1,1,8,64,256]{4,3,2,1,0:T(8,128)(2,1)}, bf16[1,1,8,64,256]{4,3,2,1,0:T(8,128)(2,1)}, u32[]{:S(2)}, u32[]{:S(2)}) collective-permute-start(bf16[1,1,8,64,256]{4,3,2,1,0:T(8,128)(2,1)} %get-tuple-element.37), channel_id=1, source_target_pairs={{0,1},{1,0},{2,3},{3,2},{4,5},{5,4},{6,7},{7,6},{8,9},{9,8},{10,11... | collective-permute-start | bytes 786440 | tf_op jit(solution)/shard_map/ppermute | solution.py:25
  8.0 15.2 %collective-permute-start.5 = (bf16[1,1,8,64,256]{4,3,2,1,0:T(8,128)(2,1)S(1)}, bf16[1,1,8,64,256]{4,3,2,1,0:T(8,128)(2,1)S(1)}, u32[]{:S(2)}, u32[]{:S(2)}) collective-permute-start(bf16[1,1,8,64,256]{4,3,2,1,0:T(8,128)(2,1)S(1)} %get-tuple-element.48), channel_id=1, source_target_pairs={{0,2},{1,3},{2,0},{3,1},{4,6},{5,7},{6,4},{7,5},{8,10},{9,11},{10,... | collective-permute-start | bytes 786440 | tf_op jit(solution)/shard_map/ppermute | solution.py:25
  10.0 13.2 %collective-permute-start.6 = (bf16[1,1,8,64,256]{4,3,2,1,0:T(8,128)(2,1)S(1)}, bf16[1,1,8,64,256]{4,3,2,1,0:T(8,128)(2,1)S(1)}, u32[]{:S(2)}, u32[]{:S(2)}) collective-permute-start(bf16[1,1,8,64,256]{4,3,2,1,0:T(8,128)(2,1)S(1)} %get-tuple-element.50), channel_id=1, source_target_pairs={{0,2},{1,3},{2,0},{3,1},{4,6},{5,7},{6,4},{7,5},{8,10},{9,11},{10,... | collective-permute-start | bytes 786440 | tf_op jit(solution)/shard_map/ppermute | solution.py:25
  15.1 5.8 %copy-start.2 = (bf16[1,1,8,64,256]{4,3,2,1,0:T(8,128)(2,1)S(1)}, bf16[1,1,8,64,256]{4,3,2,1,0:T(8,128)(2,1)}, u32[]{:S(2)}) copy-start(bf16[1,1,8,64,256]{4,3,2,1,0:T(8,128)(2,1)} %get-tuple-element.34) | copy-start | bytes 786436
  23.1 3.4 %collective-permute-start.2 = (bf16[2,2,1,2,1,4,32,256]{7,6,5,4,3,2,1,0:T(8,128)(2,1)S(1)}, bf16[2,2,1,2,1,4,32,256]{7,6,5,4,3,2,1,0:T(8,128)(2,1)S(1)}, u32[]{:S(2)}, u32[]{:S(2)}) collective-permute-start(bf16[2,2,1,2,1,4,32,256]{7,6,5,4,3,2,1,0:T(8,128)(2,1)S(1)} %get-tuple-element.41), channel_id=1, source_target_pairs={{0,8},{8,0},{16,24},{24,16},{1,9},{9,1},{17,25},{25,17},{2,10},{10... | collective-permute-start | bytes 1572872 | tf_op jit(solution)/shard_map/ppermute | solution.py:25
  25.8 3.2 %collective-permute-start.7 = (bf16[2,2,1,1,2,4,32,256]{7,6,5,4,3,2,1,0:T(8,128)(2,1)S(1)}, bf16[2,2,1,1,2,4,32,256]{7,6,5,4,3,2,1,0:T(8,128)(2,1)S(1)}, u32[]{:S(2)}, u32[]{:S(2)}) collective-permute-start(bf16[2,2,1,1,2,4,32,256]{7,6,5,4,3,2,1,0:T(8,128)(2,1)S(1)} %get-tuple-element.54), channel_id=1, source_target_pairs={{0,8},{8,0},{16,24},{24,16},{1,9},{9,1},{17,25},{25,17},{2,10},{10... | collective-permute-start | bytes 1572872 | tf_op jit(solution)/shard_map/ppermute | solution.py:25
  26.7 6.4 %collective-permute-start.10 = (bf16[1,8,32,256]{3,2,1,0:T(8,128)(2,1)S(1)}, bf16[1,8,32,256]{3,2,1,0:T(8,128)(2,1)S(1)}, u32[]{:S(2)}, u32[]{:S(2)}) collective-permute-start(bf16[1,8,32,256]{3,2,1,0:T(8,128)(2,1)S(1)} %get-tuple-element.75), channel_id=1, source_target_pairs={{0,16},{8,24},{16,0},{24,8},{1,17},{9,25},{17,1},{25,9},{2,18},{10... | collective-permute-start | bytes 393224 | tf_op jit(solution)/shard_map/ppermute | solution.py:25
  28.5 6.5 %collective-permute-start.3 = (bf16[1,8,32,256]{3,2,1,0:T(8,128)(2,1)S(1)}, bf16[1,8,32,256]{3,2,1,0:T(8,128)(2,1)S(1)}, u32[]{:S(2)}, u32[]{:S(2)}) collective-permute-start(bf16[1,8,32,256]{3,2,1,0:T(8,128)(2,1)S(1)} %get-tuple-element.73), channel_id=1, source_target_pairs={{0,16},{8,24},{16,0},{24,8},{1,17},{9,25},{17,1},{25,9},{2,18},{10... | collective-permute-start | bytes 393224 | tf_op jit(solution)/shard_map/ppermute | solution.py:25
  29.0 7.8 %collective-permute-start.12 = (bf16[2,4,32,256]{3,2,1,0:T(8,128)(2,1)S(1)}, bf16[2,4,32,256]{3,2,1,0:T(8,128)(2,1)S(1)}, u32[]{:S(2)}, u32[]{:S(2)}) collective-permute-start(bf16[2,4,32,256]{3,2,1,0:T(8,128)(2,1)S(1)} %fusion.15), channel_id=1, source_target_pairs={{0,1},{1,0},{2,3},{3,2},{4,5},{5,4},{6,7},{7,6},{8,9},{9,8},{10,11... | collective-permute-start | bytes 393224 | tf_op jit(solution)/shard_map/ppermute | solution.py:25
  30.9 7.5 %collective-permute-start.8 = (bf16[2,4,32,256]{3,2,1,0:T(8,128)(2,1)S(1)}, bf16[2,4,32,256]{3,2,1,0:T(8,128)(2,1)S(1)}, u32[]{:S(2)}, u32[]{:S(2)}) collective-permute-start(bf16[2,4,32,256]{3,2,1,0:T(8,128)(2,1)S(1)} %get-tuple-element.71), channel_id=1, source_target_pairs={{0,1},{1,0},{2,3},{3,2},{4,5},{5,4},{6,7},{7,6},{8,9},{9,8},{10,11... | collective-permute-start | bytes 393224 | tf_op jit(solution)/shard_map/ppermute | solution.py:25
  33.1 5.9 %collective-permute-start.11 = (bf16[1,4,32,256]{3,2,1,0:T(8,128)(2,1)S(1)}, bf16[1,4,32,256]{3,2,1,0:T(8,128)(2,1)S(1)}, u32[]{:S(2)}, u32[]{:S(2)}) collective-permute-start(bf16[1,4,32,256]{3,2,1,0:T(8,128)(2,1)S(1)} %fusion.36), channel_id=1, source_target_pairs={{0,2},{1,3},{2,0},{3,1},{4,6},{5,7},{6,4},{7,5},{8,10},{9,11},{10,... | collective-permute-start | bytes 196616 | tf_op jit(solution)/shard_map/ppermute | solution.py:25
  35.0 6.3 %collective-permute-start.4 = (bf16[1,4,32,256]{3,2,1,0:T(8,128)(2,1)S(1)}, bf16[1,4,32,256]{3,2,1,0:T(8,128)(2,1)S(1)}, u32[]{:S(2)}, u32[]{:S(2)}) collective-permute-start(bf16[1,4,32,256]{3,2,1,0:T(8,128)(2,1)S(1)} %fusion.34), channel_id=1, source_target_pairs={{0,2},{1,3},{2,0},{3,1},{4,6},{5,7},{6,4},{7,5},{8,10},{9,11},{10,... | collective-permute-start | bytes 196616 | tf_op jit(solution)/shard_map/ppermute | solution.py:25
  36.9 4.3 %collective-permute-start.13 = (bf16[1,4,32,256]{3,2,1,0:T(8,128)(2,1)S(1)}, bf16[1,4,32,256]{3,2,1,0:T(8,128)(2,1)S(1)}, u32[]{:S(2)}, u32[]{:S(2)}) collective-permute-start(bf16[1,4,32,256]{3,2,1,0:T(8,128)(2,1)S(1)} %fusion.37), channel_id=1, source_target_pairs={{0,16},{8,24},{16,0},{24,8},{1,17},{9,25},{17,1},{25,9},{2,18},{10... | collective-permute-start | bytes 196616 | tf_op jit(solution)/shard_map/ppermute | solution.py:25
  38.5 4.3 %collective-permute-start.9 = (bf16[1,4,32,256]{3,2,1,0:T(8,128)(2,1)S(1)}, bf16[1,4,32,256]{3,2,1,0:T(8,128)(2,1)S(1)}, u32[]{:S(2)}, u32[]{:S(2)}) collective-permute-start(bf16[1,4,32,256]{3,2,1,0:T(8,128)(2,1)S(1)} %fusion.35), channel_id=1, source_target_pairs={{0,16},{8,24},{16,0},{24,8},{1,17},{9,25},{17,1},{25,9},{2,18},{10... | collective-permute-start | bytes 196616 | tf_op jit(solution)/shard_map/ppermute | solution.py:25
  42.9 7.2 %collective-permute-start.14 = (bf16[2,4,32,256]{3,2,1,0:T(8,128)(2,1)S(1)}, bf16[2,4,32,256]{3,2,1,0:T(8,128)(2,1)S(1)}, u32[]{:S(2)}, u32[]{:S(2)}) collective-permute-start(bf16[2,4,32,256]{3,2,1,0:T(8,128)(2,1)S(1)} %pad_maximum_fusion.7), channel_id=1, source_target_pairs={{0,4},{1,5},{2,6},{3,7},{4,0},{5,1},{6,2},{7,3},{8,12},{9,13},{10,... | collective-permute-start | bytes 393224 | tf_op jit(solution)/shard_map/ppermute | solution.py:25

commit v15 on v13

--- a/solution.py
+++ b/solution.py
@@ -165,7 +165,7 @@
 def image_kernel(dims, data_ref, steer_ref, interp_ref, base_ref, step_ref, out_keep, out_send):
     leaf, each, half, beams, levels = dims
     rows = beams // leaf
-    pair = 2
+    pair = each
     piece = rows
 
     def turned(phase, re, im):

time: 48.7 us -> 48.7 us (level)
  no operation moved by 1% of the time
where the time goes in v15:
time: 48.7 us; the launch traced here: 48.6 us
  starting transfers between devices  17.8 us (37%)
  waiting for transfers between devices  14.2 us (29%)
  Pallas kernels  10 us (21%)
  other arithmetic  4.9 us (10%)
  local copies, waits for them, and re-layouts  1.05 us (2%)
    ppermute x13, starting transfers between devices, swapped(): lax.ppermute(array, axis, [(i, i ^ 1 << bit) for i in range(lax.axis_size...  17.8 us
    ppermute x13, waiting for transfers between devices, swapped(): lax.ppermute(array, axis, [(i, i ^ 1 << bit) for i in range(lax.axis_size...  14.2 us
    pallas_call x2, Pallas kernels, compress(): pl.pallas_call(functools.partial(compress_kernel, dims, has_edge), grid=(...  4.66 us
    pallas_call x2, Pallas kernels, backproject(): pl.pallas_call(functools.partial(image_kernel, (leaf, each, half, beams,...  4.62 us
    cos x2, other arithmetic, unit(): return (jnp.cos(angle), jnp.sin(angle))  2.27 us
  transfers between devices with their start and end apart: 13, of which 8 were waited for; matrix products, arithmetic and copies ran while one was open for 12% of the time, Pallas kernels for 12%

profile of v15, /device:TPU:0, one launch (start us, length us, event | category | flops | bytes accessed | tf_op | source)
XLA Modules:
  0.0 48.6 jit_solution(9701631684178123618)
XLA Ops:
  0.0 3.3 %compress.2 = (bf16[1,2,1,8,64,256]{5,4,3,2,1,0:T(8,128)(2,1)}, bf16[1,2,1,8,64,256]{5,4,3,2,1,0:T(8,128)(2,1)}) custom-call(bf16[2,128]{1,0:T(2,128)(2,1)} %chirp_ref.2, bf16[64,64,256]{2,1,0:T(8,128)(2,1)} %refs_0_.1), custom_call_target="tpu_custom_call" | custom-call | flops 536870912 | bytes 2097152 | tf_op jit(solution)/shard_map/compress/pallas_call | solution.py:142
  3.3 3.1 %collective-permute-start = (bf16[1,2,1,8,64,256]{5,4,3,2,1,0:T(8,128)(2,1)}, bf16[1,2,1,8,64,256]{5,4,3,2,1,0:T(8,128)(2,1)S(1)}, u32[]{:S(2)}, u32[]{:S(2)}) collective-permute-start(bf16[1,2,1,8,64,256]{5,4,3,2,1,0:T(8,128)(2,1)} %get-tuple-element.17), channel_id=1, source_target_pairs={{0,1},{1,0},{2,3},{3,2},{4,5},{5,4},{6,7},{7,6},{8,9},{9,8},{10,11... | collective-permute-start | bytes 1572872 | tf_op jit(solution)/shard_map/ppermute | solution.py:25
  6.4 1.4 %compress.3 = (bf16[1,1,2,8,64,256]{5,4,3,2,1,0:T(8,128)(2,1)S(1)}, bf16[1,1,2,8,64,256]{5,4,3,2,1,0:T(8,128)(2,1)S(1)}) custom-call(bf16[2,128]{1,0:T(2,128)(2,1)S(1)} %copy-done.1, bf16[64,64,256]{2,1,0:T(8,128)(2,1)S(1)} %copy-done, bf16[64,64,256]{2,1,0:T(8,128)(2,1)S(1)} %copy-done), custom_call_target="tpu_custom_call" | custom-call | flops 536870912 | bytes 2097152 | tf_op jit(solution)/shard_map/compress/pallas_call | solution.py:142
  7.8 1.6 %collective-permute-start.4 = (bf16[1,1,2,8,64,256]{5,4,3,2,1,0:T(8,128)(2,1)S(1)}, bf16[1,1,2,8,64,256]{5,4,3,2,1,0:T(8,128)(2,1)S(1)}, u32[]{:S(2)}, u32[]{:S(2)}) collective-permute-start(bf16[1,1,2,8,64,256]{5,4,3,2,1,0:T(8,128)(2,1)S(1)} %get-tuple-element.22), channel_id=1, source_target_pairs={{0,2},{1,3},{2,0},{3,1},{4,6},{5,7},{6,4},{7,5},{8,10},{9,11},{10,... | collective-permute-start | bytes 1572872 | tf_op jit(solution)/shard_map/ppermute | solution.py:25
  9.5 0.2 select_reduce_fusion.1
  10.3 0.1 copy.35
  10.6 0.4 select_reduce_fusion
  11.0 0.5 multiply_convert_fusion.1
  11.5 0.2 fusion.30
  11.9 0.2 fusion.47
  12.4 2.1 %fusion.10 = (f32[2,1,128,512]{3,2,1,0:T(8,128)S(1)}, f32[2,1,128,512]{3,2,1,0:T(8,128)S(1)}) fusion(s32[512]{0:T(512)S(1)} %iota_add_fusion, s32[2,128]{1,0:T(2,128)S(1)} %add_multiply_fusion), kind=kLoop, calls=%fused_computation.33 | loop fusion | flops 1835008 | bytes 1051648 | tf_op jit(solution)/shard_map/cos | solution.py:30
  14.6 3.9 %collective-permute-done = bf16[1,2,1,8,64,256]{5,4,3,2,1,0:T(8,128)(2,1)S(1)} collective-permute-done((bf16[1,2,1,8,64,256]{5,4,3,2,1,0:T(8,128)(2,1)}, bf16[1,2,1,8,64,256]{5,4,3,2,1,0:T(8,128)(2,1)S(1)}, u32[]{:S(2)}, u32[]{:S(2)}) %collective-permute-start) | collective-permute-done | bytes 524320 | tf_op jit(solution)/shard_map/ppermute | solution.py:25
  18.6 2.3 %image.2 = (f32[2,4,4,32,256]{4,3,2,1,0:T(8,128)S(1)}, bf16[2,4,4,32,256]{4,3,2,1,0:T(8,128)(2,1)S(1)}) custom-call(bf16[2,4,4,64,256]{4,3,2,1,0:T(8,128)(2,1)S(1)} %pad_maximum_fusion.data_ref, bf16[256,256]{1,0:T(8,128)(2,1)S(1)} %copy.44.steer_ref, bf16[1,128,256]{2,1,0:T(8,128)(2,1)S(1)} %pad_maximum_fusion.6.interp_ref, f32[4,4,128]{2,1,0:T(4,128)S(1)} %bitcast.120, ...), custom_call_target="tpu_custom_call" | custom-call | flops 402653184 | bytes 2621440 | tf_op jit(solution)/shard_map/image/pallas_call | solution.py:247
  21.0 0.2 collective-permute-done.4
  21.3 2.3 %image.3 = (f32[2,4,4,32,256]{4,3,2,1,0:T(8,128)S(1)}, bf16[2,4,4,32,256]{4,3,2,1,0:T(8,128)(2,1)S(1)}) custom-call(bf16[2,4,4,64,256]{4,3,2,1,0:T(8,128)(2,1)S(1)} %pad_maximum_fusion.2.data_ref, bf16[256,256]{1,0:T(8,128)(2,1)S(1)} %copy.45.steer_ref, bf16[1,128,256]{2,1,0:T(8,128)(2,1)S(1)} %pad_maximum_fusion.6.interp_ref, f32[4,4,128]{2,1,0:T(4,128)S(1)} %bitcast.119, ...), custom_call_target="tpu_custom_call" | custom-call | flops 402653184 | bytes 2621440 | tf_op jit(solution)/shard_map/image/pallas_call | solution.py:247
  23.8 0.3 collective-permute-start.5
  24.4 1.8 %collective-permute-start.8 = (bf16[1,8,32,256]{3,2,1,0:T(8,128)(2,1)S(1)}, bf16[1,8,32,256]{3,2,1,0:T(8,128)(2,1)S(1)}, u32[]{:S(2)}, u32[]{:S(2)}) collective-permute-start(bf16[1,8,32,256]{3,2,1,0:T(8,128)(2,1)S(1)} %get-tuple-element.39), channel_id=1, source_target_pairs={{0,16},{8,24},{16,0},{24,8},{1,17},{9,25},{17,1},{25,9},{2,18},{10... | collective-permute-start | bytes 393224 | tf_op jit(solution)/shard_map/ppermute | solution.py:25
  26.3 0.3 collective-permute-start.2
  26.8 1.8 %collective-permute-start.6 = (bf16[2,4,32,256]{3,2,1,0:T(8,128)(2,1)S(1)}, bf16[2,4,32,256]{3,2,1,0:T(8,128)(2,1)S(1)}, u32[]{:S(2)}, u32[]{:S(2)}) collective-permute-start(bf16[2,4,32,256]{3,2,1,0:T(8,128)(2,1)S(1)} %get-tuple-element.33), channel_id=1, source_target_pairs={{0,1},{1,0},{2,3},{3,2},{4,5},{5,4},{6,7},{7,6},{8,9},{9,8},{10,11... | collective-permute-start | bytes 393224 | tf_op jit(solution)/shard_map/ppermute | solution.py:25
  28.7 0.3 collective-permute-start.10
  29.0 1.7 %collective-permute-done.8 = bf16[1,8,32,256]{3,2,1,0:T(8,128)(2,1)S(1)} collective-permute-done((bf16[1,8,32,256]{3,2,1,0:T(8,128)(2,1)S(1)}, bf16[1,8,32,256]{3,2,1,0:T(8,128)(2,1)S(1)}, u32[]{:S(2)}, u32[]{:S(2)}) %collective-permute-start.8) | collective-permute-done | bytes 131104 | tf_op jit(solution)/shard_map/ppermute | solution.py:25
  30.8 1.9 %collective-permute-start.9 = (bf16[1,4,32,256]{3,2,1,0:T(8,128)(2,1)S(1)}, bf16[1,4,32,256]{3,2,1,0:T(8,128)(2,1)S(1)}, u32[]{:S(2)}, u32[]{:S(2)}) collective-permute-start(bf16[1,4,32,256]{3,2,1,0:T(8,128)(2,1)S(1)} %fusion.35), channel_id=1, source_target_pairs={{0,2},{1,3},{2,0},{3,1},{4,6},{5,7},{6,4},{7,5},{8,10},{9,11},{10,... | collective-permute-start | bytes 196616 | tf_op jit(solution)/shard_map/ppermute | solution.py:25
  32.7 0.2 collective-permute-done.2
  32.9 1.7 %collective-permute-start.3 = (bf16[1,4,32,256]{3,2,1,0:T(8,128)(2,1)S(1)}, bf16[1,4,32,256]{3,2,1,0:T(8,128)(2,1)S(1)}, u32[]{:S(2)}, u32[]{:S(2)}) collective-permute-start(bf16[1,4,32,256]{3,2,1,0:T(8,128)(2,1)S(1)} %fusion.33), channel_id=1, source_target_pairs={{0,2},{1,3},{2,0},{3,1},{4,6},{5,7},{6,4},{7,5},{8,10},{9,11},{10,... | collective-permute-start | bytes 196616 | tf_op jit(solution)/shard_map/ppermute | solution.py:25
  34.6 1.6 %collective-permute-start.7 = (bf16[1,4,32,256]{3,2,1,0:T(8,128)(2,1)S(1)}, bf16[1,4,32,256]{3,2,1,0:T(8,128)(2,1)S(1)}, u32[]{:S(2)}, u32[]{:S(2)}) collective-permute-start(bf16[1,4,32,256]{3,2,1,0:T(8,128)(2,1)S(1)} %fusion.34), channel_id=1, source_target_pairs={{0,16},{8,24},{16,0},{24,8},{1,17},{9,25},{17,1},{25,9},{2,18},{10... | collective-permute-start | bytes 196616 | tf_op jit(solution)/shard_map/ppermute | solution.py:25
  36.2 0.6 %collective-permute-start.11 = (bf16[1,4,32,256]{3,2,1,0:T(8,128)(2,1)S(1)}, bf16[1,4,32,256]{3,2,1,0:T(8,128)(2,1)S(1)}, u32[]{:S(2)}, u32[]{:S(2)}) collective-permute-start(bf16[1,4,32,256]{3,2,1,0:T(8,128)(2,1)S(1)} %fusion.36), channel_id=1, source_target_pairs={{0,16},{8,24},{16,0},{24,8},{1,17},{9,25},{17,1},{25,9},{2,18},{10... | collective-permute-start | bytes 196616 | tf_op jit(solution)/shard_map/ppermute | solution.py:25
  36.8 0.5 collective-permute-done.3
  37.2 1.7 %collective-permute-done.7 = bf16[1,4,32,256]{3,2,1,0:T(8,128)(2,1)S(1)} collective-permute-done((bf16[1,4,32,256]{3,2,1,0:T(8,128)(2,1)S(1)}, bf16[1,4,32,256]{3,2,1,0:T(8,128)(2,1)S(1)}, u32[]{:S(2)}, u32[]{:S(2)}) %collective-permute-start.7) | collective-permute-done | bytes 65568 | tf_op jit(solution)/shard_map/ppermute | solution.py:25
  39.0 1.5 %collective-permute-done.11 = bf16[1,4,32,256]{3,2,1,0:T(8,128)(2,1)S(1)} collective-permute-done((bf16[1,4,32,256]{3,2,1,0:T(8,128)(2,1)S(1)}, bf16[1,4,32,256]{3,2,1,0:T(8,128)(2,1)S(1)}, u32[]{:S(2)}, u32[]{:S(2)}) %collective-permute-start.11) | collective-permute-done | bytes 65568 | tf_op jit(solution)/shard_map/ppermute | solution.py:25
  40.6 2.7 %collective-permute-start.12 = (bf16[2,4,32,256]{3,2,1,0:T(8,128)(2,1)S(1)}, bf16[2,4,32,256]{3,2,1,0:T(8,128)(2,1)S(1)}, u32[]{:S(2)}, u32[]{:S(2)}) collective-permute-start(bf16[2,4,32,256]{3,2,1,0:T(8,128)(2,1)S(1)} %pad_maximum_fusion.5), channel_id=1, source_target_pairs={{0,4},{1,5},{2,6},{3,7},{4,0},{5,1},{6,2},{7,3},{8,12},{9,13},{10,... | collective-permute-start | bytes 393224 | tf_op jit(solution)/shard_map/ppermute | solution.py:25
  43.3 4.6 %collective-permute-done.12 = bf16[2,4,32,256]{3,2,1,0:T(8,128)(2,1)S(1)} collective-permute-done((bf16[2,4,32,256]{3,2,1,0:T(8,128)(2,1)S(1)}, bf16[2,4,32,256]{3,2,1,0:T(8,128)(2,1)S(1)}, u32[]{:S(2)}, u32[]{:S(2)}) %collective-permute-start.12) | collective-permute-done | bytes 131104 | tf_op jit(solution)/shard_map/ppermute | solution.py:25
  47.8 0.7 %last_sum.1 = bf16[32,8,256]{2,1,0:T(8,128)(2,1)} custom-call(f32[8,32,256]{2,1,0:T(8,128)S(1)} %bitcast.116, bf16[8,32,256]{2,1,0:T(8,128)(2,1)S(1)} %bitcast.118), custom_call_target="tpu_custom_call" | custom-call | tf_op jit(solution)/shard_map/last_sum/pallas_call | solution.py:290
  (81 shorter events, 2.6 us)
Async XLA Ops:
  0.0 6.4 %copy-start.1 = (bf16[2,128]{1,0:T(2,128)(2,1)S(1)}, bf16[2,128]{1,0:T(2,128)(2,1)}, u32[]{:S(2)}) copy-start(bf16[2,128]{1,0:T(2,128)(2,1)} %chirp_ref.2) | copy-start | bytes 1540
  0.0 6.4 %copy-start = (bf16[64,64,256]{2,1,0:T(8,128)(2,1)S(1)}, bf16[64,64,256]{2,1,0:T(8,128)(2,1)}, u32[]{:S(2)}) copy-start(bf16[64,64,256]{2,1,0:T(8,128)(2,1)} %refs_0_.1) | copy-start | bytes 6291460
  3.3 6.2 %copy-start.5 = (s32[1,8]{1,0:T(1,128)S(1)}, s32[1,8]{1,0:T(1,128)}, u32[]{:S(2)}) copy-start(s32[1,8]{1,0:T(1,128)} %param.9) | copy-start | bytes 100
  3.3 6.8 %copy-start.3 = (s32[2,2,128,8]{2,3,1,0:T(8,128)S(1)}, s32[2,2,128,8]{2,3,1,0:T(8,128)}, u32[]{:S(2)}) copy-start(s32[2,2,128,8]{2,3,1,0:T(8,128)} %param.8) | copy-start | bytes 49156
  3.3 7.3 %copy-start.4 = (f32[8]{0:T(128)S(1)}, f32[8]{0:T(128)}, u32[]{:S(2)}) copy-start(f32[8]{0:T(128)} %constant.177.clone) | copy-start | bytes 100
  3.3 15.2 %collective-permute-start = (bf16[1,2,1,8,64,256]{5,4,3,2,1,0:T(8,128)(2,1)}, bf16[1,2,1,8,64,256]{5,4,3,2,1,0:T(8,128)(2,1)S(1)}, u32[]{:S(2)}, u32[]{:S(2)}) collective-permute-start(bf16[1,2,1,8,64,256]{5,4,3,2,1,0:T(8,128)(2,1)} %get-tuple-element.17), channel_id=1, source_target_pairs={{0,1},{1,0},{2,3},{3,2},{4,5},{5,4},{6,7},{7,6},{8,9},{9,8},{10,11... | collective-permute-start | bytes 1572872 | tf_op jit(solution)/shard_map/ppermute | solution.py:25
  7.8 13.4 %collective-permute-start.4 = (bf16[1,1,2,8,64,256]{5,4,3,2,1,0:T(8,128)(2,1)S(1)}, bf16[1,1,2,8,64,256]{5,4,3,2,1,0:T(8,128)(2,1)S(1)}, u32[]{:S(2)}, u32[]{:S(2)}) collective-permute-start(bf16[1,1,2,8,64,256]{5,4,3,2,1,0:T(8,128)(2,1)S(1)} %get-tuple-element.22), channel_id=1, source_target_pairs={{0,2},{1,3},{2,0},{3,1},{4,6},{5,7},{6,4},{7,5},{8,10},{9,11},{10,... | collective-permute-start | bytes 1572872 | tf_op jit(solution)/shard_map/ppermute | solution.py:25
  12.1 6.4 %copy-start.2 = (bf16[1,2,1,8,64,256]{5,4,3,2,1,0:T(8,128)(2,1)S(1)}, bf16[1,2,1,8,64,256]{5,4,3,2,1,0:T(8,128)(2,1)}, u32[]{:S(2)}) copy-start(bf16[1,2,1,8,64,256]{5,4,3,2,1,0:T(8,128)(2,1)} %get-tuple-element.15) | copy-start | bytes 1572868
  20.9 3.4 %collective-permute-start.1 = (bf16[2,4,4,32,256]{4,3,2,1,0:T(8,128)(2,1)S(1)}, bf16[2,4,4,32,256]{4,3,2,1,0:T(8,128)(2,1)S(1)}, u32[]{:S(2)}, u32[]{:S(2)}) collective-permute-start(bf16[2,4,4,32,256]{4,3,2,1,0:T(8,128)(2,1)S(1)} %get-tuple-element.19), channel_id=1, source_target_pairs={{0,8},{8,0},{16,24},{24,16},{1,9},{9,1},{17,25},{25,17},{2,10},{10... | collective-permute-start | bytes 1572872 | tf_op jit(solution)/shard_map/ppermute | solution.py:25
  23.8 2.8 %collective-permute-start.5 = (bf16[2,4,4,32,256]{4,3,2,1,0:T(8,128)(2,1)S(1)}, bf16[2,4,4,32,256]{4,3,2,1,0:T(8,128)(2,1)S(1)}, u32[]{:S(2)}, u32[]{:S(2)}) collective-permute-start(bf16[2,4,4,32,256]{4,3,2,1,0:T(8,128)(2,1)S(1)} %get-tuple-element.24), channel_id=1, source_target_pairs={{0,8},{8,0},{16,24},{24,16},{1,9},{9,1},{17,25},{25,17},{2,10},{10... | collective-permute-start | bytes 1572872 | tf_op jit(solution)/shard_map/ppermute | solution.py:25
  24.4 6.4 %collective-permute-start.8 = (bf16[1,8,32,256]{3,2,1,0:T(8,128)(2,1)S(1)}, bf16[1,8,32,256]{3,2,1,0:T(8,128)(2,1)S(1)}, u32[]{:S(2)}, u32[]{:S(2)}) collective-permute-start(bf16[1,8,32,256]{3,2,1,0:T(8,128)(2,1)S(1)} %get-tuple-element.39), channel_id=1, source_target_pairs={{0,16},{8,24},{16,0},{24,8},{1,17},{9,25},{17,1},{25,9},{2,18},{10... | collective-permute-start | bytes 393224 | tf_op jit(solution)/shard_map/ppermute | solution.py:25
  26.3 6.6 %collective-permute-start.2 = (bf16[1,8,32,256]{3,2,1,0:T(8,128)(2,1)S(1)}, bf16[1,8,32,256]{3,2,1,0:T(8,128)(2,1)S(1)}, u32[]{:S(2)}, u32[]{:S(2)}) collective-permute-start(bf16[1,8,32,256]{3,2,1,0:T(8,128)(2,1)S(1)} %get-tuple-element.35), channel_id=1, source_target_pairs={{0,16},{8,24},{16,0},{24,8},{1,17},{9,25},{17,1},{25,9},{2,18},{10... | collective-permute-start | bytes 393224 | tf_op jit(solution)/shard_map/ppermute | solution.py:25
  26.8 7.8 %collective-permute-start.6 = (bf16[2,4,32,256]{3,2,1,0:T(8,128)(2,1)S(1)}, bf16[2,4,32,256]{3,2,1,0:T(8,128)(2,1)S(1)}, u32[]{:S(2)}, u32[]{:S(2)}) collective-permute-start(bf16[2,4,32,256]{3,2,1,0:T(8,128)(2,1)S(1)} %get-tuple-element.33), channel_id=1, source_target_pairs={{0,1},{1,0},{2,3},{3,2},{4,5},{5,4},{6,7},{7,6},{8,9},{9,8},{10,11... | collective-permute-start | bytes 393224 | tf_op jit(solution)/shard_map/ppermute | solution.py:25
  28.7 7.5 %collective-permute-start.10 = (bf16[2,4,32,256]{3,2,1,0:T(8,128)(2,1)S(1)}, bf16[2,4,32,256]{3,2,1,0:T(8,128)(2,1)S(1)}, u32[]{:S(2)}, u32[]{:S(2)}) collective-permute-start(bf16[2,4,32,256]{3,2,1,0:T(8,128)(2,1)S(1)} %get-tuple-element.37), channel_id=1, source_target_pairs={{0,1},{1,0},{2,3},{3,2},{4,5},{5,4},{6,7},{7,6},{8,9},{9,8},{10,11... | collective-permute-start | bytes 393224 | tf_op jit(solution)/shard_map/ppermute | solution.py:25
  30.8 8.2 %collective-permute-start.9 = (bf16[1,4,32,256]{3,2,1,0:T(8,128)(2,1)S(1)}, bf16[1,4,32,256]{3,2,1,0:T(8,128)(2,1)S(1)}, u32[]{:S(2)}, u32[]{:S(2)}) collective-permute-start(bf16[1,4,32,256]{3,2,1,0:T(8,128)(2,1)S(1)} %fusion.35), channel_id=1, source_target_pairs={{0,2},{1,3},{2,0},{3,1},{4,6},{5,7},{6,4},{7,5},{8,10},{9,11},{10,... | collective-permute-start | bytes 196616 | tf_op jit(solution)/shard_map/ppermute | solution.py:25
  32.9 4.3 %collective-permute-start.3 = (bf16[1,4,32,256]{3,2,1,0:T(8,128)(2,1)S(1)}, bf16[1,4,32,256]{3,2,1,0:T(8,128)(2,1)S(1)}, u32[]{:S(2)}, u32[]{:S(2)}) collective-permute-start(bf16[1,4,32,256]{3,2,1,0:T(8,128)(2,1)S(1)} %fusion.33), channel_id=1, source_target_pairs={{0,2},{1,3},{2,0},{3,1},{4,6},{5,7},{6,4},{7,5},{8,10},{9,11},{10,... | collective-permute-start | bytes 196616 | tf_op jit(solution)/shard_map/ppermute | solution.py:25
  34.6 4.3 %collective-permute-start.7 = (bf16[1,4,32,256]{3,2,1,0:T(8,128)(2,1)S(1)}, bf16[1,4,32,256]{3,2,1,0:T(8,128)(2,1)S(1)}, u32[]{:S(2)}, u32[]{:S(2)}) collective-permute-start(bf16[1,4,32,256]{3,2,1,0:T(8,128)(2,1)S(1)} %fusion.34), channel_id=1, source_target_pairs={{0,16},{8,24},{16,0},{24,8},{1,17},{9,25},{17,1},{25,9},{2,18},{10... | collective-permute-start | bytes 196616 | tf_op jit(solution)/shard_map/ppermute | solution.py:25
  36.2 4.3 %collective-permute-start.11 = (bf16[1,4,32,256]{3,2,1,0:T(8,128)(2,1)S(1)}, bf16[1,4,32,256]{3,2,1,0:T(8,128)(2,1)S(1)}, u32[]{:S(2)}, u32[]{:S(2)}) collective-permute-start(bf16[1,4,32,256]{3,2,1,0:T(8,128)(2,1)S(1)} %fusion.36), channel_id=1, source_target_pairs={{0,16},{8,24},{16,0},{24,8},{1,17},{9,25},{17,1},{25,9},{2,18},{10... | collective-permute-start | bytes 196616 | tf_op jit(solution)/shard_map/ppermute | solution.py:25
  40.6 7.2 %collective-permute-start.12 = (bf16[2,4,32,256]{3,2,1,0:T(8,128)(2,1)S(1)}, bf16[2,4,32,256]{3,2,1,0:T(8,128)(2,1)S(1)}, u32[]{:S(2)}, u32[]{:S(2)}) collective-permute-start(bf16[2,4,32,256]{3,2,1,0:T(8,128)(2,1)S(1)} %pad_maximum_fusion.5), channel_id=1, source_target_pairs={{0,4},{1,5},{2,6},{3,7},{4,0},{5,1},{6,2},{7,3},{8,12},{9,13},{10,... | collective-permute-start | bytes 393224 | tf_op jit(solution)/shard_map/ppermute | solution.py:25

commit v16 on v13

--- a/solution.py
+++ b/solution.py
@@ -410,7 +410,7 @@
         kept, arrived = kept.reshape(parts), arrived.reshape(parts)
         pieces.append([(kept[:, n], arrived[:, n], gone) for n in range(2)])
 
-    final = [[], []]
+    states = {}
     for n in range(2):
         for chain in range(2):
             kept, arrived, gone = pieces[chain][n]
@@ -419,16 +419,29 @@
             order = [("leaf", b) for b in range(1, levels)]
             rest = [("turn", b) for b in range(top) if b not in (0, far)]
             order = [("turn", 0)] + order if gone else order + [("turn", far)]
-            for axis, b in order + rest:
-                at = leading.index((axis, b))
-                before, after = 1 << at, (1 << len(leading) - at - 1) * each
-                leading.pop(at)
-                split = (before, 2, after, rows, width)
-                kept, sent = fold(kept.reshape(split), arrived.reshape(split))
-                arrived = swapped(sent, axis, b)
-            shape = (each, rows, width)
-            total = kept.reshape(shape) + arrived.reshape(shape).astype(jnp.float32)
-            final[n].append(total)
+            states[n, chain] = [kept, arrived, leading, order + rest]
+    for stage in range(len(states[0, 0][3])):
+        ahead = states[0, 1][1]
+        for (n, chain), state in states.items():
+            kept, arrived, leading, order = state
+            axis, b = order[stage]
+            at = leading.index((axis, b))
+            before, after = 1 << at, (1 << len(leading) - at - 1) * each
+            leading.pop(at)
+            split = (before, 2, after, rows, width)
+            kept, sent = fold(kept.reshape(split), arrived.reshape(split))
+            if stage and (n, chain) == (1, 0):
+                sent, ahead = lax.optimization_barrier((sent, ahead))
+            state[:2] = kept, swapped(sent, axis, b)
+    shape = (each, rows, width)
+    final = [
+        [
+            states[n, chain][0].reshape(shape)
+            + states[n, chain][1].reshape(shape).astype(jnp.float32)
+            for chain in range(2)
+        ]
+        for n in range(2)
+    ]
     upper = bit(own_turn, top) == 1
     sent = jnp.stack([jnp.where(upper, second, first) for first, second in final])
     kept = jnp.stack([jnp.where(upper, first, second) for first, second in final])

time: 48.7 us -> 49.7 us (1.021)
  waiting for transfers between devices: 14.2 us -> 15.3 us
    ppermute x13, waiting for transfers between devices: 14.2 us -> 15.3 us  [swapped(): lax.ppermute(array, axis, [(i, i ^ 1 << bit) for i in range(lax.axis_size...]
  transfers between devices with their start and end apart: 13 -> 13, of which waited for: 8 -> 6; matrix products, arithmetic and copies ran while one was open for 12% -> 12% of each run, Pallas kernels for 12% -> 12%
where the time goes in v16:
time: 49.7 us; the launch traced here: 49.6 us
  starting transfers between devices  17.7 us (36%)
  waiting for transfers between devices  15.3 us (31%)
  Pallas kernels  10 us (20%)
  other arithmetic  4.89 us (10%)
  local copies, waits for them, and re-layouts  1.05 us (2%)
    ppermute x13, starting transfers between devices, swapped(): lax.ppermute(array, axis, [(i, i ^ 1 << bit) for i in range(lax.axis_size...  17.7 us
    ppermute x13, waiting for transfers between devices, swapped(): lax.ppermute(array, axis, [(i, i ^ 1 << bit) for i in range(lax.axis_size...  15.3 us
    pallas_call x2, Pallas kernels, compress(): pl.pallas_call(functools.partial(compress_kernel, dims, has_edge), grid=(...  4.66 us
    pallas_call x2, Pallas kernels, backproject(): pl.pallas_call(functools.partial(image_kernel, (leaf, each, half, beams,...  4.61 us
    cos x2, other arithmetic, unit(): return (jnp.cos(angle), jnp.sin(angle))  2.27 us
  transfers between devices with their start and end apart: 13, of which 6 were waited for; matrix products, arithmetic and copies ran while one was open for 12% of the time, Pallas kernels for 12%

profile of v16, /device:TPU:0, one launch (start us, length us, event | category | flops | bytes accessed | tf_op | source)
XLA Modules:
  0.0 49.6 jit_solution(15734152362985727502)
XLA Ops:
  0.0 3.3 %compress.2 = (bf16[1,2,1,8,64,256]{5,4,3,2,1,0:T(8,128)(2,1)}, bf16[1,2,1,8,64,256]{5,4,3,2,1,0:T(8,128)(2,1)}) custom-call(bf16[2,128]{1,0:T(2,128)(2,1)} %chirp_ref.2, bf16[64,64,256]{2,1,0:T(8,128)(2,1)} %refs_0_.1), custom_call_target="tpu_custom_call" | custom-call | flops 536870912 | bytes 2097152 | tf_op jit(solution)/shard_map/compress/pallas_call | solution.py:142
  3.3 3.1 %collective-permute-start = (bf16[1,2,1,8,64,256]{5,4,3,2,1,0:T(8,128)(2,1)}, bf16[1,2,1,8,64,256]{5,4,3,2,1,0:T(8,128)(2,1)S(1)}, u32[]{:S(2)}, u32[]{:S(2)}) collective-permute-start(bf16[1,2,1,8,64,256]{5,4,3,2,1,0:T(8,128)(2,1)} %get-tuple-element.18), channel_id=1, source_target_pairs={{0,1},{1,0},{2,3},{3,2},{4,5},{5,4},{6,7},{7,6},{8,9},{9,8},{10,11... | collective-permute-start | bytes 1572872 | tf_op jit(solution)/shard_map/ppermute | solution.py:25
  6.4 1.4 %compress.3 = (bf16[1,1,2,8,64,256]{5,4,3,2,1,0:T(8,128)(2,1)S(1)}, bf16[1,1,2,8,64,256]{5,4,3,2,1,0:T(8,128)(2,1)S(1)}) custom-call(bf16[2,128]{1,0:T(2,128)(2,1)S(1)} %copy-done.1, bf16[64,64,256]{2,1,0:T(8,128)(2,1)S(1)} %copy-done, bf16[64,64,256]{2,1,0:T(8,128)(2,1)S(1)} %copy-done), custom_call_target="tpu_custom_call" | custom-call | flops 536870912 | bytes 2097152 | tf_op jit(solution)/shard_map/compress/pallas_call | solution.py:142
  7.8 1.6 %collective-permute-start.4 = (bf16[1,1,2,8,64,256]{5,4,3,2,1,0:T(8,128)(2,1)S(1)}, bf16[1,1,2,8,64,256]{5,4,3,2,1,0:T(8,128)(2,1)S(1)}, u32[]{:S(2)}, u32[]{:S(2)}) collective-permute-start(bf16[1,1,2,8,64,256]{5,4,3,2,1,0:T(8,128)(2,1)S(1)} %get-tuple-element.23), channel_id=1, source_target_pairs={{0,2},{1,3},{2,0},{3,1},{4,6},{5,7},{6,4},{7,5},{8,10},{9,11},{10,... | collective-permute-start | bytes 1572872 | tf_op jit(solution)/shard_map/ppermute | solution.py:25
  9.5 0.2 select_reduce_fusion.1
  10.3 0.1 copy.35
  10.6 0.4 select_reduce_fusion
  11.0 0.5 multiply_convert_fusion.1
  11.5 0.2 fusion.30
  11.9 0.2 fusion.47
  12.3 0.1 copy.44.steer_ref
  12.4 2.1 %fusion.10 = (f32[2,1,128,512]{3,2,1,0:T(8,128)S(1)}, f32[2,1,128,512]{3,2,1,0:T(8,128)S(1)}) fusion(s32[512]{0:T(512)S(1)} %iota_add_fusion, s32[2,128]{1,0:T(2,128)S(1)} %add_multiply_fusion), kind=kLoop, calls=%fused_computation.33 | loop fusion | flops 1835008 | bytes 1051648 | tf_op jit(solution)/shard_map/cos | solution.py:30
  14.6 3.9 %collective-permute-done = bf16[1,2,1,8,64,256]{5,4,3,2,1,0:T(8,128)(2,1)S(1)} collective-permute-done((bf16[1,2,1,8,64,256]{5,4,3,2,1,0:T(8,128)(2,1)}, bf16[1,2,1,8,64,256]{5,4,3,2,1,0:T(8,128)(2,1)S(1)}, u32[]{:S(2)}, u32[]{:S(2)}) %collective-permute-start) | collective-permute-done | bytes 524320 | tf_op jit(solution)/shard_map/ppermute | solution.py:25
  18.6 2.3 %image.2 = (f32[2,4,4,32,256]{4,3,2,1,0:T(8,128)S(1)}, bf16[2,4,4,32,256]{4,3,2,1,0:T(8,128)(2,1)S(1)}) custom-call(bf16[2,4,4,64,256]{4,3,2,1,0:T(8,128)(2,1)S(1)} %pad_maximum_fusion.data_ref, bf16[256,256]{1,0:T(8,128)(2,1)S(1)} %copy.44.steer_ref, bf16[1,128,256]{2,1,0:T(8,128)(2,1)S(1)} %pad_maximum_fusion.6.interp_ref, f32[4,4,128]{2,1,0:T(4,128)S(1)} %bitcast.120, ...), custom_call_target="tpu_custom_call" | custom-call | flops 402653184 | bytes 2621440 | tf_op jit(solution)/shard_map/image/pallas_call | solution.py:247
  21.0 0.2 collective-permute-done.4
  21.3 2.3 %image.3 = (f32[2,4,4,32,256]{4,3,2,1,0:T(8,128)S(1)}, bf16[2,4,4,32,256]{4,3,2,1,0:T(8,128)(2,1)S(1)}) custom-call(bf16[2,4,4,64,256]{4,3,2,1,0:T(8,128)(2,1)S(1)} %pad_maximum_fusion.2.data_ref, bf16[256,256]{1,0:T(8,128)(2,1)S(1)} %copy.45.steer_ref, bf16[1,128,256]{2,1,0:T(8,128)(2,1)S(1)} %pad_maximum_fusion.6.interp_ref, f32[4,4,128]{2,1,0:T(4,128)S(1)} %bitcast.119, ...), custom_call_target="tpu_custom_call" | custom-call | flops 402653184 | bytes 2621440 | tf_op jit(solution)/shard_map/image/pallas_call | solution.py:247
  23.6 0.1 fusion.62
  23.8 0.4 collective-permute-start.5
  24.4 1.8 %collective-permute-start.8 = (bf16[1,8,32,256]{3,2,1,0:T(8,128)(2,1)S(1)}, bf16[1,8,32,256]{3,2,1,0:T(8,128)(2,1)S(1)}, u32[]{:S(2)}, u32[]{:S(2)}) collective-permute-start(bf16[1,8,32,256]{3,2,1,0:T(8,128)(2,1)S(1)} %get-tuple-element.41), channel_id=1, source_target_pairs={{0,16},{8,24},{16,0},{24,8},{1,17},{9,25},{17,1},{25,9},{2,18},{10... | collective-permute-start | bytes 393224 | tf_op jit(solution)/shard_map/ppermute | solution.py:25
  26.3 0.3 collective-permute-start.2
  26.8 1.8 %collective-permute-start.10 = (bf16[2,4,32,256]{3,2,1,0:T(8,128)(2,1)S(1)}, bf16[2,4,32,256]{3,2,1,0:T(8,128)(2,1)S(1)}, u32[]{:S(2)}, u32[]{:S(2)}) collective-permute-start(bf16[2,4,32,256]{3,2,1,0:T(8,128)(2,1)S(1)} %get-tuple-element.39), channel_id=1, source_target_pairs={{0,1},{1,0},{2,3},{3,2},{4,5},{5,4},{6,7},{7,6},{8,9},{9,8},{10,11... | collective-permute-start | bytes 393224 | tf_op jit(solution)/shard_map/ppermute | solution.py:25
  28.7 0.3 collective-permute-start.6
  29.0 3.8 %collective-permute-done.2 = bf16[1,8,32,256]{3,2,1,0:T(8,128)(2,1)S(1)} collective-permute-done((bf16[1,8,32,256]{3,2,1,0:T(8,128)(2,1)S(1)}, bf16[1,8,32,256]{3,2,1,0:T(8,128)(2,1)S(1)}, u32[]{:S(2)}, u32[]{:S(2)}) %collective-permute-start.2) | collective-permute-done | bytes 131104 | tf_op jit(solution)/shard_map/ppermute | solution.py:25
  32.9 1.7 %collective-permute-start.3 = (bf16[1,4,32,256]{3,2,1,0:T(8,128)(2,1)S(1)}, bf16[1,4,32,256]{3,2,1,0:T(8,128)(2,1)S(1)}, u32[]{:S(2)}, u32[]{:S(2)}) collective-permute-start(bf16[1,4,32,256]{3,2,1,0:T(8,128)(2,1)S(1)} %fusion.33), channel_id=1, source_target_pairs={{0,2},{1,3},{2,0},{3,1},{4,6},{5,7},{6,4},{7,5},{8,10},{9,11},{10,... | collective-permute-start | bytes 196616 | tf_op jit(solution)/shard_map/ppermute | solution.py:25
  34.6 1.6 %collective-permute-start.11 = (bf16[1,4,32,256]{3,2,1,0:T(8,128)(2,1)S(1)}, bf16[1,4,32,256]{3,2,1,0:T(8,128)(2,1)S(1)}, u32[]{:S(2)}, u32[]{:S(2)}) collective-permute-start(bf16[1,4,32,256]{3,2,1,0:T(8,128)(2,1)S(1)} %fusion.36), channel_id=1, source_target_pairs={{0,16},{8,24},{16,0},{24,8},{1,17},{9,25},{17,1},{25,9},{2,18},{10... | collective-permute-start | bytes 196616 | tf_op jit(solution)/shard_map/ppermute | solution.py:25
  36.2 0.6 %collective-permute-start.7 = (bf16[1,4,32,256]{3,2,1,0:T(8,128)(2,1)S(1)}, bf16[1,4,32,256]{3,2,1,0:T(8,128)(2,1)S(1)}, u32[]{:S(2)}, u32[]{:S(2)}) collective-permute-start(bf16[1,4,32,256]{3,2,1,0:T(8,128)(2,1)S(1)} %fusion.34), channel_id=1, source_target_pairs={{0,16},{8,24},{16,0},{24,8},{1,17},{9,25},{17,1},{25,9},{2,18},{10... | collective-permute-start | bytes 196616 | tf_op jit(solution)/shard_map/ppermute | solution.py:25
  36.8 1.2 %collective-permute-start.9 = (bf16[1,4,32,256]{3,2,1,0:T(8,128)(2,1)S(1)}, bf16[1,4,32,256]{3,2,1,0:T(8,128)(2,1)S(1)}, u32[]{:S(2)}, u32[]{:S(2)}) collective-permute-start(bf16[1,4,32,256]{3,2,1,0:T(8,128)(2,1)S(1)} %fusion.35), channel_id=1, source_target_pairs={{0,2},{1,3},{2,0},{3,1},{4,6},{5,7},{6,4},{7,5},{8,10},{9,11},{10,... | collective-permute-start | bytes 196616 | tf_op jit(solution)/shard_map/ppermute | solution.py:25
  38.0 2.5 %collective-permute-done.7 = bf16[1,4,32,256]{3,2,1,0:T(8,128)(2,1)S(1)} collective-permute-done((bf16[1,4,32,256]{3,2,1,0:T(8,128)(2,1)S(1)}, bf16[1,4,32,256]{3,2,1,0:T(8,128)(2,1)S(1)}, u32[]{:S(2)}, u32[]{:S(2)}) %collective-permute-start.7) | collective-permute-done | bytes 65568 | tf_op jit(solution)/shard_map/ppermute | solution.py:25
  40.6 0.6 %collective-permute-done.9 = bf16[1,4,32,256]{3,2,1,0:T(8,128)(2,1)S(1)} collective-permute-done((bf16[1,4,32,256]{3,2,1,0:T(8,128)(2,1)S(1)}, bf16[1,4,32,256]{3,2,1,0:T(8,128)(2,1)S(1)}, u32[]{:S(2)}, u32[]{:S(2)}) %collective-permute-start.9) | collective-permute-done | bytes 65568 | tf_op jit(solution)/shard_map/ppermute | solution.py:25
  41.2 3.3 %collective-permute-start.12 = (bf16[2,4,32,256]{3,2,1,0:T(8,128)(2,1)S(1)}, bf16[2,4,32,256]{3,2,1,0:T(8,128)(2,1)S(1)}, u32[]{:S(2)}, u32[]{:S(2)}) collective-permute-start(bf16[2,4,32,256]{3,2,1,0:T(8,128)(2,1)S(1)} %pad_maximum_fusion.5), channel_id=1, source_target_pairs={{0,4},{1,5},{2,6},{3,7},{4,0},{5,1},{6,2},{7,3},{8,12},{9,13},{10,... | collective-permute-start | bytes 393224 | tf_op jit(solution)/shard_map/ppermute | solution.py:25
  44.5 4.3 %collective-permute-done.12 = bf16[2,4,32,256]{3,2,1,0:T(8,128)(2,1)S(1)} collective-permute-done((bf16[2,4,32,256]{3,2,1,0:T(8,128)(2,1)S(1)}, bf16[2,4,32,256]{3,2,1,0:T(8,128)(2,1)S(1)}, u32[]{:S(2)}, u32[]{:S(2)}) %collective-permute-start.12) | collective-permute-done | bytes 131104 | tf_op jit(solution)/shard_map/ppermute | solution.py:25
  48.8 0.7 %last_sum.1 = bf16[32,8,256]{2,1,0:T(8,128)(2,1)} custom-call(f32[8,32,256]{2,1,0:T(8,128)S(1)} %bitcast.116, bf16[8,32,256]{2,1,0:T(8,128)(2,1)S(1)} %bitcast.118), custom_call_target="tpu_custom_call" | custom-call | tf_op jit(solution)/shard_map/last_sum/pallas_call | solution.py:290
  (81 shorter events, 2.4 us)
Async XLA Ops:
  0.0 6.4 %copy-start.1 = (bf16[2,128]{1,0:T(2,128)(2,1)S(1)}, bf16[2,128]{1,0:T(2,128)(2,1)}, u32[]{:S(2)}) copy-start(bf16[2,128]{1,0:T(2,128)(2,1)} %chirp_ref.2) | copy-start | bytes 1540
  0.0 6.4 %copy-start = (bf16[64,64,256]{2,1,0:T(8,128)(2,1)S(1)}, bf16[64,64,256]{2,1,0:T(8,128)(2,1)}, u32[]{:S(2)}) copy-start(bf16[64,64,256]{2,1,0:T(8,128)(2,1)} %refs_0_.1) | copy-start | bytes 6291460
  3.3 6.2 %copy-start.5 = (s32[1,8]{1,0:T(1,128)S(1)}, s32[1,8]{1,0:T(1,128)}, u32[]{:S(2)}) copy-start(s32[1,8]{1,0:T(1,128)} %param.9) | copy-start | bytes 100
  3.3 6.8 %copy-start.3 = (s32[2,2,128,8]{2,3,1,0:T(8,128)S(1)}, s32[2,2,128,8]{2,3,1,0:T(8,128)}, u32[]{:S(2)}) copy-start(s32[2,2,128,8]{2,3,1,0:T(8,128)} %param.8) | copy-start | bytes 49156
  3.3 7.3 %copy-start.4 = (f32[8]{0:T(128)S(1)}, f32[8]{0:T(128)}, u32[]{:S(2)}) copy-start(f32[8]{0:T(128)} %constant.177.clone) | copy-start | bytes 100
  3.3 15.2 %collective-permute-start = (bf16[1,2,1,8,64,256]{5,4,3,2,1,0:T(8,128)(2,1)}, bf16[1,2,1,8,64,256]{5,4,3,2,1,0:T(8,128)(2,1)S(1)}, u32[]{:S(2)}, u32[]{:S(2)}) collective-permute-start(bf16[1,2,1,8,64,256]{5,4,3,2,1,0:T(8,128)(2,1)} %get-tuple-element.18), channel_id=1, source_target_pairs={{0,1},{1,0},{2,3},{3,2},{4,5},{5,4},{6,7},{7,6},{8,9},{9,8},{10,11... | collective-permute-start | bytes 1572872 | tf_op jit(solution)/shard_map/ppermute | solution.py:25
  7.8 13.4 %collective-permute-start.4 = (bf16[1,1,2,8,64,256]{5,4,3,2,1,0:T(8,128)(2,1)S(1)}, bf16[1,1,2,8,64,256]{5,4,3,2,1,0:T(8,128)(2,1)S(1)}, u32[]{:S(2)}, u32[]{:S(2)}) collective-permute-start(bf16[1,1,2,8,64,256]{5,4,3,2,1,0:T(8,128)(2,1)S(1)} %get-tuple-element.23), channel_id=1, source_target_pairs={{0,2},{1,3},{2,0},{3,1},{4,6},{5,7},{6,4},{7,5},{8,10},{9,11},{10,... | collective-permute-start | bytes 1572872 | tf_op jit(solution)/shard_map/ppermute | solution.py:25
  12.1 6.4 %copy-start.2 = (bf16[1,2,1,8,64,256]{5,4,3,2,1,0:T(8,128)(2,1)S(1)}, bf16[1,2,1,8,64,256]{5,4,3,2,1,0:T(8,128)(2,1)}, u32[]{:S(2)}) copy-start(bf16[1,2,1,8,64,256]{5,4,3,2,1,0:T(8,128)(2,1)} %get-tuple-element.16) | copy-start | bytes 1572868
  20.9 3.4 %collective-permute-start.1 = (bf16[2,4,4,32,256]{4,3,2,1,0:T(8,128)(2,1)S(1)}, bf16[2,4,4,32,256]{4,3,2,1,0:T(8,128)(2,1)S(1)}, u32[]{:S(2)}, u32[]{:S(2)}) collective-permute-start(bf16[2,4,4,32,256]{4,3,2,1,0:T(8,128)(2,1)S(1)} %get-tuple-element.20), channel_id=1, source_target_pairs={{0,8},{8,0},{16,24},{24,16},{1,9},{9,1},{17,25},{25,17},{2,10},{10... | collective-permute-start | bytes 1572872 | tf_op jit(solution)/shard_map/ppermute | solution.py:25
  23.8 2.8 %collective-permute-start.5 = (bf16[2,4,4,32,256]{4,3,2,1,0:T(8,128)(2,1)S(1)}, bf16[2,4,4,32,256]{4,3,2,1,0:T(8,128)(2,1)S(1)}, u32[]{:S(2)}, u32[]{:S(2)}) collective-permute-start(bf16[2,4,4,32,256]{4,3,2,1,0:T(8,128)(2,1)S(1)} %get-tuple-element.25), channel_id=1, source_target_pairs={{0,8},{8,0},{16,24},{24,16},{1,9},{9,1},{17,25},{25,17},{2,10},{10... | collective-permute-start | bytes 1572872 | tf_op jit(solution)/shard_map/ppermute | solution.py:25
  24.4 12.4 %collective-permute-start.8 = (bf16[1,8,32,256]{3,2,1,0:T(8,128)(2,1)S(1)}, bf16[1,8,32,256]{3,2,1,0:T(8,128)(2,1)S(1)}, u32[]{:S(2)}, u32[]{:S(2)}) collective-permute-start(bf16[1,8,32,256]{3,2,1,0:T(8,128)(2,1)S(1)} %get-tuple-element.41), channel_id=1, source_target_pairs={{0,16},{8,24},{16,0},{24,8},{1,17},{9,25},{17,1},{25,9},{2,18},{10... | collective-permute-start | bytes 393224 | tf_op jit(solution)/shard_map/ppermute | solution.py:25
  26.3 6.6 %collective-permute-start.2 = (bf16[1,8,32,256]{3,2,1,0:T(8,128)(2,1)S(1)}, bf16[1,8,32,256]{3,2,1,0:T(8,128)(2,1)S(1)}, u32[]{:S(2)}, u32[]{:S(2)}) collective-permute-start(bf16[1,8,32,256]{3,2,1,0:T(8,128)(2,1)S(1)} %get-tuple-element.37), channel_id=1, source_target_pairs={{0,16},{8,24},{16,0},{24,8},{1,17},{9,25},{17,1},{25,9},{2,18},{10... | collective-permute-start | bytes 393224 | tf_op jit(solution)/shard_map/ppermute | solution.py:25
  26.8 7.8 %collective-permute-start.10 = (bf16[2,4,32,256]{3,2,1,0:T(8,128)(2,1)S(1)}, bf16[2,4,32,256]{3,2,1,0:T(8,128)(2,1)S(1)}, u32[]{:S(2)}, u32[]{:S(2)}) collective-permute-start(bf16[2,4,32,256]{3,2,1,0:T(8,128)(2,1)S(1)} %get-tuple-element.39), channel_id=1, source_target_pairs={{0,1},{1,0},{2,3},{3,2},{4,5},{5,4},{6,7},{7,6},{8,9},{9,8},{10,11... | collective-permute-start | bytes 393224 | tf_op jit(solution)/shard_map/ppermute | solution.py:25
  28.7 7.5 %collective-permute-start.6 = (bf16[2,4,32,256]{3,2,1,0:T(8,128)(2,1)S(1)}, bf16[2,4,32,256]{3,2,1,0:T(8,128)(2,1)S(1)}, u32[]{:S(2)}, u32[]{:S(2)}) collective-permute-start(bf16[2,4,32,256]{3,2,1,0:T(8,128)(2,1)S(1)} %get-tuple-element.36), channel_id=1, source_target_pairs={{0,1},{1,0},{2,3},{3,2},{4,5},{5,4},{6,7},{7,6},{8,9},{9,8},{10,11... | collective-permute-start | bytes 393224 | tf_op jit(solution)/shard_map/ppermute | solution.py:25
  32.9 5.1 %collective-permute-start.3 = (bf16[1,4,32,256]{3,2,1,0:T(8,128)(2,1)S(1)}, bf16[1,4,32,256]{3,2,1,0:T(8,128)(2,1)S(1)}, u32[]{:S(2)}, u32[]{:S(2)}) collective-permute-start(bf16[1,4,32,256]{3,2,1,0:T(8,128)(2,1)S(1)} %fusion.33), channel_id=1, source_target_pairs={{0,2},{1,3},{2,0},{3,1},{4,6},{5,7},{6,4},{7,5},{8,10},{9,11},{10,... | collective-permute-start | bytes 196616 | tf_op jit(solution)/shard_map/ppermute | solution.py:25
  34.6 6.0 %collective-permute-start.11 = (bf16[1,4,32,256]{3,2,1,0:T(8,128)(2,1)S(1)}, bf16[1,4,32,256]{3,2,1,0:T(8,128)(2,1)S(1)}, u32[]{:S(2)}, u32[]{:S(2)}) collective-permute-start(bf16[1,4,32,256]{3,2,1,0:T(8,128)(2,1)S(1)} %fusion.36), channel_id=1, source_target_pairs={{0,16},{8,24},{16,0},{24,8},{1,17},{9,25},{17,1},{25,9},{2,18},{10... | collective-permute-start | bytes 196616 | tf_op jit(solution)/shard_map/ppermute | solution.py:25
  36.2 4.3 %collective-permute-start.7 = (bf16[1,4,32,256]{3,2,1,0:T(8,128)(2,1)S(1)}, bf16[1,4,32,256]{3,2,1,0:T(8,128)(2,1)S(1)}, u32[]{:S(2)}, u32[]{:S(2)}) collective-permute-start(bf16[1,4,32,256]{3,2,1,0:T(8,128)(2,1)S(1)} %fusion.34), channel_id=1, source_target_pairs={{0,16},{8,24},{16,0},{24,8},{1,17},{9,25},{17,1},{25,9},{2,18},{10... | collective-permute-start | bytes 196616 | tf_op jit(solution)/shard_map/ppermute | solution.py:25
  36.8 4.3 %collective-permute-start.9 = (bf16[1,4,32,256]{3,2,1,0:T(8,128)(2,1)S(1)}, bf16[1,4,32,256]{3,2,1,0:T(8,128)(2,1)S(1)}, u32[]{:S(2)}, u32[]{:S(2)}) collective-permute-start(bf16[1,4,32,256]{3,2,1,0:T(8,128)(2,1)S(1)} %fusion.35), channel_id=1, source_target_pairs={{0,2},{1,3},{2,0},{3,1},{4,6},{5,7},{6,4},{7,5},{8,10},{9,11},{10,... | collective-permute-start | bytes 196616 | tf_op jit(solution)/shard_map/ppermute | solution.py:25
  41.2 7.6 %collective-permute-start.12 = (bf16[2,4,32,256]{3,2,1,0:T(8,128)(2,1)S(1)}, bf16[2,4,32,256]{3,2,1,0:T(8,128)(2,1)S(1)}, u32[]{:S(2)}, u32[]{:S(2)}) collective-permute-start(bf16[2,4,32,256]{3,2,1,0:T(8,128)(2,1)S(1)} %pad_maximum_fusion.5), channel_id=1, source_target_pairs={{0,4},{1,5},{2,6},{3,7},{4,0},{5,1},{6,2},{7,3},{8,12},{9,13},{10,... | collective-permute-start | bytes 393224 | tf_op jit(solution)/shard_map/ppermute | solution.py:25

commit v17 on v16

--- a/solution.py
+++ b/solution.py
@@ -421,7 +421,7 @@
             order = [("turn", 0)] + order if gone else order + [("turn", far)]
             states[n, chain] = [kept, arrived, leading, order + rest]
     for stage in range(len(states[0, 0][3])):
-        ahead = states[0, 1][1]
+        ahead = states[1, 1][1]
         for (n, chain), state in states.items():
             kept, arrived, leading, order = state
             axis, b = order[stage]
@@ -430,7 +430,7 @@
             leading.pop(at)
             split = (before, 2, after, rows, width)
             kept, sent = fold(kept.reshape(split), arrived.reshape(split))
-            if stage and (n, chain) == (1, 0):
+            if stage and (n, chain) == (0, 0):
                 sent, ahead = lax.optimization_barrier((sent, ahead))
             state[:2] = kept, swapped(sent, axis, b)
     shape = (each, rows, width)

time: 49.7 us -> 49 us (0.986)
  waiting for transfers between devices: 15.3 us -> 13.5 us
  starting transfers between devices: 17.7 us -> 18.9 us
    ppermute x13, waiting for transfers between devices: 15.3 us -> 13.5 us  [swapped(): lax.ppermute(array, axis, [(i, i ^ 1 << bit) for i in range(lax.axis_size...]
    ppermute x13, starting transfers between devices: 17.7 us -> 18.9 us  [swapped(): lax.ppermute(array, axis, [(i, i ^ 1 << bit) for i in range(lax.axis_size...]
  transfers between devices with their start and end apart: 13 -> 13, of which waited for: 6 -> 7; matrix products, arithmetic and copies ran while one was open for 12% -> 12% of each run, Pallas kernels for 12% -> 12%
where the time goes in v17:
time: 49 us; the launch traced here: 48.9 us
  starting transfers between devices  18.9 us (39%)
  waiting for transfers between devices  13.5 us (28%)
  Pallas kernels  10 us (20%)
  other arithmetic  4.9 us (10%)
  local copies, waits for them, and re-layouts  1.05 us (2%)
    ppermute x13, starting transfers between devices, swapped(): lax.ppermute(array, axis, [(i, i ^ 1 << bit) for i in range(lax.axis_size...  18.9 us
    ppermute x13, waiting for transfers between devices, swapped(): lax.ppermute(array, axis, [(i, i ^ 1 << bit) for i in range(lax.axis_size...  13.5 us
    pallas_call x2, Pallas kernels, compress(): pl.pallas_call(functools.partial(compress_kernel, dims, has_edge), grid=(...  4.66 us
    pallas_call x2, Pallas kernels, backproject(): pl.pallas_call(functools.partial(image_kernel, (leaf, each, half, beams,...  4.61 us
    cos x2, other arithmetic, unit(): return (jnp.cos(angle), jnp.sin(angle))  2.27 us
  transfers between devices with their start and end apart: 13, of which 7 were waited for; matrix products, arithmetic and copies ran while one was open for 12% of the time, Pallas kernels for 12%

profile of v17, /device:TPU:0, one launch (start us, length us, event | category | flops | bytes accessed | tf_op | source)
XLA Modules:
  0.0 48.9 jit_solution(16532709823450559171)
XLA Ops:
  0.0 3.3 %compress.2 = (bf16[1,2,1,8,64,256]{5,4,3,2,1,0:T(8,128)(2,1)}, bf16[1,2,1,8,64,256]{5,4,3,2,1,0:T(8,128)(2,1)}) custom-call(bf16[2,128]{1,0:T(2,128)(2,1)} %chirp_ref.2, bf16[64,64,256]{2,1,0:T(8,128)(2,1)} %refs_0_.1), custom_call_target="tpu_custom_call" | custom-call | flops 536870912 | bytes 2097152 | tf_op jit(solution)/shard_map/compress/pallas_call | solution.py:142
  3.3 3.1 %collective-permute-start = (bf16[1,2,1,8,64,256]{5,4,3,2,1,0:T(8,128)(2,1)}, bf16[1,2,1,8,64,256]{5,4,3,2,1,0:T(8,128)(2,1)S(1)}, u32[]{:S(2)}, u32[]{:S(2)}) collective-permute-start(bf16[1,2,1,8,64,256]{5,4,3,2,1,0:T(8,128)(2,1)} %get-tuple-element.18), channel_id=1, source_target_pairs={{0,1},{1,0},{2,3},{3,2},{4,5},{5,4},{6,7},{7,6},{8,9},{9,8},{10,11... | collective-permute-start | bytes 1572872 | tf_op jit(solution)/shard_map/ppermute | solution.py:25
  6.4 1.4 %compress.3 = (bf16[1,1,2,8,64,256]{5,4,3,2,1,0:T(8,128)(2,1)S(1)}, bf16[1,1,2,8,64,256]{5,4,3,2,1,0:T(8,128)(2,1)S(1)}) custom-call(bf16[2,128]{1,0:T(2,128)(2,1)S(1)} %copy-done.1, bf16[64,64,256]{2,1,0:T(8,128)(2,1)S(1)} %copy-done, bf16[64,64,256]{2,1,0:T(8,128)(2,1)S(1)} %copy-done), custom_call_target="tpu_custom_call" | custom-call | flops 536870912 | bytes 2097152 | tf_op jit(solution)/shard_map/compress/pallas_call | solution.py:142
  7.8 1.6 %collective-permute-start.3 = (bf16[1,1,2,8,64,256]{5,4,3,2,1,0:T(8,128)(2,1)S(1)}, bf16[1,1,2,8,64,256]{5,4,3,2,1,0:T(8,128)(2,1)S(1)}, u32[]{:S(2)}, u32[]{:S(2)}) collective-permute-start(bf16[1,1,2,8,64,256]{5,4,3,2,1,0:T(8,128)(2,1)S(1)} %get-tuple-element.23), channel_id=1, source_target_pairs={{0,2},{1,3},{2,0},{3,1},{4,6},{5,7},{6,4},{7,5},{8,10},{9,11},{10,... | collective-permute-start | bytes 1572872 | tf_op jit(solution)/shard_map/ppermute | solution.py:25
  9.5 0.2 select_reduce_fusion.1
  10.3 0.1 copy.35
  10.6 0.4 select_reduce_fusion
  11.0 0.5 multiply_convert_fusion.1
  11.5 0.2 fusion.30
  11.9 0.2 fusion.47
  12.4 2.1 %fusion.10 = (f32[2,1,128,512]{3,2,1,0:T(8,128)S(1)}, f32[2,1,128,512]{3,2,1,0:T(8,128)S(1)}) fusion(s32[512]{0:T(512)S(1)} %iota_add_fusion, s32[2,128]{1,0:T(2,128)S(1)} %add_multiply_fusion), kind=kLoop, calls=%fused_computation.33 | loop fusion | flops 1835008 | bytes 1051648 | tf_op jit(solution)/shard_map/cos | solution.py:30
  14.6 3.9 %collective-permute-done = bf16[1,2,1,8,64,256]{5,4,3,2,1,0:T(8,128)(2,1)S(1)} collective-permute-done((bf16[1,2,1,8,64,256]{5,4,3,2,1,0:T(8,128)(2,1)}, bf16[1,2,1,8,64,256]{5,4,3,2,1,0:T(8,128)(2,1)S(1)}, u32[]{:S(2)}, u32[]{:S(2)}) %collective-permute-start) | collective-permute-done | bytes 524320 | tf_op jit(solution)/shard_map/ppermute | solution.py:25
  18.6 2.3 %image.2 = (f32[2,4,4,32,256]{4,3,2,1,0:T(8,128)S(1)}, bf16[2,4,4,32,256]{4,3,2,1,0:T(8,128)(2,1)S(1)}) custom-call(bf16[2,4,4,64,256]{4,3,2,1,0:T(8,128)(2,1)S(1)} %pad_maximum_fusion.data_ref, bf16[256,256]{1,0:T(8,128)(2,1)S(1)} %copy.44.steer_ref, bf16[1,128,256]{2,1,0:T(8,128)(2,1)S(1)} %pad_maximum_fusion.6.interp_ref, f32[4,4,128]{2,1,0:T(4,128)S(1)} %bitcast.120, ...), custom_call_target="tpu_custom_call" | custom-call | flops 402653184 | bytes 2621440 | tf_op jit(solution)/shard_map/image/pallas_call | solution.py:247
  21.0 0.2 collective-permute-done.3
  21.3 2.3 %image.3 = (f32[2,4,4,32,256]{4,3,2,1,0:T(8,128)S(1)}, bf16[2,4,4,32,256]{4,3,2,1,0:T(8,128)(2,1)S(1)}) custom-call(bf16[2,4,4,64,256]{4,3,2,1,0:T(8,128)(2,1)S(1)} %pad_maximum_fusion.2.data_ref, bf16[256,256]{1,0:T(8,128)(2,1)S(1)} %copy.45.steer_ref, bf16[1,128,256]{2,1,0:T(8,128)(2,1)S(1)} %pad_maximum_fusion.6.interp_ref, f32[4,4,128]{2,1,0:T(4,128)S(1)} %bitcast.119, ...), custom_call_target="tpu_custom_call" | custom-call | flops 402653184 | bytes 2621440 | tf_op jit(solution)/shard_map/image/pallas_call | solution.py:247
  23.6 0.1 fusion.61
  23.8 0.4 collective-permute-start.4
  24.4 1.8 %collective-permute-start.9 = (bf16[1,8,32,256]{3,2,1,0:T(8,128)(2,1)S(1)}, bf16[1,8,32,256]{3,2,1,0:T(8,128)(2,1)S(1)}, u32[]{:S(2)}, u32[]{:S(2)}) collective-permute-start(bf16[1,8,32,256]{3,2,1,0:T(8,128)(2,1)S(1)} %get-tuple-element.41), channel_id=1, source_target_pairs={{0,16},{8,24},{16,0},{24,8},{1,17},{9,25},{17,1},{25,9},{2,18},{10... | collective-permute-start | bytes 393224 | tf_op jit(solution)/shard_map/ppermute | solution.py:25
  26.3 0.3 collective-permute-start.2
  26.8 1.8 %collective-permute-start.7 = (bf16[2,4,32,256]{3,2,1,0:T(8,128)(2,1)S(1)}, bf16[2,4,32,256]{3,2,1,0:T(8,128)(2,1)S(1)}, u32[]{:S(2)}, u32[]{:S(2)}) collective-permute-start(bf16[2,4,32,256]{3,2,1,0:T(8,128)(2,1)S(1)} %get-tuple-element.35), channel_id=1, source_target_pairs={{0,1},{1,0},{2,3},{3,2},{4,5},{5,4},{6,7},{7,6},{8,9},{9,8},{10,11... | collective-permute-start | bytes 393224 | tf_op jit(solution)/shard_map/ppermute | solution.py:25
  28.7 0.3 collective-permute-start.5
  29.0 1.7 %collective-permute-done.9 = bf16[1,8,32,256]{3,2,1,0:T(8,128)(2,1)S(1)} collective-permute-done((bf16[1,8,32,256]{3,2,1,0:T(8,128)(2,1)S(1)}, bf16[1,8,32,256]{3,2,1,0:T(8,128)(2,1)S(1)}, u32[]{:S(2)}, u32[]{:S(2)}) %collective-permute-start.9) | collective-permute-done | bytes 131104 | tf_op jit(solution)/shard_map/ppermute | solution.py:25
  30.8 1.9 %collective-permute-start.10 = (bf16[1,4,32,256]{3,2,1,0:T(8,128)(2,1)S(1)}, bf16[1,4,32,256]{3,2,1,0:T(8,128)(2,1)S(1)}, u32[]{:S(2)}, u32[]{:S(2)}) collective-permute-start(bf16[1,4,32,256]{3,2,1,0:T(8,128)(2,1)S(1)} %fusion.35), channel_id=1, source_target_pairs={{0,2},{1,3},{2,0},{3,1},{4,6},{5,7},{6,4},{7,5},{8,10},{9,11},{10,... | collective-permute-start | bytes 196616 | tf_op jit(solution)/shard_map/ppermute | solution.py:25
  32.7 0.6 %collective-permute-done.7 = bf16[2,4,32,256]{3,2,1,0:T(8,128)(2,1)S(1)} collective-permute-done((bf16[2,4,32,256]{3,2,1,0:T(8,128)(2,1)S(1)}, bf16[2,4,32,256]{3,2,1,0:T(8,128)(2,1)S(1)}, u32[]{:S(2)}, u32[]{:S(2)}) %collective-permute-start.7) | collective-permute-done | bytes 131104 | tf_op jit(solution)/shard_map/ppermute | solution.py:25
  33.3 1.7 %collective-permute-start.8 = (bf16[1,4,32,256]{3,2,1,0:T(8,128)(2,1)S(1)}, bf16[1,4,32,256]{3,2,1,0:T(8,128)(2,1)S(1)}, u32[]{:S(2)}, u32[]{:S(2)}) collective-permute-start(bf16[1,4,32,256]{3,2,1,0:T(8,128)(2,1)S(1)} %fusion.34), channel_id=1, source_target_pairs={{0,16},{8,24},{16,0},{24,8},{1,17},{9,25},{17,1},{25,9},{2,18},{10... | collective-permute-start | bytes 196616 | tf_op jit(solution)/shard_map/ppermute | solution.py:25
  35.0 1.4 %collective-permute-start.11 = (bf16[1,4,32,256]{3,2,1,0:T(8,128)(2,1)S(1)}, bf16[1,4,32,256]{3,2,1,0:T(8,128)(2,1)S(1)}, u32[]{:S(2)}, u32[]{:S(2)}) collective-permute-start(bf16[1,4,32,256]{3,2,1,0:T(8,128)(2,1)S(1)} %fusion.36), channel_id=1, source_target_pairs={{0,16},{8,24},{16,0},{24,8},{1,17},{9,25},{17,1},{25,9},{2,18},{10... | collective-permute-start | bytes 196616 | tf_op jit(solution)/shard_map/ppermute | solution.py:25
  36.4 1.6 %collective-permute-start.6 = (bf16[1,4,32,256]{3,2,1,0:T(8,128)(2,1)S(1)}, bf16[1,4,32,256]{3,2,1,0:T(8,128)(2,1)S(1)}, u32[]{:S(2)}, u32[]{:S(2)}) collective-permute-start(bf16[1,4,32,256]{3,2,1,0:T(8,128)(2,1)S(1)} %fusion.33), channel_id=1, source_target_pairs={{0,2},{1,3},{2,0},{3,1},{4,6},{5,7},{6,4},{7,5},{8,10},{9,11},{10,... | collective-permute-start | bytes 196616 | tf_op jit(solution)/shard_map/ppermute | solution.py:25
  38.0 1.3 %collective-permute-done.11 = bf16[1,4,32,256]{3,2,1,0:T(8,128)(2,1)S(1)} collective-permute-done((bf16[1,4,32,256]{3,2,1,0:T(8,128)(2,1)S(1)}, bf16[1,4,32,256]{3,2,1,0:T(8,128)(2,1)S(1)}, u32[]{:S(2)}, u32[]{:S(2)}) %collective-permute-start.11) | collective-permute-done | bytes 65568 | tf_op jit(solution)/shard_map/ppermute | solution.py:25
  39.4 1.3 %collective-permute-done.6 = bf16[1,4,32,256]{3,2,1,0:T(8,128)(2,1)S(1)} collective-permute-done((bf16[1,4,32,256]{3,2,1,0:T(8,128)(2,1)S(1)}, bf16[1,4,32,256]{3,2,1,0:T(8,128)(2,1)S(1)}, u32[]{:S(2)}, u32[]{:S(2)}) %collective-permute-start.6) | collective-permute-done | bytes 65568 | tf_op jit(solution)/shard_map/ppermute | solution.py:25
  40.8 2.9 %collective-permute-start.12 = (bf16[2,4,32,256]{3,2,1,0:T(8,128)(2,1)S(1)}, bf16[2,4,32,256]{3,2,1,0:T(8,128)(2,1)S(1)}, u32[]{:S(2)}, u32[]{:S(2)}) collective-permute-start(bf16[2,4,32,256]{3,2,1,0:T(8,128)(2,1)S(1)} %pad_maximum_fusion.5), channel_id=1, source_target_pairs={{0,4},{1,5},{2,6},{3,7},{4,0},{5,1},{6,2},{7,3},{8,12},{9,13},{10,... | collective-permute-start | bytes 393224 | tf_op jit(solution)/shard_map/ppermute | solution.py:25
  43.7 4.4 %collective-permute-done.12 = bf16[2,4,32,256]{3,2,1,0:T(8,128)(2,1)S(1)} collective-permute-done((bf16[2,4,32,256]{3,2,1,0:T(8,128)(2,1)S(1)}, bf16[2,4,32,256]{3,2,1,0:T(8,128)(2,1)S(1)}, u32[]{:S(2)}, u32[]{:S(2)}) %collective-permute-start.12) | collective-permute-done | bytes 131104 | tf_op jit(solution)/shard_map/ppermute | solution.py:25
  48.1 0.7 %last_sum.1 = bf16[32,8,256]{2,1,0:T(8,128)(2,1)} custom-call(f32[8,32,256]{2,1,0:T(8,128)S(1)} %bitcast.116, bf16[8,32,256]{2,1,0:T(8,128)(2,1)S(1)} %bitcast.118), custom_call_target="tpu_custom_call" | custom-call | tf_op jit(solution)/shard_map/last_sum/pallas_call | solution.py:290
  (81 shorter events, 2.5 us)
Async XLA Ops:
  0.0 6.4 %copy-start.1 = (bf16[2,128]{1,0:T(2,128)(2,1)S(1)}, bf16[2,128]{1,0:T(2,128)(2,1)}, u32[]{:S(2)}) copy-start(bf16[2,128]{1,0:T(2,128)(2,1)} %chirp_ref.2) | copy-start | bytes 1540
  0.0 6.4 %copy-start = (bf16[64,64,256]{2,1,0:T(8,128)(2,1)S(1)}, bf16[64,64,256]{2,1,0:T(8,128)(2,1)}, u32[]{:S(2)}) copy-start(bf16[64,64,256]{2,1,0:T(8,128)(2,1)} %refs_0_.1) | copy-start | bytes 6291460
  3.3 6.2 %copy-start.5 = (s32[1,8]{1,0:T(1,128)S(1)}, s32[1,8]{1,0:T(1,128)}, u32[]{:S(2)}) copy-start(s32[1,8]{1,0:T(1,128)} %param.9) | copy-start | bytes 100
  3.3 6.8 %copy-start.3 = (s32[2,2,128,8]{2,3,1,0:T(8,128)S(1)}, s32[2,2,128,8]{2,3,1,0:T(8,128)}, u32[]{:S(2)}) copy-start(s32[2,2,128,8]{2,3,1,0:T(8,128)} %param.8) | copy-start | bytes 49156
  3.3 7.3 %copy-start.4 = (f32[8]{0:T(128)S(1)}, f32[8]{0:T(128)}, u32[]{:S(2)}) copy-start(f32[8]{0:T(128)} %constant.177.clone) | copy-start | bytes 100
  3.3 15.2 %collective-permute-start = (bf16[1,2,1,8,64,256]{5,4,3,2,1,0:T(8,128)(2,1)}, bf16[1,2,1,8,64,256]{5,4,3,2,1,0:T(8,128)(2,1)S(1)}, u32[]{:S(2)}, u32[]{:S(2)}) collective-permute-start(bf16[1,2,1,8,64,256]{5,4,3,2,1,0:T(8,128)(2,1)} %get-tuple-element.18), channel_id=1, source_target_pairs={{0,1},{1,0},{2,3},{3,2},{4,5},{5,4},{6,7},{7,6},{8,9},{9,8},{10,11... | collective-permute-start | bytes 1572872 | tf_op jit(solution)/shard_map/ppermute | solution.py:25
  7.8 13.4 %collective-permute-start.3 = (bf16[1,1,2,8,64,256]{5,4,3,2,1,0:T(8,128)(2,1)S(1)}, bf16[1,1,2,8,64,256]{5,4,3,2,1,0:T(8,128)(2,1)S(1)}, u32[]{:S(2)}, u32[]{:S(2)}) collective-permute-start(bf16[1,1,2,8,64,256]{5,4,3,2,1,0:T(8,128)(2,1)S(1)} %get-tuple-element.23), channel_id=1, source_target_pairs={{0,2},{1,3},{2,0},{3,1},{4,6},{5,7},{6,4},{7,5},{8,10},{9,11},{10,... | collective-permute-start | bytes 1572872 | tf_op jit(solution)/shard_map/ppermute | solution.py:25
  12.1 6.4 %copy-start.2 = (bf16[1,2,1,8,64,256]{5,4,3,2,1,0:T(8,128)(2,1)S(1)}, bf16[1,2,1,8,64,256]{5,4,3,2,1,0:T(8,128)(2,1)}, u32[]{:S(2)}) copy-start(bf16[1,2,1,8,64,256]{5,4,3,2,1,0:T(8,128)(2,1)} %get-tuple-element.16) | copy-start | bytes 1572868
  20.9 3.4 %collective-permute-start.1 = (bf16[2,4,4,32,256]{4,3,2,1,0:T(8,128)(2,1)S(1)}, bf16[2,4,4,32,256]{4,3,2,1,0:T(8,128)(2,1)S(1)}, u32[]{:S(2)}, u32[]{:S(2)}) collective-permute-start(bf16[2,4,4,32,256]{4,3,2,1,0:T(8,128)(2,1)S(1)} %get-tuple-element.20), channel_id=1, source_target_pairs={{0,8},{8,0},{16,24},{24,16},{1,9},{9,1},{17,25},{25,17},{2,10},{10... | collective-permute-start | bytes 1572872 | tf_op jit(solution)/shard_map/ppermute | solution.py:25
  23.8 2.8 %collective-permute-start.4 = (bf16[2,4,4,32,256]{4,3,2,1,0:T(8,128)(2,1)S(1)}, bf16[2,4,4,32,256]{4,3,2,1,0:T(8,128)(2,1)S(1)}, u32[]{:S(2)}, u32[]{:S(2)}) collective-permute-start(bf16[2,4,4,32,256]{4,3,2,1,0:T(8,128)(2,1)S(1)} %get-tuple-element.25), channel_id=1, source_target_pairs={{0,8},{8,0},{16,24},{24,16},{1,9},{9,1},{17,25},{25,17},{2,10},{10... | collective-permute-start | bytes 1572872 | tf_op jit(solution)/shard_map/ppermute | solution.py:25
  24.4 6.4 %collective-permute-start.9 = (bf16[1,8,32,256]{3,2,1,0:T(8,128)(2,1)S(1)}, bf16[1,8,32,256]{3,2,1,0:T(8,128)(2,1)S(1)}, u32[]{:S(2)}, u32[]{:S(2)}) collective-permute-start(bf16[1,8,32,256]{3,2,1,0:T(8,128)(2,1)S(1)} %get-tuple-element.41), channel_id=1, source_target_pairs={{0,16},{8,24},{16,0},{24,8},{1,17},{9,25},{17,1},{25,9},{2,18},{10... | collective-permute-start | bytes 393224 | tf_op jit(solution)/shard_map/ppermute | solution.py:25
  26.3 10.1 %collective-permute-start.2 = (bf16[1,8,32,256]{3,2,1,0:T(8,128)(2,1)S(1)}, bf16[1,8,32,256]{3,2,1,0:T(8,128)(2,1)S(1)}, u32[]{:S(2)}, u32[]{:S(2)}) collective-permute-start(bf16[1,8,32,256]{3,2,1,0:T(8,128)(2,1)S(1)} %get-tuple-element.37), channel_id=1, source_target_pairs={{0,16},{8,24},{16,0},{24,8},{1,17},{9,25},{17,1},{25,9},{2,18},{10... | collective-permute-start | bytes 393224 | tf_op jit(solution)/shard_map/ppermute | solution.py:25
  26.8 6.5 %collective-permute-start.7 = (bf16[2,4,32,256]{3,2,1,0:T(8,128)(2,1)S(1)}, bf16[2,4,32,256]{3,2,1,0:T(8,128)(2,1)S(1)}, u32[]{:S(2)}, u32[]{:S(2)}) collective-permute-start(bf16[2,4,32,256]{3,2,1,0:T(8,128)(2,1)S(1)} %get-tuple-element.35), channel_id=1, source_target_pairs={{0,1},{1,0},{2,3},{3,2},{4,5},{5,4},{6,7},{7,6},{8,9},{9,8},{10,11... | collective-permute-start | bytes 393224 | tf_op jit(solution)/shard_map/ppermute | solution.py:25
  28.7 6.2 %collective-permute-start.5 = (bf16[2,4,32,256]{3,2,1,0:T(8,128)(2,1)S(1)}, bf16[2,4,32,256]{3,2,1,0:T(8,128)(2,1)S(1)}, u32[]{:S(2)}, u32[]{:S(2)}) collective-permute-start(bf16[2,4,32,256]{3,2,1,0:T(8,128)(2,1)S(1)} %get-tuple-element.39), channel_id=1, source_target_pairs={{0,1},{1,0},{2,3},{3,2},{4,5},{5,4},{6,7},{7,6},{8,9},{9,8},{10,11... | collective-permute-start | bytes 393224 | tf_op jit(solution)/shard_map/ppermute | solution.py:25
  30.8 7.2 %collective-permute-start.10 = (bf16[1,4,32,256]{3,2,1,0:T(8,128)(2,1)S(1)}, bf16[1,4,32,256]{3,2,1,0:T(8,128)(2,1)S(1)}, u32[]{:S(2)}, u32[]{:S(2)}) collective-permute-start(bf16[1,4,32,256]{3,2,1,0:T(8,128)(2,1)S(1)} %fusion.35), channel_id=1, source_target_pairs={{0,2},{1,3},{2,0},{3,1},{4,6},{5,7},{6,4},{7,5},{8,10},{9,11},{10,... | collective-permute-start | bytes 196616 | tf_op jit(solution)/shard_map/ppermute | solution.py:25
  33.3 6.1 %collective-permute-start.8 = (bf16[1,4,32,256]{3,2,1,0:T(8,128)(2,1)S(1)}, bf16[1,4,32,256]{3,2,1,0:T(8,128)(2,1)S(1)}, u32[]{:S(2)}, u32[]{:S(2)}) collective-permute-start(bf16[1,4,32,256]{3,2,1,0:T(8,128)(2,1)S(1)} %fusion.34), channel_id=1, source_target_pairs={{0,16},{8,24},{16,0},{24,8},{1,17},{9,25},{17,1},{25,9},{2,18},{10... | collective-permute-start | bytes 196616 | tf_op jit(solution)/shard_map/ppermute | solution.py:25
  35.0 4.3 %collective-permute-start.11 = (bf16[1,4,32,256]{3,2,1,0:T(8,128)(2,1)S(1)}, bf16[1,4,32,256]{3,2,1,0:T(8,128)(2,1)S(1)}, u32[]{:S(2)}, u32[]{:S(2)}) collective-permute-start(bf16[1,4,32,256]{3,2,1,0:T(8,128)(2,1)S(1)} %fusion.36), channel_id=1, source_target_pairs={{0,16},{8,24},{16,0},{24,8},{1,17},{9,25},{17,1},{25,9},{2,18},{10... | collective-permute-start | bytes 196616 | tf_op jit(solution)/shard_map/ppermute | solution.py:25
  36.4 4.3 %collective-permute-start.6 = (bf16[1,4,32,256]{3,2,1,0:T(8,128)(2,1)S(1)}, bf16[1,4,32,256]{3,2,1,0:T(8,128)(2,1)S(1)}, u32[]{:S(2)}, u32[]{:S(2)}) collective-permute-start(bf16[1,4,32,256]{3,2,1,0:T(8,128)(2,1)S(1)} %fusion.33), channel_id=1, source_target_pairs={{0,2},{1,3},{2,0},{3,1},{4,6},{5,7},{6,4},{7,5},{8,10},{9,11},{10,... | collective-permute-start | bytes 196616 | tf_op jit(solution)/shard_map/ppermute | solution.py:25
  40.8 7.3 %collective-permute-start.12 = (bf16[2,4,32,256]{3,2,1,0:T(8,128)(2,1)S(1)}, bf16[2,4,32,256]{3,2,1,0:T(8,128)(2,1)S(1)}, u32[]{:S(2)}, u32[]{:S(2)}) collective-permute-start(bf16[2,4,32,256]{3,2,1,0:T(8,128)(2,1)S(1)} %pad_maximum_fusion.5), channel_id=1, source_target_pairs={{0,4},{1,5},{2,6},{3,7},{4,0},{5,1},{6,2},{7,3},{8,12},{9,13},{10,... | collective-permute-start | bytes 393224 | tf_op jit(solution)/shard_map/ppermute | solution.py:25

commit v18 on v13

--- a/solution.py
+++ b/solution.py
@@ -210,7 +210,7 @@
                         both = jnp.concatenate(both, axis=1)
                         g = first // rows
                         if g < leaf // 2:
-                            out_keep[g, 0, at + i] = both
+                            out_keep[g, 0, at + i] = both.astype(jnp.bfloat16)
                         else:
                             out_send[g - leaf // 2, 0, at + i] = both.astype(jnp.bfloat16)
                         continue
@@ -256,7 +256,7 @@
         ],
         out_specs=[out_spec, out_spec],
         out_shape=[
-            jax.ShapeDtypeStruct(shape, jnp.float32),
+            jax.ShapeDtypeStruct(shape, jnp.bfloat16),
             jax.ShapeDtypeStruct(shape, jnp.bfloat16),
         ],
         compiler_params=pltpu.CompilerParams(vmem_limit_bytes=10 * 2**20),

time: 48.7 us -> 48.5 us (level)
  no operation moved by 1% of the time
where the time goes in v18:
time: 48.5 us; the launch traced here: 48.3 us
  starting transfers between devices  17.8 us (37%)
  waiting for transfers between devices  14.3 us (29%)
  Pallas kernels  9.96 us (21%)
  other arithmetic  4.82 us (10%)
  local copies, waits for them, and re-layouts  0.9 us (2%)
    ppermute x13, starting transfers between devices, swapped(): lax.ppermute(array, axis, [(i, i ^ 1 << bit) for i in range(lax.axis_size...  17.8 us
    ppermute x13, waiting for transfers between devices, swapped(): lax.ppermute(array, axis, [(i, i ^ 1 << bit) for i in range(lax.axis_size...  14.3 us
    pallas_call x2, Pallas kernels, compress(): pl.pallas_call(functools.partial(compress_kernel, dims, has_edge), grid=(...  4.66 us
    pallas_call x2, Pallas kernels, backproject(): pl.pallas_call(functools.partial(image_kernel, (leaf, each, half, beams,...  4.57 us
    cos x2, other arithmetic, unit(): return (jnp.cos(angle), jnp.sin(angle))  2.27 us
  transfers between devices with their start and end apart: 13, of which 8 were waited for; matrix products, arithmetic and copies ran while one was open for 12% of the time, Pallas kernels for 12%

profile of v18, /device:TPU:0, one launch (start us, length us, event | category | flops | bytes accessed | tf_op | source)
XLA Modules:
  0.0 48.3 jit_solution(546062110529107759)
XLA Ops:
  0.0 3.3 %compress.2 = (bf16[1,2,1,8,64,256]{5,4,3,2,1,0:T(8,128)(2,1)}, bf16[1,2,1,8,64,256]{5,4,3,2,1,0:T(8,128)(2,1)}) custom-call(bf16[2,128]{1,0:T(2,128)(2,1)} %chirp_ref.2, bf16[64,64,256]{2,1,0:T(8,128)(2,1)} %refs_0_.1), custom_call_target="tpu_custom_call" | custom-call | flops 536870912 | bytes 2097152 | tf_op jit(solution)/shard_map/compress/pallas_call | solution.py:142
  3.3 3.1 %collective-permute-start = (bf16[1,2,1,8,64,256]{5,4,3,2,1,0:T(8,128)(2,1)}, bf16[1,2,1,8,64,256]{5,4,3,2,1,0:T(8,128)(2,1)S(1)}, u32[]{:S(2)}, u32[]{:S(2)}) collective-permute-start(bf16[1,2,1,8,64,256]{5,4,3,2,1,0:T(8,128)(2,1)} %get-tuple-element.17), channel_id=1, source_target_pairs={{0,1},{1,0},{2,3},{3,2},{4,5},{5,4},{6,7},{7,6},{8,9},{9,8},{10,11... | collective-permute-start | bytes 1572872 | tf_op jit(solution)/shard_map/ppermute | solution.py:25
  6.4 1.4 %compress.3 = (bf16[1,1,2,8,64,256]{5,4,3,2,1,0:T(8,128)(2,1)S(1)}, bf16[1,1,2,8,64,256]{5,4,3,2,1,0:T(8,128)(2,1)S(1)}) custom-call(bf16[2,128]{1,0:T(2,128)(2,1)S(1)} %copy-done.1, bf16[64,64,256]{2,1,0:T(8,128)(2,1)S(1)} %copy-done, bf16[64,64,256]{2,1,0:T(8,128)(2,1)S(1)} %copy-done), custom_call_target="tpu_custom_call" | custom-call | flops 536870912 | bytes 2097152 | tf_op jit(solution)/shard_map/compress/pallas_call | solution.py:142
  7.8 1.6 %collective-permute-start.4 = (bf16[1,1,2,8,64,256]{5,4,3,2,1,0:T(8,128)(2,1)S(1)}, bf16[1,1,2,8,64,256]{5,4,3,2,1,0:T(8,128)(2,1)S(1)}, u32[]{:S(2)}, u32[]{:S(2)}) collective-permute-start(bf16[1,1,2,8,64,256]{5,4,3,2,1,0:T(8,128)(2,1)S(1)} %get-tuple-element.22), channel_id=1, source_target_pairs={{0,2},{1,3},{2,0},{3,1},{4,6},{5,7},{6,4},{7,5},{8,10},{9,11},{10,... | collective-permute-start | bytes 1572872 | tf_op jit(solution)/shard_map/ppermute | solution.py:25
  9.5 0.2 select_reduce_fusion.1
  10.3 0.1 copy.35
  10.6 0.4 select_reduce_fusion
  11.0 0.5 multiply_convert_fusion.1
  11.5 0.2 fusion.24
  11.9 0.2 fusion.41
  12.4 2.1 %fusion.4 = (f32[2,1,128,512]{3,2,1,0:T(8,128)S(1)}, f32[2,1,128,512]{3,2,1,0:T(8,128)S(1)}) fusion(s32[512]{0:T(512)S(1)} %iota_add_fusion, s32[2,128]{1,0:T(2,128)S(1)} %add_multiply_fusion), kind=kLoop, calls=%fused_computation.27 | loop fusion | flops 1835008 | bytes 1051648 | tf_op jit(solution)/shard_map/cos | solution.py:30
  14.6 3.9 %collective-permute-done = bf16[1,2,1,8,64,256]{5,4,3,2,1,0:T(8,128)(2,1)S(1)} collective-permute-done((bf16[1,2,1,8,64,256]{5,4,3,2,1,0:T(8,128)(2,1)}, bf16[1,2,1,8,64,256]{5,4,3,2,1,0:T(8,128)(2,1)S(1)}, u32[]{:S(2)}, u32[]{:S(2)}) %collective-permute-start) | collective-permute-done | bytes 524320 | tf_op jit(solution)/shard_map/ppermute | solution.py:25
  18.6 2.3 %image.2 = (bf16[2,4,4,32,256]{4,3,2,1,0:T(8,128)(2,1)S(1)}, bf16[2,4,4,32,256]{4,3,2,1,0:T(8,128)(2,1)S(1)}) custom-call(bf16[2,4,4,64,256]{4,3,2,1,0:T(8,128)(2,1)S(1)} %pad_maximum_fusion.data_ref, bf16[256,256]{1,0:T(8,128)(2,1)S(1)} %copy.44.steer_ref, bf16[1,128,256]{2,1,0:T(8,128)(2,1)S(1)} %pad_maximum_fusion.6.interp_ref, ...), custom_call_target="tpu_custom_call" | custom-call | flops 402653184 | bytes 2621440 | tf_op jit(solution)/shard_map/image/pallas_call | solution.py:247
  20.9 0.2 collective-permute-done.4
  21.3 2.3 %image.3 = (bf16[2,4,4,32,256]{4,3,2,1,0:T(8,128)(2,1)S(1)}, bf16[2,4,4,32,256]{4,3,2,1,0:T(8,128)(2,1)S(1)}) custom-call(bf16[2,4,4,64,256]{4,3,2,1,0:T(8,128)(2,1)S(1)} %pad_maximum_fusion.2.data_ref, bf16[256,256]{1,0:T(8,128)(2,1)S(1)} %copy.45.steer_ref, bf16[1,128,256]{2,1,0:T(8,128)(2,1)S(1)} %pad_maximum_fusion.6.interp_ref, ...), custom_call_target="tpu_custom_call" | custom-call | flops 402653184 | bytes 2621440 | tf_op jit(solution)/shard_map/image/pallas_call | solution.py:247
  23.7 0.3 collective-permute-start.5
  24.2 1.8 %collective-permute-start.8 = (bf16[1,8,32,256]{3,2,1,0:T(8,128)(2,1)S(1)}, bf16[1,8,32,256]{3,2,1,0:T(8,128)(2,1)S(1)}, u32[]{:S(2)}, u32[]{:S(2)}) collective-permute-start(bf16[1,8,32,256]{3,2,1,0:T(8,128)(2,1)S(1)} %get-tuple-element.43), channel_id=1, source_target_pairs={{0,16},{8,24},{16,0},{24,8},{1,17},{9,25},{17,1},{25,9},{2,18},{10... | collective-permute-start | bytes 393224 | tf_op jit(solution)/shard_map/ppermute | solution.py:25
  26.1 0.3 collective-permute-start.2
  26.5 1.8 %collective-permute-start.6 = (bf16[2,4,32,256]{3,2,1,0:T(8,128)(2,1)S(1)}, bf16[2,4,32,256]{3,2,1,0:T(8,128)(2,1)S(1)}, u32[]{:S(2)}, u32[]{:S(2)}) collective-permute-start(bf16[2,4,32,256]{3,2,1,0:T(8,128)(2,1)S(1)} %get-tuple-element.29), channel_id=1, source_target_pairs={{0,1},{1,0},{2,3},{3,2},{4,5},{5,4},{6,7},{7,6},{8,9},{9,8},{10,11... | collective-permute-start | bytes 393224 | tf_op jit(solution)/shard_map/ppermute | solution.py:25
  28.4 0.3 collective-permute-start.10
  28.8 1.8 %collective-permute-done.8 = bf16[1,8,32,256]{3,2,1,0:T(8,128)(2,1)S(1)} collective-permute-done((bf16[1,8,32,256]{3,2,1,0:T(8,128)(2,1)S(1)}, bf16[1,8,32,256]{3,2,1,0:T(8,128)(2,1)S(1)}, u32[]{:S(2)}, u32[]{:S(2)}) %collective-permute-start.8) | collective-permute-done | bytes 131104 | tf_op jit(solution)/shard_map/ppermute | solution.py:25
  30.6 1.9 %collective-permute-start.9 = (bf16[1,4,32,256]{3,2,1,0:T(8,128)(2,1)S(1)}, bf16[1,4,32,256]{3,2,1,0:T(8,128)(2,1)S(1)}, u32[]{:S(2)}, u32[]{:S(2)}) collective-permute-start(bf16[1,4,32,256]{3,2,1,0:T(8,128)(2,1)S(1)} %fusion.29), channel_id=1, source_target_pairs={{0,2},{1,3},{2,0},{3,1},{4,6},{5,7},{6,4},{7,5},{8,10},{9,11},{10,... | collective-permute-start | bytes 196616 | tf_op jit(solution)/shard_map/ppermute | solution.py:25
  32.5 0.2 collective-permute-done.2
  32.7 1.7 %collective-permute-start.3 = (bf16[1,4,32,256]{3,2,1,0:T(8,128)(2,1)S(1)}, bf16[1,4,32,256]{3,2,1,0:T(8,128)(2,1)S(1)}, u32[]{:S(2)}, u32[]{:S(2)}) collective-permute-start(bf16[1,4,32,256]{3,2,1,0:T(8,128)(2,1)S(1)} %fusion.27), channel_id=1, source_target_pairs={{0,2},{1,3},{2,0},{3,1},{4,6},{5,7},{6,4},{7,5},{8,10},{9,11},{10,... | collective-permute-start | bytes 196616 | tf_op jit(solution)/shard_map/ppermute | solution.py:25
  34.4 1.6 %collective-permute-start.7 = (bf16[1,4,32,256]{3,2,1,0:T(8,128)(2,1)S(1)}, bf16[1,4,32,256]{3,2,1,0:T(8,128)(2,1)S(1)}, u32[]{:S(2)}, u32[]{:S(2)}) collective-permute-start(bf16[1,4,32,256]{3,2,1,0:T(8,128)(2,1)S(1)} %fusion.28), channel_id=1, source_target_pairs={{0,16},{8,24},{16,0},{24,8},{1,17},{9,25},{17,1},{25,9},{2,18},{10... | collective-permute-start | bytes 196616 | tf_op jit(solution)/shard_map/ppermute | solution.py:25
  36.0 0.6 %collective-permute-start.11 = (bf16[1,4,32,256]{3,2,1,0:T(8,128)(2,1)S(1)}, bf16[1,4,32,256]{3,2,1,0:T(8,128)(2,1)S(1)}, u32[]{:S(2)}, u32[]{:S(2)}) collective-permute-start(bf16[1,4,32,256]{3,2,1,0:T(8,128)(2,1)S(1)} %fusion.30), channel_id=1, source_target_pairs={{0,16},{8,24},{16,0},{24,8},{1,17},{9,25},{17,1},{25,9},{2,18},{10... | collective-permute-start | bytes 196616 | tf_op jit(solution)/shard_map/ppermute | solution.py:25
  36.6 0.5 collective-permute-done.3
  37.0 1.7 %collective-permute-done.7 = bf16[1,4,32,256]{3,2,1,0:T(8,128)(2,1)S(1)} collective-permute-done((bf16[1,4,32,256]{3,2,1,0:T(8,128)(2,1)S(1)}, bf16[1,4,32,256]{3,2,1,0:T(8,128)(2,1)S(1)}, u32[]{:S(2)}, u32[]{:S(2)}) %collective-permute-start.7) | collective-permute-done | bytes 65568 | tf_op jit(solution)/shard_map/ppermute | solution.py:25
  38.8 1.5 %collective-permute-done.11 = bf16[1,4,32,256]{3,2,1,0:T(8,128)(2,1)S(1)} collective-permute-done((bf16[1,4,32,256]{3,2,1,0:T(8,128)(2,1)S(1)}, bf16[1,4,32,256]{3,2,1,0:T(8,128)(2,1)S(1)}, u32[]{:S(2)}, u32[]{:S(2)}) %collective-permute-start.11) | collective-permute-done | bytes 65568 | tf_op jit(solution)/shard_map/ppermute | solution.py:25
  40.4 2.7 %collective-permute-start.12 = (bf16[2,4,32,256]{3,2,1,0:T(8,128)(2,1)S(1)}, bf16[2,4,32,256]{3,2,1,0:T(8,128)(2,1)S(1)}, u32[]{:S(2)}, u32[]{:S(2)}) collective-permute-start(bf16[2,4,32,256]{3,2,1,0:T(8,128)(2,1)S(1)} %pad_maximum_fusion.5), channel_id=1, source_target_pairs={{0,4},{1,5},{2,6},{3,7},{4,0},{5,1},{6,2},{7,3},{8,12},{9,13},{10,... | collective-permute-start | bytes 393224 | tf_op jit(solution)/shard_map/ppermute | solution.py:25
  43.1 4.6 %collective-permute-done.12 = bf16[2,4,32,256]{3,2,1,0:T(8,128)(2,1)S(1)} collective-permute-done((bf16[2,4,32,256]{3,2,1,0:T(8,128)(2,1)S(1)}, bf16[2,4,32,256]{3,2,1,0:T(8,128)(2,1)S(1)}, u32[]{:S(2)}, u32[]{:S(2)}) %collective-permute-start.12) | collective-permute-done | bytes 131104 | tf_op jit(solution)/shard_map/ppermute | solution.py:25
  47.6 0.7 %last_sum.1 = bf16[32,8,256]{2,1,0:T(8,128)(2,1)} custom-call(f32[8,32,256]{2,1,0:T(8,128)S(1)} %bitcast.114, bf16[8,32,256]{2,1,0:T(8,128)(2,1)S(1)} %bitcast.118), custom_call_target="tpu_custom_call" | custom-call | tf_op jit(solution)/shard_map/last_sum/pallas_call | solution.py:290
  (81 shorter events, 2.3 us)
Async XLA Ops:
  0.0 6.4 %copy-start.1 = (bf16[2,128]{1,0:T(2,128)(2,1)S(1)}, bf16[2,128]{1,0:T(2,128)(2,1)}, u32[]{:S(2)}) copy-start(bf16[2,128]{1,0:T(2,128)(2,1)} %chirp_ref.2) | copy-start | bytes 1540
  0.0 6.4 %copy-start = (bf16[64,64,256]{2,1,0:T(8,128)(2,1)S(1)}, bf16[64,64,256]{2,1,0:T(8,128)(2,1)}, u32[]{:S(2)}) copy-start(bf16[64,64,256]{2,1,0:T(8,128)(2,1)} %refs_0_.1) | copy-start | bytes 6291460
  3.3 6.2 %copy-start.5 = (s32[1,8]{1,0:T(1,128)S(1)}, s32[1,8]{1,0:T(1,128)}, u32[]{:S(2)}) copy-start(s32[1,8]{1,0:T(1,128)} %param.9) | copy-start | bytes 100
  3.3 6.8 %copy-start.3 = (s32[2,2,128,8]{2,3,1,0:T(8,128)S(1)}, s32[2,2,128,8]{2,3,1,0:T(8,128)}, u32[]{:S(2)}) copy-start(s32[2,2,128,8]{2,3,1,0:T(8,128)} %param.8) | copy-start | bytes 49156
  3.3 7.3 %copy-start.4 = (f32[8]{0:T(128)S(1)}, f32[8]{0:T(128)}, u32[]{:S(2)}) copy-start(f32[8]{0:T(128)} %constant.177.clone) | copy-start | bytes 100
  3.3 15.2 %collective-permute-start = (bf16[1,2,1,8,64,256]{5,4,3,2,1,0:T(8,128)(2,1)}, bf16[1,2,1,8,64,256]{5,4,3,2,1,0:T(8,128)(2,1)S(1)}, u32[]{:S(2)}, u32[]{:S(2)}) collective-permute-start(bf16[1,2,1,8,64,256]{5,4,3,2,1,0:T(8,128)(2,1)} %get-tuple-element.17), channel_id=1, source_target_pairs={{0,1},{1,0},{2,3},{3,2},{4,5},{5,4},{6,7},{7,6},{8,9},{9,8},{10,11... | collective-permute-start | bytes 1572872 | tf_op jit(solution)/shard_map/ppermute | solution.py:25
  7.8 13.4 %collective-permute-start.4 = (bf16[1,1,2,8,64,256]{5,4,3,2,1,0:T(8,128)(2,1)S(1)}, bf16[1,1,2,8,64,256]{5,4,3,2,1,0:T(8,128)(2,1)S(1)}, u32[]{:S(2)}, u32[]{:S(2)}) collective-permute-start(bf16[1,1,2,8,64,256]{5,4,3,2,1,0:T(8,128)(2,1)S(1)} %get-tuple-element.22), channel_id=1, source_target_pairs={{0,2},{1,3},{2,0},{3,1},{4,6},{5,7},{6,4},{7,5},{8,10},{9,11},{10,... | collective-permute-start | bytes 1572872 | tf_op jit(solution)/shard_map/ppermute | solution.py:25
  12.1 6.4 %copy-start.2 = (bf16[1,2,1,8,64,256]{5,4,3,2,1,0:T(8,128)(2,1)S(1)}, bf16[1,2,1,8,64,256]{5,4,3,2,1,0:T(8,128)(2,1)}, u32[]{:S(2)}) copy-start(bf16[1,2,1,8,64,256]{5,4,3,2,1,0:T(8,128)(2,1)} %get-tuple-element.15) | copy-start | bytes 1572868
  20.9 3.2 %collective-permute-start.1 = (bf16[2,4,4,32,256]{4,3,2,1,0:T(8,128)(2,1)S(1)}, bf16[2,4,4,32,256]{4,3,2,1,0:T(8,128)(2,1)S(1)}, u32[]{:S(2)}, u32[]{:S(2)}) collective-permute-start(bf16[2,4,4,32,256]{4,3,2,1,0:T(8,128)(2,1)S(1)} %get-tuple-element.19), channel_id=1, source_target_pairs={{0,8},{8,0},{16,24},{24,16},{1,9},{9,1},{17,25},{25,17},{2,10},{10... | collective-permute-start | bytes 1572872 | tf_op jit(solution)/shard_map/ppermute | solution.py:25
  23.7 2.7 %collective-permute-start.5 = (bf16[2,4,4,32,256]{4,3,2,1,0:T(8,128)(2,1)S(1)}, bf16[2,4,4,32,256]{4,3,2,1,0:T(8,128)(2,1)S(1)}, u32[]{:S(2)}, u32[]{:S(2)}) collective-permute-start(bf16[2,4,4,32,256]{4,3,2,1,0:T(8,128)(2,1)S(1)} %get-tuple-element.24), channel_id=1, source_target_pairs={{0,8},{8,0},{16,24},{24,16},{1,9},{9,1},{17,25},{25,17},{2,10},{10... | collective-permute-start | bytes 1572872 | tf_op jit(solution)/shard_map/ppermute | solution.py:25
  24.2 6.4 %collective-permute-start.8 = (bf16[1,8,32,256]{3,2,1,0:T(8,128)(2,1)S(1)}, bf16[1,8,32,256]{3,2,1,0:T(8,128)(2,1)S(1)}, u32[]{:S(2)}, u32[]{:S(2)}) collective-permute-start(bf16[1,8,32,256]{3,2,1,0:T(8,128)(2,1)S(1)} %get-tuple-element.43), channel_id=1, source_target_pairs={{0,16},{8,24},{16,0},{24,8},{1,17},{9,25},{17,1},{25,9},{2,18},{10... | collective-permute-start | bytes 393224 | tf_op jit(solution)/shard_map/ppermute | solution.py:25
  26.1 6.6 %collective-permute-start.2 = (bf16[1,8,32,256]{3,2,1,0:T(8,128)(2,1)S(1)}, bf16[1,8,32,256]{3,2,1,0:T(8,128)(2,1)S(1)}, u32[]{:S(2)}, u32[]{:S(2)}) collective-permute-start(bf16[1,8,32,256]{3,2,1,0:T(8,128)(2,1)S(1)} %get-tuple-element.35), channel_id=1, source_target_pairs={{0,16},{8,24},{16,0},{24,8},{1,17},{9,25},{17,1},{25,9},{2,18},{10... | collective-permute-start | bytes 393224 | tf_op jit(solution)/shard_map/ppermute | solution.py:25
  26.5 7.8 %collective-permute-start.6 = (bf16[2,4,32,256]{3,2,1,0:T(8,128)(2,1)S(1)}, bf16[2,4,32,256]{3,2,1,0:T(8,128)(2,1)S(1)}, u32[]{:S(2)}, u32[]{:S(2)}) collective-permute-start(bf16[2,4,32,256]{3,2,1,0:T(8,128)(2,1)S(1)} %get-tuple-element.29), channel_id=1, source_target_pairs={{0,1},{1,0},{2,3},{3,2},{4,5},{5,4},{6,7},{7,6},{8,9},{9,8},{10,11... | collective-permute-start | bytes 393224 | tf_op jit(solution)/shard_map/ppermute | solution.py:25
  28.4 7.5 %collective-permute-start.10 = (bf16[2,4,32,256]{3,2,1,0:T(8,128)(2,1)S(1)}, bf16[2,4,32,256]{3,2,1,0:T(8,128)(2,1)S(1)}, u32[]{:S(2)}, u32[]{:S(2)}) collective-permute-start(bf16[2,4,32,256]{3,2,1,0:T(8,128)(2,1)S(1)} %get-tuple-element.41), channel_id=1, source_target_pairs={{0,1},{1,0},{2,3},{3,2},{4,5},{5,4},{6,7},{7,6},{8,9},{9,8},{10,11... | collective-permute-start | bytes 393224 | tf_op jit(solution)/shard_map/ppermute | solution.py:25
  30.6 8.2 %collective-permute-start.9 = (bf16[1,4,32,256]{3,2,1,0:T(8,128)(2,1)S(1)}, bf16[1,4,32,256]{3,2,1,0:T(8,128)(2,1)S(1)}, u32[]{:S(2)}, u32[]{:S(2)}) collective-permute-start(bf16[1,4,32,256]{3,2,1,0:T(8,128)(2,1)S(1)} %fusion.29), channel_id=1, source_target_pairs={{0,2},{1,3},{2,0},{3,1},{4,6},{5,7},{6,4},{7,5},{8,10},{9,11},{10,... | collective-permute-start | bytes 196616 | tf_op jit(solution)/shard_map/ppermute | solution.py:25
  32.7 4.3 %collective-permute-start.3 = (bf16[1,4,32,256]{3,2,1,0:T(8,128)(2,1)S(1)}, bf16[1,4,32,256]{3,2,1,0:T(8,128)(2,1)S(1)}, u32[]{:S(2)}, u32[]{:S(2)}) collective-permute-start(bf16[1,4,32,256]{3,2,1,0:T(8,128)(2,1)S(1)} %fusion.27), channel_id=1, source_target_pairs={{0,2},{1,3},{2,0},{3,1},{4,6},{5,7},{6,4},{7,5},{8,10},{9,11},{10,... | collective-permute-start | bytes 196616 | tf_op jit(solution)/shard_map/ppermute | solution.py:25
  34.4 4.3 %collective-permute-start.7 = (bf16[1,4,32,256]{3,2,1,0:T(8,128)(2,1)S(1)}, bf16[1,4,32,256]{3,2,1,0:T(8,128)(2,1)S(1)}, u32[]{:S(2)}, u32[]{:S(2)}) collective-permute-start(bf16[1,4,32,256]{3,2,1,0:T(8,128)(2,1)S(1)} %fusion.28), channel_id=1, source_target_pairs={{0,16},{8,24},{16,0},{24,8},{1,17},{9,25},{17,1},{25,9},{2,18},{10... | collective-permute-start | bytes 196616 | tf_op jit(solution)/shard_map/ppermute | solution.py:25
  36.0 4.3 %collective-permute-start.11 = (bf16[1,4,32,256]{3,2,1,0:T(8,128)(2,1)S(1)}, bf16[1,4,32,256]{3,2,1,0:T(8,128)(2,1)S(1)}, u32[]{:S(2)}, u32[]{:S(2)}) collective-permute-start(bf16[1,4,32,256]{3,2,1,0:T(8,128)(2,1)S(1)} %fusion.30), channel_id=1, source_target_pairs={{0,16},{8,24},{16,0},{24,8},{1,17},{9,25},{17,1},{25,9},{2,18},{10... | collective-permute-start | bytes 196616 | tf_op jit(solution)/shard_map/ppermute | solution.py:25
  40.4 7.2 %collective-permute-start.12 = (bf16[2,4,32,256]{3,2,1,0:T(8,128)(2,1)S(1)}, bf16[2,4,32,256]{3,2,1,0:T(8,128)(2,1)S(1)}, u32[]{:S(2)}, u32[]{:S(2)}) collective-permute-start(bf16[2,4,32,256]{3,2,1,0:T(8,128)(2,1)S(1)} %pad_maximum_fusion.5), channel_id=1, source_target_pairs={{0,4},{1,5},{2,6},{3,7},{4,0},{5,1},{6,2},{7,3},{8,12},{9,13},{10,... | collective-permute-start | bytes 393224 | tf_op jit(solution)/shard_map/ppermute | solution.py:25

commit v19 on v18

--- a/solution.py
+++ b/solution.py
@@ -151,7 +151,7 @@
             pltpu.VMEM((pulses, width), jnp.bfloat16),
         ],
         compiler_params=pltpu.CompilerParams(
-            vmem_limit_bytes=VMEM_BYTES if near_chain else 20 * 2**20
+            vmem_limit_bytes=20 * 2**20 if near_chain else VMEM_BYTES
         ),
         cost_estimate=pl.CostEstimate(
             flops=2 * pulses * blocks * width * width,
@@ -343,11 +343,11 @@
     rows = beams // leaf
     own_leaf, own_turn = lax.axis_index("leaf"), lax.axis_index("turn")
 
+    keep_z, send_z = compress(chirp, echoes, high, mids, False, far, 0)
+    chirp, send_z = lax.optimization_barrier((chirp, send_z))
+    got_z = swapped(send_z, "turn", far)
     keep_y, send_y = compress(chirp, echoes, high, mids, True, far, high)
-    chirp, send_y = lax.optimization_barrier((chirp, send_y))
     got_y = swapped(send_y, "turn", 0)
-    keep_z, send_z = compress(chirp, echoes, high, mids, False, far, 0)
-    got_z = swapped(send_z, "turn", far)
 
     own_sides = [bit(own_leaf, level) for level in range(levels)]
     row = jnp.arange(beams, dtype=jnp.int32)

time: 48.5 us -> 49 us (1.010)
  starting transfers between devices: 17.8 us -> 19.1 us
  waiting for transfers between devices: 14.3 us -> 13.2 us
    ppermute x13, starting transfers between devices: 17.8 us -> 19.1 us  [swapped(): lax.ppermute(array, axis, [(i, i ^ 1 << bit) for i in range(lax.axis_size...]
    ppermute x13, waiting for transfers between devices: 14.3 us -> 13.2 us  [swapped(): lax.ppermute(array, axis, [(i, i ^ 1 << bit) for i in range(lax.axis_size...]
  transfers between devices with their start and end apart: 13 -> 13, of which waited for: 8 -> 7; matrix products, arithmetic and copies ran while one was open for 12% -> 12% of each run, Pallas kernels for 12% -> 12%
where the time goes in v19:
time: 49 us; the launch traced here: 48.8 us
  starting transfers between devices  19.1 us (39%)
  waiting for transfers between devices  13.2 us (27%)
  Pallas kernels  10.2 us (21%)
  other arithmetic  4.82 us (10%)
  local copies, waits for them, and re-layouts  0.89 us (2%)
    ppermute x13, starting transfers between devices, swapped(): lax.ppermute(array, axis, [(i, i ^ 1 << bit) for i in range(lax.axis_size...  19.1 us
    ppermute x13, waiting for transfers between devices, swapped(): lax.ppermute(array, axis, [(i, i ^ 1 << bit) for i in range(lax.axis_size...  13.2 us
    pallas_call x2, Pallas kernels, compress(): pl.pallas_call(functools.partial(compress_kernel, dims, has_edge), grid=(...  4.93 us
    pallas_call x2, Pallas kernels, backproject(): pl.pallas_call(functools.partial(image_kernel, (leaf, each, half, beams,...  4.57 us
    cos x2, other arithmetic, unit(): return (jnp.cos(angle), jnp.sin(angle))  2.27 us
  transfers between devices with their start and end apart: 13, of which 7 were waited for; matrix products, arithmetic and copies ran while one was open for 12% of the time, Pallas kernels for 12%

profile of v19, /device:TPU:0, one launch (start us, length us, event | category | flops | bytes accessed | tf_op | source)
XLA Modules:
  0.0 48.8 jit_solution(5298908598303315892)
XLA Ops:
  0.0 3.6 %compress.2 = (bf16[1,1,2,8,64,256]{5,4,3,2,1,0:T(8,128)(2,1)}, bf16[1,1,2,8,64,256]{5,4,3,2,1,0:T(8,128)(2,1)}) custom-call(bf16[2,128]{1,0:T(2,128)(2,1)} %chirp_ref.2, bf16[64,64,256]{2,1,0:T(8,128)(2,1)} %echo_ref.3, bf16[64,64,256]{2,1,0:T(8,128)(2,1)} %echo_ref.3), custom_call_target="tpu_custom_call" | custom-call | flops 536870912 | bytes 2097152 | tf_op jit(solution)/shard_map/compress/pallas_call | solution.py:142
  3.6 3.1 %collective-permute-start.4 = (bf16[1,1,2,8,64,256]{5,4,3,2,1,0:T(8,128)(2,1)}, bf16[1,1,2,8,64,256]{5,4,3,2,1,0:T(8,128)(2,1)S(1)}, u32[]{:S(2)}, u32[]{:S(2)}) collective-permute-start(bf16[1,1,2,8,64,256]{5,4,3,2,1,0:T(8,128)(2,1)} %get-tuple-element.22), channel_id=1, source_target_pairs={{0,2},{1,3},{2,0},{3,1},{4,6},{5,7},{6,4},{7,5},{8,10},{9,11},{10,... | collective-permute-start | bytes 1572872 | tf_op jit(solution)/shard_map/ppermute | solution.py:25
  6.7 1.3 %compress.3 = (bf16[1,2,1,8,64,256]{5,4,3,2,1,0:T(8,128)(2,1)S(1)}, bf16[1,2,1,8,64,256]{5,4,3,2,1,0:T(8,128)(2,1)S(1)}) custom-call(bf16[2,128]{1,0:T(2,128)(2,1)S(1)} %copy-done.1, bf16[64,64,256]{2,1,0:T(8,128)(2,1)S(1)} %copy-done), custom_call_target="tpu_custom_call" | custom-call | flops 536870912 | bytes 2097152 | tf_op jit(solution)/shard_map/compress/pallas_call | solution.py:142
  8.1 1.6 %collective-permute-start = (bf16[1,2,1,8,64,256]{5,4,3,2,1,0:T(8,128)(2,1)S(1)}, bf16[1,2,1,8,64,256]{5,4,3,2,1,0:T(8,128)(2,1)S(1)}, u32[]{:S(2)}, u32[]{:S(2)}) collective-permute-start(bf16[1,2,1,8,64,256]{5,4,3,2,1,0:T(8,128)(2,1)S(1)} %get-tuple-element.18), channel_id=1, source_target_pairs={{0,1},{1,0},{2,3},{3,2},{4,5},{5,4},{6,7},{7,6},{8,9},{9,8},{10,11... | collective-permute-start | bytes 1572872 | tf_op jit(solution)/shard_map/ppermute | solution.py:25
  9.7 0.2 select_reduce_fusion.1
  10.5 0.1 copy.35
  10.8 0.4 select_reduce_fusion
  11.2 0.5 multiply_convert_fusion.1
  11.7 0.2 fusion.24
  12.2 0.2 fusion.41
  12.4 0.1 copy.45.steer_ref
  12.5 0.1 copy.44.steer_ref
  12.7 2.1 %fusion.4 = (f32[2,1,128,512]{3,2,1,0:T(8,128)S(1)}, f32[2,1,128,512]{3,2,1,0:T(8,128)S(1)}) fusion(s32[512]{0:T(512)S(1)} %iota_add_fusion, s32[2,128]{1,0:T(2,128)S(1)} %add_multiply_fusion), kind=kLoop, calls=%fused_computation.27 | loop fusion | flops 1835008 | bytes 1051648 | tf_op jit(solution)/shard_map/cos | solution.py:30
  14.9 4.0 %collective-permute-done.4 = bf16[1,1,2,8,64,256]{5,4,3,2,1,0:T(8,128)(2,1)S(1)} collective-permute-done((bf16[1,1,2,8,64,256]{5,4,3,2,1,0:T(8,128)(2,1)}, bf16[1,1,2,8,64,256]{5,4,3,2,1,0:T(8,128)(2,1)S(1)}, u32[]{:S(2)}, u32[]{:S(2)}) %collective-permute-start.4) | collective-permute-done | bytes 524320 | tf_op jit(solution)/shard_map/ppermute | solution.py:25
  19.0 2.3 %image.3 = (bf16[2,4,4,32,256]{4,3,2,1,0:T(8,128)(2,1)S(1)}, bf16[2,4,4,32,256]{4,3,2,1,0:T(8,128)(2,1)S(1)}) custom-call(bf16[2,4,4,64,256]{4,3,2,1,0:T(8,128)(2,1)S(1)} %pad_maximum_fusion.2.data_ref, bf16[256,256]{1,0:T(8,128)(2,1)S(1)} %copy.45.steer_ref, bf16[1,128,256]{2,1,0:T(8,128)(2,1)S(1)} %pad_maximum_fusion.6.interp_ref, ...), custom_call_target="tpu_custom_call" | custom-call | flops 402653184 | bytes 2621440 | tf_op jit(solution)/shard_map/image/pallas_call | solution.py:247
  21.6 2.3 %image.2 = (bf16[2,4,4,32,256]{4,3,2,1,0:T(8,128)(2,1)S(1)}, bf16[2,4,4,32,256]{4,3,2,1,0:T(8,128)(2,1)S(1)}) custom-call(bf16[2,4,4,64,256]{4,3,2,1,0:T(8,128)(2,1)S(1)} %pad_maximum_fusion.data_ref, bf16[256,256]{1,0:T(8,128)(2,1)S(1)} %copy.44.steer_ref, bf16[1,128,256]{2,1,0:T(8,128)(2,1)S(1)} %pad_maximum_fusion.6.interp_ref, ...), custom_call_target="tpu_custom_call" | custom-call | flops 402653184 | bytes 2621440 | tf_op jit(solution)/shard_map/image/pallas_call | solution.py:247
  23.9 0.5 collective-permute-start.1
  24.6 1.8 %collective-permute-start.6 = (bf16[2,4,32,256]{3,2,1,0:T(8,128)(2,1)S(1)}, bf16[2,4,32,256]{3,2,1,0:T(8,128)(2,1)S(1)}, u32[]{:S(2)}, u32[]{:S(2)}) collective-permute-start(bf16[2,4,32,256]{3,2,1,0:T(8,128)(2,1)S(1)} %get-tuple-element.29), channel_id=1, source_target_pairs={{0,1},{1,0},{2,3},{3,2},{4,5},{5,4},{6,7},{7,6},{8,9},{9,8},{10,11... | collective-permute-start | bytes 393224 | tf_op jit(solution)/shard_map/ppermute | solution.py:25
  26.4 0.4 collective-permute-start.10
  26.9 1.7 %collective-permute-start.8 = (bf16[1,8,32,256]{3,2,1,0:T(8,128)(2,1)S(1)}, bf16[1,8,32,256]{3,2,1,0:T(8,128)(2,1)S(1)}, u32[]{:S(2)}, u32[]{:S(2)}) collective-permute-start(bf16[1,8,32,256]{3,2,1,0:T(8,128)(2,1)S(1)} %get-tuple-element.43), channel_id=1, source_target_pairs={{0,16},{8,24},{16,0},{24,8},{1,17},{9,25},{17,1},{25,9},{2,18},{10... | collective-permute-start | bytes 393224 | tf_op jit(solution)/shard_map/ppermute | solution.py:25
  28.7 0.4 collective-permute-start.2
  29.2 1.8 %collective-permute-done.6 = bf16[2,4,32,256]{3,2,1,0:T(8,128)(2,1)S(1)} collective-permute-done((bf16[2,4,32,256]{3,2,1,0:T(8,128)(2,1)S(1)}, bf16[2,4,32,256]{3,2,1,0:T(8,128)(2,1)S(1)}, u32[]{:S(2)}, u32[]{:S(2)}) %collective-permute-start.6) | collective-permute-done | bytes 131104 | tf_op jit(solution)/shard_map/ppermute | solution.py:25
  31.0 1.7 %collective-permute-start.7 = (bf16[1,4,32,256]{3,2,1,0:T(8,128)(2,1)S(1)}, bf16[1,4,32,256]{3,2,1,0:T(8,128)(2,1)S(1)}, u32[]{:S(2)}, u32[]{:S(2)}) collective-permute-start(bf16[1,4,32,256]{3,2,1,0:T(8,128)(2,1)S(1)} %fusion.28), channel_id=1, source_target_pairs={{0,16},{8,24},{16,0},{24,8},{1,17},{9,25},{17,1},{25,9},{2,18},{10... | collective-permute-start | bytes 196616 | tf_op jit(solution)/shard_map/ppermute | solution.py:25
  32.7 0.2 collective-permute-done.10
  33.0 1.6 %collective-permute-start.11 = (bf16[1,4,32,256]{3,2,1,0:T(8,128)(2,1)S(1)}, bf16[1,4,32,256]{3,2,1,0:T(8,128)(2,1)S(1)}, u32[]{:S(2)}, u32[]{:S(2)}) collective-permute-start(bf16[1,4,32,256]{3,2,1,0:T(8,128)(2,1)S(1)} %fusion.30), channel_id=1, source_target_pairs={{0,16},{8,24},{16,0},{24,8},{1,17},{9,25},{17,1},{25,9},{2,18},{10... | collective-permute-start | bytes 196616 | tf_op jit(solution)/shard_map/ppermute | solution.py:25
  34.6 1.6 %collective-permute-start.9 = (bf16[1,4,32,256]{3,2,1,0:T(8,128)(2,1)S(1)}, bf16[1,4,32,256]{3,2,1,0:T(8,128)(2,1)S(1)}, u32[]{:S(2)}, u32[]{:S(2)}) collective-permute-start(bf16[1,4,32,256]{3,2,1,0:T(8,128)(2,1)S(1)} %fusion.29), channel_id=1, source_target_pairs={{0,2},{1,3},{2,0},{3,1},{4,6},{5,7},{6,4},{7,5},{8,10},{9,11},{10,... | collective-permute-start | bytes 196616 | tf_op jit(solution)/shard_map/ppermute | solution.py:25
  36.3 1.5 %collective-permute-start.3 = (bf16[1,4,32,256]{3,2,1,0:T(8,128)(2,1)S(1)}, bf16[1,4,32,256]{3,2,1,0:T(8,128)(2,1)S(1)}, u32[]{:S(2)}, u32[]{:S(2)}) collective-permute-start(bf16[1,4,32,256]{3,2,1,0:T(8,128)(2,1)S(1)} %fusion.27), channel_id=1, source_target_pairs={{0,2},{1,3},{2,0},{3,1},{4,6},{5,7},{6,4},{7,5},{8,10},{9,11},{10,... | collective-permute-start | bytes 196616 | tf_op jit(solution)/shard_map/ppermute | solution.py:25
  37.8 1.1 %collective-permute-done.9 = bf16[1,4,32,256]{3,2,1,0:T(8,128)(2,1)S(1)} collective-permute-done((bf16[1,4,32,256]{3,2,1,0:T(8,128)(2,1)S(1)}, bf16[1,4,32,256]{3,2,1,0:T(8,128)(2,1)S(1)}, u32[]{:S(2)}, u32[]{:S(2)}) %collective-permute-start.9) | collective-permute-done | bytes 65568 | tf_op jit(solution)/shard_map/ppermute | solution.py:25
  39.0 1.6 %collective-permute-done.3 = bf16[1,4,32,256]{3,2,1,0:T(8,128)(2,1)S(1)} collective-permute-done((bf16[1,4,32,256]{3,2,1,0:T(8,128)(2,1)S(1)}, bf16[1,4,32,256]{3,2,1,0:T(8,128)(2,1)S(1)}, u32[]{:S(2)}, u32[]{:S(2)}) %collective-permute-start.3) | collective-permute-done | bytes 65568 | tf_op jit(solution)/shard_map/ppermute | solution.py:25
  40.7 3.0 %collective-permute-start.12 = (bf16[2,4,32,256]{3,2,1,0:T(8,128)(2,1)S(1)}, bf16[2,4,32,256]{3,2,1,0:T(8,128)(2,1)S(1)}, u32[]{:S(2)}, u32[]{:S(2)}) collective-permute-start(bf16[2,4,32,256]{3,2,1,0:T(8,128)(2,1)S(1)} %pad_maximum_fusion.5), channel_id=1, source_target_pairs={{0,4},{1,5},{2,6},{3,7},{4,0},{5,1},{6,2},{7,3},{8,12},{9,13},{10,... | collective-permute-start | bytes 393224 | tf_op jit(solution)/shard_map/ppermute | solution.py:25
  43.8 4.3 %collective-permute-done.12 = bf16[2,4,32,256]{3,2,1,0:T(8,128)(2,1)S(1)} collective-permute-done((bf16[2,4,32,256]{3,2,1,0:T(8,128)(2,1)S(1)}, bf16[2,4,32,256]{3,2,1,0:T(8,128)(2,1)S(1)}, u32[]{:S(2)}, u32[]{:S(2)}) %collective-permute-start.12) | collective-permute-done | bytes 131104 | tf_op jit(solution)/shard_map/ppermute | solution.py:25
  48.1 0.7 %last_sum.1 = bf16[32,8,256]{2,1,0:T(8,128)(2,1)} custom-call(f32[8,32,256]{2,1,0:T(8,128)S(1)} %bitcast.114, bf16[8,32,256]{2,1,0:T(8,128)(2,1)S(1)} %bitcast.118), custom_call_target="tpu_custom_call" | custom-call | tf_op jit(solution)/shard_map/last_sum/pallas_call | solution.py:290
  (81 shorter events, 2.2 us)
Async XLA Ops:
  0.0 6.7 %copy-start.1 = (bf16[2,128]{1,0:T(2,128)(2,1)S(1)}, bf16[2,128]{1,0:T(2,128)(2,1)}, u32[]{:S(2)}) copy-start(bf16[2,128]{1,0:T(2,128)(2,1)} %chirp_ref.2) | copy-start | bytes 1540
  0.0 6.7 %copy-start = (bf16[64,64,256]{2,1,0:T(8,128)(2,1)S(1)}, bf16[64,64,256]{2,1,0:T(8,128)(2,1)}, u32[]{:S(2)}) copy-start(bf16[64,64,256]{2,1,0:T(8,128)(2,1)} %echo_ref.3) | copy-start | bytes 6291460
  3.6 6.1 %copy-start.5 = (s32[1,8]{1,0:T(1,128)S(1)}, s32[1,8]{1,0:T(1,128)}, u32[]{:S(2)}) copy-start(s32[1,8]{1,0:T(1,128)} %param.9) | copy-start | bytes 100
  3.6 6.7 %copy-start.3 = (s32[2,2,128,8]{2,3,1,0:T(8,128)S(1)}, s32[2,2,128,8]{2,3,1,0:T(8,128)}, u32[]{:S(2)}) copy-start(s32[2,2,128,8]{2,3,1,0:T(8,128)} %param.8) | copy-start | bytes 49156
  3.6 7.2 %copy-start.4 = (f32[8]{0:T(128)S(1)}, f32[8]{0:T(128)}, u32[]{:S(2)}) copy-start(f32[8]{0:T(128)} %constant.177.clone) | copy-start | bytes 100
  3.6 15.2 %collective-permute-start.4 = (bf16[1,1,2,8,64,256]{5,4,3,2,1,0:T(8,128)(2,1)}, bf16[1,1,2,8,64,256]{5,4,3,2,1,0:T(8,128)(2,1)S(1)}, u32[]{:S(2)}, u32[]{:S(2)}) collective-permute-start(bf16[1,1,2,8,64,256]{5,4,3,2,1,0:T(8,128)(2,1)} %get-tuple-element.22), channel_id=1, source_target_pairs={{0,2},{1,3},{2,0},{3,1},{4,6},{5,7},{6,4},{7,5},{8,10},{9,11},{10,... | collective-permute-start | bytes 1572872 | tf_op jit(solution)/shard_map/ppermute | solution.py:25
  8.1 13.4 %collective-permute-start = (bf16[1,2,1,8,64,256]{5,4,3,2,1,0:T(8,128)(2,1)S(1)}, bf16[1,2,1,8,64,256]{5,4,3,2,1,0:T(8,128)(2,1)S(1)}, u32[]{:S(2)}, u32[]{:S(2)}) collective-permute-start(bf16[1,2,1,8,64,256]{5,4,3,2,1,0:T(8,128)(2,1)S(1)} %get-tuple-element.18), channel_id=1, source_target_pairs={{0,1},{1,0},{2,3},{3,2},{4,5},{5,4},{6,7},{7,6},{8,9},{9,8},{10,11... | collective-permute-start | bytes 1572872 | tf_op jit(solution)/shard_map/ppermute | solution.py:25
  12.4 6.5 %copy-start.2 = (bf16[1,1,2,8,64,256]{5,4,3,2,1,0:T(8,128)(2,1)S(1)}, bf16[1,1,2,8,64,256]{5,4,3,2,1,0:T(8,128)(2,1)}, u32[]{:S(2)}) copy-start(bf16[1,1,2,8,64,256]{5,4,3,2,1,0:T(8,128)(2,1)} %get-tuple-element.21) | copy-start | bytes 1572868
  21.2 3.2 %collective-permute-start.5 = (bf16[2,4,4,32,256]{4,3,2,1,0:T(8,128)(2,1)S(1)}, bf16[2,4,4,32,256]{4,3,2,1,0:T(8,128)(2,1)S(1)}, u32[]{:S(2)}, u32[]{:S(2)}) collective-permute-start(bf16[2,4,4,32,256]{4,3,2,1,0:T(8,128)(2,1)S(1)} %get-tuple-element.24), channel_id=1, source_target_pairs={{0,8},{8,0},{16,24},{24,16},{1,9},{9,1},{17,25},{25,17},{2,10},{10... | collective-permute-start | bytes 1572872 | tf_op jit(solution)/shard_map/ppermute | solution.py:25
  23.9 2.9 %collective-permute-start.1 = (bf16[2,4,4,32,256]{4,3,2,1,0:T(8,128)(2,1)S(1)}, bf16[2,4,4,32,256]{4,3,2,1,0:T(8,128)(2,1)S(1)}, u32[]{:S(2)}, u32[]{:S(2)}) collective-permute-start(bf16[2,4,4,32,256]{4,3,2,1,0:T(8,128)(2,1)S(1)} %get-tuple-element.20), channel_id=1, source_target_pairs={{0,8},{8,0},{16,24},{24,16},{1,9},{9,1},{17,25},{25,17},{2,10},{10... | collective-permute-start | bytes 1572872 | tf_op jit(solution)/shard_map/ppermute | solution.py:25
  24.6 6.4 %collective-permute-start.6 = (bf16[2,4,32,256]{3,2,1,0:T(8,128)(2,1)S(1)}, bf16[2,4,32,256]{3,2,1,0:T(8,128)(2,1)S(1)}, u32[]{:S(2)}, u32[]{:S(2)}) collective-permute-start(bf16[2,4,32,256]{3,2,1,0:T(8,128)(2,1)S(1)} %get-tuple-element.29), channel_id=1, source_target_pairs={{0,1},{1,0},{2,3},{3,2},{4,5},{5,4},{6,7},{7,6},{8,9},{9,8},{10,11... | collective-permute-start | bytes 393224 | tf_op jit(solution)/shard_map/ppermute | solution.py:25
  26.4 6.5 %collective-permute-start.10 = (bf16[2,4,32,256]{3,2,1,0:T(8,128)(2,1)S(1)}, bf16[2,4,32,256]{3,2,1,0:T(8,128)(2,1)S(1)}, u32[]{:S(2)}, u32[]{:S(2)}) collective-permute-start(bf16[2,4,32,256]{3,2,1,0:T(8,128)(2,1)S(1)} %get-tuple-element.41), channel_id=1, source_target_pairs={{0,1},{1,0},{2,3},{3,2},{4,5},{5,4},{6,7},{7,6},{8,9},{9,8},{10,11... | collective-permute-start | bytes 393224 | tf_op jit(solution)/shard_map/ppermute | solution.py:25
  26.9 7.7 %collective-permute-start.8 = (bf16[1,8,32,256]{3,2,1,0:T(8,128)(2,1)S(1)}, bf16[1,8,32,256]{3,2,1,0:T(8,128)(2,1)S(1)}, u32[]{:S(2)}, u32[]{:S(2)}) collective-permute-start(bf16[1,8,32,256]{3,2,1,0:T(8,128)(2,1)S(1)} %get-tuple-element.43), channel_id=1, source_target_pairs={{0,16},{8,24},{16,0},{24,8},{1,17},{9,25},{17,1},{25,9},{2,18},{10... | collective-permute-start | bytes 393224 | tf_op jit(solution)/shard_map/ppermute | solution.py:25
  28.7 7.6 %collective-permute-start.2 = (bf16[1,8,32,256]{3,2,1,0:T(8,128)(2,1)S(1)}, bf16[1,8,32,256]{3,2,1,0:T(8,128)(2,1)S(1)}, u32[]{:S(2)}, u32[]{:S(2)}) collective-permute-start(bf16[1,8,32,256]{3,2,1,0:T(8,128)(2,1)S(1)} %get-tuple-element.35), channel_id=1, source_target_pairs={{0,16},{8,24},{16,0},{24,8},{1,17},{9,25},{17,1},{25,9},{2,18},{10... | collective-permute-start | bytes 393224 | tf_op jit(solution)/shard_map/ppermute | solution.py:25
  31.0 8.0 %collective-permute-start.7 = (bf16[1,4,32,256]{3,2,1,0:T(8,128)(2,1)S(1)}, bf16[1,4,32,256]{3,2,1,0:T(8,128)(2,1)S(1)}, u32[]{:S(2)}, u32[]{:S(2)}) collective-permute-start(bf16[1,4,32,256]{3,2,1,0:T(8,128)(2,1)S(1)} %fusion.28), channel_id=1, source_target_pairs={{0,16},{8,24},{16,0},{24,8},{1,17},{9,25},{17,1},{25,9},{2,18},{10... | collective-permute-start | bytes 196616 | tf_op jit(solution)/shard_map/ppermute | solution.py:25
  33.0 4.9 %collective-permute-start.11 = (bf16[1,4,32,256]{3,2,1,0:T(8,128)(2,1)S(1)}, bf16[1,4,32,256]{3,2,1,0:T(8,128)(2,1)S(1)}, u32[]{:S(2)}, u32[]{:S(2)}) collective-permute-start(bf16[1,4,32,256]{3,2,1,0:T(8,128)(2,1)S(1)} %fusion.30), channel_id=1, source_target_pairs={{0,16},{8,24},{16,0},{24,8},{1,17},{9,25},{17,1},{25,9},{2,18},{10... | collective-permute-start | bytes 196616 | tf_op jit(solution)/shard_map/ppermute | solution.py:25
  34.6 4.3 %collective-permute-start.9 = (bf16[1,4,32,256]{3,2,1,0:T(8,128)(2,1)S(1)}, bf16[1,4,32,256]{3,2,1,0:T(8,128)(2,1)S(1)}, u32[]{:S(2)}, u32[]{:S(2)}) collective-permute-start(bf16[1,4,32,256]{3,2,1,0:T(8,128)(2,1)S(1)} %fusion.29), channel_id=1, source_target_pairs={{0,2},{1,3},{2,0},{3,1},{4,6},{5,7},{6,4},{7,5},{8,10},{9,11},{10,... | collective-permute-start | bytes 196616 | tf_op jit(solution)/shard_map/ppermute | solution.py:25
  36.3 4.3 %collective-permute-start.3 = (bf16[1,4,32,256]{3,2,1,0:T(8,128)(2,1)S(1)}, bf16[1,4,32,256]{3,2,1,0:T(8,128)(2,1)S(1)}, u32[]{:S(2)}, u32[]{:S(2)}) collective-permute-start(bf16[1,4,32,256]{3,2,1,0:T(8,128)(2,1)S(1)} %fusion.27), channel_id=1, source_target_pairs={{0,2},{1,3},{2,0},{3,1},{4,6},{5,7},{6,4},{7,5},{8,10},{9,11},{10,... | collective-permute-start | bytes 196616 | tf_op jit(solution)/shard_map/ppermute | solution.py:25
  40.7 7.4 %collective-permute-start.12 = (bf16[2,4,32,256]{3,2,1,0:T(8,128)(2,1)S(1)}, bf16[2,4,32,256]{3,2,1,0:T(8,128)(2,1)S(1)}, u32[]{:S(2)}, u32[]{:S(2)}) collective-permute-start(bf16[2,4,32,256]{3,2,1,0:T(8,128)(2,1)S(1)} %pad_maximum_fusion.5), channel_id=1, source_target_pairs={{0,4},{1,5},{2,6},{3,7},{4,0},{5,1},{6,2},{7,3},{8,12},{9,13},{10,... | collective-permute-start | bytes 393224 | tf_op jit(solution)/shard_map/ppermute | solution.py:25

commit v20 on v18

--- a/solution.py
+++ b/solution.py
@@ -274,28 +274,6 @@
     return stay, gone.astype(jnp.bfloat16)
 
 
-def last_kernel(keep_ref, got_ref, out_ref, rows_ref):
-    blocks, rows, width = keep_ref.shape
-    for i in range(blocks):
-        value = keep_ref[i] + got_ref[i].astype(jnp.float32)
-        for c in range(2):
-            cols = slice(c * width // 2, (c + 1) * width // 2)
-            rows_ref[c, pl.ds(i, rows, stride=blocks), :] = value[:, cols]
-    both = jnp.concatenate([rows_ref[0], rows_ref[1]], axis=1)
-    out_ref[...] = both.reshape(rows, blocks, width).astype(jnp.bfloat16)
-
-
-def last_sum(keep, got):
-    blocks, rows, width = keep.shape
-    return pl.pallas_call(
-        last_kernel,
-        out_shape=jax.ShapeDtypeStruct((rows, blocks, width), jnp.bfloat16),
-        scratch_shapes=[pltpu.VMEM((2, rows * blocks, width // 2), jnp.float32)],
-        compiler_params=pltpu.CompilerParams(vmem_limit_bytes=8 * 2**20),
-        name="last_sum",
-    )(keep, got)
-
-
 def interpolation(taps, beams):
     cells = jnp.arange(beams, dtype=jnp.int32)
     weights = jnp.array(WEIGHTS, jnp.float32)
@@ -434,7 +412,8 @@
     kept = jnp.stack([jnp.where(upper, first, second) for first, second in final])
     shape = (tile, rows, width)
     got = swapped(sent.astype(jnp.bfloat16), "turn", top)
-    return last_sum(kept.reshape(shape), got.reshape(shape))
+    total = kept.reshape(shape) + got.reshape(shape).astype(jnp.float32)
+    return total.transpose(1, 0, 2).astype(jnp.bfloat16)
 
 
 def solution(mesh):

time: 48.5 us -> 48.5 us (level)
  Pallas kernels: 9.96 us -> 9.22 us
  local copies, waits for them, and re-layouts: 0.9 us -> 1.61 us
    convert_element_type x0 -> x1, local copies, waits for them, and re-layouts: none -> 0.73 us  [per_device(): return total.transpose(1, 0, 2).astype(jnp.bfloat16)]
    pallas_call x1 -> x0, Pallas kernels: 0.73 us -> none  [last_sum(): pl.pallas_call(last_kernel, out_shape=jax.ShapeDtypeStruct((rows, blocks,...]
  transfers between devices with their start and end apart: 13 -> 13, of which waited for: 8 -> 7; matrix products, arithmetic and copies ran while one was open for 12% -> 12% of each run, Pallas kernels for 12% -> 12%
where the time goes in v20:
time: 48.5 us; the launch traced here: 48.4 us
  starting transfers between devices  17.9 us (37%)
  waiting for transfers between devices  14.3 us (29%)
  Pallas kernels  9.22 us (19%)
  other arithmetic  4.83 us (10%)
  local copies, waits for them, and re-layouts  1.61 us (3%)
    ppermute x13, starting transfers between devices, swapped(): lax.ppermute(array, axis, [(i, i ^ 1 << bit) for i in range(lax.axis_size...  17.9 us
    ppermute x13, waiting for transfers between devices, swapped(): lax.ppermute(array, axis, [(i, i ^ 1 << bit) for i in range(lax.axis_size...  14.3 us
    pallas_call x2, Pallas kernels, compress(): pl.pallas_call(functools.partial(compress_kernel, dims, has_edge), grid=(...  4.65 us
    pallas_call x2, Pallas kernels, backproject(): pl.pallas_call(functools.partial(image_kernel, (leaf, each, half, beams,...  4.57 us
    cos x2, other arithmetic, unit(): return (jnp.cos(angle), jnp.sin(angle))  2.27 us
  transfers between devices with their start and end apart: 13, of which 7 were waited for; matrix products, arithmetic and copies ran while one was open for 12% of the time, Pallas kernels for 12%

profile of v20, /device:TPU:0, one launch (start us, length us, event | category | flops | bytes accessed | tf_op | source)
XLA Modules:
  0.0 48.4 jit_solution(15613699564498615284)
XLA Ops:
  0.0 3.3 %compress.2 = (bf16[1,2,1,8,64,256]{5,4,3,2,1,0:T(8,128)(2,1)}, bf16[1,2,1,8,64,256]{5,4,3,2,1,0:T(8,128)(2,1)}) custom-call(bf16[2,128]{1,0:T(2,128)(2,1)} %chirp_ref.2, bf16[64,64,256]{2,1,0:T(8,128)(2,1)} %refs_0_.1), custom_call_target="tpu_custom_call" | custom-call | flops 536870912 | bytes 2097152 | tf_op jit(solution)/shard_map/compress/pallas_call | solution.py:142
  3.3 3.1 %collective-permute-start = (bf16[1,2,1,8,64,256]{5,4,3,2,1,0:T(8,128)(2,1)}, bf16[1,2,1,8,64,256]{5,4,3,2,1,0:T(8,128)(2,1)S(1)}, u32[]{:S(2)}, u32[]{:S(2)}) collective-permute-start(bf16[1,2,1,8,64,256]{5,4,3,2,1,0:T(8,128)(2,1)} %get-tuple-element.17), channel_id=1, source_target_pairs={{0,1},{1,0},{2,3},{3,2},{4,5},{5,4},{6,7},{7,6},{8,9},{9,8},{10,11... | collective-permute-start | bytes 1572872 | tf_op jit(solution)/shard_map/ppermute | solution.py:25
  6.4 1.4 %compress.3 = (bf16[1,1,2,8,64,256]{5,4,3,2,1,0:T(8,128)(2,1)S(1)}, bf16[1,1,2,8,64,256]{5,4,3,2,1,0:T(8,128)(2,1)S(1)}) custom-call(bf16[2,128]{1,0:T(2,128)(2,1)S(1)} %copy-done.1, bf16[64,64,256]{2,1,0:T(8,128)(2,1)S(1)} %copy-done, bf16[64,64,256]{2,1,0:T(8,128)(2,1)S(1)} %copy-done), custom_call_target="tpu_custom_call" | custom-call | flops 536870912 | bytes 2097152 | tf_op jit(solution)/shard_map/compress/pallas_call | solution.py:142
  7.7 1.7 %collective-permute-start.4 = (bf16[1,1,2,8,64,256]{5,4,3,2,1,0:T(8,128)(2,1)S(1)}, bf16[1,1,2,8,64,256]{5,4,3,2,1,0:T(8,128)(2,1)S(1)}, u32[]{:S(2)}, u32[]{:S(2)}) collective-permute-start(bf16[1,1,2,8,64,256]{5,4,3,2,1,0:T(8,128)(2,1)S(1)} %get-tuple-element.22), channel_id=1, source_target_pairs={{0,2},{1,3},{2,0},{3,1},{4,6},{5,7},{6,4},{7,5},{8,10},{9,11},{10,... | collective-permute-start | bytes 1572872 | tf_op jit(solution)/shard_map/ppermute | solution.py:25
  9.5 0.2 select_reduce_fusion.1
  10.3 0.1 copy.43
  10.6 0.4 select_reduce_fusion
  11.0 0.5 multiply_convert_fusion.1
  11.5 0.2 fusion.26
  11.9 0.2 fusion.43
  12.2 0.1 copy.55.steer_ref
  12.4 2.1 %fusion.6 = (f32[2,1,128,512]{3,2,1,0:T(8,128)S(1)}, f32[2,1,128,512]{3,2,1,0:T(8,128)S(1)}) fusion(s32[512]{0:T(512)S(1)} %iota_add_fusion, s32[2,128]{1,0:T(2,128)S(1)} %add_multiply_fusion), kind=kLoop, calls=%fused_computation.29 | loop fusion | flops 1835008 | bytes 1051648 | tf_op jit(solution)/shard_map/cos | solution.py:30
  14.6 3.8 %collective-permute-done = bf16[1,2,1,8,64,256]{5,4,3,2,1,0:T(8,128)(2,1)S(1)} collective-permute-done((bf16[1,2,1,8,64,256]{5,4,3,2,1,0:T(8,128)(2,1)}, bf16[1,2,1,8,64,256]{5,4,3,2,1,0:T(8,128)(2,1)S(1)}, u32[]{:S(2)}, u32[]{:S(2)}) %collective-permute-start) | collective-permute-done | bytes 524320 | tf_op jit(solution)/shard_map/ppermute | solution.py:25
  18.6 2.3 %image.2 = (bf16[2,4,4,32,256]{4,3,2,1,0:T(8,128)(2,1)S(1)}, bf16[2,4,4,32,256]{4,3,2,1,0:T(8,128)(2,1)S(1)}) custom-call(bf16[2,4,4,64,256]{4,3,2,1,0:T(8,128)(2,1)S(1)} %pad_maximum_fusion.data_ref, bf16[256,256]{1,0:T(8,128)(2,1)S(1)} %copy.54.steer_ref, bf16[1,128,256]{2,1,0:T(8,128)(2,1)S(1)} %pad_maximum_fusion.5.interp_ref, ...), custom_call_target="tpu_custom_call" | custom-call | flops 402653184 | bytes 2621440 | tf_op jit(solution)/shard_map/image/pallas_call | solution.py:247
  20.9 0.2 collective-permute-done.4
  21.3 2.3 %image.3 = (bf16[2,4,4,32,256]{4,3,2,1,0:T(8,128)(2,1)S(1)}, bf16[2,4,4,32,256]{4,3,2,1,0:T(8,128)(2,1)S(1)}) custom-call(bf16[2,4,4,64,256]{4,3,2,1,0:T(8,128)(2,1)S(1)} %pad_maximum_fusion.2.data_ref, bf16[256,256]{1,0:T(8,128)(2,1)S(1)} %copy.55.steer_ref, bf16[1,128,256]{2,1,0:T(8,128)(2,1)S(1)} %pad_maximum_fusion.5.interp_ref, ...), custom_call_target="tpu_custom_call" | custom-call | flops 402653184 | bytes 2621440 | tf_op jit(solution)/shard_map/image/pallas_call | solution.py:247
  23.7 0.3 collective-permute-start.5
  24.2 1.8 %collective-permute-start.8 = (bf16[1,8,32,256]{3,2,1,0:T(8,128)(2,1)S(1)}, bf16[1,8,32,256]{3,2,1,0:T(8,128)(2,1)S(1)}, u32[]{:S(2)}, u32[]{:S(2)}) collective-permute-start(bf16[1,8,32,256]{3,2,1,0:T(8,128)(2,1)S(1)} %get-tuple-element.41), channel_id=1, source_target_pairs={{0,16},{8,24},{16,0},{24,8},{1,17},{9,25},{17,1},{25,9},{2,18},{10... | collective-permute-start | bytes 393224 | tf_op jit(solution)/shard_map/ppermute | solution.py:25
  26.1 0.3 collective-permute-start.2
  26.5 1.8 %collective-permute-start.10 = (bf16[2,4,32,256]{3,2,1,0:T(8,128)(2,1)S(1)}, bf16[2,4,32,256]{3,2,1,0:T(8,128)(2,1)S(1)}, u32[]{:S(2)}, u32[]{:S(2)}) collective-permute-start(bf16[2,4,32,256]{3,2,1,0:T(8,128)(2,1)S(1)} %fusion.10), channel_id=1, source_target_pairs={{0,1},{1,0},{2,3},{3,2},{4,5},{5,4},{6,7},{7,6},{8,9},{9,8},{10,11... | collective-permute-start | bytes 393224 | tf_op jit(solution)/shard_map/ppermute | solution.py:25
  28.4 0.3 collective-permute-start.6
  28.8 1.8 %collective-permute-done.8 = bf16[1,8,32,256]{3,2,1,0:T(8,128)(2,1)S(1)} collective-permute-done((bf16[1,8,32,256]{3,2,1,0:T(8,128)(2,1)S(1)}, bf16[1,8,32,256]{3,2,1,0:T(8,128)(2,1)S(1)}, u32[]{:S(2)}, u32[]{:S(2)}) %collective-permute-start.8) | collective-permute-done | bytes 131104 | tf_op jit(solution)/shard_map/ppermute | solution.py:25
  30.6 1.9 %collective-permute-start.9 = (bf16[1,4,32,256]{3,2,1,0:T(8,128)(2,1)S(1)}, bf16[1,4,32,256]{3,2,1,0:T(8,128)(2,1)S(1)}, u32[]{:S(2)}, u32[]{:S(2)}) collective-permute-start(bf16[1,4,32,256]{3,2,1,0:T(8,128)(2,1)S(1)} %fusion.31), channel_id=1, source_target_pairs={{0,2},{1,3},{2,0},{3,1},{4,6},{5,7},{6,4},{7,5},{8,10},{9,11},{10,... | collective-permute-start | bytes 196616 | tf_op jit(solution)/shard_map/ppermute | solution.py:25
  32.5 0.2 collective-permute-done.2
  32.7 1.7 %collective-permute-start.3 = (bf16[1,4,32,256]{3,2,1,0:T(8,128)(2,1)S(1)}, bf16[1,4,32,256]{3,2,1,0:T(8,128)(2,1)S(1)}, u32[]{:S(2)}, u32[]{:S(2)}) collective-permute-start(bf16[1,4,32,256]{3,2,1,0:T(8,128)(2,1)S(1)} %fusion.29), channel_id=1, source_target_pairs={{0,2},{1,3},{2,0},{3,1},{4,6},{5,7},{6,4},{7,5},{8,10},{9,11},{10,... | collective-permute-start | bytes 196616 | tf_op jit(solution)/shard_map/ppermute | solution.py:25
  34.4 1.6 %collective-permute-start.11 = (bf16[1,4,32,256]{3,2,1,0:T(8,128)(2,1)S(1)}, bf16[1,4,32,256]{3,2,1,0:T(8,128)(2,1)S(1)}, u32[]{:S(2)}, u32[]{:S(2)}) collective-permute-start(bf16[1,4,32,256]{3,2,1,0:T(8,128)(2,1)S(1)} %fusion.32), channel_id=1, source_target_pairs={{0,16},{8,24},{16,0},{24,8},{1,17},{9,25},{17,1},{25,9},{2,18},{10... | collective-permute-start | bytes 196616 | tf_op jit(solution)/shard_map/ppermute | solution.py:25
  36.0 0.6 %collective-permute-start.7 = (bf16[1,4,32,256]{3,2,1,0:T(8,128)(2,1)S(1)}, bf16[1,4,32,256]{3,2,1,0:T(8,128)(2,1)S(1)}, u32[]{:S(2)}, u32[]{:S(2)}) collective-permute-start(bf16[1,4,32,256]{3,2,1,0:T(8,128)(2,1)S(1)} %fusion.30), channel_id=1, source_target_pairs={{0,16},{8,24},{16,0},{24,8},{1,17},{9,25},{17,1},{25,9},{2,18},{10... | collective-permute-start | bytes 196616 | tf_op jit(solution)/shard_map/ppermute | solution.py:25
  36.6 2.1 %collective-permute-done.11 = bf16[1,4,32,256]{3,2,1,0:T(8,128)(2,1)S(1)} collective-permute-done((bf16[1,4,32,256]{3,2,1,0:T(8,128)(2,1)S(1)}, bf16[1,4,32,256]{3,2,1,0:T(8,128)(2,1)S(1)}, u32[]{:S(2)}, u32[]{:S(2)}) %collective-permute-start.11) | collective-permute-done | bytes 65568 | tf_op jit(solution)/shard_map/ppermute | solution.py:25
  38.8 1.5 %collective-permute-done.7 = bf16[1,4,32,256]{3,2,1,0:T(8,128)(2,1)S(1)} collective-permute-done((bf16[1,4,32,256]{3,2,1,0:T(8,128)(2,1)S(1)}, bf16[1,4,32,256]{3,2,1,0:T(8,128)(2,1)S(1)}, u32[]{:S(2)}, u32[]{:S(2)}) %collective-permute-start.7) | collective-permute-done | bytes 65568 | tf_op jit(solution)/shard_map/ppermute | solution.py:25
  40.4 2.6 %collective-permute-start.12 = (bf16[2,4,32,256]{3,2,1,0:T(8,128)(2,1)S(1)}, bf16[2,4,32,256]{3,2,1,0:T(8,128)(2,1)S(1)}, u32[]{:S(2)}, u32[]{:S(2)}) collective-permute-start(bf16[2,4,32,256]{3,2,1,0:T(8,128)(2,1)S(1)} %pad_maximum_fusion.4), channel_id=1, source_target_pairs={{0,4},{1,5},{2,6},{3,7},{4,0},{5,1},{6,2},{7,3},{8,12},{9,13},{10,... | collective-permute-start | bytes 393224 | tf_op jit(solution)/shard_map/ppermute | solution.py:25
  43.1 4.5 %collective-permute-done.12 = bf16[2,4,32,256]{3,2,1,0:T(8,128)(2,1)S(1)} collective-permute-done((bf16[2,4,32,256]{3,2,1,0:T(8,128)(2,1)S(1)}, bf16[2,4,32,256]{3,2,1,0:T(8,128)(2,1)S(1)}, u32[]{:S(2)}, u32[]{:S(2)}) %collective-permute-start.12) | collective-permute-done | bytes 131104 | tf_op jit(solution)/shard_map/ppermute | solution.py:25
  47.6 0.7 %copy.68 = bf16[8,32,256]{2,0,1:T(8,128)(2,1)} copy(bf16[8,32,256]{2,1,0:T(8,128)(2,1)S(1)} %bitcast.145) | data formatting | bytes 262144 | tf_op jit(solution)/shard_map/convert_element_type | solution.py:416
  (81 shorter events, 2.2 us)
Async XLA Ops:
  0.0 6.3 %copy-start.1 = (bf16[2,128]{1,0:T(2,128)(2,1)S(1)}, bf16[2,128]{1,0:T(2,128)(2,1)}, u32[]{:S(2)}) copy-start(bf16[2,128]{1,0:T(2,128)(2,1)} %chirp_ref.2) | copy-start | bytes 1540
  0.0 6.3 %copy-start = (bf16[64,64,256]{2,1,0:T(8,128)(2,1)S(1)}, bf16[64,64,256]{2,1,0:T(8,128)(2,1)}, u32[]{:S(2)}) copy-start(bf16[64,64,256]{2,1,0:T(8,128)(2,1)} %refs_0_.1) | copy-start | bytes 6291460
  3.3 6.2 %copy-start.5 = (s32[1,8]{1,0:T(1,128)S(1)}, s32[1,8]{1,0:T(1,128)}, u32[]{:S(2)}) copy-start(s32[1,8]{1,0:T(1,128)} %param.9) | copy-start | bytes 100
  3.3 6.8 %copy-start.3 = (s32[2,2,128,8]{2,3,1,0:T(8,128)S(1)}, s32[2,2,128,8]{2,3,1,0:T(8,128)}, u32[]{:S(2)}) copy-start(s32[2,2,128,8]{2,3,1,0:T(8,128)} %param.8) | copy-start | bytes 49156
  3.3 7.3 %copy-start.4 = (f32[8]{0:T(128)S(1)}, f32[8]{0:T(128)}, u32[]{:S(2)}) copy-start(f32[8]{0:T(128)} %constant.177.clone) | copy-start | bytes 100
  3.3 15.2 %collective-permute-start = (bf16[1,2,1,8,64,256]{5,4,3,2,1,0:T(8,128)(2,1)}, bf16[1,2,1,8,64,256]{5,4,3,2,1,0:T(8,128)(2,1)S(1)}, u32[]{:S(2)}, u32[]{:S(2)}) collective-permute-start(bf16[1,2,1,8,64,256]{5,4,3,2,1,0:T(8,128)(2,1)} %get-tuple-element.17), channel_id=1, source_target_pairs={{0,1},{1,0},{2,3},{3,2},{4,5},{5,4},{6,7},{7,6},{8,9},{9,8},{10,11... | collective-permute-start | bytes 1572872 | tf_op jit(solution)/shard_map/ppermute | solution.py:25
  7.7 13.4 %collective-permute-start.4 = (bf16[1,1,2,8,64,256]{5,4,3,2,1,0:T(8,128)(2,1)S(1)}, bf16[1,1,2,8,64,256]{5,4,3,2,1,0:T(8,128)(2,1)S(1)}, u32[]{:S(2)}, u32[]{:S(2)}) collective-permute-start(bf16[1,1,2,8,64,256]{5,4,3,2,1,0:T(8,128)(2,1)S(1)} %get-tuple-element.22), channel_id=1, source_target_pairs={{0,2},{1,3},{2,0},{3,1},{4,6},{5,7},{6,4},{7,5},{8,10},{9,11},{10,... | collective-permute-start | bytes 1572872 | tf_op jit(solution)/shard_map/ppermute | solution.py:25
  12.1 6.4 %copy-start.2 = (bf16[1,2,1,8,64,256]{5,4,3,2,1,0:T(8,128)(2,1)S(1)}, bf16[1,2,1,8,64,256]{5,4,3,2,1,0:T(8,128)(2,1)}, u32[]{:S(2)}) copy-start(bf16[1,2,1,8,64,256]{5,4,3,2,1,0:T(8,128)(2,1)} %get-tuple-element.15) | copy-start | bytes 1572868
  20.9 3.2 %collective-permute-start.1 = (bf16[2,4,4,32,256]{4,3,2,1,0:T(8,128)(2,1)S(1)}, bf16[2,4,4,32,256]{4,3,2,1,0:T(8,128)(2,1)S(1)}, u32[]{:S(2)}, u32[]{:S(2)}) collective-permute-start(bf16[2,4,4,32,256]{4,3,2,1,0:T(8,128)(2,1)S(1)} %get-tuple-element.19), channel_id=1, source_target_pairs={{0,8},{8,0},{16,24},{24,16},{1,9},{9,1},{17,25},{25,17},{2,10},{10... | collective-permute-start | bytes 1572872 | tf_op jit(solution)/shard_map/ppermute | solution.py:25
  23.7 2.7 %collective-permute-start.5 = (bf16[2,4,4,32,256]{4,3,2,1,0:T(8,128)(2,1)S(1)}, bf16[2,4,4,32,256]{4,3,2,1,0:T(8,128)(2,1)S(1)}, u32[]{:S(2)}, u32[]{:S(2)}) collective-permute-start(bf16[2,4,4,32,256]{4,3,2,1,0:T(8,128)(2,1)S(1)} %get-tuple-element.24), channel_id=1, source_target_pairs={{0,8},{8,0},{16,24},{24,16},{1,9},{9,1},{17,25},{25,17},{2,10},{10... | collective-permute-start | bytes 1572872 | tf_op jit(solution)/shard_map/ppermute | solution.py:25
  24.2 6.4 %collective-permute-start.8 = (bf16[1,8,32,256]{3,2,1,0:T(8,128)(2,1)S(1)}, bf16[1,8,32,256]{3,2,1,0:T(8,128)(2,1)S(1)}, u32[]{:S(2)}, u32[]{:S(2)}) collective-permute-start(bf16[1,8,32,256]{3,2,1,0:T(8,128)(2,1)S(1)} %get-tuple-element.41), channel_id=1, source_target_pairs={{0,16},{8,24},{16,0},{24,8},{1,17},{9,25},{17,1},{25,9},{2,18},{10... | collective-permute-start | bytes 393224 | tf_op jit(solution)/shard_map/ppermute | solution.py:25
  26.1 6.6 %collective-permute-start.2 = (bf16[1,8,32,256]{3,2,1,0:T(8,128)(2,1)S(1)}, bf16[1,8,32,256]{3,2,1,0:T(8,128)(2,1)S(1)}, u32[]{:S(2)}, u32[]{:S(2)}) collective-permute-start(bf16[1,8,32,256]{3,2,1,0:T(8,128)(2,1)S(1)} %get-tuple-element.35), channel_id=1, source_target_pairs={{0,16},{8,24},{16,0},{24,8},{1,17},{9,25},{17,1},{25,9},{2,18},{10... | collective-permute-start | bytes 393224 | tf_op jit(solution)/shard_map/ppermute | solution.py:25
  26.5 7.9 %collective-permute-start.10 = (bf16[2,4,32,256]{3,2,1,0:T(8,128)(2,1)S(1)}, bf16[2,4,32,256]{3,2,1,0:T(8,128)(2,1)S(1)}, u32[]{:S(2)}, u32[]{:S(2)}) collective-permute-start(bf16[2,4,32,256]{3,2,1,0:T(8,128)(2,1)S(1)} %fusion.10), channel_id=1, source_target_pairs={{0,1},{1,0},{2,3},{3,2},{4,5},{5,4},{6,7},{7,6},{8,9},{9,8},{10,11... | collective-permute-start | bytes 393224 | tf_op jit(solution)/shard_map/ppermute | solution.py:25
  28.4 7.6 %collective-permute-start.6 = (bf16[2,4,32,256]{3,2,1,0:T(8,128)(2,1)S(1)}, bf16[2,4,32,256]{3,2,1,0:T(8,128)(2,1)S(1)}, u32[]{:S(2)}, u32[]{:S(2)}) collective-permute-start(bf16[2,4,32,256]{3,2,1,0:T(8,128)(2,1)S(1)} %get-tuple-element.29), channel_id=1, source_target_pairs={{0,1},{1,0},{2,3},{3,2},{4,5},{5,4},{6,7},{7,6},{8,9},{9,8},{10,11... | collective-permute-start | bytes 393224 | tf_op jit(solution)/shard_map/ppermute | solution.py:25
  30.6 6.0 %collective-permute-start.9 = (bf16[1,4,32,256]{3,2,1,0:T(8,128)(2,1)S(1)}, bf16[1,4,32,256]{3,2,1,0:T(8,128)(2,1)S(1)}, u32[]{:S(2)}, u32[]{:S(2)}) collective-permute-start(bf16[1,4,32,256]{3,2,1,0:T(8,128)(2,1)S(1)} %fusion.31), channel_id=1, source_target_pairs={{0,2},{1,3},{2,0},{3,1},{4,6},{5,7},{6,4},{7,5},{8,10},{9,11},{10,... | collective-permute-start | bytes 196616 | tf_op jit(solution)/shard_map/ppermute | solution.py:25
  32.7 6.1 %collective-permute-start.3 = (bf16[1,4,32,256]{3,2,1,0:T(8,128)(2,1)S(1)}, bf16[1,4,32,256]{3,2,1,0:T(8,128)(2,1)S(1)}, u32[]{:S(2)}, u32[]{:S(2)}) collective-permute-start(bf16[1,4,32,256]{3,2,1,0:T(8,128)(2,1)S(1)} %fusion.29), channel_id=1, source_target_pairs={{0,2},{1,3},{2,0},{3,1},{4,6},{5,7},{6,4},{7,5},{8,10},{9,11},{10,... | collective-permute-start | bytes 196616 | tf_op jit(solution)/shard_map/ppermute | solution.py:25
  34.4 4.3 %collective-permute-start.11 = (bf16[1,4,32,256]{3,2,1,0:T(8,128)(2,1)S(1)}, bf16[1,4,32,256]{3,2,1,0:T(8,128)(2,1)S(1)}, u32[]{:S(2)}, u32[]{:S(2)}) collective-permute-start(bf16[1,4,32,256]{3,2,1,0:T(8,128)(2,1)S(1)} %fusion.32), channel_id=1, source_target_pairs={{0,16},{8,24},{16,0},{24,8},{1,17},{9,25},{17,1},{25,9},{2,18},{10... | collective-permute-start | bytes 196616 | tf_op jit(solution)/shard_map/ppermute | solution.py:25
  36.0 4.3 %collective-permute-start.7 = (bf16[1,4,32,256]{3,2,1,0:T(8,128)(2,1)S(1)}, bf16[1,4,32,256]{3,2,1,0:T(8,128)(2,1)S(1)}, u32[]{:S(2)}, u32[]{:S(2)}) collective-permute-start(bf16[1,4,32,256]{3,2,1,0:T(8,128)(2,1)S(1)} %fusion.30), channel_id=1, source_target_pairs={{0,16},{8,24},{16,0},{24,8},{1,17},{9,25},{17,1},{25,9},{2,18},{10... | collective-permute-start | bytes 196616 | tf_op jit(solution)/shard_map/ppermute | solution.py:25
  40.4 7.2 %collective-permute-start.12 = (bf16[2,4,32,256]{3,2,1,0:T(8,128)(2,1)S(1)}, bf16[2,4,32,256]{3,2,1,0:T(8,128)(2,1)S(1)}, u32[]{:S(2)}, u32[]{:S(2)}) collective-permute-start(bf16[2,4,32,256]{3,2,1,0:T(8,128)(2,1)S(1)} %pad_maximum_fusion.4), channel_id=1, source_target_pairs={{0,4},{1,5},{2,6},{3,7},{4,0},{5,1},{6,2},{7,3},{8,12},{9,13},{10,... | collective-permute-start | bytes 393224 | tf_op jit(solution)/shard_map/ppermute | solution.py:25
